TPU v7x, 128 devices: a whole 4x4x4 slice. The times are simulated.
128 devices in a mesh: pre: 4 (over z), dec: 32 (over y, x, core).
Axes of the slice: x: 4, y: 4, z: 4, core: 2. Of those that a mesh axis runs over, the one named last changes fastest.
Arguments:
- hidden: bfloat16 [32768, 7168], P(('pre', 'dec')), may hold values from -6 to 6
- w_down: bfloat16 [7168, 576], replicated, may hold values from -0.0625 to 0.0625
- kv_gain: float32 [512], replicated, may hold values from 0.25 to 1.75
- query_latent: bfloat16 [4, 8, 128, 512], P(None, None, 'pre')
- query_rope: bfloat16 [4, 8, 128, 64], P(None, None, 'pre'), may hold values from -9 to 9
- w_up_value: bfloat16 [128, 512, 128], P('pre'), may hold values from -0.25 to 0.25
- request_rows: int32 [4], replicated, may hold values from 1 to 16384, as said below
- row_request: int32 [8], replicated, may hold values from 0 to 3, as said below
- step_position: int32 [4, 8], replicated, may hold values from 1 to 16384, as said below
- destination: int32 [4096], replicated, may hold values from 0 to 4095, as said below
Outputs:
- attention_out: bfloat16 [4, 8, 16384], P(None, None, 'pre')
- latent_cache: bfloat16 [32768, 576], P('dec')
Inputs may be any that keep to these rules, and one draw needn't show every extreme that they name: `request_rows`: the counts sum to 32768; each is at least a tenth of 8192; one request holds exactly 16384 rows. `row_request`: every request has some decode row. `step_position`: the 4 positions of a row are consecutive and at most its request's row count. `destination`: a permutation of the blocks; cache block c is held by owner c // 128; the blocks of prefill device g * 32 + e go to slots g * 32 to g * 32 + 31 of their owners; each owner receives exactly 32 blocks from each group, and each prefill device sends at most 2 blocks to one owner, exactly 2 to one of them.
All inputs are finite; a program needn't handle non-finite values.
Results may differ from a plain program's by a relative error of at most 0.008.
The roundings to bfloat16 on the way count: a program that leaves them out, or rounds other values in their place, can miss the bound.
Values may be sent and summed in bfloat16 or wider, within the bound.
No kernel may reach another device: no remote copies, remote signals or barrier semaphores. Data moves between devices by JAX's collectives and lax.ppermute only.
A program may use at most 192 MiB of HBM per device.

v0:
```python
import math

import jax
import jax.numpy as jnp
from jax import lax
from jax.sharding import PartitionSpec as P

LAT = 512
MOST = 2


score_scale = 0.07216878364870323
mask_value = -1e30
norm_eps = 1e-06


def combined_all(value, axis, combine):
    everything = jax.tree.map(lambda part: lax.all_gather(part, axis), value)
    initial = jax.tree.map(lambda part: part[0], everything)

    def step(k, so_far):
        return combine(so_far, jax.tree.map(lambda part: part[k], everything))

    return lax.fori_loop(1, lax.axis_size(axis), step, initial)


def locate(lengths, row_ids):
    row_ends = jnp.cumsum(lengths)
    row_starts = row_ends - lengths
    request_of = jnp.sum((row_ids[:, None] >= row_ends[None, :]).astype(jnp.int32), axis=1)
    onehot = request_of[:, None] == jnp.arange(lengths.shape[0], dtype=jnp.int32)[None, :]
    first_rows = jnp.sum(jnp.where(onehot, row_starts[None, :], 0), axis=1)
    return (request_of, row_ids - first_rows)


def rotate(rotary, places):
    half_width = rotary.shape[-1] // 2
    pair_index = jnp.arange(half_width).astype(jnp.float32)
    frequency = jnp.exp(pair_index * (-2.0 * math.log(10000.0) / rotary.shape[-1]))
    angles = places.astype(jnp.float32)[:, None] * frequency[None, :]
    cosine = jnp.cos(angles)
    sine_part = jnp.sin(angles)
    first_half = rotary[:, :half_width]
    second_half = rotary[:, half_width:]
    return jnp.concatenate(
        [
            first_half * cosine - second_half * sine_part,
            second_half * cosine + first_half * sine_part,
        ],
        axis=1,
    )


def produce(hidden, w_down, kv_gain, places):
    raw_rows = jnp.dot(hidden, w_down, preferred_element_type=jnp.float32)
    latent_width = kv_gain.shape[0]
    latent = raw_rows[:, :latent_width]
    inverse_rms = lax.rsqrt(jnp.mean(latent * latent, axis=1, keepdims=True) + norm_eps)
    normed = latent * inverse_rms * kv_gain[None, :]
    return jnp.concatenate([normed, rotate(raw_rows[:, latent_width:], places)], axis=1).astype(
        jnp.bfloat16
    )


def block_ranks(owner_ids):
    count = owner_ids.shape[-1]
    same_owner = owner_ids[..., :, None] == owner_ids[..., None, :]
    earlier = jnp.arange(count)[None, :] < jnp.arange(count)[:, None]
    return jnp.sum((same_owner & earlier).astype(jnp.int32), axis=-1)


def pack_blocks(blocks, owner_ids, owner_count, capacity):
    count = owner_ids.shape[0]
    ranks_here = block_ranks(owner_ids)
    select = (
        owner_ids[None, None, :] == jnp.arange(owner_count, dtype=jnp.int32)[:, None, None]
    ) & (ranks_here[None, None, :] == jnp.arange(capacity, dtype=jnp.int32)[None, :, None])
    select = select.reshape(owner_count * capacity, count).astype(jnp.bfloat16)
    packed = jnp.dot(select, blocks.reshape(count, -1), preferred_element_type=jnp.float32)
    return packed.astype(jnp.bfloat16).reshape((owner_count, capacity) + blocks.shape[1:])


def place_blocks(arrived, owner_ids, slot_ids, owner_index, slot_count, capacity):
    ranks_here = block_ranks(owner_ids)
    arrives = owner_ids == owner_index
    target = (
        (slot_ids[:, :, None] == jnp.arange(slot_count, dtype=jnp.int32)[None, None, :])
        & arrives[:, :, None]
    ).astype(jnp.float32)
    by_rank = (
        ranks_here[:, :, None] == jnp.arange(capacity, dtype=jnp.int32)[None, None, :]
    ).astype(jnp.float32)
    placing = (
        jnp.einsum("sjt,sjk->tsk", target, by_rank).reshape(slot_count, -1).astype(jnp.bfloat16)
    )
    sources = arrived.shape[0] * arrived.shape[1]
    placed = jnp.dot(placing, arrived.reshape(sources, -1), preferred_element_type=jnp.float32)
    return placed.astype(jnp.bfloat16)


def attend(queries, context, context_rows, request_rows, row_request, step_position):
    request_of, places = locate(request_rows, context_rows)
    latent_rows = context[:, :LAT]
    maxima = []
    totals = []
    sums = []
    for step_index in range(queries.shape[0]):
        batch_rows, head_count, row_width = queries.shape[1:]
        flat_query = queries[step_index].reshape(batch_rows * head_count, row_width)
        scores = lax.dot_general(
            flat_query, context, (((1,), (1,)), ((), ())), preferred_element_type=jnp.float32
        )
        scores = scores.reshape(batch_rows, head_count, -1) * score_scale
        visible = (request_of[None, :] == row_request[:, None]) & (
            places[None, :] < step_position[step_index][:, None]
        )
        masked = jnp.where(visible[:, None, :], scores, mask_value)
        row_peak = jnp.max(masked, axis=2)
        weights = jnp.where(visible[:, None, :], jnp.exp(masked - row_peak[:, :, None]), 0.0)
        maxima.append(row_peak)
        totals.append(jnp.sum(weights, axis=2))
        sums.append(
            jnp.einsum(
                "bht,tl->bhl",
                weights.astype(jnp.bfloat16),
                latent_rows,
                preferred_element_type=jnp.float32,
            )
        )
    return (jnp.stack(maxima), jnp.stack(totals), jnp.stack(sums))


def combine(first_part, second_part):
    first_peak, first_total, first_sum = first_part
    second_peak, second_total, second_sum = second_part
    joint_peak = jnp.maximum(first_peak, second_peak)
    first_factor = jnp.exp(first_peak - joint_peak)
    second_factor = jnp.exp(second_peak - joint_peak)
    joint_total = first_total * first_factor + second_total * second_factor
    joint_sum = first_sum * first_factor[..., None] + second_sum * second_factor[..., None]
    return (joint_peak, joint_total, joint_sum)


def per_device(
    hidden,
    w_down,
    kv_gain,
    query_latent,
    query_rope,
    w_up_value,
    request_rows,
    row_request,
    step_position,
    destination,
):
    groups = lax.axis_size("pre")
    owners = lax.axis_size("dec")
    group_index = lax.axis_index("pre")
    owner_index = lax.axis_index("dec")
    cache_blocks = groups * owners
    local_rows = hidden.shape[0]
    block_rows = local_rows // owners
    row_width = w_down.shape[1]
    first_row = (group_index * owners + owner_index) * local_rows
    rows_here = first_row + jnp.arange(local_rows, dtype=jnp.int32)
    unused_ids, places = locate(request_rows, rows_here)
    produced = produce(hidden, w_down, kv_gain, places)
    queries = jnp.concatenate([query_latent, query_rope], axis=3)
    dest_grid = destination.reshape(groups, owners, owners)
    row_grid = lax.dynamic_index_in_dim(dest_grid, group_index, 0, keepdims=False)
    own_dest = lax.dynamic_index_in_dim(row_grid, owner_index, 0, keepdims=False)
    packed = pack_blocks(
        produced.reshape(owners, block_rows, row_width), own_dest // cache_blocks, owners, MOST
    )
    arrived = lax.all_to_all(packed, "dec", split_axis=0, concat_axis=0, tiled=True)
    quarter = place_blocks(
        arrived,
        row_grid // cache_blocks,
        row_grid % cache_blocks - group_index * owners,
        owner_index,
        owners,
        MOST,
    )
    kv_cache = lax.all_gather(
        quarter.reshape(owners * block_rows, row_width), "pre", axis=0, tiled=True
    )
    total_blocks = destination.shape[0]
    inverse = (
        jnp.zeros((total_blocks,), jnp.int32)
        .at[destination]
        .set(jnp.arange(total_blocks, dtype=jnp.int32))
    )
    source_blocks = lax.dynamic_slice_in_dim(inverse, owner_index * cache_blocks, cache_blocks)
    cache_rows = (
        source_blocks[:, None] * block_rows + jnp.arange(block_rows, dtype=jnp.int32)[None, :]
    ).reshape(-1)
    partials = attend(queries, kv_cache, cache_rows, request_rows, row_request, step_position)
    weights_up = w_up_value.astype(jnp.float32)
    maxima, totals, sums = partials
    maxima, totals, sums = combined_all((maxima, totals, sums), "dec", combine)
    result = jnp.einsum(
        "sbhl,hlv->sbhv", sums / totals[..., None], weights_up, precision=lax.Precision.HIGHEST
    )
    attention_out = result.reshape(result.shape[0], result.shape[1], -1).astype(jnp.bfloat16)
    return (attention_out, kv_cache)


def solution(mesh):
    return jax.shard_map(
        per_device,
        mesh=mesh,
        in_specs=(
            P(("pre", "dec"), None),
            P(),
            P(),
            P(None, None, "pre", None),
            P(None, None, "pre", None),
            P("pre", None, None),
            P(),
            P(),
            P(),
            P(),
        ),
        out_specs=(P(None, None, "pre"), P("dec", None)),
        check_vma=False,
    )
```

profile of v0, /device:TPU:1, one launch (start us, length us, event | category | flops | bytes accessed | tf_op | source)
XLA Modules:
  0.0 388.0 jit_solution(18281373056110278479)
XLA Ops:
  10.0 6.8 %fusion.79 = f32[256,576]{0,1:T(8,128)S(1)} fusion(bf16[256,7168]{1,0:T(8,128)(2,1)} %param.12, bf16[7168,576]{0,1:T(8,128)(2,1)} %param.13), kind=kOutput, calls=%fused_computation.150 | convolution fusion | flops 2113929216 | bytes 12517376 | tf_op jit(solution)/shard_map/dot_general | solution.py:55
  19.4 8.6 %all-to-all-start = ((bf16[32,2,8,576]{3,2,1,0:T(8,128)(2,1)}), bf16[32,2,8,576]{3,2,1,0:T(8,128)(2,1)S(1)}, u32[]{:S(2)}, u32[]{:S(2)}) async-start(bf16[32,2,8,576]{3,2,1,0:T(8,128)(2,1)} %reshape.537), calls=%async_computation | async-start | bytes 1310720 | tf_op jit(solution)/shard_map/all_to_all | solution.py:175
  29.3 11.5 %all-to-all-done = bf16[32,2,8,576]{3,2,1,0:T(8,128)(2,1)S(1)} async-done(((bf16[32,2,8,576]{3,2,1,0:T(8,128)(2,1)}), bf16[32,2,8,576]{3,2,1,0:T(8,128)(2,1)S(1)}, u32[]{:S(2)}, u32[]{:S(2)}) %all-to-all-start) | async-done | bytes 589856 | tf_op jit(solution)/shard_map/all_to_all | solution.py:175
  42.9 15.5 %scatter_custom_fusion = s32[4096]{0:T(1024)S(1)} fusion(s32[4096]{0:T(1024)S(1)} %compare_select_fusion, s32[4096]{0:T(1024)S(1)} %iota.69, s32[]{:T(128)} %constant.116.clone.1), kind=kCustom, calls=%fused_computation.113 | custom fusion | bytes 16388 | tf_op jit(solution)/shard_map/scatter | solution.py:191
  59.2 8.3 %all-gather.6.cloned.1.call-done = bf16[1024,576]{0,1:T(8,128)(2,1)} async-done(((bf16[256,576]{0,1:T(8,128)(2,1)}), bf16[1024,576]{0,1:T(8,128)(2,1)}) %all-gather.6.cloned.1.call-update) | async-done | bytes 1179664 | tf_op jit(solution)/shard_map/all_gather | solution.py:184
  77.2 26.7 %all-gather = f32[128,8,32]{2,1,0:T(8,128)S(1)} all-gather(f32[4,8,32]{2,1,0:T(8,128)S(1)} %pad_maximum_fusion.2), channel_id=2, replica_groups=mesh['pre'=4,'dec'=32] {'dec'}, dimensions={0}, use_global_device_ids=true | all-gather | bytes 135168 | tf_op jit(solution)/shard_map/all_gather | solution.py:18
  107.4 24.4 %all-gather.1 = f32[128,8,32]{2,1,0:T(8,128)S(1)} all-gather(f32[4,8,32]{2,1,0:T(8,128)S(1)} %pad_maximum_fusion.3), channel_id=3, replica_groups=mesh['pre'=4,'dec'=32] {'dec'}, dimensions={0}, use_global_device_ids=true | all-gather | bytes 135168 | tf_op jit(solution)/shard_map/all_gather | solution.py:18
  132.6 149.2 %all-gather.8.cloned.1.call-done = f32[128,8,32,512]{3,2,1,0:T(8,128)} async-done(((f32[4,8,32,512]{3,2,1,0:T(8,128)}), f32[128,8,32,512]{3,2,1,0:T(8,128)}) %all-gather.8.cloned.1.call-update) | async-done | bytes 67108880 | tf_op jit(solution)/shard_map/all_gather | solution.py:18
  283.7 90.4 %while.19 = (s32[]{:T(128)}, f32[4,8,32]{2,1,0:T(8,128)S(1)}, f32[4,8,32]{2,1,0:T(8,128)S(1)}, f32[4,8,32,512]{3,2,1,0:T(8,128)S(1)}, f32[32,4,8,32]{3,2,1,0:T(8...) while((s32[]{:T(128)}, f32[4,8,32]{2,1,0:T(8,128)S(1)}, ...), condition=%wide.region_18.19_spmd, body=%wide.region_17.18_spmd.sunk | while | flops 1579013 | bytes 6332559 | solution.py:24
  284.5 2.1 fusion.89
  287.4 2.1 fusion.89
  290.3 2.1 fusion.89
  293.2 2.1 fusion.89
  296.1 2.1 fusion.89
  299.0 2.1 fusion.89
  302.0 2.1 fusion.89
  304.9 2.1 fusion.89
  307.8 2.1 fusion.89
  310.7 2.1 fusion.89
  313.6 2.1 fusion.89
  316.5 2.1 fusion.89
  319.5 2.1 fusion.89
  348.6 2.1 fusion.89
  376.3 3.1 fusion.19
  (165 shorter events, 88.5 us)
Async XLA Ops:
  10.0 7.1 %copy-start.21 = (f32[512]{0:T(512)S(1)}, f32[512]{0:T(512)}, u32[]{:S(2)}) copy-start(f32[512]{0:T(512)} %param.14) | copy-start | bytes 6148
  19.4 21.5 %all-to-all-start = ((bf16[32,2,8,576]{3,2,1,0:T(8,128)(2,1)}), bf16[32,2,8,576]{3,2,1,0:T(8,128)(2,1)S(1)}, u32[]{:S(2)}, u32[]{:S(2)}) async-start(bf16[32,2,8,576]{3,2,1,0:T(8,128)(2,1)} %reshape.537), calls=%async_computation | async-start | bytes 1310720 | tf_op jit(solution)/shard_map/all_to_all | solution.py:175
  28.0 39.6 %all-gather.6.cloned.1.call-start = ((), (), s32[]{:S(2)}) async-start(), calls=%async_computation.1 | async-start | bytes 1474560 | tf_op jit(solution)/shard_map/all_gather | solution.py:184
  28.9 14.0 %copy-start.10 = (s32[4096]{0:T(1024)S(1)}, s32[4096]{0:T(1024)}, u32[]{:S(2)}) copy-start(s32[4096]{0:T(1024)} %param.21) | copy-start | bytes 49156
  28.9 30.0 %copy-start.2 = (bf16[4,8,32,512]{3,2,1,0:T(8,128)(2,1)S(1)}, bf16[4,8,32,512]{3,2,1,0:T(8,128)(2,1)}, u32[]{:S(2)}) copy-start(bf16[4,8,32,512]{3,2,1,0:T(8,128)(2,1)} %param.15) | copy-start | bytes 3145732
  41.6 17.4 %copy-start.9 = (bf16[4,8,32,64]{3,2,1,0:T(8,128)(2,1)S(1)}, bf16[4,8,32,64]{3,2,1,0:T(8,128)(2,1)}, u32[]{:S(2)}) copy-start(bf16[4,8,32,64]{3,2,1,0:T(8,128)(2,1)} %param.16) | copy-start | bytes 393220
  41.6 17.5 %copy-start.22 = (s32[4,8]{1,0:T(4,128)S(1)}, s32[4,8]{1,0:T(4,128)}, u32[]{:S(2)}) copy-start(s32[4,8]{1,0:T(4,128)} %param.20) | copy-start | bytes 388
  41.6 17.5 %copy-start.23 = (s32[8]{0:T(128)S(1)}, s32[8]{0:T(128)}, u32[]{:S(2)}) copy-start(s32[8]{0:T(128)} %param.19) | copy-start | bytes 100
  42.8 239.0 %all-gather.8.cloned.1.call-start = ((), (), s32[]{:S(2)}) async-start(), calls=%async_computation.2 | async-start | bytes 69206016 | tf_op jit(solution)/shard_map/all_gather | solution.py:18
  59.0 11.3 %copy-start.6 = (bf16[4,8,32,576]{3,2,1,0:T(8,128)(2,1)}, bf16[4,8,32,576]{3,2,1,0:T(8,128)(2,1)S(1)}, u32[]{:S(2)}) copy-start(bf16[4,8,32,576]{3,2,1,0:T(8,128)(2,1)S(1)} %constant_dynamic-update-slice_fusion) | copy-start | bytes 3538948
  59.2 11.1 %copy-start.11 = (pred[8,1024]{1,0:T(8,128)(4,1)}, pred[8,1024]{1,0:T(8,128)(4,1)S(1)}, u32[]{:S(2)}) copy-start(pred[8,1024]{1,0:T(8,128)(4,1)S(1)} %get-tuple-element.206) | copy-start | bytes 24580
  59.2 11.1 %copy-start.13 = (pred[8,1024]{1,0:T(8,128)(4,1)}, pred[8,1024]{1,0:T(8,128)(4,1)S(1)}, u32[]{:S(2)}) copy-start(pred[8,1024]{1,0:T(8,128)(4,1)S(1)} %get-tuple-element.207) | copy-start | bytes 24580
  67.5 2.1 copy-start.1
  69.6 3.1 copy-start.5
  69.6 3.1 copy-start.19
  70.3 2.9 copy-start.3
  70.3 2.9 copy-start.17
  71.0 2.9 copy-start.15
  71.0 1.7 copy-start.14
  76.4 0.7 copy-start.20
  76.5 29.8 %copy-start.4 = (f32[8,32,1024]{2,1,0:T(8,128)S(1)}, f32[8,32,1024]{2,1,0:T(8,128)}, u32[]{:S(2)}) copy-start(f32[8,32,1024]{2,1,0:T(8,128)} %copy-done.3) | copy-start | bytes 3145732
  103.8 0.8 copy-start.7
  131.8 0.8 copy-start.8
  374.1 2.2 copy-start
  (3 other events, 2.1 us)
Sparse Core Ops, SparseCore 0:
  42.9 24.5 all-gather.5
  76.6 205.1 all-gather.7
where the time goes:
time: 394 us; the launch traced here: 388 us
  waiting for transfers between devices  169 us (43%)
  other arithmetic  97.7 us (25%)
  blocking collectives  51.1 us (13%)
  local copies, waits for them, and re-layouts  28 us (7%)
  matrix products  17.9 us (5%)
  between operations  14.6 us (4%)
  starting transfers between devices  8.67 us (2%)
    all_gather x1, waiting for transfers between devices, combined_all(): everything = jax.tree.map(lambda part: lax.all_gather(part, axis), value)  149 us
    add x31, other arithmetic, combine(): first_sum * first_factor[..., None] + second_sum * second_factor[..., None]  66 us
    all_gather x2, blocking collectives, combined_all(): everything = jax.tree.map(lambda part: lax.all_gather(part, axis), value)  51.1 us
    add x31, other arithmetic, combine(): joint_total = first_total * first_factor + second_total * second_factor  23.6 us
    scatter x1, local copies, waits for them, and re-layouts, per_device(): inverse = jnp.zeros((total_blocks,), jnp.int32).at[destination].set(jnp.a...  15.5 us
    all_to_all x1, waiting for transfers between devices, per_device(): lax.all_to_all(packed, 'dec', split_axis=0, concat_axis=0, tiled=True)  11.5 us
    all_to_all x1, starting transfers between devices, per_device(): lax.all_to_all(packed, 'dec', split_axis=0, concat_axis=0, tiled=True)  8.59 us
    all_gather x1, waiting for transfers between devices, per_device(): lax.all_gather(quarter.reshape(owners * block_rows, row_width), 'pre', ax...  8.33 us
  transfers between devices with their start and end apart: 3, of which 3 were waited for; matrix products, arithmetic and copies ran while one was open for 5% of the time, Pallas kernels for 0%

commit v1 on v0

v1 whole, which is shorter than its diff:
```python
import functools
import math

import jax
import jax.numpy as jnp
import numpy as np
from jax import lax
from jax.experimental import pallas as pl
from jax.experimental.pallas import tpu as pltpu
from jax.sharding import PartitionSpec as P

LAT = 512
ROPE = 64
MOST = 2
PAD = 8
SIDE = 4
CUT_HEADS = 8
DEPTH = 1024

score_scale = 0.07216878364870323
mask_value = -1e30
norm_eps = 1e-06
log2_e = 1.4426950408889634


def frequencies():
    half = ROPE // 2
    pair_index = np.arange(half, dtype=np.float64)
    frequency = np.exp(pair_index * (-2.0 * math.log(10000.0) / ROPE)).astype(np.float32)
    return np.tile(frequency[:, None], (1, 128))


def params(megabytes):
    return pltpu.CompilerParams(vmem_limit_bytes=megabytes * 1024 * 1024)


def produce_kernel(
    owners, lengths_hbm, hidden_hbm, w_hbm, gain_hbm, freq_hbm,
    out_ref, hidden_ref, w_ref, acc_ref, lengths_ref, gain_ref, freq_ref, sems, small_sems,
):
    pieces, rows, depth = hidden_ref.shape
    half = ROPE // 2
    small = [
        pltpu.make_async_copy(source, target, small_sems.at[k])
        for k, (source, target) in enumerate(
            ((lengths_hbm, lengths_ref), (gain_hbm, gain_ref), (freq_hbm, freq_ref))
        )
    ]

    def copies(k):
        columns = pl.ds(pl.multiple_of(k * depth, depth), depth)
        return (
            pltpu.make_async_copy(hidden_hbm.at[:, columns], hidden_ref.at[k], sems.at[0, k]),
            pltpu.make_async_copy(w_hbm.at[:, columns], w_ref.at[k], sems.at[1, k]),
        )

    def begin(k, carry):
        for copy in copies(k):
            copy.start()
        return carry

    lax.fori_loop(0, pieces, begin, 0)
    for copy in small:
        copy.start()
    acc_ref[...] = jnp.zeros_like(acc_ref)

    def body(k, carry):
        for copy in copies(k):
            copy.wait()
        acc_ref[...] += lax.dot_general(
            w_ref[k],
            hidden_ref[k],
            (((1,), (1,)), ((), ())),
            preferred_element_type=jnp.float32,
        )
        return carry

    lax.fori_loop(0, pieces, body, 0)
    for copy in small:
        copy.wait()
    device = lax.axis_index("pre") * owners + lax.axis_index("dec")
    row = device * rows + lax.broadcasted_iota(jnp.int32, (1, rows), 1)
    start = jnp.zeros((1, rows), jnp.int32)
    first_row = jnp.int32(0)
    for r in range(lengths_ref.shape[0] - 1):
        first_row = first_row + lengths_ref[r]
        start = jnp.where(row >= first_row, first_row, start)
    angles = freq_ref[:, 0:1] * (row - start).astype(jnp.float32)
    cosine = jnp.cos(angles)
    sine = jnp.sin(angles)
    gain = jnp.transpose(jnp.broadcast_to(gain_ref[...], (128, LAT)))[:, 0:1]
    latent = acc_ref[:LAT, :]
    inverse_rms = lax.rsqrt(jnp.mean(latent * latent, axis=0, keepdims=True) + norm_eps)
    out_ref[:LAT, :] = (latent * inverse_rms * gain).astype(out_ref.dtype)
    first = acc_ref[LAT : LAT + half, :]
    second = acc_ref[LAT + half :, :]
    turned = first * cosine - second * sine
    out_ref[LAT : LAT + half, :] = turned.astype(out_ref.dtype)
    turned = second * cosine + first * sine
    out_ref[LAT + half :, :] = turned.astype(out_ref.dtype)


def produce(owners, lengths, hidden, w_turned, gain):
    rows, width = hidden.shape
    row_width = w_turned.shape[0]
    pieces = width // DEPTH
    return pl.pallas_call(
        functools.partial(produce_kernel, owners),
        in_specs=[pl.BlockSpec(memory_space=pltpu.HBM)] * 5,
        out_specs=pl.BlockSpec(memory_space=pltpu.VMEM),
        out_shape=jax.ShapeDtypeStruct((row_width, rows), jnp.bfloat16),
        scratch_shapes=[
            pltpu.VMEM((pieces, rows, DEPTH), jnp.bfloat16),
            pltpu.VMEM((pieces, row_width, DEPTH), jnp.bfloat16),
            pltpu.VMEM((row_width, rows), jnp.float32),
            pltpu.SMEM(lengths.shape, jnp.int32),
            pltpu.VMEM((1, LAT), jnp.float32),
            pltpu.VMEM((ROPE // 2, 128), jnp.float32),
            pltpu.SemaphoreType.DMA((2, pieces)),
            pltpu.SemaphoreType.DMA((3,)),
        ],
        compiler_params=params(20),
        name="produce",
    )(lengths, hidden, w_turned, gain.reshape(1, -1), jnp.asarray(frequencies()))


WIDE = 640


def pack_kernel(groups, owners, dest_ref, rows_ref, out_ref, turned_ref, count_ref):
    width, rows = rows_ref.shape
    block_rows = out_ref.shape[1]
    blocks = rows // block_rows
    group = lax.axis_index("pre")
    first = (group * owners + lax.axis_index("dec")) * blocks
    for at in range(0, width, 128):
        count = min(128, width - at)
        wide = rows_ref[at : at + count, :].astype(jnp.float32)
        if count < 128:
            wide = jnp.concatenate([wide, jnp.zeros((128 - count, rows), jnp.float32)], axis=0)
        turned_ref[:, :, at : at + 128] = jnp.transpose(wide).reshape(blocks, block_rows, 128)

    def clear(owner, carry):
        count_ref[owner] = 0
        for rank in range(MOST):
            out_ref[owner * MOST + rank] = jnp.full(out_ref.shape[1:], -1.0, out_ref.dtype)
        return carry

    lax.fori_loop(0, owners, clear, 0)
    lane = lax.broadcasted_iota(jnp.int32, (block_rows, WIDE), 1)

    def put(b, carry):
        target = dest_ref[first + b]
        owner = lax.div(target, groups * owners)
        slot = lax.rem(target, groups * owners) - group * owners
        rank = count_ref[owner]
        count_ref[owner] = rank + 1
        block = jnp.where(lane < width, turned_ref[b], slot.astype(jnp.float32))
        out_ref[owner * MOST + rank] = block.astype(out_ref.dtype)
        return carry

    lax.fori_loop(0, blocks, put, 0)


def pack(groups, owners, destination, produced):
    width, rows = produced.shape
    block_rows = rows // owners
    return pl.pallas_call(
        functools.partial(pack_kernel, groups, owners),
        in_specs=[pl.BlockSpec(memory_space=pltpu.SMEM), pl.BlockSpec(memory_space=pltpu.VMEM)],
        out_specs=pl.BlockSpec(memory_space=pltpu.VMEM),
        out_shape=jax.ShapeDtypeStruct((owners * MOST, block_rows, WIDE), produced.dtype),
        scratch_shapes=[
            pltpu.VMEM((owners, block_rows, WIDE), jnp.float32),
            pltpu.SMEM((owners,), jnp.int32),
        ],
        compiler_params=params(8),
        name="pack",
    )(destination, produced)


def place_kernel(arrived_ref, out_ref, rows_ref):
    blocks, block_rows, _ = arrived_ref.shape
    width, rows = out_ref.shape
    part = 128 // block_rows
    row = lax.broadcasted_iota(jnp.int32, (rows, 128), 0).astype(jnp.float32)
    lane = lax.broadcasted_iota(jnp.int32, (1, 128), 1)
    within = lax.rem(lane, block_rows).astype(jnp.float32)
    rows_ref[...] = jnp.zeros_like(rows_ref)

    def body(k, carry):
        source = arrived_ref[pl.ds(k * part, part)].astype(jnp.float32).reshape(128, WIDE)
        slot = jnp.transpose(source[:, WIDE - 128 :])[127:128, :]
        select = jnp.where(row == slot * block_rows + within, 1.0, 0.0).astype(jnp.bfloat16)
        rows_ref[...] += jnp.dot(
            select, source.astype(jnp.bfloat16), preferred_element_type=jnp.float32
        )
        return carry

    lax.fori_loop(0, blocks // part, body, 0)
    for at in range(0, width, 128):
        count = min(128, width - at)
        turned = jnp.transpose(rows_ref[:, at : at + 128])
        out_ref[at : at + count, :] = turned[:count].astype(out_ref.dtype)


def place(arrived, width, rows):
    vmem = pl.BlockSpec(memory_space=pltpu.VMEM)
    return pl.pallas_call(
        place_kernel,
        in_specs=[vmem],
        out_specs=vmem,
        out_shape=jax.ShapeDtypeStruct((width, rows), arrived.dtype),
        scratch_shapes=[pltpu.VMEM((rows, WIDE), jnp.float32)],
        compiler_params=params(8),
        name="place",
    )(arrived)


def assemble_kernel(*refs):
    pieces, out_ref = refs[:-1], refs[-1]
    groups = len(pieces)
    group = lax.axis_index("pre")
    width, rows = pieces[0].shape
    step = 64

    def body(k, carry):
        part = pl.ds(pl.multiple_of(k * step, step), step)
        for shift, piece in zip((0, groups - 1, 1, 2), pieces):
            at = pl.multiple_of(lax.rem(group + shift, groups) * rows, rows)
            out_ref[part, pl.ds(at, rows)] = piece[part, :]
        return carry

    lax.fori_loop(0, width // step, body, 0)


def assemble(pieces):
    width, rows = pieces[0].shape
    vmem = pl.BlockSpec(memory_space=pltpu.VMEM)
    return pl.pallas_call(
        assemble_kernel,
        in_specs=[vmem] * len(pieces),
        out_specs=vmem,
        out_shape=jax.ShapeDtypeStruct((width, rows * len(pieces)), pieces[0].dtype),
        compiler_params=params(4),
        name="assemble",
    )(*pieces)


def fill_bias(owners, groups, shifts, lengths_ref, request_ref, position_ref, bias_ref, valid_ref):
    group, owner = lax.axis_index("pre"), lax.axis_index("dec")
    steps, batch = position_ref.shape
    heads = CUT_HEADS
    count = bias_ref.shape[1] // len(shifts)
    row = lax.broadcasted_iota(jnp.int32, (heads, count), 1)
    bases = [
        (lax.rem(group + shift, groups) * owners + owner) * count for shift in range(groups)
    ]

    def body(item, carry):
        b = lax.rem(item, batch)
        request = request_ref[b]
        start = jnp.int32(0)
        for r in range(lengths_ref.shape[0] - 1):
            start = start + jnp.where(request > r, lengths_ref[r], 0)
        stop = start + position_ref[lax.div(item, batch), b]
        at = pl.ds(pl.multiple_of(item * heads, heads), heads)
        for c, shift in enumerate(shifts):
            base = bases[shift]
            bias_ref[at, c * count : (c + 1) * count] = jnp.where(
                (row >= start - base) & (row < stop - base), 0.0, mask_value
            )
        if valid_ref is not None:
            seen = jnp.int32(0)
            for base in bases:
                seen = seen + jnp.where((start < base + count) & (stop > base), 1, 0)
            valid_ref[at, :] = jnp.full((heads, 128), seen, jnp.int32)
        return carry

    lax.fori_loop(0, steps * batch, body, 0)


def update_state(latent, rope, chunk_refs, bias_ref, state):
    rows = latent.shape[0]
    scores = []
    for c, chunk_ref in enumerate(chunk_refs):
        count = chunk_ref.shape[1]
        s = jnp.dot(latent, chunk_ref[:LAT, :], preferred_element_type=jnp.float32)
        s += jnp.dot(rope, chunk_ref[LAT:, :], preferred_element_type=jnp.float32)
        scores.append(s + bias_ref[:, c * count : (c + 1) * count])
    peaks = [jnp.max(s, axis=1, keepdims=True) for s in scores]
    if state is None:
        total = jnp.zeros((rows, 1), jnp.float32)
        mixed = jnp.zeros((rows, LAT), jnp.float32)
    else:
        old_peak, total, mixed = state
        peaks.append(old_peak)
    peak = functools.reduce(jnp.maximum, peaks)
    if state is not None:
        factor = jnp.exp2((old_peak - peak) * (score_scale * log2_e))
        total, mixed = total * factor, mixed * factor
    for s, chunk_ref in zip(scores, chunk_refs):
        p = jnp.exp2((s - peak) * (score_scale * log2_e))
        total += jnp.sum(p, axis=1, keepdims=True)
        mixed += lax.dot_general(
            p.astype(jnp.bfloat16),
            chunk_ref[:LAT, :],
            (((1,), (1,)), ((), ())),
            preferred_element_type=jnp.float32,
        )
    return peak, total, mixed


def near_kernel(
    owners, groups, lengths_ref, request_ref, position_ref, latent_ref, rope_ref,
    k0, k1, k2, mixed_ref, stat_ref, bias_ref,
):
    items, heads, _ = latent_ref.shape
    rows = items * heads
    cut = pl.program_id(0)

    @pl.when(cut == 0)
    def _():
        fill_bias(
            owners, groups, (0, groups - 1, 1),
            lengths_ref, request_ref, position_ref, bias_ref, None,
        )

    latent = latent_ref[...].reshape(rows, LAT)
    rope = rope_ref[...].reshape(rows, ROPE)
    peak, total, mixed = update_state(latent, rope, (k0, k1, k2), bias_ref, None)
    mixed_ref[cut] = mixed
    lane = lax.broadcasted_iota(jnp.int32, (rows, 128), 1)
    stat_ref[cut] = jnp.where(lane == 0, peak, total)


def far_kernel(
    owners, groups, lengths_ref, request_ref, position_ref, latent_ref, rope_ref,
    k3, mixed_ref, stat_ref, w_ref, out_ref, bias_ref, valid_ref,
):
    items, heads, _ = latent_ref.shape
    rows = items * heads
    all_heads = out_ref.shape[1] - PAD
    cut = pl.program_id(0)

    @pl.when(cut == 0)
    def _():
        fill_bias(
            owners, groups, (2,),
            lengths_ref, request_ref, position_ref, bias_ref, valid_ref,
        )
        out_ref[:, all_heads:, :] = jnp.zeros((items, PAD, 128), jnp.float32)

    latent = latent_ref[...].reshape(rows, LAT)
    rope = rope_ref[...].reshape(rows, ROPE)
    stat = stat_ref[cut]
    state = (stat[:, 0:1], stat[:, 1:2], mixed_ref[cut])
    peak, total, mixed = update_state(latent, rope, (k3,), bias_ref, state)
    valid = valid_ref[:, 0:1] > 0
    mixed = mixed * jnp.where(valid, 1.0 / total, 0.0)
    level = jnp.where(valid, peak * score_scale + jnp.log(total), mask_value)
    upper = mixed.astype(jnp.bfloat16)
    lower = (mixed - upper.astype(jnp.float32)).astype(jnp.bfloat16)
    head = lax.broadcasted_iota(jnp.int32, (rows, 128), 0) % heads
    result = jnp.zeros((rows, 128), jnp.float32)
    for h in range(0, heads, 2):
        pair = jnp.concatenate([w_ref[cut * heads + h], w_ref[cut * heads + h + 1]], axis=1)
        y = jnp.dot(upper, pair, preferred_element_type=jnp.float32)
        y += jnp.dot(lower, pair, preferred_element_type=jnp.float32)
        result = jnp.where(head == h, y[:, :128], result)
        result = jnp.where(head == h + 1, y[:, 128:], result)
    at = pl.multiple_of(cut * heads, heads)
    out_ref[:, pl.ds(at, heads), :] = result.reshape(items, heads, 128)
    lane = lax.broadcasted_iota(jnp.int32, (rows, 128), 1)
    lines = jnp.where(lane == head + at, level, 0.0).reshape(items, heads, 128)
    lines = jnp.sum(lines, axis=1, keepdims=True)
    out_ref[:, all_heads:, :] += jnp.broadcast_to(lines, (items, PAD, 128))


def attend(owners, lengths, row_request, step_position, latent, rope, chunks, w_up):
    items, heads, _ = latent.shape
    groups = len(chunks)
    cut = heads // CUT_HEADS
    rows = items * CUT_HEADS
    count = chunks[0].shape[1]
    smem = pl.BlockSpec(memory_space=pltpu.SMEM)
    vmem = pl.BlockSpec(memory_space=pltpu.VMEM)
    query_specs = [
        pl.BlockSpec((items, CUT_HEADS, LAT), lambda i: (0, i, 0)),
        pl.BlockSpec((items, CUT_HEADS, ROPE), lambda i: (0, i, 0)),
    ]
    scalars = (lengths, row_request, step_position)
    mixed, stat = pl.pallas_call(
        functools.partial(near_kernel, owners, groups),
        grid=(cut,),
        in_specs=[smem] * 3 + query_specs + [vmem] * 3,
        out_specs=[vmem, vmem],
        out_shape=[
            jax.ShapeDtypeStruct((cut, rows, LAT), jnp.float32),
            jax.ShapeDtypeStruct((cut, rows, 128), jnp.float32),
        ],
        scratch_shapes=[pltpu.VMEM((rows, 3 * count), jnp.float32)],
        compiler_params=params(16),
        name="attend_near",
    )(*scalars, latent, rope, *chunks[:3])
    return pl.pallas_call(
        functools.partial(far_kernel, owners, groups),
        grid=(cut,),
        in_specs=[smem] * 3 + query_specs + [vmem] * 4,
        out_specs=vmem,
        out_shape=jax.ShapeDtypeStruct((items, heads + PAD, 128), jnp.float32),
        scratch_shapes=[
            pltpu.VMEM((rows, count), jnp.float32),
            pltpu.VMEM((rows, 128), jnp.int32),
        ],
        compiler_params=params(16),
        name="attend_far",
    )(*scalars, latent, rope, chunks[3], mixed, stat, w_up)


def merge_kernel(last, *refs):
    parts, out_ref, scale_ref = refs[:-2], refs[-2], refs[-1]
    folded = len(parts) == 1
    sources = parts[0].shape[0] if folded else len(parts)
    items, depth, lanes = parts[0].shape[-3:]
    heads = depth - PAD
    part = (lambda k: parts[0].at[k]) if folded else (lambda k: parts[k])
    levels = [part(k)[:, heads:, :] for k in range(sources)]
    peak = functools.reduce(jnp.maximum, levels)
    scales = [jnp.exp(level - peak) for level in levels]
    total = functools.reduce(jnp.add, scales)
    for k in range(sources):
        scale_ref[k] = scales[k] / total
    lane = lax.broadcasted_iota(jnp.int32, (items, heads, lanes), 2)
    row = lax.broadcasted_iota(jnp.int32, (items, heads, lanes), 1)

    def term(k, here):
        line = scale_ref[k][:, 0:1, :]
        column = jnp.sum(jnp.where(lane == row, line, 0.0), axis=2, keepdims=True)
        return here[:, :heads, :] * column

    result = jnp.zeros((items, heads, lanes), jnp.float32)
    if folded:
        result = lax.fori_loop(
            0, sources, lambda k, so_far: so_far + term(k, parts[0].at[k]), result, unroll=4
        )
    else:
        for k in range(sources):
            result += term(k, parts[k])
    if last:
        result = result.astype(out_ref.dtype)
        for copy in range(out_ref.shape[0]):
            out_ref[copy] = result
    else:
        out_ref[:, :heads, :] = result
        out_ref[:, heads:, :] = peak + jnp.log(total)


def merge(parts, copies):
    items, depth, lanes = parts[0].shape[-3:]
    sources = parts[0].shape[0] if len(parts) == 1 else len(parts)
    last = copies > 0
    vmem = pl.BlockSpec(memory_space=pltpu.VMEM)
    if last:
        out_shape = jax.ShapeDtypeStruct((copies, items, depth - PAD, lanes), jnp.bfloat16)
    else:
        out_shape = jax.ShapeDtypeStruct((items, depth, lanes), jnp.float32)
    return pl.pallas_call(
        functools.partial(merge_kernel, last),
        in_specs=[vmem] * len(parts),
        out_specs=vmem,
        out_shape=out_shape,
        scratch_shapes=[pltpu.VMEM((sources, items, PAD, lanes), jnp.float32)],
        compiler_params=params(4),
        name="merge",
    )(*parts)


def spread_kernel(in_ref, out_ref, wide_ref):
    items, heads, lanes = in_ref.shape
    wide_ref[...] = in_ref[...].astype(jnp.float32).reshape(items * heads, lanes)

    def body(h, carry):
        rows = wide_ref[pl.ds(h, items, stride=heads), :]
        at = pl.multiple_of(h * lanes, lanes)
        out_ref[:, pl.ds(at, lanes)] = rows.astype(out_ref.dtype)
        return carry

    lax.fori_loop(0, heads, body, 0, unroll=4)


def spread(result):
    items, heads, lanes = result.shape
    vmem = pl.BlockSpec(memory_space=pltpu.VMEM)
    return pl.pallas_call(
        spread_kernel,
        in_specs=[vmem],
        out_specs=vmem,
        out_shape=jax.ShapeDtypeStruct((items, heads * lanes), result.dtype),
        scratch_shapes=[pltpu.VMEM((items * heads, lanes), jnp.float32)],
        compiler_params=params(4),
        name="spread",
    )(result)


def around(piece, groups, owners):
    core = lax.axis_index("dec") % 2
    before = lax.ppermute(piece, "pre", [(i, (i + 1) % groups) for i in range(groups)])
    after = lax.ppermute(piece, "pre", [(i, (i - 1) % groups) for i in range(groups)])
    forward = [
        (g * owners + d, (g + (1 if d % 2 == 0 else -1)) % groups * owners + d)
        for g in range(groups)
        for d in range(owners)
    ]
    far = lax.ppermute(jnp.where(core == 0, before, after), ("pre", "dec"), forward)
    return [piece, before, after, far]


def per_device(
    hidden,
    w_down,
    kv_gain,
    query_latent,
    query_rope,
    w_up_value,
    request_rows,
    row_request,
    step_position,
    destination,
):
    groups = lax.axis_size("pre")
    owners = lax.axis_size("dec")
    steps, batch, heads, _ = query_latent.shape
    items = steps * batch
    plane = [[2 * k + core for k in range(SIDE * SIDE)] for core in range(2)]
    sibling = [(d, d ^ 1) for d in range(owners)]

    produced = produce(owners, request_rows, hidden, w_down.T, kv_gain)
    chunks = around(produced, groups, owners)

    exchanged = functools.partial(
        lax.all_to_all, axis_name="dec", split_axis=0, concat_axis=0, tiled=True
    )
    parts = attend(
        owners,
        request_rows,
        row_request,
        step_position,
        query_latent.reshape(items, heads, -1),
        query_rope.reshape(items, heads, -1),
        chunks,
        w_up_value,
    )
    parts = exchanged(parts, axis_index_groups=plane)
    mine = merge([parts.reshape((SIDE * SIDE, 2) + parts.shape[1:])], 0)
    result = merge([mine, lax.ppermute(mine, "dec", sibling)], SIDE * SIDE)
    result = exchanged(result, axis_index_groups=plane)
    attention_out = spread(result.reshape((items,) + result.shape[2:])).reshape(steps, batch, -1)

    arrived = exchanged(pack(groups, owners, destination, produced))
    quarter = place(arrived, *produced.shape)
    kv_cache = assemble(around(quarter, groups, owners)).T
    return (attention_out, kv_cache)


def solution(mesh):
    return jax.shard_map(
        per_device,
        mesh=mesh,
        in_specs=(
            P(("pre", "dec"), None),
            P(),
            P(),
            P(None, None, "pre", None),
            P(None, None, "pre", None),
            P("pre", None, None),
            P(),
            P(),
            P(),
            P(),
        ),
        out_specs=(P(None, None, "pre"), P("dec", None)),
        check_vma=False,
    )
```

time: 394 us -> 87 us (0.22); the launches traced: 388 us -> 86.4 us
  waiting for transfers between devices: 169 us -> 14.3 us
  other arithmetic: 97.7 us -> 0.07 us
  blocking collectives: 51.1 us -> 0 us
  Pallas kernels: 0 us -> 28.4 us
  starting transfers between devices: 8.67 us -> 33.2 us
  local copies, waits for them, and re-layouts: 28 us -> 9.64 us
  matrix products: 17.9 us -> 0 us
  between operations: 14.6 us -> 0.81 us
    all_gather x2 -> x0, waiting for transfers between devices: 158 us -> none  [the longest x1 149 us: combined_all(): everything = jax.tree.map(lambda part: lax.all_gather(part, axis), value)]
    add x64 -> x0, other arithmetic: 89.6 us -> none  [the longest x31 66 us: combine(): first_sum * first_factor[..., None] + second_sum * second_factor[..., None]]
    all_gather x2 -> x0, blocking collectives: 51.1 us -> none  [combined_all(): everything = jax.tree.map(lambda part: lax.all_gather(part, axis), value)]
    pallas_call x0 -> x9, Pallas kernels: none -> 28.4 us  [the longest x1 9.2 us: attend(): pl.pallas_call(functools.partial(far_kernel, owners, groups), grid=(cut,)...]
    dot_general x13 -> x0, matrix products: 17.9 us -> none  [the longest x1 6.79 us: produce(): raw_rows = jnp.dot(hidden, w_down, preferred_element_type=jnp.float32)]
    scatter x1 -> x0, local copies, waits for them, and re-layouts: 15.5 us -> none  [per_device(): inverse = jnp.zeros((total_blocks,), jnp.int32).at[destination].set(jnp.a...]
    ppermute x0 -> x7, starting transfers between devices: none -> 12.6 us  [the longest x2 4.85 us: around(): lax.ppermute(piece, 'pre', [(i, (i - 1) % groups) for i in range(groups)])]
    all_to_all x1 -> x3, starting transfers between devices: 8.59 us -> 20.6 us  [the longest x1 8.06 us: per_device(): arrived = exchanged(pack(groups, owners, destination, produced))]
  transfers between devices with their start and end apart: 3 -> 10, of which waited for: 3 -> 3; matrix products, arithmetic and copies ran while one was open for 5% -> 0% of each run, Pallas kernels for 0% -> 25%
where the time goes in v1:
time: 87 us; the launch traced here: 86.4 us
  starting transfers between devices  33.2 us (38%)
  Pallas kernels  28.4 us (33%)
  waiting for transfers between devices  14.3 us (16%)
  local copies, waits for them, and re-layouts  9.64 us (11%)
    unnamed x24, local copies, waits for them, and re-layouts  9.64 us
    pallas_call x1, Pallas kernels, attend(): pl.pallas_call(functools.partial(far_kernel, owners, groups), grid=(cut,)...  9.2 us
    all_to_all x1, starting transfers between devices, per_device(): arrived = exchanged(pack(groups, owners, destination, produced))  8.06 us
    all_to_all x1, waiting for transfers between devices, per_device(): result = exchanged(result, axis_index_groups=plane)  7.13 us
    all_to_all x1, starting transfers between devices, per_device(): parts = exchanged(parts, axis_index_groups=plane)  6.69 us
    ppermute x2, waiting for transfers between devices, around(): lax.ppermute(piece, 'pre', [(i, (i + 1) % groups) for i in range(groups)])  6.32 us
    pallas_call x1, Pallas kernels, attend(): pl.pallas_call(functools.partial(near_kernel, owners, groups), grid=(cut,...  6.12 us
    all_to_all x1, starting transfers between devices, per_device(): result = exchanged(result, axis_index_groups=plane)  5.84 us
  transfers between devices with their start and end apart: 10, of which 3 were waited for; matrix products, arithmetic and copies ran while one was open for 0% of the time, Pallas kernels for 25%

profile of v1, /device:TPU:1, one launch (start us, length us, event | category | flops | bytes accessed | tf_op | source)
XLA Modules:
  0.0 86.4 jit_solution(16420442874685172402)
XLA Ops:
  0.6 3.3 %copy-done = bf16[7168,576]{0,1:T(8,128)(2,1)S(1)} copy-done((bf16[7168,576]{0,1:T(8,128)(2,1)S(1)}, bf16[7168,576]{0,1:T(8,128)(2,1)}, u32[]{:S(2)}) %copy-start) | copy-done | bytes 8257560
  4.0 2.0 %copy-done.3 = bf16[256,7168]{1,0:T(8,128)(2,1)S(1)} copy-done((bf16[256,7168]{1,0:T(8,128)(2,1)S(1)}, bf16[256,7168]{1,0:T(8,128)(2,1)}, u32[]{:S(2)}) %copy-start.3) | copy-done | bytes 3670040
  6.0 0.7 copy-done.6
  8.1 5.5 %produce.1.k0.rows_ref = bf16[576,256]{1,0:T(8,128)(2,1)S(1)} custom-call(s32[4]{0:T(128)S(1)} %copy-done.8, bf16[256,7168]{1,0:T(8,128)(2,1)S(1)} %copy-done.3, bf16[576,7168]{1,0:T(8,128)(2,1)S(1)} %bitcast.8, f32[1,512]{1,0:T(1,128)S(1)} %bitcast.15, f32[32,128]{1,0:T(8,128)S(1)} %copy-done.6), custom_call_target="tpu_custom_call" | custom-call | tf_op jit(solution)/shard_map/produce/pallas_call | solution.py:107
  13.6 2.5 %collective-permute-start = (bf16[576,256]{1,0:T(8,128)(2,1)S(1)}, bf16[576,256]{1,0:T(8,128)(2,1)S(1)}, u32[]{:S(2)}, u32[]{:S(2)}) collective-permute-start(bf16[576,256]{1,0:T(8,128)(2,1)S(1)} %produce.1.k0.rows_ref), channel_id=1, source_target_pairs={{0,32},{32,64},{64,96},{96,0},{1,33},{33,65},{65,97},{97,1},{2,34}... | collective-permute-start | bytes 884744 | tf_op jit(solution)/shard_map/ppermute | solution.py:508
  16.2 2.2 %collective-permute-start.1 = (bf16[576,256]{1,0:T(8,128)(2,1)S(1)}, bf16[576,256]{1,0:T(8,128)(2,1)S(1)}, u32[]{:S(2)}, u32[]{:S(2)}) collective-permute-start(bf16[576,256]{1,0:T(8,128)(2,1)S(1)} %produce.1.k0.rows_ref), channel_id=1, source_target_pairs={{0,96},{32,0},{64,32},{96,64},{1,97},{33,1},{65,33},{97,65},{2,98}... | collective-permute-start | bytes 884744 | tf_op jit(solution)/shard_map/ppermute | solution.py:509
  18.4 2.4 %pack.1 = bf16[64,8,640]{2,1,0:T(8,128)(2,1)} custom-call(s32[4096]{0:T(1024)S(1)} %copy-done.5, bf16[576,256]{1,0:T(8,128)(2,1)S(1)} %produce.1.k0.rows_ref), custom_call_target="tpu_custom_call" | custom-call | tf_op jit(solution)/shard_map/pack/pallas_call | solution.py:168
  20.8 8.1 %all-to-all-start.2 = ((bf16[64,8,640]{2,1,0:T(8,128)(2,1)}), bf16[64,8,640]{2,1,0:T(8,128)(2,1)S(1)}, u32[]{:S(2)}, u32[]{:S(2)}) async-start(bf16[64,8,640]{2,1,0:T(8,128)(2,1)} %pack.1), calls=%async_computation.2 | async-start | bytes 1310720 | tf_op jit(solution)/shard_map/all_to_all | solution.py:560
  29.0 1.7 %collective-permute-start.2 = (bf16[576,256]{1,0:T(8,128)(2,1)S(1)}, bf16[576,256]{1,0:T(8,128)(2,1)S(1)}, u32[]{:S(2)}, u32[]{:S(2)}) collective-permute-start(bf16[576,256]{1,0:T(8,128)(2,1)S(1)} %broadcast_select_fusion.1), channel_id=1, source_target_pairs={{0,32},{1,97},{2,34},{3,99},{4,36},{5,101},{6,38},{7,103},{8,40},{... | collective-permute-start | bytes 884744 | tf_op jit(solution)/shard_map/ppermute | solution.py:515
  30.7 6.1 %attend_near.1 = (f32[4,256,512]{2,1,0:T(8,128)S(1)}, f32[4,256,128]{2,1,0:T(8,128)S(1)}) custom-call(s32[4]{0:T(128)S(1)} %copy-done.9, s32[8]{0:T(128)S(1)} %copy-done.11, s32[4,8]{1,0:T(4,128)S(1)} %copy-done.7, bf16[32,32,512]{2,1,0:T(8,128)(2,1)S(1)} %bitcast.9, bf16[32,32,64]{2,1,0:T(8,128)(2,1)S(1)} %bitcast.13, ...), custom_call_target="tpu_custom_call" | custom-call | tf_op jit(solution)/shard_map/attend_near/pallas_call | solution.py:393
  36.9 2.2 %copy-done.1 = bf16[32,512,128]{2,1,0:T(8,128)(2,1)S(1)} copy-done((bf16[32,512,128]{2,1,0:T(8,128)(2,1)S(1)}, bf16[32,512,128]{2,1,0:T(8,128)(2,1)}, u32[]{:S(2)}) %copy-start.1) | copy-done | bytes 4194328
  39.0 9.2 %attend_far.1 = f32[32,40,128]{2,1,0:T(8,128)} custom-call(s32[4]{0:T(128)S(1)} %copy-done.9, s32[8]{0:T(128)S(1)} %copy-done.11, s32[4,8]{1,0:T(4,128)S(1)} %copy-done.7, bf16[32,32,512]{2,1,0:T(8,128)(2,1)S(1)} %bitcast.10, bf16[32,32,64]{2,1,0:T(8,128)(2,1)S(1)} %bitcast.14, bf16[576,256]{1,0:T(8,128)(2,1)S(1)} %collective-permute-done.2.k3, ...), custom_call_target="tpu_custom_call" | custom-call | tf_op jit(solution)/shard_map/attend_far/pallas_call | solution.py:406
  48.2 6.7 %all-to-all-start = ((f32[32,40,128]{2,1,0:T(8,128)}), f32[32,40,128]{2,1,0:T(8,128)S(1)}, u32[]{:S(2)}, u32[]{:S(2)}) async-start(f32[32,40,128]{2,1,0:T(8,128)} %attend_far.1), calls=%async_computation | async-start | bytes 1310720 | tf_op jit(solution)/shard_map/all_to_all | solution.py:554
  54.9 1.5 %place.1.refs_0_ = bf16[576,256]{1,0:T(8,128)(2,1)S(1)} custom-call(bf16[64,8,640]{2,1,0:T(8,128)(2,1)S(1)} %all-to-all-done.2.arrived_ref), custom_call_target="tpu_custom_call" | custom-call | tf_op jit(solution)/shard_map/place/pallas_call | solution.py:209
  56.5 2.7 %collective-permute-start.5 = (bf16[576,256]{1,0:T(8,128)(2,1)S(1)}, bf16[576,256]{1,0:T(8,128)(2,1)S(1)}, u32[]{:S(2)}, u32[]{:S(2)}) collective-permute-start(bf16[576,256]{1,0:T(8,128)(2,1)S(1)} %place.1.refs_0_), channel_id=1, source_target_pairs={{0,96},{32,0},{64,32},{96,64},{1,97},{33,1},{65,33},{97,65},{2,98}... | collective-permute-start | bytes 884744 | tf_op jit(solution)/shard_map/ppermute | solution.py:509
  59.2 6.3 %collective-permute-done.4.refs_1_ = bf16[576,256]{1,0:T(8,128)(2,1)S(1)} collective-permute-done((bf16[576,256]{1,0:T(8,128)(2,1)S(1)}, bf16[576,256]{1,0:T(8,128)(2,1)S(1)}, u32[]{:S(2)}, u32[]{:S(2)}) %collective-permute-start.4) | collective-permute-done | bytes 294944 | tf_op jit(solution)/shard_map/ppermute | solution.py:508
  65.5 2.4 %collective-permute-start.6 = (bf16[576,256]{1,0:T(8,128)(2,1)S(1)}, bf16[576,256]{1,0:T(8,128)(2,1)S(1)}, u32[]{:S(2)}, u32[]{:S(2)}) collective-permute-start(bf16[576,256]{1,0:T(8,128)(2,1)S(1)} %broadcast_select_fusion), channel_id=1, source_target_pairs={{0,32},{1,97},{2,34},{3,99},{4,36},{5,101},{6,38},{7,103},{8,40},{... | collective-permute-start | bytes 884744 | tf_op jit(solution)/shard_map/ppermute | solution.py:515
  68.5 1.0 %collective-permute-start.3 = (f32[2,40,128]{2,1,0:T(8,128)S(1)}, f32[2,40,128]{2,1,0:T(8,128)S(1)}, u32[]{:S(2)}, u32[]{:S(2)}) collective-permute-start(f32[2,40,128]{2,1,0:T(8,128)S(1)} %merge.2.refs_0_), channel_id=1, source_target_pairs={{0,1},{1,0},{2,3},{3,2},{4,5},{5,4},{6,7},{7,6},{8,9},{9,8},{10,11... | collective-permute-start | bytes 122888 | tf_op jit(solution)/shard_map/ppermute | solution.py:556
  69.4 0.9 %collective-permute-done.3.refs_1_ = f32[2,40,128]{2,1,0:T(8,128)S(1)} collective-permute-done((f32[2,40,128]{2,1,0:T(8,128)S(1)}, f32[2,40,128]{2,1,0:T(8,128)S(1)}, u32[]{:S(2)}, u32[]{:S(2)}) %collective-permute-start.3) | collective-permute-done | bytes 40992 | tf_op jit(solution)/shard_map/ppermute | solution.py:556
  70.3 0.8 merge.3
  71.1 5.8 %all-to-all-start.1 = ((bf16[16,2,32,128]{3,2,1,0:T(8,128)(2,1)}), bf16[16,2,32,128]{3,2,1,0:T(8,128)(2,1)S(1)}, u32[]{:S(2)}, u32[]{:S(2)}) async-start(bf16[16,2,32,128]{3,2,1,0:T(8,128)(2,1)} %merge.3), calls=%async_computation.1 | async-start | bytes 524288 | tf_op jit(solution)/shard_map/all_to_all | solution.py:557
  77.0 1.2 %assemble.1 = bf16[576,1024]{1,0:T(8,128)(2,1)} custom-call(bf16[576,256]{1,0:T(8,128)(2,1)S(1)} %place.1.refs_0_, bf16[576,256]{1,0:T(8,128)(2,1)S(1)} %collective-permute-done.4.refs_1_, bf16[576,256]{1,0:T(8,128)(2,1)S(1)} %collective-permute-done.5.refs_2_, bf16[576,256]{1,0:T(8,128)(2,1)S(1)} %collective-permute-done.6.refs_3_), custom_call_target="tpu_custom_call" | custom-call | tf_op jit(solution)/shard_map/assemble/pallas_call | solution.py:240
  78.2 7.1 %all-to-all-done.1 = bf16[16,2,32,128]{3,2,1,0:T(8,128)(2,1)S(1)} async-done(((bf16[16,2,32,128]{3,2,1,0:T(8,128)(2,1)}), bf16[16,2,32,128]{3,2,1,0:T(8,128)(2,1)S(1)}, u32[]{:S(2)}, u32[]{:S(2)}) %all-to-all-start.1) | async-done | bytes 262176 | tf_op jit(solution)/shard_map/all_to_all | solution.py:557
  85.3 1.1 %spread.1 = bf16[32,4096]{1,0:T(8,128)(2,1)} custom-call(bf16[32,32,128]{2,1,0:T(8,128)(2,1)S(1)} %bitcast.12), custom_call_target="tpu_custom_call" | custom-call | tf_op jit(solution)/shard_map/spread/pallas_call | solution.py:495
  (31 shorter events, 2.0 us)
Async XLA Ops:
  0.6 3.3 %copy-start = (bf16[7168,576]{0,1:T(8,128)(2,1)S(1)}, bf16[7168,576]{0,1:T(8,128)(2,1)}, u32[]{:S(2)}) copy-start(bf16[7168,576]{0,1:T(8,128)(2,1)} %param.12) | copy-start | bytes 24772612
  4.0 2.0 %copy-start.3 = (bf16[256,7168]{1,0:T(8,128)(2,1)S(1)}, bf16[256,7168]{1,0:T(8,128)(2,1)}, u32[]{:S(2)}) copy-start(bf16[256,7168]{1,0:T(8,128)(2,1)} %hidden_hbm.1) | copy-start | bytes 11010052
  6.0 0.7 copy-start.6
  6.7 0.7 copy-start.8
  7.4 0.7 copy-start.10
  8.1 10.3 %copy-start.5 = (s32[4096]{0:T(1024)S(1)}, s32[4096]{0:T(1024)}, u32[]{:S(2)}) copy-start(s32[4096]{0:T(1024)} %dest_ref.1) | copy-start | bytes 49156
  8.1 22.6 %copy-start.4 = (bf16[4,8,32,64]{3,2,1,0:T(8,128)(2,1)S(1)}, bf16[4,8,32,64]{3,2,1,0:T(8,128)(2,1)}, u32[]{:S(2)}) copy-start(bf16[4,8,32,64]{3,2,1,0:T(8,128)(2,1)} %param.15) | copy-start | bytes 393220
  8.1 22.6 %copy-start.7 = (s32[4,8]{1,0:T(4,128)S(1)}, s32[4,8]{1,0:T(4,128)}, u32[]{:S(2)}) copy-start(s32[4,8]{1,0:T(4,128)} %position_ref.3) | copy-start | bytes 388
  8.1 22.6 %copy-start.9 = (s32[4]{0:T(128)S(1)}, s32[4]{0:T(128)}, u32[]{:S(2)}) copy-start(s32[4]{0:T(128)} %lengths_ref.3) | copy-start | bytes 52
  8.1 22.6 %copy-start.11 = (s32[8]{0:T(128)S(1)}, s32[8]{0:T(128)}, u32[]{:S(2)}) copy-start(s32[8]{0:T(128)} %request_ref.3) | copy-start | bytes 100
  13.6 17.1 %copy-start.2 = (bf16[4,8,32,512]{3,2,1,0:T(8,128)(2,1)S(1)}, bf16[4,8,32,512]{3,2,1,0:T(8,128)(2,1)}, u32[]{:S(2)}) copy-start(bf16[4,8,32,512]{3,2,1,0:T(8,128)(2,1)} %param.14) | copy-start | bytes 3145732
  13.6 15.2 %collective-permute-start = (bf16[576,256]{1,0:T(8,128)(2,1)S(1)}, bf16[576,256]{1,0:T(8,128)(2,1)S(1)}, u32[]{:S(2)}, u32[]{:S(2)}) collective-permute-start(bf16[576,256]{1,0:T(8,128)(2,1)S(1)} %produce.1.k0.rows_ref), channel_id=1, source_target_pairs={{0,32},{32,64},{64,96},{96,0},{1,33},{33,65},{65,97},{97,1},{2,34}... | collective-permute-start | bytes 884744 | tf_op jit(solution)/shard_map/ppermute | solution.py:508
  16.2 12.7 %collective-permute-start.1 = (bf16[576,256]{1,0:T(8,128)(2,1)S(1)}, bf16[576,256]{1,0:T(8,128)(2,1)S(1)}, u32[]{:S(2)}, u32[]{:S(2)}) collective-permute-start(bf16[576,256]{1,0:T(8,128)(2,1)S(1)} %produce.1.k0.rows_ref), channel_id=1, source_target_pairs={{0,96},{32,0},{64,32},{96,64},{1,97},{33,1},{65,33},{97,65},{2,98}... | collective-permute-start | bytes 884744 | tf_op jit(solution)/shard_map/ppermute | solution.py:509
  20.8 27.4 %all-to-all-start.2 = ((bf16[64,8,640]{2,1,0:T(8,128)(2,1)}), bf16[64,8,640]{2,1,0:T(8,128)(2,1)S(1)}, u32[]{:S(2)}, u32[]{:S(2)}) async-start(bf16[64,8,640]{2,1,0:T(8,128)(2,1)} %pack.1), calls=%async_computation.2 | async-start | bytes 1310720 | tf_op jit(solution)/shard_map/all_to_all | solution.py:560
  29.0 7.9 %collective-permute-start.2 = (bf16[576,256]{1,0:T(8,128)(2,1)S(1)}, bf16[576,256]{1,0:T(8,128)(2,1)S(1)}, u32[]{:S(2)}, u32[]{:S(2)}) collective-permute-start(bf16[576,256]{1,0:T(8,128)(2,1)S(1)} %broadcast_select_fusion.1), channel_id=1, source_target_pairs={{0,32},{1,97},{2,34},{3,99},{4,36},{5,101},{6,38},{7,103},{8,40},{... | collective-permute-start | bytes 884744 | tf_op jit(solution)/shard_map/ppermute | solution.py:515
  36.8 2.2 %copy-start.1 = (bf16[32,512,128]{2,1,0:T(8,128)(2,1)S(1)}, bf16[32,512,128]{2,1,0:T(8,128)(2,1)}, u32[]{:S(2)}) copy-start(bf16[32,512,128]{2,1,0:T(8,128)(2,1)} %w_ref.1) | copy-start | bytes 12582916
  48.2 19.7 %all-to-all-start = ((f32[32,40,128]{2,1,0:T(8,128)}), f32[32,40,128]{2,1,0:T(8,128)S(1)}, u32[]{:S(2)}, u32[]{:S(2)}) async-start(f32[32,40,128]{2,1,0:T(8,128)} %attend_far.1), calls=%async_computation | async-start | bytes 1310720 | tf_op jit(solution)/shard_map/all_to_all | solution.py:554
  56.4 9.1 %collective-permute-start.4 = (bf16[576,256]{1,0:T(8,128)(2,1)S(1)}, bf16[576,256]{1,0:T(8,128)(2,1)S(1)}, u32[]{:S(2)}, u32[]{:S(2)}) collective-permute-start(bf16[576,256]{1,0:T(8,128)(2,1)S(1)} %place.1.refs_0_), channel_id=1, source_target_pairs={{0,32},{32,64},{64,96},{96,0},{1,33},{33,65},{65,97},{97,1},{2,34}... | collective-permute-start | bytes 884744 | tf_op jit(solution)/shard_map/ppermute | solution.py:508
  56.5 9.0 %collective-permute-start.5 = (bf16[576,256]{1,0:T(8,128)(2,1)S(1)}, bf16[576,256]{1,0:T(8,128)(2,1)S(1)}, u32[]{:S(2)}, u32[]{:S(2)}) collective-permute-start(bf16[576,256]{1,0:T(8,128)(2,1)S(1)} %place.1.refs_0_), channel_id=1, source_target_pairs={{0,96},{32,0},{64,32},{96,64},{1,97},{33,1},{65,33},{97,65},{2,98}... | collective-permute-start | bytes 884744 | tf_op jit(solution)/shard_map/ppermute | solution.py:509
  65.5 11.5 %collective-permute-start.6 = (bf16[576,256]{1,0:T(8,128)(2,1)S(1)}, bf16[576,256]{1,0:T(8,128)(2,1)S(1)}, u32[]{:S(2)}, u32[]{:S(2)}) collective-permute-start(bf16[576,256]{1,0:T(8,128)(2,1)S(1)} %broadcast_select_fusion), channel_id=1, source_target_pairs={{0,32},{1,97},{2,34},{3,99},{4,36},{5,101},{6,38},{7,103},{8,40},{... | collective-permute-start | bytes 884744 | tf_op jit(solution)/shard_map/ppermute | solution.py:515
  68.5 1.8 %collective-permute-start.3 = (f32[2,40,128]{2,1,0:T(8,128)S(1)}, f32[2,40,128]{2,1,0:T(8,128)S(1)}, u32[]{:S(2)}, u32[]{:S(2)}) collective-permute-start(f32[2,40,128]{2,1,0:T(8,128)S(1)} %merge.2.refs_0_), channel_id=1, source_target_pairs={{0,1},{1,0},{2,3},{3,2},{4,5},{5,4},{6,7},{7,6},{8,9},{9,8},{10,11... | collective-permute-start | bytes 122888 | tf_op jit(solution)/shard_map/ppermute | solution.py:556
  71.1 14.2 %all-to-all-start.1 = ((bf16[16,2,32,128]{3,2,1,0:T(8,128)(2,1)}), bf16[16,2,32,128]{3,2,1,0:T(8,128)(2,1)S(1)}, u32[]{:S(2)}, u32[]{:S(2)}) async-start(bf16[16,2,32,128]{3,2,1,0:T(8,128)(2,1)} %merge.3), calls=%async_computation.1 | async-start | bytes 524288 | tf_op jit(solution)/shard_map/all_to_all | solution.py:557

commit v2 on v1

--- a/solution.py
+++ b/solution.py
@@ -119,7 +119,6 @@
             pltpu.SemaphoreType.DMA((2, pieces)),
             pltpu.SemaphoreType.DMA((3,)),
         ],
-        compiler_params=params(20),
         name="produce",
     )(lengths, hidden, w_turned, gain.reshape(1, -1), jnp.asarray(frequencies()))
 
@@ -127,32 +126,47 @@
 WIDE = 640
 
 
-def pack_kernel(groups, owners, dest_ref, rows_ref, out_ref, turned_ref, count_ref):
+def shift_of(count):
+    assert count & (count - 1) == 0
+    return count.bit_length() - 1
+
+
+def pack_kernel(
+    groups, owners, dest_hbm, rows_hbm, out_ref, turned_ref, dest_ref, rows_ref, count_ref, sems
+):
+    copies = [
+        pltpu.make_async_copy(rows_hbm, rows_ref, sems.at[0]),
+        pltpu.make_async_copy(dest_hbm, dest_ref, sems.at[1]),
+    ]
+    for copy in copies:
+        copy.start()
     width, rows = rows_ref.shape
     block_rows = out_ref.shape[1]
     blocks = rows // block_rows
     group = lax.axis_index("pre")
     first = (group * owners + lax.axis_index("dec")) * blocks
+    def clear(k, carry):
+        for j in range(4):
+            count_ref[k * 4 + j] = 0
+        at = pl.ds(k * 4 * MOST, 4 * MOST)
+        out_ref[at] = jnp.full((4 * MOST,) + out_ref.shape[1:], -1.0, out_ref.dtype)
+        return carry
+
+    lax.fori_loop(0, owners // 4, clear, 0)
+    for copy in copies:
+        copy.wait()
     for at in range(0, width, 128):
         count = min(128, width - at)
         wide = rows_ref[at : at + count, :].astype(jnp.float32)
         if count < 128:
             wide = jnp.concatenate([wide, jnp.zeros((128 - count, rows), jnp.float32)], axis=0)
         turned_ref[:, :, at : at + 128] = jnp.transpose(wide).reshape(blocks, block_rows, 128)
-
-    def clear(owner, carry):
-        count_ref[owner] = 0
-        for rank in range(MOST):
-            out_ref[owner * MOST + rank] = jnp.full(out_ref.shape[1:], -1.0, out_ref.dtype)
-        return carry
-
-    lax.fori_loop(0, owners, clear, 0)
     lane = lax.broadcasted_iota(jnp.int32, (block_rows, WIDE), 1)
 
     def put(b, carry):
         target = dest_ref[first + b]
-        owner = lax.div(target, groups * owners)
-        slot = lax.rem(target, groups * owners) - group * owners
+        owner = lax.shift_right_logical(target, shift_of(groups * owners))
+        slot = (target & (groups * owners - 1)) - group * owners
         rank = count_ref[owner]
         count_ref[owner] = rank + 1
         block = jnp.where(lane < width, turned_ref[b], slot.astype(jnp.float32))
@@ -167,14 +181,16 @@
     block_rows = rows // owners
     return pl.pallas_call(
         functools.partial(pack_kernel, groups, owners),
-        in_specs=[pl.BlockSpec(memory_space=pltpu.SMEM), pl.BlockSpec(memory_space=pltpu.VMEM)],
+        in_specs=[pl.BlockSpec(memory_space=pltpu.HBM)] * 2,
         out_specs=pl.BlockSpec(memory_space=pltpu.VMEM),
         out_shape=jax.ShapeDtypeStruct((owners * MOST, block_rows, WIDE), produced.dtype),
         scratch_shapes=[
             pltpu.VMEM((owners, block_rows, WIDE), jnp.float32),
+            pltpu.SMEM(destination.shape, jnp.int32),
+            pltpu.VMEM(produced.shape, produced.dtype),
             pltpu.SMEM((owners,), jnp.int32),
+            pltpu.SemaphoreType.DMA((2,)),
         ],
-        compiler_params=params(8),
         name="pack",
     )(destination, produced)
 
@@ -257,27 +273,27 @@
         (lax.rem(group + shift, groups) * owners + owner) * count for shift in range(groups)
     ]
 
-    def body(item, carry):
-        b = lax.rem(item, batch)
+    def body(b, carry):
         request = request_ref[b]
         start = jnp.int32(0)
         for r in range(lengths_ref.shape[0] - 1):
             start = start + jnp.where(request > r, lengths_ref[r], 0)
-        stop = start + position_ref[lax.div(item, batch), b]
-        at = pl.ds(pl.multiple_of(item * heads, heads), heads)
-        for c, shift in enumerate(shifts):
-            base = bases[shift]
-            bias_ref[at, c * count : (c + 1) * count] = jnp.where(
-                (row >= start - base) & (row < stop - base), 0.0, mask_value
-            )
-        if valid_ref is not None:
-            seen = jnp.int32(0)
-            for base in bases:
-                seen = seen + jnp.where((start < base + count) & (stop > base), 1, 0)
-            valid_ref[at, :] = jnp.full((heads, 128), seen, jnp.int32)
-        return carry
-
-    lax.fori_loop(0, steps * batch, body, 0)
+        for s in range(steps):
+            stop = start + position_ref[s, b]
+            at = pl.ds(pl.multiple_of((s * batch + b) * heads, heads), heads)
+            for c, shift in enumerate(shifts):
+                base = bases[shift]
+                bias_ref[at, c * count : (c + 1) * count] = jnp.where(
+                    (row >= start - base) & (row < stop - base), 0.0, mask_value
+                )
+            if valid_ref is not None:
+                seen = jnp.int32(0)
+                for base in bases:
+                    seen = seen + jnp.where((start < base + count) & (stop > base), 1, 0)
+                valid_ref[at, :] = jnp.full((heads, 128), seen, jnp.int32)
+        return carry
+
+    lax.fori_loop(0, batch, body, 0)
 
 
 def update_state(latent, rope, chunk_refs, bias_ref, state):
@@ -299,9 +315,9 @@
     if state is not None:
         factor = jnp.exp2((old_peak - peak) * (score_scale * log2_e))
         total, mixed = total * factor, mixed * factor
-    for s, chunk_ref in zip(scores, chunk_refs):
-        p = jnp.exp2((s - peak) * (score_scale * log2_e))
-        total += jnp.sum(p, axis=1, keepdims=True)
+    weights = [jnp.exp2((s - peak) * (score_scale * log2_e)) for s in scores]
+    total += jnp.sum(functools.reduce(jnp.add, weights), axis=1, keepdims=True)
+    for p, chunk_ref in zip(weights, chunk_refs):
         mixed += lax.dot_general(
             p.astype(jnp.bfloat16),
             chunk_ref[:LAT, :],
@@ -329,14 +345,14 @@
     latent = latent_ref[...].reshape(rows, LAT)
     rope = rope_ref[...].reshape(rows, ROPE)
     peak, total, mixed = update_state(latent, rope, (k0, k1, k2), bias_ref, None)
-    mixed_ref[cut] = mixed
+    mixed_ref[...] = mixed
     lane = lax.broadcasted_iota(jnp.int32, (rows, 128), 1)
-    stat_ref[cut] = jnp.where(lane == 0, peak, total)
+    stat_ref[...] = jnp.where(lane == 0, peak, total)
 
 
 def far_kernel(
     owners, groups, lengths_ref, request_ref, position_ref, latent_ref, rope_ref,
-    k3, mixed_ref, stat_ref, w_ref, out_ref, bias_ref, valid_ref,
+    k3, mixed_ref, stat_ref, w_ref, keep_ref, send_ref, out_ref, bias_ref, valid_ref,
 ):
     items, heads, _ = latent_ref.shape
     rows = items * heads
@@ -353,8 +369,7 @@
 
     latent = latent_ref[...].reshape(rows, LAT)
     rope = rope_ref[...].reshape(rows, ROPE)
-    stat = stat_ref[cut]
-    state = (stat[:, 0:1], stat[:, 1:2], mixed_ref[cut])
+    state = (stat_ref[:, 0:1], stat_ref[:, 1:2], mixed_ref[...])
     peak, total, mixed = update_state(latent, rope, (k3,), bias_ref, state)
     valid = valid_ref[:, 0:1] > 0
     mixed = mixed * jnp.where(valid, 1.0 / total, 0.0)
@@ -364,7 +379,7 @@
     head = lax.broadcasted_iota(jnp.int32, (rows, 128), 0) % heads
     result = jnp.zeros((rows, 128), jnp.float32)
     for h in range(0, heads, 2):
-        pair = jnp.concatenate([w_ref[cut * heads + h], w_ref[cut * heads + h + 1]], axis=1)
+        pair = jnp.concatenate([w_ref[h], w_ref[h + 1]], axis=1)
         y = jnp.dot(upper, pair, preferred_element_type=jnp.float32)
         y += jnp.dot(lower, pair, preferred_element_type=jnp.float32)
         result = jnp.where(head == h, y[:, :128], result)
@@ -376,6 +391,18 @@
     lines = jnp.sum(lines, axis=1, keepdims=True)
     out_ref[:, all_heads:, :] += jnp.broadcast_to(lines, (items, PAD, 128))
 
+    @pl.when(cut == pl.num_programs(0) - 1)
+    def _():
+        half = items // 2
+        core = lax.axis_index("dec") & 1
+
+        def hand(i, carry):
+            keep_ref[i] = out_ref[core * half + i]
+            send_ref[i] = out_ref[(1 - core) * half + i]
+            return carry
+
+        lax.fori_loop(0, half, hand, 0)
+
 
 def attend(owners, lengths, row_request, step_position, latent, rope, chunks, w_up):
     items, heads, _ = latent.shape
@@ -384,129 +411,166 @@
     rows = items * CUT_HEADS
     count = chunks[0].shape[1]
     smem = pl.BlockSpec(memory_space=pltpu.SMEM)
-    vmem = pl.BlockSpec(memory_space=pltpu.VMEM)
     query_specs = [
         pl.BlockSpec((items, CUT_HEADS, LAT), lambda i: (0, i, 0)),
         pl.BlockSpec((items, CUT_HEADS, ROPE), lambda i: (0, i, 0)),
     ]
     scalars = (lengths, row_request, step_position)
+    state_specs = [
+        pl.BlockSpec((rows, LAT), lambda i: (i, 0)),
+        pl.BlockSpec((rows, 128), lambda i: (i, 0)),
+    ]
+    fixed = pl.BlockSpec(chunks[0].shape, lambda i: (0, 0))
     mixed, stat = pl.pallas_call(
         functools.partial(near_kernel, owners, groups),
         grid=(cut,),
-        in_specs=[smem] * 3 + query_specs + [vmem] * 3,
-        out_specs=[vmem, vmem],
+        in_specs=[smem] * 3 + query_specs + [fixed] * 3,
+        out_specs=state_specs,
         out_shape=[
-            jax.ShapeDtypeStruct((cut, rows, LAT), jnp.float32),
-            jax.ShapeDtypeStruct((cut, rows, 128), jnp.float32),
+            jax.ShapeDtypeStruct((cut * rows, LAT), jnp.float32),
+            jax.ShapeDtypeStruct((cut * rows, 128), jnp.float32),
         ],
         scratch_shapes=[pltpu.VMEM((rows, 3 * count), jnp.float32)],
-        compiler_params=params(16),
+        compiler_params=params(20),
         name="attend_near",
     )(*scalars, latent, rope, *chunks[:3])
+    out_shape = jax.ShapeDtypeStruct((items // 2, heads + PAD, 128), jnp.float32)
+    out_spec = pl.BlockSpec(out_shape.shape, lambda i: (0, 0, 0))
     return pl.pallas_call(
         functools.partial(far_kernel, owners, groups),
         grid=(cut,),
-        in_specs=[smem] * 3 + query_specs + [vmem] * 4,
-        out_specs=vmem,
-        out_shape=jax.ShapeDtypeStruct((items, heads + PAD, 128), jnp.float32),
+        in_specs=[smem] * 3
+        + query_specs
+        + [fixed]
+        + state_specs
+        + [pl.BlockSpec((CUT_HEADS,) + w_up.shape[1:], lambda i: (i, 0, 0))],
+        out_specs=[out_spec] * 2,
+        out_shape=[out_shape] * 2,
         scratch_shapes=[
+            pltpu.VMEM((items, heads + PAD, 128), jnp.float32),
             pltpu.VMEM((rows, count), jnp.float32),
             pltpu.VMEM((rows, 128), jnp.int32),
         ],
-        compiler_params=params(16),
+        compiler_params=params(48),
         name="attend_far",
     )(*scalars, latent, rope, chunks[3], mixed, stat, w_up)
 
 
-def merge_kernel(last, *refs):
-    parts, out_ref, scale_ref = refs[:-2], refs[-2], refs[-1]
-    folded = len(parts) == 1
-    sources = parts[0].shape[0] if folded else len(parts)
-    items, depth, lanes = parts[0].shape[-3:]
-    heads = depth - PAD
-    part = (lambda k: parts[0].at[k]) if folded else (lambda k: parts[k])
-    levels = [part(k)[:, heads:, :] for k in range(sources)]
+def merge_step(levels):
     peak = functools.reduce(jnp.maximum, levels)
     scales = [jnp.exp(level - peak) for level in levels]
     total = functools.reduce(jnp.add, scales)
+    return [scale / total for scale in scales], peak + jnp.log(total)
+
+
+def spread_columns(line, heads):
+    shape = line.shape[:-2] + (heads, line.shape[-1])
+    axis = len(shape) - 1
+    lane = lax.broadcasted_iota(jnp.int32, shape, axis)
+    row = lax.broadcasted_iota(jnp.int32, shape, axis - 1)
+    return jnp.sum(jnp.where(lane == row, line, 0.0), axis=axis, keepdims=True)
+
+
+def pair_kernel(mine_ref, other_ref, out_ref):
+    items, depth, _ = mine_ref.shape
+    heads = depth - PAD
+    step = 4
+
+    def body(k, carry):
+        at = pl.ds(k * step, step)
+        parts = [mine_ref[at], other_ref[at]]
+        scales, level = merge_step([part[:, heads:, :] for part in parts])
+        result = sum(
+            part[:, :heads, :] * spread_columns(scale[:, 0:1, :], heads)
+            for part, scale in zip(parts, scales)
+        )
+        out_ref[at, :heads, :] = result
+        out_ref[at, heads:, :] = level
+        return carry
+
+    lax.fori_loop(0, items // step, body, 0)
+
+
+def merge_pair(mine, other):
+    vmem = pl.BlockSpec(memory_space=pltpu.VMEM)
+    return pl.pallas_call(
+        pair_kernel,
+        in_specs=[vmem] * 2,
+        out_specs=vmem,
+        out_shape=jax.ShapeDtypeStruct(mine.shape, mine.dtype),
+        compiler_params=params(4),
+        name="merge_pair",
+    )(mine, other)
+
+
+def merge_kernel(parts_ref, out_ref, scale_ref):
+    sources, depth, lanes = parts_ref.shape
+    heads = depth - PAD
+    scales, _ = merge_step([parts_ref[k, heads:, :] for k in range(sources)])
     for k in range(sources):
-        scale_ref[k] = scales[k] / total
-    lane = lax.broadcasted_iota(jnp.int32, (items, heads, lanes), 2)
-    row = lax.broadcasted_iota(jnp.int32, (items, heads, lanes), 1)
-
-    def term(k, here):
-        line = scale_ref[k][:, 0:1, :]
-        column = jnp.sum(jnp.where(lane == row, line, 0.0), axis=2, keepdims=True)
-        return here[:, :heads, :] * column
-
-    result = jnp.zeros((items, heads, lanes), jnp.float32)
-    if folded:
-        result = lax.fori_loop(
-            0, sources, lambda k, so_far: so_far + term(k, parts[0].at[k]), result, unroll=4
-        )
-    else:
-        for k in range(sources):
-            result += term(k, parts[k])
-    if last:
-        result = result.astype(out_ref.dtype)
-        for copy in range(out_ref.shape[0]):
-            out_ref[copy] = result
-    else:
-        out_ref[:, :heads, :] = result
-        out_ref[:, heads:, :] = peak + jnp.log(total)
-
-
-def merge(parts, copies):
-    items, depth, lanes = parts[0].shape[-3:]
-    sources = parts[0].shape[0] if len(parts) == 1 else len(parts)
-    last = copies > 0
+        scale_ref[k] = scales[k]
+
+    def body(k, so_far):
+        return so_far + parts_ref[k, :heads, :] * spread_columns(scale_ref[k][0:1, :], heads)
+
+    result = lax.fori_loop(
+        0, sources, body, jnp.zeros((heads, lanes), jnp.float32), unroll=4
+    ).astype(out_ref.dtype)
+    for copy in range(out_ref.shape[0]):
+        out_ref[copy] = result
+
+
+def merge(parts):
+    sources, depth, lanes = parts.shape
     vmem = pl.BlockSpec(memory_space=pltpu.VMEM)
-    if last:
-        out_shape = jax.ShapeDtypeStruct((copies, items, depth - PAD, lanes), jnp.bfloat16)
-    else:
-        out_shape = jax.ShapeDtypeStruct((items, depth, lanes), jnp.float32)
-    return pl.pallas_call(
-        functools.partial(merge_kernel, last),
-        in_specs=[vmem] * len(parts),
+    return pl.pallas_call(
+        merge_kernel,
+        in_specs=[vmem],
         out_specs=vmem,
-        out_shape=out_shape,
-        scratch_shapes=[pltpu.VMEM((sources, items, PAD, lanes), jnp.float32)],
+        out_shape=jax.ShapeDtypeStruct((sources, depth - PAD, lanes), jnp.bfloat16),
+        scratch_shapes=[pltpu.VMEM((sources, PAD, lanes), jnp.float32)],
         compiler_params=params(4),
         name="merge",
-    )(*parts)
-
-
-def spread_kernel(in_ref, out_ref, wide_ref):
-    items, heads, lanes = in_ref.shape
-    wide_ref[...] = in_ref[...].astype(jnp.float32).reshape(items * heads, lanes)
+    )(parts)
+
+
+def spread_kernel(mine_ref, other_ref, out_ref, wide_ref):
+    half, heads, lanes = mine_ref.shape
+    core = lax.axis_index("dec") & 1
+    rows = half * heads
+    for place_at, ref in ((core, mine_ref), (1 - core, other_ref)):
+        at = pl.ds(pl.multiple_of(place_at * rows, rows), rows)
+        wide_ref[at, :] = ref[...].astype(jnp.float32).reshape(rows, lanes)
 
     def body(h, carry):
-        rows = wide_ref[pl.ds(h, items, stride=heads), :]
+        piece = wide_ref[pl.ds(h, 2 * half, stride=heads), :]
         at = pl.multiple_of(h * lanes, lanes)
-        out_ref[:, pl.ds(at, lanes)] = rows.astype(out_ref.dtype)
+        out_ref[:, pl.ds(at, lanes)] = piece.astype(out_ref.dtype)
         return carry
 
     lax.fori_loop(0, heads, body, 0, unroll=4)
 
 
-def spread(result):
-    items, heads, lanes = result.shape
+def spread(mine, other):
+    half, heads, lanes = mine.shape
     vmem = pl.BlockSpec(memory_space=pltpu.VMEM)
     return pl.pallas_call(
         spread_kernel,
-        in_specs=[vmem],
+        in_specs=[vmem] * 2,
         out_specs=vmem,
-        out_shape=jax.ShapeDtypeStruct((items, heads * lanes), result.dtype),
-        scratch_shapes=[pltpu.VMEM((items * heads, lanes), jnp.float32)],
+        out_shape=jax.ShapeDtypeStruct((2 * half, heads * lanes), mine.dtype),
+        scratch_shapes=[pltpu.VMEM((2 * half * heads, lanes), jnp.float32)],
         compiler_params=params(4),
         name="spread",
-    )(result)
-
-
-def around(piece, groups, owners):
+    )(mine, other)
+
+
+def around(piece, groups, owners, gate=None):
     core = lax.axis_index("dec") % 2
     before = lax.ppermute(piece, "pre", [(i, (i + 1) % groups) for i in range(groups)])
     after = lax.ppermute(piece, "pre", [(i, (i - 1) % groups) for i in range(groups)])
+    if gate is not None:
+        before, after, _ = lax.optimization_barrier((before, after, gate))
     forward = [
         (g * owners + d, (g + (1 if d % 2 == 0 else -1)) % groups * owners + d)
         for g in range(groups)
@@ -541,7 +605,7 @@
     exchanged = functools.partial(
         lax.all_to_all, axis_name="dec", split_axis=0, concat_axis=0, tiled=True
     )
-    parts = attend(
+    keep, send = attend(
         owners,
         request_rows,
         row_request,
@@ -551,15 +615,16 @@
         chunks,
         w_up_value,
     )
-    parts = exchanged(parts, axis_index_groups=plane)
-    mine = merge([parts.reshape((SIDE * SIDE, 2) + parts.shape[1:])], 0)
-    result = merge([mine, lax.ppermute(mine, "dec", sibling)], SIDE * SIDE)
-    result = exchanged(result, axis_index_groups=plane)
-    attention_out = spread(result.reshape((items,) + result.shape[2:])).reshape(steps, batch, -1)
+    parts = merge_pair(keep, lax.ppermute(send, "dec", sibling))
+    result = merge(exchanged(parts, axis_index_groups=plane))
 
     arrived = exchanged(pack(groups, owners, destination, produced))
     quarter = place(arrived, *produced.shape)
-    kv_cache = assemble(around(quarter, groups, owners)).T
+    kv_cache = assemble(around(quarter, groups, owners, result)).T
+
+    result = exchanged(result, axis_index_groups=plane)
+    result = spread(result, lax.ppermute(result, "dec", sibling))
+    attention_out = result.reshape(steps, batch, -1)
     return (attention_out, kv_cache)
 
 

time: 87 us -> 80.7 us (0.928)
  blocking collectives: 0 us -> 13.6 us
  local copies, waits for them, and re-layouts: 9.64 us -> 0.98 us
  starting transfers between devices: 33.2 us -> 27.2 us
  waiting for transfers between devices: 14.3 us -> 8.85 us
    all_to_all x0 -> x1, blocking collectives: none -> 13.6 us  [per_device(): result = exchanged(result, axis_index_groups=plane)]
    unnamed x24 -> x12, local copies, waits for them, and re-layouts: 9.64 us -> 0.98 us
    all_to_all x2 -> x1, starting transfers between devices: 12.5 us -> 6.68 us  [per_device(): result = merge(exchanged(parts, axis_index_groups=plane))]
    ppermute x2, waiting for transfers between devices: 6.32 us -> 1.4 us  [around(): lax.ppermute(piece, 'pre', [(i, (i + 1) % groups) for i in range(groups)])]
    all_to_all x2 -> x1, waiting for transfers between devices: 7.14 us -> 4.83 us  [per_device(): result = merge(exchanged(parts, axis_index_groups=plane))]
    ppermute x1 -> x2, waiting for transfers between devices: 0.87 us -> 2.6 us  [the longest x1 1.62 us: per_device(): parts = merge_pair(keep, lax.ppermute(send, 'dec', sibling))]
  transfers between devices with their start and end apart: 10 -> 10, of which waited for: 3 -> 4; matrix products, arithmetic and copies ran while one was open for 0% -> 0% of each run, Pallas kernels for 25% -> 27%
where the time goes in v2:
time: 80.7 us; the launch traced here: 80.3 us
  Pallas kernels  28.8 us (36%)
  starting transfers between devices  27.2 us (34%)
  blocking collectives  13.6 us (17%)
  waiting for transfers between devices  8.85 us (11%)
  local copies, waits for them, and re-layouts  0.98 us (1%)
  between operations  0.82 us (1%)
    all_to_all x1, blocking collectives, per_device(): result = exchanged(result, axis_index_groups=plane)  13.6 us
    pallas_call x1, Pallas kernels, attend(): pl.pallas_call(functools.partial(far_kernel, owners, groups), grid=(cut,)...  8.77 us
    all_to_all x1, starting transfers between devices, per_device(): arrived = exchanged(pack(groups, owners, destination, produced))  8.03 us
    all_to_all x1, starting transfers between devices, per_device(): result = merge(exchanged(parts, axis_index_groups=plane))  6.68 us
    pallas_call x1, Pallas kernels, produce(): pl.pallas_call(functools.partial(produce_kernel, owners), in_specs=[pl.Bl...  6.26 us
    pallas_call x1, Pallas kernels, attend(): pl.pallas_call(functools.partial(near_kernel, owners, groups), grid=(cut,...  5.89 us
    ppermute x2, starting transfers between devices, around(): lax.ppermute(piece, 'pre', [(i, (i - 1) % groups) for i in range(groups)])  4.86 us
    all_to_all x1, waiting for transfers between devices, per_device(): result = merge(exchanged(parts, axis_index_groups=plane))  4.83 us
  transfers between devices with their start and end apart: 10, of which 4 were waited for; matrix products, arithmetic and copies ran while one was open for 0% of the time, Pallas kernels for 27%

profile of v2, /device:TPU:1, one launch (start us, length us, event | category | flops | bytes accessed | tf_op | source)
XLA Modules:
  0.0 80.3 jit_solution(1107948067872683469)
XLA Ops:
  0.7 6.3 %produce.1.k0.rows_hbm = bf16[576,256]{1,0:T(8,128)(2,1)} custom-call(s32[4]{0:T(128)} %lengths_ref.3, bf16[256,7168]{1,0:T(8,128)(2,1)} %hidden_hbm.1, bf16[576,7168]{1,0:T(8,128)(2,1)} %bitcast.10, f32[1,512]{1,0:T(1,128)} %bitcast.13, f32[32,128]{1,0:T(8,128)} %constant.22.clone.freq_hbm), custom_call_target="tpu_custom_call" | custom-call | tf_op jit(solution)/shard_map/produce/pallas_call | solution.py:107
  6.9 2.5 %collective-permute-start = (bf16[576,256]{1,0:T(8,128)(2,1)}, bf16[576,256]{1,0:T(8,128)(2,1)S(1)}, u32[]{:S(2)}, u32[]{:S(2)}) collective-permute-start(bf16[576,256]{1,0:T(8,128)(2,1)} %produce.1.k0.rows_hbm), channel_id=1, source_target_pairs={{0,32},{32,64},{64,96},{96,0},{1,33},{33,65},{65,97},{97,1},{2,34}... | collective-permute-start | bytes 884744 | tf_op jit(solution)/shard_map/ppermute | solution.py:570
  9.5 2.2 %collective-permute-start.1 = (bf16[576,256]{1,0:T(8,128)(2,1)}, bf16[576,256]{1,0:T(8,128)(2,1)S(1)}, u32[]{:S(2)}, u32[]{:S(2)}) collective-permute-start(bf16[576,256]{1,0:T(8,128)(2,1)} %produce.1.k0.rows_hbm), channel_id=1, source_target_pairs={{0,96},{32,0},{64,32},{96,64},{1,97},{33,1},{65,33},{97,65},{2,98}... | collective-permute-start | bytes 884744 | tf_op jit(solution)/shard_map/ppermute | solution.py:571
  11.7 2.4 %pack.1 = bf16[64,8,640]{2,1,0:T(8,128)(2,1)} custom-call(s32[4096]{0:T(1024)} %dest_hbm.1, bf16[576,256]{1,0:T(8,128)(2,1)} %produce.1.k0.rows_hbm), custom_call_target="tpu_custom_call" | custom-call | tf_op jit(solution)/shard_map/pack/pallas_call | solution.py:182
  14.1 8.0 %all-to-all-start.2 = ((bf16[64,8,640]{2,1,0:T(8,128)(2,1)}), bf16[64,8,640]{2,1,0:T(8,128)(2,1)S(1)}, u32[]{:S(2)}, u32[]{:S(2)}) async-start(bf16[64,8,640]{2,1,0:T(8,128)(2,1)} %pack.1), calls=%async_computation.2 | async-start | bytes 1310720 | tf_op jit(solution)/shard_map/all_to_all | solution.py:621
  22.2 1.7 %collective-permute-start.2 = (bf16[576,256]{1,0:T(8,128)(2,1)S(1)}, bf16[576,256]{1,0:T(8,128)(2,1)S(1)}, u32[]{:S(2)}, u32[]{:S(2)}) collective-permute-start(bf16[576,256]{1,0:T(8,128)(2,1)S(1)} %broadcast_select_fusion.1), channel_id=1, source_target_pairs={{0,32},{1,97},{2,34},{3,99},{4,36},{5,101},{6,38},{7,103},{8,40},{... | collective-permute-start | bytes 884744 | tf_op jit(solution)/shard_map/ppermute | solution.py:579
  24.0 1.0 %copy-done.1 = bf16[576,256]{1,0:T(8,128)(2,1)S(1)} copy-done((bf16[576,256]{1,0:T(8,128)(2,1)S(1)}, bf16[576,256]{1,0:T(8,128)(2,1)}, u32[]{:S(2)}) %copy-start.1) | copy-done | bytes 294936
  24.9 5.9 %attend_near.1 = (f32[1024,512]{1,0:T(8,128)S(1)}, f32[1024,128]{1,0:T(8,128)S(1)}) custom-call(s32[4]{0:T(128)S(1)} %copy-done.4, s32[8]{0:T(128)S(1)} %copy-done.5, s32[4,8]{1,0:T(4,128)S(1)} %copy-done.3, bf16[32,32,512]{2,1,0:T(8,128)(2,1)S(1)} %bitcast.6, bf16[32,32,64]{2,1,0:T(8,128)(2,1)S(1)} %bitcast.8, bf16[576,256]{1,0:T(8,128)(2,1)S(1)} %copy-done.1, ...), custom_call_target="tpu_custom_call" | custom-call | tf_op jit(solution)/shard_map/attend_near/pallas_call | solution.py:424
  30.9 8.8 %attend_far.1 = (f32[16,40,128]{2,1,0:T(8,128)S(1)}, f32[16,40,128]{2,1,0:T(8,128)S(1)}) custom-call(s32[4]{0:T(128)S(1)} %copy-done.4, s32[8]{0:T(128)S(1)} %copy-done.5, s32[4,8]{1,0:T(4,128)S(1)} %copy-done.3, bf16[32,32,512]{2,1,0:T(8,128)(2,1)S(1)} %bitcast.7, bf16[32,32,64]{2,1,0:T(8,128)(2,1)S(1)} %bitcast.9, ...), custom_call_target="tpu_custom_call" | custom-call | tf_op jit(solution)/shard_map/attend_far/pallas_call | solution.py:439
  39.6 0.1 collective-permute-start.3
  39.7 1.6 %collective-permute-done.3.other_ref = f32[16,40,128]{2,1,0:T(8,128)S(1)} collective-permute-done((f32[16,40,128]{2,1,0:T(8,128)S(1)}, f32[16,40,128]{2,1,0:T(8,128)S(1)}, u32[]{:S(2)}, u32[]{:S(2)}) %collective-permute-start.3) | collective-permute-done | bytes 327712 | tf_op jit(solution)/shard_map/ppermute | solution.py:618
  41.3 1.2 %merge_pair.1 = f32[16,40,128]{2,1,0:T(8,128)} custom-call(f32[16,40,128]{2,1,0:T(8,128)S(1)} %get-tuple-element.10.mine_ref, f32[16,40,128]{2,1,0:T(8,128)S(1)} %collective-permute-done.3.other_ref), custom_call_target="tpu_custom_call" | custom-call | tf_op jit(solution)/shard_map/merge_pair/pallas_call | solution.py:496
  42.6 6.7 %all-to-all-start = ((f32[16,40,128]{2,1,0:T(8,128)}), f32[16,40,128]{2,1,0:T(8,128)S(1)}, u32[]{:S(2)}, u32[]{:S(2)}) async-start(f32[16,40,128]{2,1,0:T(8,128)} %merge_pair.1), calls=%async_computation | async-start | bytes 655360 | tf_op jit(solution)/shard_map/all_to_all | solution.py:619
  49.3 1.5 %place.1.refs_0_ = bf16[576,256]{1,0:T(8,128)(2,1)S(1)} custom-call(bf16[64,8,640]{2,1,0:T(8,128)(2,1)S(1)} %all-to-all-done.2.arrived_ref), custom_call_target="tpu_custom_call" | custom-call | tf_op jit(solution)/shard_map/place/pallas_call | solution.py:225
  50.9 2.7 %collective-permute-start.6 = (bf16[576,256]{1,0:T(8,128)(2,1)S(1)}, bf16[576,256]{1,0:T(8,128)(2,1)S(1)}, u32[]{:S(2)}, u32[]{:S(2)}) collective-permute-start(bf16[576,256]{1,0:T(8,128)(2,1)S(1)} %place.1.refs_0_), channel_id=1, source_target_pairs={{0,96},{32,0},{64,32},{96,64},{1,97},{33,1},{65,33},{97,65},{2,98}... | collective-permute-start | bytes 884744 | tf_op jit(solution)/shard_map/ppermute | solution.py:571
  53.5 4.8 %all-to-all-done.parts_ref = f32[16,40,128]{2,1,0:T(8,128)S(1)} async-done(((f32[16,40,128]{2,1,0:T(8,128)}), f32[16,40,128]{2,1,0:T(8,128)S(1)}, u32[]{:S(2)}, u32[]{:S(2)}) %all-to-all-start) | async-done | bytes 327712 | tf_op jit(solution)/shard_map/all_to_all | solution.py:619
  58.4 0.4 merge.1
  58.8 1.4 %collective-permute-done.5.refs_1_ = bf16[576,256]{1,0:T(8,128)(2,1)S(1)} collective-permute-done((bf16[576,256]{1,0:T(8,128)(2,1)S(1)}, bf16[576,256]{1,0:T(8,128)(2,1)S(1)}, u32[]{:S(2)}, u32[]{:S(2)}) %collective-permute-start.5) | collective-permute-done | bytes 294944 | tf_op jit(solution)/shard_map/ppermute | solution.py:570
  60.2 2.4 %collective-permute-start.7 = (bf16[576,256]{1,0:T(8,128)(2,1)S(1)}, bf16[576,256]{1,0:T(8,128)(2,1)S(1)}, u32[]{:S(2)}, u32[]{:S(2)}) collective-permute-start(bf16[576,256]{1,0:T(8,128)(2,1)S(1)} %broadcast_select_fusion), channel_id=1, source_target_pairs={{0,32},{1,97},{2,34},{3,99},{4,36},{5,101},{6,38},{7,103},{8,40},{... | collective-permute-start | bytes 884744 | tf_op jit(solution)/shard_map/ppermute | solution.py:579
  62.7 13.6 %all_to_all.15.mine_ref = bf16[16,32,128]{2,1,0:T(8,128)(2,1)S(1)} all-to-all(bf16[16,32,128]{2,1,0:T(8,128)(2,1)S(1)} %merge.1), channel_id=1, replica_groups={{0,2,4,6,8,10,12,14,16,18,20,22,24,26,28,30},{1,3,5,7,9,11,13,15,17,19,..., dimensions={0} | all-to-all | bytes 262144 | tf_op jit(solution)/shard_map/all_to_all | solution.py:625
  76.3 0.7 collective-permute-start.4
  77.0 1.0 %collective-permute-done.4.other_ref = bf16[16,32,128]{2,1,0:T(8,128)(2,1)S(1)} collective-permute-done((bf16[16,32,128]{2,1,0:T(8,128)(2,1)S(1)}, bf16[16,32,128]{2,1,0:T(8,128)(2,1)S(1)}, u32[]{:S(2)}, u32[]{:S(2)}) %collective-permute-start.4) | collective-permute-done | bytes 131104 | tf_op jit(solution)/shard_map/ppermute | solution.py:626
  78.0 1.1 %spread.1 = bf16[32,4096]{1,0:T(8,128)(2,1)} custom-call(bf16[16,32,128]{2,1,0:T(8,128)(2,1)S(1)} %all_to_all.15.mine_ref, bf16[16,32,128]{2,1,0:T(8,128)(2,1)S(1)} %collective-permute-done.4.other_ref), custom_call_target="tpu_custom_call" | custom-call | tf_op jit(solution)/shard_map/spread/pallas_call | solution.py:557
  79.1 1.2 %assemble.1 = bf16[576,1024]{1,0:T(8,128)(2,1)} custom-call(bf16[576,256]{1,0:T(8,128)(2,1)S(1)} %place.1.refs_0_, bf16[576,256]{1,0:T(8,128)(2,1)S(1)} %collective-permute-done.5.refs_1_, bf16[576,256]{1,0:T(8,128)(2,1)S(1)} %collective-permute-done.6.refs_2_, bf16[576,256]{1,0:T(8,128)(2,1)S(1)} %collective-permute-done.7.refs_3_), custom_call_target="tpu_custom_call" | custom-call | tf_op jit(solution)/shard_map/assemble/pallas_call | solution.py:256
  (20 shorter events, 0.2 us)
Async XLA Ops:
  0.6 23.3 %copy-start.2 = (bf16[4,8,32,64]{3,2,1,0:T(8,128)(2,1)S(1)}, bf16[4,8,32,64]{3,2,1,0:T(8,128)(2,1)}, u32[]{:S(2)}) copy-start(bf16[4,8,32,64]{3,2,1,0:T(8,128)(2,1)} %param.15) | copy-start | bytes 393220
  0.6 23.3 %copy-start.3 = (s32[4,8]{1,0:T(4,128)S(1)}, s32[4,8]{1,0:T(4,128)}, u32[]{:S(2)}) copy-start(s32[4,8]{1,0:T(4,128)} %position_ref.3) | copy-start | bytes 388
  0.7 23.3 %copy-start.4 = (s32[4]{0:T(128)S(1)}, s32[4]{0:T(128)}, u32[]{:S(2)}) copy-start(s32[4]{0:T(128)} %lengths_ref.3) | copy-start | bytes 52
  0.7 23.3 %copy-start.5 = (s32[8]{0:T(128)S(1)}, s32[8]{0:T(128)}, u32[]{:S(2)}) copy-start(s32[8]{0:T(128)} %request_ref.3) | copy-start | bytes 100
  6.9 17.0 %copy-start = (bf16[4,8,32,512]{3,2,1,0:T(8,128)(2,1)S(1)}, bf16[4,8,32,512]{3,2,1,0:T(8,128)(2,1)}, u32[]{:S(2)}) copy-start(bf16[4,8,32,512]{3,2,1,0:T(8,128)(2,1)} %param.14) | copy-start | bytes 3145732
  6.9 15.2 %collective-permute-start = (bf16[576,256]{1,0:T(8,128)(2,1)}, bf16[576,256]{1,0:T(8,128)(2,1)S(1)}, u32[]{:S(2)}, u32[]{:S(2)}) collective-permute-start(bf16[576,256]{1,0:T(8,128)(2,1)} %produce.1.k0.rows_hbm), channel_id=1, source_target_pairs={{0,32},{32,64},{64,96},{96,0},{1,33},{33,65},{65,97},{97,1},{2,34}... | collective-permute-start | bytes 884744 | tf_op jit(solution)/shard_map/ppermute | solution.py:570
  9.5 12.7 %collective-permute-start.1 = (bf16[576,256]{1,0:T(8,128)(2,1)}, bf16[576,256]{1,0:T(8,128)(2,1)S(1)}, u32[]{:S(2)}, u32[]{:S(2)}) collective-permute-start(bf16[576,256]{1,0:T(8,128)(2,1)} %produce.1.k0.rows_hbm), channel_id=1, source_target_pairs={{0,96},{32,0},{64,32},{96,64},{1,97},{33,1},{65,33},{97,65},{2,98}... | collective-permute-start | bytes 884744 | tf_op jit(solution)/shard_map/ppermute | solution.py:571
  14.1 28.5 %all-to-all-start.2 = ((bf16[64,8,640]{2,1,0:T(8,128)(2,1)}), bf16[64,8,640]{2,1,0:T(8,128)(2,1)S(1)}, u32[]{:S(2)}, u32[]{:S(2)}) async-start(bf16[64,8,640]{2,1,0:T(8,128)(2,1)} %pack.1), calls=%async_computation.2 | async-start | bytes 1310720 | tf_op jit(solution)/shard_map/all_to_all | solution.py:621
  22.2 8.6 %collective-permute-start.2 = (bf16[576,256]{1,0:T(8,128)(2,1)S(1)}, bf16[576,256]{1,0:T(8,128)(2,1)S(1)}, u32[]{:S(2)}, u32[]{:S(2)}) collective-permute-start(bf16[576,256]{1,0:T(8,128)(2,1)S(1)} %broadcast_select_fusion.1), channel_id=1, source_target_pairs={{0,32},{1,97},{2,34},{3,99},{4,36},{5,101},{6,38},{7,103},{8,40},{... | collective-permute-start | bytes 884744 | tf_op jit(solution)/shard_map/ppermute | solution.py:579
  24.0 1.0 %copy-start.1 = (bf16[576,256]{1,0:T(8,128)(2,1)S(1)}, bf16[576,256]{1,0:T(8,128)(2,1)}, u32[]{:S(2)}) copy-start(bf16[576,256]{1,0:T(8,128)(2,1)} %produce.1.k0.rows_hbm) | copy-start | bytes 884740
  39.6 1.7 %collective-permute-start.3 = (f32[16,40,128]{2,1,0:T(8,128)S(1)}, f32[16,40,128]{2,1,0:T(8,128)S(1)}, u32[]{:S(2)}, u32[]{:S(2)}) collective-permute-start(f32[16,40,128]{2,1,0:T(8,128)S(1)} %get-tuple-element.11), channel_id=1, source_target_pairs={{0,1},{1,0},{2,3},{3,2},{4,5},{5,4},{6,7},{7,6},{8,9},{9,8},{10,11... | collective-permute-start | bytes 983048 | tf_op jit(solution)/shard_map/ppermute | solution.py:618
  42.6 15.8 %all-to-all-start = ((f32[16,40,128]{2,1,0:T(8,128)}), f32[16,40,128]{2,1,0:T(8,128)S(1)}, u32[]{:S(2)}, u32[]{:S(2)}) async-start(f32[16,40,128]{2,1,0:T(8,128)} %merge_pair.1), calls=%async_computation | async-start | bytes 655360 | tf_op jit(solution)/shard_map/all_to_all | solution.py:619
  50.8 9.4 %collective-permute-start.5 = (bf16[576,256]{1,0:T(8,128)(2,1)S(1)}, bf16[576,256]{1,0:T(8,128)(2,1)S(1)}, u32[]{:S(2)}, u32[]{:S(2)}) collective-permute-start(bf16[576,256]{1,0:T(8,128)(2,1)S(1)} %place.1.refs_0_), channel_id=1, source_target_pairs={{0,32},{32,64},{64,96},{96,0},{1,33},{33,65},{65,97},{97,1},{2,34}... | collective-permute-start | bytes 884744 | tf_op jit(solution)/shard_map/ppermute | solution.py:570
  50.9 9.4 %collective-permute-start.6 = (bf16[576,256]{1,0:T(8,128)(2,1)S(1)}, bf16[576,256]{1,0:T(8,128)(2,1)S(1)}, u32[]{:S(2)}, u32[]{:S(2)}) collective-permute-start(bf16[576,256]{1,0:T(8,128)(2,1)S(1)} %place.1.refs_0_), channel_id=1, source_target_pairs={{0,96},{32,0},{64,32},{96,64},{1,97},{33,1},{65,33},{97,65},{2,98}... | collective-permute-start | bytes 884744 | tf_op jit(solution)/shard_map/ppermute | solution.py:571
  60.2 18.9 %collective-permute-start.7 = (bf16[576,256]{1,0:T(8,128)(2,1)S(1)}, bf16[576,256]{1,0:T(8,128)(2,1)S(1)}, u32[]{:S(2)}, u32[]{:S(2)}) collective-permute-start(bf16[576,256]{1,0:T(8,128)(2,1)S(1)} %broadcast_select_fusion), channel_id=1, source_target_pairs={{0,32},{1,97},{2,34},{3,99},{4,36},{5,101},{6,38},{7,103},{8,40},{... | collective-permute-start | bytes 884744 | tf_op jit(solution)/shard_map/ppermute | solution.py:579
  76.3 1.7 %collective-permute-start.4 = (bf16[16,32,128]{2,1,0:T(8,128)(2,1)S(1)}, bf16[16,32,128]{2,1,0:T(8,128)(2,1)S(1)}, u32[]{:S(2)}, u32[]{:S(2)}) collective-permute-start(bf16[16,32,128]{2,1,0:T(8,128)(2,1)S(1)} %all_to_all.15.mine_ref), channel_id=1, source_target_pairs={{0,1},{1,0},{2,3},{3,2},{4,5},{5,4},{6,7},{7,6},{8,9},{9,8},{10,11... | collective-permute-start | bytes 393224 | tf_op jit(solution)/shard_map/ppermute | solution.py:626

commit v3 on v2

v3 whole, which is shorter than its diff:
```python
import functools
import math

import jax
import jax.numpy as jnp
import numpy as np
from jax import lax
from jax.experimental import pallas as pl
from jax.experimental.pallas import tpu as pltpu
from jax.sharding import PartitionSpec as P

LAT = 512
ROPE = 64
MOST = 2
PAD = 8
SIDE = 4
TURNS = (0, 3, 1, 2)
CUT_HEADS = 8
DEPTH = 1024

score_scale = 0.07216878364870323
mask_value = -1e30
norm_eps = 1e-06
log2_e = 1.4426950408889634


def frequencies():
    half = ROPE // 2
    pair_index = np.arange(half, dtype=np.float64)
    frequency = np.exp(pair_index * (-2.0 * math.log(10000.0) / ROPE)).astype(np.float32)
    return np.tile(frequency[:, None], (1, 128))


WIDE = 640


def shift_of(count):
    assert count & (count - 1) == 0
    return count.bit_length() - 1


def params(megabytes):
    return pltpu.CompilerParams(vmem_limit_bytes=megabytes * 1024 * 1024)


def produce_kernel(
    groups, owners, lengths_hbm, dest_hbm, hidden_hbm, w_hbm, gain_hbm, freq_hbm,
    out_ref, packed_ref, hidden_ref, w_ref, acc_ref, lengths_ref, dest_ref, gain_ref, freq_ref,
    turn_ref, column_ref, rows_ref, count_ref, slot_ref, sems, small_sems,
):
    pieces, rows, depth = hidden_ref.shape
    half = ROPE // 2
    small = [
        pltpu.make_async_copy(source, target, small_sems.at[k])
        for k, (source, target) in enumerate(
            (
                (lengths_hbm, lengths_ref),
                (dest_hbm, dest_ref),
                (gain_hbm, gain_ref),
                (freq_hbm, freq_ref),
            )
        )
    ]

    def copies(k):
        columns = pl.ds(pl.multiple_of(k * depth, depth), depth)
        return (
            pltpu.make_async_copy(hidden_hbm.at[:, columns], hidden_ref.at[k], sems.at[0, k]),
            pltpu.make_async_copy(w_hbm.at[:, columns], w_ref.at[k], sems.at[1, k]),
        )

    def begin(k, carry):
        for copy in copies(k):
            copy.start()
        return carry

    for copy in small:
        copy.start()
    lax.fori_loop(0, pieces, begin, 0)
    acc_ref[...] = jnp.zeros_like(acc_ref)
    packed_ref[...] = jnp.full(packed_ref.shape, -1.0, packed_ref.dtype)
    for copy in small:
        copy.wait()
    group = lax.axis_index("pre")
    device = group * owners + lax.axis_index("dec")
    block_rows = packed_ref.shape[1]
    blocks = rows // block_rows

    def clear(owner, carry):
        count_ref[owner] = 0
        return carry

    def choose(b, carry):
        owner = lax.shift_right_logical(dest_ref[device * blocks + b], shift_of(groups * owners))
        rank = count_ref[owner]
        count_ref[owner] = rank + 1
        slot_ref[b] = owner * MOST + rank
        return carry

    lax.fori_loop(0, owners, clear, 0)
    lax.fori_loop(0, blocks, choose, 0)
    row = device * rows + lax.broadcasted_iota(jnp.int32, (1, rows), 1)
    start = jnp.zeros((1, rows), jnp.int32)
    first_row = jnp.int32(0)
    for r in range(lengths_ref.shape[0] - 1):
        first_row = first_row + lengths_ref[r]
        start = jnp.where(row >= first_row, first_row, start)
    angles = freq_ref[:, 0:1] * (row - start).astype(jnp.float32)
    turn_ref[:half, :] = jnp.cos(angles)
    turn_ref[half:, :] = jnp.sin(angles)
    column_ref[...] = jnp.transpose(jnp.broadcast_to(gain_ref[...], (128, LAT)))

    def body(k, carry):
        for copy in copies(k):
            copy.wait()
        acc_ref[...] += lax.dot_general(
            w_ref[k],
            hidden_ref[k],
            (((1,), (1,)), ((), ())),
            preferred_element_type=jnp.float32,
        )
        return carry

    lax.fori_loop(0, pieces, body, 0)
    latent = acc_ref[:LAT, :]
    inverse_rms = lax.rsqrt(jnp.mean(latent * latent, axis=0, keepdims=True) + norm_eps)
    out_ref[:LAT, :] = (latent * inverse_rms * column_ref[:, 0:1]).astype(out_ref.dtype)
    cosine, sine = turn_ref[:half, :], turn_ref[half:, :]
    first = acc_ref[LAT : LAT + half, :]
    second = acc_ref[LAT + half :, :]
    turned = first * cosine - second * sine
    out_ref[LAT : LAT + half, :] = turned.astype(out_ref.dtype)
    turned = second * cosine + first * sine
    out_ref[LAT + half :, :] = turned.astype(out_ref.dtype)
    width = out_ref.shape[0]
    for at in range(0, width, 128):
        count = min(128, width - at)
        wide = out_ref[at : at + count, :].astype(jnp.float32)
        if count < 128:
            wide = jnp.concatenate([wide, jnp.zeros((128 - count, rows), jnp.float32)], axis=0)
        rows_ref[:, :, at : at + 128] = jnp.transpose(wide).reshape(blocks, block_rows, 128)
    lane = lax.broadcasted_iota(jnp.int32, (block_rows, WIDE), 1)

    def put(b, carry):
        place_at = (dest_ref[device * blocks + b] & (groups * owners - 1)) - group * owners
        block = jnp.where(lane < width, rows_ref[b], place_at.astype(jnp.float32))
        packed_ref[slot_ref[b]] = block.astype(packed_ref.dtype)
        return carry

    lax.fori_loop(0, blocks, put, 0, unroll=4)


def produce(groups, owners, lengths, destination, hidden, w_turned, gain):
    rows, width = hidden.shape
    row_width = w_turned.shape[0]
    pieces = width // DEPTH
    block_rows = rows // owners
    vmem = pl.BlockSpec(memory_space=pltpu.VMEM)
    return pl.pallas_call(
        functools.partial(produce_kernel, groups, owners),
        in_specs=[pl.BlockSpec(memory_space=pltpu.HBM)] * 6,
        out_specs=[vmem, vmem],
        out_shape=[
            jax.ShapeDtypeStruct((row_width, rows), jnp.bfloat16),
            jax.ShapeDtypeStruct((owners * MOST, block_rows, WIDE), jnp.bfloat16),
        ],
        scratch_shapes=[
            pltpu.VMEM((pieces, rows, DEPTH), jnp.bfloat16),
            pltpu.VMEM((pieces, row_width, DEPTH), jnp.bfloat16),
            pltpu.VMEM((row_width, rows), jnp.float32),
            pltpu.SMEM(lengths.shape, jnp.int32),
            pltpu.SMEM(destination.shape, jnp.int32),
            pltpu.VMEM((1, LAT), jnp.float32),
            pltpu.VMEM((ROPE // 2, 128), jnp.float32),
            pltpu.VMEM((ROPE, rows), jnp.float32),
            pltpu.VMEM((LAT, 128), jnp.float32),
            pltpu.VMEM((owners, block_rows, WIDE), jnp.float32),
            pltpu.SMEM((owners,), jnp.int32),
            pltpu.SMEM((owners,), jnp.int32),
            pltpu.SemaphoreType.DMA((2, pieces)),
            pltpu.SemaphoreType.DMA((4,)),
        ],
        name="produce",
    )(
        lengths,
        destination,
        hidden,
        w_turned,
        gain.reshape(1, -1),
        jnp.asarray(frequencies()),
    )


def place_kernel(arrived_ref, out_ref, rows_ref):
    blocks, block_rows, _ = arrived_ref.shape
    width, rows = out_ref.shape
    part = 128 // block_rows
    row = lax.broadcasted_iota(jnp.int32, (rows, 128), 0).astype(jnp.float32)
    lane = lax.broadcasted_iota(jnp.int32, (1, 128), 1)
    within = lax.rem(lane, block_rows).astype(jnp.float32)
    rows_ref[...] = jnp.zeros_like(rows_ref)

    def body(k, carry):
        source = arrived_ref[pl.ds(k * part, part)].astype(jnp.float32).reshape(128, WIDE)
        slot = jnp.transpose(source[:, WIDE - 128 :])[127:128, :]
        select = jnp.where(row == slot * block_rows + within, 1.0, 0.0).astype(jnp.bfloat16)
        rows_ref[...] += jnp.dot(
            select, source.astype(jnp.bfloat16), preferred_element_type=jnp.float32
        )
        return carry

    lax.fori_loop(0, blocks // part, body, 0)
    for at in range(0, width, 128):
        count = min(128, width - at)
        turned = jnp.transpose(rows_ref[:, at : at + 128])
        out_ref[at : at + count, :] = turned[:count].astype(out_ref.dtype)


def place(arrived, width, rows):
    vmem = pl.BlockSpec(memory_space=pltpu.VMEM)
    return pl.pallas_call(
        place_kernel,
        in_specs=[vmem],
        out_specs=vmem,
        out_shape=jax.ShapeDtypeStruct((width, rows), arrived.dtype),
        scratch_shapes=[pltpu.VMEM((rows, WIDE), jnp.float32)],
        compiler_params=params(8),
        name="place",
    )(arrived)


def assemble_kernel(*refs):
    pieces, out_ref = refs[:-1], refs[-1]
    groups = len(pieces)
    group = lax.axis_index("pre")
    width, rows = pieces[0].shape
    step = 64

    def body(k, carry):
        part = pl.ds(pl.multiple_of(k * step, step), step)
        for turn, piece in zip(TURNS, pieces):
            at = pl.multiple_of((group ^ turn) * rows, rows)
            out_ref[part, pl.ds(at, rows)] = piece[part, :]
        return carry

    lax.fori_loop(0, width // step, body, 0)


def assemble(pieces):
    width, rows = pieces[0].shape
    vmem = pl.BlockSpec(memory_space=pltpu.VMEM)
    return pl.pallas_call(
        assemble_kernel,
        in_specs=[vmem] * len(pieces),
        out_specs=vmem,
        out_shape=jax.ShapeDtypeStruct((width, rows * len(pieces)), pieces[0].dtype),
        compiler_params=params(4),
        name="assemble",
    )(*pieces)


def prepare_kernel(
    owners, groups, lengths_ref, request_ref, position_ref, own_hbm,
    bias_ref, valid_ref, own_ref, sem,
):
    copy = pltpu.make_async_copy(own_hbm, own_ref, sem)
    copy.start()
    steps, batch = position_ref.shape
    heads = CUT_HEADS
    count = own_ref.shape[1]
    group, owner = lax.axis_index("pre"), lax.axis_index("dec")
    row = lax.broadcasted_iota(jnp.int32, (heads, count), 1)
    bases = [((group ^ turn) * owners + owner) * count for turn in TURNS]

    def fill(b, carry):
        request = request_ref[b]
        start = jnp.int32(0)
        for r in range(lengths_ref.shape[0] - 1):
            start = start + jnp.where(request > r, lengths_ref[r], 0)
        for s in range(steps):
            stop = start + position_ref[s, b]
            at = pl.ds(pl.multiple_of((s * batch + b) * heads, heads), heads)
            seen = jnp.int32(0)
            for c, base in enumerate(bases):
                bias_ref[at, c * count : (c + 1) * count] = jnp.where(
                    (row >= start - base) & (row < stop - base), 0.0, mask_value
                )
                seen = seen + jnp.where((start < base + count) & (stop > base), 1, 0)
            valid_ref[at, :] = jnp.full((heads, 128), seen, jnp.int32)
        return carry

    lax.fori_loop(0, batch, fill, 0)
    copy.wait()


def prepare(owners, groups, lengths, row_request, step_position, own):
    rows = step_position.size * CUT_HEADS
    smem = pl.BlockSpec(memory_space=pltpu.SMEM)
    vmem = pl.BlockSpec(memory_space=pltpu.VMEM)
    return pl.pallas_call(
        functools.partial(prepare_kernel, owners, groups),
        in_specs=[smem] * 3 + [pl.BlockSpec(memory_space=pl.ANY)],
        out_specs=[vmem] * 3,
        out_shape=[
            jax.ShapeDtypeStruct((rows, groups * own.shape[1]), jnp.float32),
            jax.ShapeDtypeStruct((rows, 128), jnp.int32),
            jax.ShapeDtypeStruct(own.shape, own.dtype),
        ],
        scratch_shapes=[pltpu.SemaphoreType.DMA(())],
        compiler_params=params(8),
        name="prepare",
    )(lengths, row_request, step_position, own)


def attend_kernel(
    bias_ref, valid_ref, latent_ref, rope_ref, k0, k1, k2, k3, w_hbm,
    keep_ref, send_ref, out_ref, w_ref, sems,
):
    chunk_refs = (k0, k1, k2, k3)
    items, cuts, heads, _ = latent_ref.shape
    rows = items * heads
    all_heads = cuts * heads
    count = k0.shape[1]

    def weights_of(cut):
        part = pl.ds(cut * heads, heads)
        return pltpu.make_async_copy(w_hbm.at[part], w_ref.at[part], sems.at[cut])

    for cut in range(cuts):
        weights_of(cut).start()
    out_ref[:, all_heads:, :] = jnp.zeros((items, PAD, 128), jnp.float32)
    head = lax.broadcasted_iota(jnp.int32, (rows, 128), 0) % heads
    lane = lax.broadcasted_iota(jnp.int32, (rows, 128), 1)

    def body(cut, carry):
        latent = latent_ref[:, cut].reshape(rows, LAT)
        rope = rope_ref[:, cut].reshape(rows, ROPE)
        scores = []
        for c, chunk_ref in enumerate(chunk_refs):
            s = jnp.dot(latent, chunk_ref[:LAT, :], preferred_element_type=jnp.float32)
            s += jnp.dot(rope, chunk_ref[LAT:, :], preferred_element_type=jnp.float32)
            scores.append(s + bias_ref[:, c * count : (c + 1) * count])
        peak = jnp.max(functools.reduce(jnp.maximum, scores), axis=1, keepdims=True)
        weights = [jnp.exp2((s - peak) * (score_scale * log2_e)) for s in scores]
        total = jnp.sum(functools.reduce(jnp.add, weights), axis=1, keepdims=True)
        mixed = sum(
            lax.dot_general(
                p.astype(jnp.bfloat16),
                chunk_ref[:LAT, :],
                (((1,), (1,)), ((), ())),
                preferred_element_type=jnp.float32,
            )
            for p, chunk_ref in zip(weights, chunk_refs)
        )
        valid = valid_ref[:, 0:1] > 0
        mixed = mixed * jnp.where(valid, 1.0 / total, 0.0)
        level = jnp.where(valid, peak * score_scale + jnp.log(total), mask_value)
        upper = mixed.astype(jnp.bfloat16)
        lower = (mixed - upper.astype(jnp.float32)).astype(jnp.bfloat16)
        weights_of(cut).wait()
        result = jnp.zeros((rows, 128), jnp.float32)
        for h in range(0, heads, 2):
            pair = jnp.concatenate([w_ref[cut * heads + h], w_ref[cut * heads + h + 1]], axis=1)
            y = jnp.dot(upper, pair, preferred_element_type=jnp.float32)
            y += jnp.dot(lower, pair, preferred_element_type=jnp.float32)
            result = jnp.where(head == h, y[:, :128], result)
            result = jnp.where(head == h + 1, y[:, 128:], result)
        at = pl.multiple_of(cut * heads, heads)
        out_ref[:, pl.ds(at, heads), :] = result.reshape(items, heads, 128)
        lines = jnp.where(lane == head + at, level, 0.0).reshape(items, heads, 128)
        lines = jnp.sum(lines, axis=1, keepdims=True)
        out_ref[:, all_heads:, :] += jnp.broadcast_to(lines, (items, PAD, 128))
        return carry

    lax.fori_loop(0, cuts, body, 0)
    half = items // 2
    core = lax.axis_index("dec") & 1

    def hand(i, carry):
        keep_ref[i] = out_ref[core * half + i]
        send_ref[i] = out_ref[(1 - core) * half + i]
        return carry

    lax.fori_loop(0, half, hand, 0)


def attend(bias, valid, latent, rope, chunks, w_up):
    items, heads, _ = latent.shape
    cuts = heads // CUT_HEADS
    vmem = pl.BlockSpec(memory_space=pltpu.VMEM)
    out_shape = jax.ShapeDtypeStruct((items // 2, heads + PAD, 128), jnp.float32)
    return pl.pallas_call(
        attend_kernel,
        in_specs=[vmem] * 8 + [pl.BlockSpec(memory_space=pl.ANY)],
        out_specs=[vmem] * 2,
        out_shape=[out_shape] * 2,
        scratch_shapes=[
            pltpu.VMEM((items, heads + PAD, 128), jnp.float32),
            pltpu.VMEM(w_up.shape, w_up.dtype),
            pltpu.SemaphoreType.DMA((cuts,)),
        ],
        compiler_params=params(48),
        name="attend",
    )(
        bias,
        valid,
        latent.reshape(items, cuts, CUT_HEADS, -1),
        rope.reshape(items, cuts, CUT_HEADS, -1),
        *chunks,
        w_up,
    )


def merge_step(levels):
    peak = functools.reduce(jnp.maximum, levels)
    scales = [jnp.exp(level - peak) for level in levels]
    total = functools.reduce(jnp.add, scales)
    return [scale / total for scale in scales], peak + jnp.log(total)


def spread_columns(line, heads):
    shape = line.shape[:-2] + (heads, line.shape[-1])
    axis = len(shape) - 1
    lane = lax.broadcasted_iota(jnp.int32, shape, axis)
    row = lax.broadcasted_iota(jnp.int32, shape, axis - 1)
    return jnp.sum(jnp.where(lane == row, line, 0.0), axis=axis, keepdims=True)


def pair_kernel(mine_ref, other_ref, out_ref):
    items, depth, _ = mine_ref.shape
    heads = depth - PAD
    step = 4

    def body(k, carry):
        at = pl.ds(k * step, step)
        parts = [mine_ref[at], other_ref[at]]
        scales, level = merge_step([part[:, heads:, :] for part in parts])
        result = sum(
            part[:, :heads, :] * spread_columns(scale[:, 0:1, :], heads)
            for part, scale in zip(parts, scales)
        )
        out_ref[at, :heads, :] = result
        out_ref[at, heads:, :] = level
        return carry

    lax.fori_loop(0, items // step, body, 0)


def merge_pair(mine, other):
    vmem = pl.BlockSpec(memory_space=pltpu.VMEM)
    return pl.pallas_call(
        pair_kernel,
        in_specs=[vmem] * 2,
        out_specs=vmem,
        out_shape=jax.ShapeDtypeStruct(mine.shape, mine.dtype),
        compiler_params=params(4),
        name="merge_pair",
    )(mine, other)


def merge_kernel(parts_ref, out_ref, scale_ref):
    sources, depth, lanes = parts_ref.shape
    heads = depth - PAD
    scales, _ = merge_step([parts_ref[k, heads:, :] for k in range(sources)])
    for k in range(sources):
        scale_ref[k] = scales[k]

    def body(k, so_far):
        return so_far + parts_ref[k, :heads, :] * spread_columns(scale_ref[k][0:1, :], heads)

    result = lax.fori_loop(
        0, sources, body, jnp.zeros((heads, lanes), jnp.float32), unroll=4
    ).astype(out_ref.dtype)
    for copy in range(out_ref.shape[0]):
        out_ref[copy] = result


def merge(parts):
    sources, depth, lanes = parts.shape
    vmem = pl.BlockSpec(memory_space=pltpu.VMEM)
    return pl.pallas_call(
        merge_kernel,
        in_specs=[vmem],
        out_specs=vmem,
        out_shape=jax.ShapeDtypeStruct((sources, depth - PAD, lanes), jnp.bfloat16),
        scratch_shapes=[pltpu.VMEM((sources, PAD, lanes), jnp.float32)],
        compiler_params=params(4),
        name="merge",
    )(parts)


def spread_kernel(mine_ref, other_ref, out_ref, wide_ref):
    half, heads, lanes = mine_ref.shape
    core = lax.axis_index("dec") & 1
    rows = half * heads
    for place_at, ref in ((core, mine_ref), (1 - core, other_ref)):
        for k in range(half):
            at = pl.ds(pl.multiple_of(place_at * rows + (half - 1 - k) * heads, heads), heads)
            wide_ref[at, :] = ref[k].astype(jnp.float32)

    def body(h, carry):
        piece = wide_ref[pl.ds(h, 2 * half, stride=heads), :]
        at = pl.multiple_of(h * lanes, lanes)
        out_ref[:, pl.ds(at, lanes)] = piece.astype(out_ref.dtype)
        return carry

    lax.fori_loop(0, heads, body, 0, unroll=4)


def spread(mine, other):
    half, heads, lanes = mine.shape
    vmem = pl.BlockSpec(memory_space=pltpu.VMEM)
    return pl.pallas_call(
        spread_kernel,
        in_specs=[vmem] * 2,
        out_specs=vmem,
        out_shape=jax.ShapeDtypeStruct((2 * half, heads * lanes), mine.dtype),
        scratch_shapes=[pltpu.VMEM((2 * half * heads, lanes), jnp.float32)],
        compiler_params=params(4),
        name="spread",
    )(mine, other)


def exchange(piece, groups, turn):
    return lax.ppermute(piece, "pre", [(i, i ^ turn) for i in range(groups)])


def around(piece, groups, owners):
    core = lax.axis_index("dec") % 2
    first = exchange(piece, groups, 3)
    second = exchange(piece, groups, 1)
    forward = [
        (g * owners + d, (g ^ (1 if d % 2 == 0 else 3)) * owners + d)
        for g in range(groups)
        for d in range(owners)
    ]
    chosen = jnp.where(core == 0, first, second)
    far = lax.ppermute(chosen, ("pre", "dec"), forward)
    return [piece, first, second, far], chosen


def per_device(
    hidden,
    w_down,
    kv_gain,
    query_latent,
    query_rope,
    w_up_value,
    request_rows,
    row_request,
    step_position,
    destination,
):
    groups = lax.axis_size("pre")
    owners = lax.axis_size("dec")
    steps, batch, heads, _ = query_latent.shape
    items = steps * batch
    plane = [[2 * k + core for k in range(SIDE * SIDE)] for core in range(2)]
    reverse = [group[::-1] for group in plane]
    sibling = [(d, d ^ 1) for d in range(owners)]

    produced, packed = produce(
        groups, owners, request_rows, destination, hidden, w_down.T, kv_gain
    )
    chunks, chosen = around(produced, groups, owners)

    exchanged = functools.partial(
        lax.all_to_all, axis_name="dec", split_axis=0, concat_axis=0, tiled=True
    )
    lengths, _ = lax.optimization_barrier((request_rows, chosen))
    bias, valid, chunks[0] = prepare(
        owners, groups, lengths, row_request, step_position, produced
    )
    keep, send = attend(
        bias,
        valid,
        query_latent.reshape(items, heads, -1),
        query_rope.reshape(items, heads, -1),
        chunks,
        w_up_value,
    )
    arrived = exchanged(packed)
    quarter = place(arrived, *produced.shape)
    pieces = [quarter] + [exchange(quarter, groups, turn) for turn in TURNS[1:]]
    kv_cache = assemble(pieces).T

    keep, _ = lax.optimization_barrier((keep, quarter))
    parts = merge_pair(keep, lax.ppermute(send, "dec", sibling))
    result = merge(exchanged(parts, axis_index_groups=plane))
    result = exchanged(result, axis_index_groups=reverse)
    result = spread(result, lax.ppermute(result, "dec", sibling))
    attention_out = result.reshape(steps, batch, -1)
    return (attention_out, kv_cache)


def solution(mesh):
    return jax.shard_map(
        per_device,
        mesh=mesh,
        in_specs=(
            P(("pre", "dec"), None),
            P(),
            P(),
            P(None, None, "pre", None),
            P(None, None, "pre", None),
            P("pre", None, None),
            P(),
            P(),
            P(),
            P(),
        ),
        out_specs=(P(None, None, "pre"), P("dec", None)),
        check_vma=False,
    )
```

time: 80.7 us -> 70 us (0.87)
  Pallas kernels: 28.8 us -> 20.8 us
  blocking collectives: 13.6 us -> 9.34 us
  starting transfers between devices: 27.2 us -> 28.6 us
    pallas_call x4 -> x3, Pallas kernels: 23.3 us -> 15.4 us  [the longest x1 7.46 us: attend(): pl.pallas_call(attend_kernel, in_specs=[vmem] * 8 + [pl.BlockSpec(memory_...]
    all_to_all x1, blocking collectives: 13.6 us -> 9.34 us  [per_device(): result = exchanged(result, axis_index_groups=reverse)]
    ppermute x6, waiting for transfers between devices: 1.41 us -> 3.93 us  [the longest x1 3.92 us: around(): far = lax.ppermute(chosen, ('pre', 'dec'), forward)]
    ppermute x1, starting transfers between devices: 0.74 us -> 2.64 us  [per_device(): result = spread(result, lax.ppermute(result, 'dec', sibling))]
    ppermute x6, starting transfers between devices: 11.6 us -> 9.8 us  [the longest x5 8.56 us: exchange(): return lax.ppermute(piece, 'pre', [(i, i ^ turn) for i in range(groups)])]
    ppermute x1, waiting for transfers between devices: 1.62 us -> 0.01 us  [per_device(): parts = merge_pair(keep, lax.ppermute(send, 'dec', sibling))]
    ppermute x1, starting transfers between devices: 0.09 us -> 1.24 us  [per_device(): parts = merge_pair(keep, lax.ppermute(send, 'dec', sibling))]
    ppermute x1, waiting for transfers between devices: 0.99 us -> 0.01 us  [per_device(): result = spread(result, lax.ppermute(result, 'dec', sibling))]
  transfers between devices with their start and end apart: 10 -> 10, of which waited for: 4 -> 2; matrix products, arithmetic and copies ran while one was open for 0% -> 0% of each run, Pallas kernels for 27% -> 17%
where the time goes in v3:
time: 70 us; the launch traced here: 69.6 us
  starting transfers between devices  28.6 us (41%)
  Pallas kernels  20.8 us (30%)
  blocking collectives  9.34 us (13%)
  waiting for transfers between devices  9.07 us (13%)
  local copies, waits for them, and re-layouts  0.98 us (1%)
  between operations  0.79 us (1%)
    all_to_all x1, blocking collectives, per_device(): result = exchanged(result, axis_index_groups=reverse)  9.34 us
    ppermute x5, starting transfers between devices, exchange(): return lax.ppermute(piece, 'pre', [(i, i ^ turn) for i in range(groups)])  8.56 us
    all_to_all x1, starting transfers between devices, per_device(): arrived = exchanged(packed)  8.07 us
    pallas_call x1, Pallas kernels, attend(): pl.pallas_call(attend_kernel, in_specs=[vmem] * 8 + [pl.BlockSpec(memory_...  7.46 us
    pallas_call x1, Pallas kernels, produce(): pl.pallas_call(functools.partial(produce_kernel, groups, owners), in_spec...  6.94 us
    all_to_all x1, starting transfers between devices, per_device(): result = merge(exchanged(parts, axis_index_groups=plane))  6.8 us
    all_to_all x1, waiting for transfers between devices, per_device(): result = merge(exchanged(parts, axis_index_groups=plane))  5.13 us
    ppermute x1, waiting for transfers between devices, around(): far = lax.ppermute(chosen, ('pre', 'dec'), forward)  3.92 us
  transfers between devices with their start and end apart: 10, of which 2 were waited for; matrix products, arithmetic and copies ran while one was open for 0% of the time, Pallas kernels for 17%

profile of v3, /device:TPU:1, one launch (start us, length us, event | category | flops | bytes accessed | tf_op | source)
XLA Modules:
  0.0 69.6 jit_solution(9451083591858140770)
XLA Ops:
  0.7 6.9 %produce.1 = (bf16[576,256]{1,0:T(8,128)(2,1)}, bf16[64,8,640]{2,1,0:T(8,128)(2,1)}) custom-call(s32[4]{0:T(128)} %lengths_ref, s32[4096]{0:T(1024)} %dest_hbm.1, bf16[256,7168]{1,0:T(8,128)(2,1)} %hidden_hbm.1, bf16[576,7168]{1,0:T(8,128)(2,1)} %bitcast.8, f32[1,512]{1,0:T(1,128)} %bitcast.11, f32[32,128]{1,0:T(8,128)} %constant.20.clone.freq_hbm), custom_call_target="tpu_custom_call" | custom-call | tf_op jit(solution)/shard_map/produce/pallas_call | solution.py:159
  7.6 4.6 %collective-permute-start = (bf16[576,256]{1,0:T(8,128)(2,1)}, bf16[576,256]{1,0:T(8,128)(2,1)S(1)}, u32[]{:S(2)}, u32[]{:S(2)}) collective-permute-start(bf16[576,256]{1,0:T(8,128)(2,1)} %get-tuple-element.11.own_hbm), channel_id=1, source_target_pairs={{0,96},{32,64},{64,32},{96,0},{1,97},{33,65},{65,33},{97,1},{2,98}... | collective-permute-start | bytes 884744 | tf_op jit(solution)/shard_map/ppermute | solution.py:525
  12.2 8.1 %all-to-all-start = ((bf16[64,8,640]{2,1,0:T(8,128)(2,1)}), bf16[64,8,640]{2,1,0:T(8,128)(2,1)S(1)}, u32[]{:S(2)}, u32[]{:S(2)}) async-start(bf16[64,8,640]{2,1,0:T(8,128)(2,1)} %get-tuple-element.17), calls=%async_computation | async-start | bytes 1310720 | tf_op jit(solution)/shard_map/all_to_all | solution.py:582
  20.3 0.0 collective-permute-done.1.k2
  20.4 1.2 %collective-permute-start.2 = (bf16[576,256]{1,0:T(8,128)(2,1)S(1)}, bf16[576,256]{1,0:T(8,128)(2,1)S(1)}, u32[]{:S(2)}, u32[]{:S(2)}) collective-permute-start(bf16[576,256]{1,0:T(8,128)(2,1)S(1)} %broadcast_select_fusion), channel_id=1, source_target_pairs={{0,32},{1,97},{2,34},{3,99},{4,36},{5,101},{6,38},{7,103},{8,40},{... | collective-permute-start | bytes 884744 | tf_op jit(solution)/shard_map/ppermute | solution.py:538
  21.7 1.0 %copy-done.1 = bf16[576,256]{1,0:T(8,128)(2,1)S(1)} copy-done((bf16[576,256]{1,0:T(8,128)(2,1)S(1)}, bf16[576,256]{1,0:T(8,128)(2,1)}, u32[]{:S(2)}) %copy-start.1) | copy-done | bytes 294936
  22.6 1.0 %prepare.1 = (f32[256,1024]{1,0:T(8,128)S(1)}, s32[256,128]{1,0:T(8,128)S(1)}, bf16[576,256]{1,0:T(8,128)(2,1)S(1)}) custom-call(s32[4]{0:T(128)S(1)} %copy-done.4, s32[8]{0:T(128)S(1)} %copy-done.5, s32[4,8]{1,0:T(4,128)S(1)} %copy-done.3, bf16[576,256]{1,0:T(8,128)(2,1)S(1)} %copy-done.1), custom_call_target="tpu_custom_call" | custom-call | tf_op jit(solution)/shard_map/prepare/pallas_call | solution.py:300
  23.6 3.9 %collective-permute-done.2.k3 = bf16[576,256]{1,0:T(8,128)(2,1)S(1)} collective-permute-done((bf16[576,256]{1,0:T(8,128)(2,1)S(1)}, bf16[576,256]{1,0:T(8,128)(2,1)S(1)}, u32[]{:S(2)}, u32[]{:S(2)}) %collective-permute-start.2) | collective-permute-done | bytes 294944 | tf_op jit(solution)/shard_map/ppermute | solution.py:538
  27.6 7.5 %attend.1 = (f32[16,40,128]{2,1,0:T(8,128)S(1)}, f32[16,40,128]{2,1,0:T(8,128)S(1)}) custom-call(f32[256,1024]{1,0:T(8,128)S(1)} %get-tuple-element.13.bias_ref, s32[256,128]{1,0:T(8,128)S(1)} %get-tuple-element.14.valid_ref, bf16[32,4,8,512]{3,2,1,0:T(8,128)(2,1)S(1)} %bitcast.6, bf16[32,4,8,64]{3,2,1,0:T(8,128)(2,1)S(1)} %bitcast.7, ...), custom_call_target="tpu_custom_call" | custom-call | tf_op jit(solution)/shard_map/attend/pallas_call | solution.py:392
  35.0 1.2 %collective-permute-start.3 = (f32[16,40,128]{2,1,0:T(8,128)S(1)}, f32[16,40,128]{2,1,0:T(8,128)S(1)}, u32[]{:S(2)}, u32[]{:S(2)}) collective-permute-start(f32[16,40,128]{2,1,0:T(8,128)S(1)} %get-tuple-element.19), channel_id=1, source_target_pairs={{0,1},{1,0},{2,3},{3,2},{4,5},{5,4},{6,7},{7,6},{8,9},{9,8},{10,11... | collective-permute-start | bytes 983048 | tf_op jit(solution)/shard_map/ppermute | solution.py:588
  36.3 0.0 all-to-all-done.arrived_ref
  36.3 1.5 %place.1.refs_0_ = bf16[576,256]{1,0:T(8,128)(2,1)S(1)} custom-call(bf16[64,8,640]{2,1,0:T(8,128)(2,1)S(1)} %all-to-all-done.arrived_ref), custom_call_target="tpu_custom_call" | custom-call | tf_op jit(solution)/shard_map/place/pallas_call | solution.py:221
  37.7 0.0 collective-permute-done.3.other_ref
  37.8 1.2 %merge_pair.1 = f32[16,40,128]{2,1,0:T(8,128)} custom-call(f32[16,40,128]{2,1,0:T(8,128)S(1)} %get-tuple-element.18.mine_ref, f32[16,40,128]{2,1,0:T(8,128)S(1)} %collective-permute-done.3.other_ref), custom_call_target="tpu_custom_call" | custom-call | tf_op jit(solution)/shard_map/merge_pair/pallas_call | solution.py:451
  39.0 6.8 %all-to-all-start.1 = ((f32[16,40,128]{2,1,0:T(8,128)}), f32[16,40,128]{2,1,0:T(8,128)S(1)}, u32[]{:S(2)}, u32[]{:S(2)}) async-start(f32[16,40,128]{2,1,0:T(8,128)} %merge_pair.1), calls=%async_computation.1 | async-start | bytes 655360 | tf_op jit(solution)/shard_map/all_to_all | solution.py:589
  45.8 1.3 %collective-permute-start.5 = (bf16[576,256]{1,0:T(8,128)(2,1)S(1)}, bf16[576,256]{1,0:T(8,128)(2,1)S(1)}, u32[]{:S(2)}, u32[]{:S(2)}) collective-permute-start(bf16[576,256]{1,0:T(8,128)(2,1)S(1)} %place.1.refs_0_), channel_id=1, source_target_pairs={{0,96},{32,64},{64,32},{96,0},{1,97},{33,65},{65,33},{97,1},{2,98}... | collective-permute-start | bytes 884744 | tf_op jit(solution)/shard_map/ppermute | solution.py:525
  47.1 2.6 %collective-permute-start.7 = (bf16[576,256]{1,0:T(8,128)(2,1)S(1)}, bf16[576,256]{1,0:T(8,128)(2,1)S(1)}, u32[]{:S(2)}, u32[]{:S(2)}) collective-permute-start(bf16[576,256]{1,0:T(8,128)(2,1)S(1)} %place.1.refs_0_), channel_id=1, source_target_pairs={{0,64},{32,96},{64,0},{96,32},{1,65},{33,97},{65,1},{97,33},{2,66}... | collective-permute-start | bytes 884744 | tf_op jit(solution)/shard_map/ppermute | solution.py:525
  49.8 5.1 %all-to-all-done.1.parts_ref = f32[16,40,128]{2,1,0:T(8,128)S(1)} async-done(((f32[16,40,128]{2,1,0:T(8,128)}), f32[16,40,128]{2,1,0:T(8,128)S(1)}, u32[]{:S(2)}, u32[]{:S(2)}) %all-to-all-start.1) | async-done | bytes 327712 | tf_op jit(solution)/shard_map/all_to_all | solution.py:589
  54.9 0.4 merge.1
  55.3 9.3 %all_to_all.15.mine_ref = bf16[16,32,128]{2,1,0:T(8,128)(2,1)S(1)} all-to-all(bf16[16,32,128]{2,1,0:T(8,128)(2,1)S(1)} %merge.1), channel_id=1, replica_groups={{30,28,26,24,22,20,18,16,14,12,10,8,6,4,2,0},{31,29,27,25,23,21,19,17,1..., dimensions={0} | all-to-all | bytes 262144 | tf_op jit(solution)/shard_map/all_to_all | solution.py:590
  64.7 2.6 %collective-permute-start.4 = (bf16[16,32,128]{2,1,0:T(8,128)(2,1)S(1)}, bf16[16,32,128]{2,1,0:T(8,128)(2,1)S(1)}, u32[]{:S(2)}, u32[]{:S(2)}) collective-permute-start(bf16[16,32,128]{2,1,0:T(8,128)(2,1)S(1)} %all_to_all.15.mine_ref), channel_id=1, source_target_pairs={{0,1},{1,0},{2,3},{3,2},{4,5},{5,4},{6,7},{7,6},{8,9},{9,8},{10,11... | collective-permute-start | bytes 393224 | tf_op jit(solution)/shard_map/ppermute | solution.py:591
  67.3 0.0 collective-permute-done.5.refs_1_
  67.3 1.2 %assemble.1 = bf16[576,1024]{1,0:T(8,128)(2,1)} custom-call(bf16[576,256]{1,0:T(8,128)(2,1)S(1)} %place.1.refs_0_, bf16[576,256]{1,0:T(8,128)(2,1)S(1)} %collective-permute-done.5.refs_1_, bf16[576,256]{1,0:T(8,128)(2,1)S(1)} %collective-permute-done.6.refs_2_, bf16[576,256]{1,0:T(8,128)(2,1)S(1)} %collective-permute-done.7.refs_3_), custom_call_target="tpu_custom_call" | custom-call | tf_op jit(solution)/shard_map/assemble/pallas_call | solution.py:252
  68.5 1.1 %spread.1 = bf16[32,4096]{1,0:T(8,128)(2,1)} custom-call(bf16[16,32,128]{2,1,0:T(8,128)(2,1)S(1)} %all_to_all.15.mine_ref, bf16[16,32,128]{2,1,0:T(8,128)(2,1)S(1)} %collective-permute-done.4.other_ref), custom_call_target="tpu_custom_call" | custom-call | tf_op jit(solution)/shard_map/spread/pallas_call | solution.py:513
  (18 shorter events, 0.1 us)
Async XLA Ops:
  0.6 21.0 %copy-start.3 = (s32[4,8]{1,0:T(4,128)S(1)}, s32[4,8]{1,0:T(4,128)}, u32[]{:S(2)}) copy-start(s32[4,8]{1,0:T(4,128)} %position_ref.1) | copy-start | bytes 388
  0.6 21.0 %copy-start.4 = (s32[4]{0:T(128)S(1)}, s32[4]{0:T(128)}, u32[]{:S(2)}) copy-start(s32[4]{0:T(128)} %lengths_ref) | copy-start | bytes 52
  0.7 21.0 %copy-start.5 = (s32[8]{0:T(128)S(1)}, s32[8]{0:T(128)}, u32[]{:S(2)}) copy-start(s32[8]{0:T(128)} %request_ref.1) | copy-start | bytes 100
  0.7 26.9 %copy-start = (bf16[4,8,32,512]{3,2,1,0:T(8,128)(2,1)S(1)}, bf16[4,8,32,512]{3,2,1,0:T(8,128)(2,1)}, u32[]{:S(2)}) copy-start(bf16[4,8,32,512]{3,2,1,0:T(8,128)(2,1)} %param.14) | copy-start | bytes 3145732
  0.7 26.9 %copy-start.2 = (bf16[4,8,32,64]{3,2,1,0:T(8,128)(2,1)S(1)}, bf16[4,8,32,64]{3,2,1,0:T(8,128)(2,1)}, u32[]{:S(2)}) copy-start(bf16[4,8,32,64]{3,2,1,0:T(8,128)(2,1)} %param.15) | copy-start | bytes 393220
  7.6 12.7 %collective-permute-start = (bf16[576,256]{1,0:T(8,128)(2,1)}, bf16[576,256]{1,0:T(8,128)(2,1)S(1)}, u32[]{:S(2)}, u32[]{:S(2)}) collective-permute-start(bf16[576,256]{1,0:T(8,128)(2,1)} %get-tuple-element.11.own_hbm), channel_id=1, source_target_pairs={{0,96},{32,64},{64,32},{96,0},{1,97},{33,65},{65,33},{97,1},{2,98}... | collective-permute-start | bytes 884744 | tf_op jit(solution)/shard_map/ppermute | solution.py:525
  12.2 8.1 %collective-permute-start.1 = (bf16[576,256]{1,0:T(8,128)(2,1)}, bf16[576,256]{1,0:T(8,128)(2,1)S(1)}, u32[]{:S(2)}, u32[]{:S(2)}) collective-permute-start(bf16[576,256]{1,0:T(8,128)(2,1)} %get-tuple-element.11.own_hbm), channel_id=1, source_target_pairs={{0,32},{32,0},{64,96},{96,64},{1,33},{33,1},{65,97},{97,65},{2,34}... | collective-permute-start | bytes 884744 | tf_op jit(solution)/shard_map/ppermute | solution.py:525
  12.2 24.0 %all-to-all-start = ((bf16[64,8,640]{2,1,0:T(8,128)(2,1)}), bf16[64,8,640]{2,1,0:T(8,128)(2,1)S(1)}, u32[]{:S(2)}, u32[]{:S(2)}) async-start(bf16[64,8,640]{2,1,0:T(8,128)(2,1)} %get-tuple-element.17), calls=%async_computation | async-start | bytes 1310720 | tf_op jit(solution)/shard_map/all_to_all | solution.py:582
  20.4 7.2 %collective-permute-start.2 = (bf16[576,256]{1,0:T(8,128)(2,1)S(1)}, bf16[576,256]{1,0:T(8,128)(2,1)S(1)}, u32[]{:S(2)}, u32[]{:S(2)}) collective-permute-start(bf16[576,256]{1,0:T(8,128)(2,1)S(1)} %broadcast_select_fusion), channel_id=1, source_target_pairs={{0,32},{1,97},{2,34},{3,99},{4,36},{5,101},{6,38},{7,103},{8,40},{... | collective-permute-start | bytes 884744 | tf_op jit(solution)/shard_map/ppermute | solution.py:538
  21.7 1.0 %copy-start.1 = (bf16[576,256]{1,0:T(8,128)(2,1)S(1)}, bf16[576,256]{1,0:T(8,128)(2,1)}, u32[]{:S(2)}) copy-start(bf16[576,256]{1,0:T(8,128)(2,1)} %get-tuple-element.11.own_hbm) | copy-start | bytes 884740
  35.0 2.7 %collective-permute-start.3 = (f32[16,40,128]{2,1,0:T(8,128)S(1)}, f32[16,40,128]{2,1,0:T(8,128)S(1)}, u32[]{:S(2)}, u32[]{:S(2)}) collective-permute-start(f32[16,40,128]{2,1,0:T(8,128)S(1)} %get-tuple-element.19), channel_id=1, source_target_pairs={{0,1},{1,0},{2,3},{3,2},{4,5},{5,4},{6,7},{7,6},{8,9},{9,8},{10,11... | collective-permute-start | bytes 983048 | tf_op jit(solution)/shard_map/ppermute | solution.py:588
  39.0 15.9 %all-to-all-start.1 = ((f32[16,40,128]{2,1,0:T(8,128)}), f32[16,40,128]{2,1,0:T(8,128)S(1)}, u32[]{:S(2)}, u32[]{:S(2)}) async-start(f32[16,40,128]{2,1,0:T(8,128)} %merge_pair.1), calls=%async_computation.1 | async-start | bytes 655360 | tf_op jit(solution)/shard_map/all_to_all | solution.py:589
  45.8 21.5 %collective-permute-start.5 = (bf16[576,256]{1,0:T(8,128)(2,1)S(1)}, bf16[576,256]{1,0:T(8,128)(2,1)S(1)}, u32[]{:S(2)}, u32[]{:S(2)}) collective-permute-start(bf16[576,256]{1,0:T(8,128)(2,1)S(1)} %place.1.refs_0_), channel_id=1, source_target_pairs={{0,96},{32,64},{64,32},{96,0},{1,97},{33,65},{65,33},{97,1},{2,98}... | collective-permute-start | bytes 884744 | tf_op jit(solution)/shard_map/ppermute | solution.py:525
  47.1 20.2 %collective-permute-start.6 = (bf16[576,256]{1,0:T(8,128)(2,1)S(1)}, bf16[576,256]{1,0:T(8,128)(2,1)S(1)}, u32[]{:S(2)}, u32[]{:S(2)}) collective-permute-start(bf16[576,256]{1,0:T(8,128)(2,1)S(1)} %place.1.refs_0_), channel_id=1, source_target_pairs={{0,32},{32,0},{64,96},{96,64},{1,33},{33,1},{65,97},{97,65},{2,34}... | collective-permute-start | bytes 884744 | tf_op jit(solution)/shard_map/ppermute | solution.py:525
  47.1 20.2 %collective-permute-start.7 = (bf16[576,256]{1,0:T(8,128)(2,1)S(1)}, bf16[576,256]{1,0:T(8,128)(2,1)S(1)}, u32[]{:S(2)}, u32[]{:S(2)}) collective-permute-start(bf16[576,256]{1,0:T(8,128)(2,1)S(1)} %place.1.refs_0_), channel_id=1, source_target_pairs={{0,64},{32,96},{64,0},{96,32},{1,65},{33,97},{65,1},{97,33},{2,66}... | collective-permute-start | bytes 884744 | tf_op jit(solution)/shard_map/ppermute | solution.py:525
  64.7 3.8 %collective-permute-start.4 = (bf16[16,32,128]{2,1,0:T(8,128)(2,1)S(1)}, bf16[16,32,128]{2,1,0:T(8,128)(2,1)S(1)}, u32[]{:S(2)}, u32[]{:S(2)}) collective-permute-start(bf16[16,32,128]{2,1,0:T(8,128)(2,1)S(1)} %all_to_all.15.mine_ref), channel_id=1, source_target_pairs={{0,1},{1,0},{2,3},{3,2},{4,5},{5,4},{6,7},{7,6},{8,9},{9,8},{10,11... | collective-permute-start | bytes 393224 | tf_op jit(solution)/shard_map/ppermute | solution.py:591

commit v4 on v3

--- a/solution.py
+++ b/solution.py
@@ -359,10 +359,11 @@
         lower = (mixed - upper.astype(jnp.float32)).astype(jnp.bfloat16)
         weights_of(cut).wait()
         result = jnp.zeros((rows, 128), jnp.float32)
+        both = jnp.concatenate([upper, lower], axis=0)
         for h in range(0, heads, 2):
             pair = jnp.concatenate([w_ref[cut * heads + h], w_ref[cut * heads + h + 1]], axis=1)
-            y = jnp.dot(upper, pair, preferred_element_type=jnp.float32)
-            y += jnp.dot(lower, pair, preferred_element_type=jnp.float32)
+            y = jnp.dot(both, pair, preferred_element_type=jnp.float32)
+            y = y[:rows] + y[rows:]
             result = jnp.where(head == h, y[:, :128], result)
             result = jnp.where(head == h + 1, y[:, 128:], result)
         at = pl.multiple_of(cut * heads, heads)
@@ -458,32 +459,32 @@
     )(mine, other)
 
 
-def merge_kernel(parts_ref, out_ref, scale_ref):
-    sources, depth, lanes = parts_ref.shape
+def merge_kernel(last, parts_ref, out_ref):
+    sources, _, depth, _ = parts_ref.shape
     heads = depth - PAD
-    scales, _ = merge_step([parts_ref[k, heads:, :] for k in range(sources)])
-    for k in range(sources):
-        scale_ref[k] = scales[k]
-
-    def body(k, so_far):
-        return so_far + parts_ref[k, :heads, :] * spread_columns(scale_ref[k][0:1, :], heads)
-
-    result = lax.fori_loop(
-        0, sources, body, jnp.zeros((heads, lanes), jnp.float32), unroll=4
+    scales, level = merge_step([parts_ref[k, :, heads:, :] for k in range(sources)])
+    result = sum(
+        parts_ref[k, :, :heads, :] * spread_columns(scales[k][:, 0:1, :], heads)
+        for k in range(sources)
     ).astype(out_ref.dtype)
     for copy in range(out_ref.shape[0]):
-        out_ref[copy] = result
-
-
-def merge(parts):
-    sources, depth, lanes = parts.shape
-    vmem = pl.BlockSpec(memory_space=pltpu.VMEM)
-    return pl.pallas_call(
-        merge_kernel,
+        out_ref[copy, :, :heads, :] = result
+        if not last:
+            out_ref[copy, :, heads:, :] = level
+
+
+def merge(parts, last):
+    sources, items, depth, lanes = parts.shape
+    vmem = pl.BlockSpec(memory_space=pltpu.VMEM)
+    if last:
+        out_shape = jax.ShapeDtypeStruct((SIDE, items, depth - PAD, lanes), jnp.bfloat16)
+    else:
+        out_shape = jax.ShapeDtypeStruct((SIDE, items, depth, lanes), jnp.float32)
+    return pl.pallas_call(
+        functools.partial(merge_kernel, last),
         in_specs=[vmem],
         out_specs=vmem,
-        out_shape=jax.ShapeDtypeStruct((sources, depth - PAD, lanes), jnp.bfloat16),
-        scratch_shapes=[pltpu.VMEM((sources, PAD, lanes), jnp.float32)],
+        out_shape=out_shape,
         compiler_params=params(4),
         name="merge",
     )(parts)
@@ -492,10 +493,9 @@
 def spread_kernel(mine_ref, other_ref, out_ref, wide_ref):
     half, heads, lanes = mine_ref.shape
     core = lax.axis_index("dec") & 1
-    rows = half * heads
     for place_at, ref in ((core, mine_ref), (1 - core, other_ref)):
         for k in range(half):
-            at = pl.ds(pl.multiple_of(place_at * rows + (half - 1 - k) * heads, heads), heads)
+            at = pl.ds(pl.multiple_of((place_at * half + k) * heads, heads), heads)
             wide_ref[at, :] = ref[k].astype(jnp.float32)
 
     def body(h, carry):
@@ -555,8 +555,12 @@
     owners = lax.axis_size("dec")
     steps, batch, heads, _ = query_latent.shape
     items = steps * batch
-    plane = [[2 * k + core for k in range(SIDE * SIDE)] for core in range(2)]
-    reverse = [group[::-1] for group in plane]
+    line_x = [
+        [2 * (y * SIDE + x) + core for x in range(SIDE)] for y in range(SIDE) for core in range(2)
+    ]
+    line_y = [
+        [2 * (y * SIDE + x) + core for y in range(SIDE)] for x in range(SIDE) for core in range(2)
+    ]
     sibling = [(d, d ^ 1) for d in range(owners)]
 
     produced, packed = produce(
@@ -581,14 +585,18 @@
     )
     arrived = exchanged(packed)
     quarter = place(arrived, *produced.shape)
-    pieces = [quarter] + [exchange(quarter, groups, turn) for turn in TURNS[1:]]
-    kv_cache = assemble(pieces).T
-
     keep, _ = lax.optimization_barrier((keep, quarter))
     parts = merge_pair(keep, lax.ppermute(send, "dec", sibling))
-    result = merge(exchanged(parts, axis_index_groups=plane))
-    result = exchanged(result, axis_index_groups=reverse)
+    parts = exchanged(parts, axis_index_groups=line_x)
+    parts = merge(parts.reshape((SIDE, SIDE) + parts.shape[1:]), False)
+    late_quarter, _ = lax.optimization_barrier((quarter, parts))
+    result = merge(exchanged(parts, axis_index_groups=line_y), True)
+    result = exchanged(result, axis_index_groups=line_x)
+    result = result.reshape((SIDE * SIDE,) + result.shape[2:])
     result = spread(result, lax.ppermute(result, "dec", sibling))
+
+    pieces = [quarter] + [exchange(quarter, groups, turn) for turn in TURNS[1:3]]
+    kv_cache = assemble(pieces + [exchange(late_quarter, groups, TURNS[3])]).T
     attention_out = result.reshape(steps, batch, -1)
     return (attention_out, kv_cache)
 

time: 70 us -> 74.1 us (1.059)
  blocking collectives: 9.34 us -> 17.8 us
  waiting for transfers between devices: 9.07 us -> 5.96 us
  starting transfers between devices: 28.6 us -> 27.4 us
    all_to_all x1 -> x2, blocking collectives: 9.34 us -> 17.8 us  [the longest x1 10.6 us: per_device(): parts = exchanged(parts, axis_index_groups=line_x)]
    all_to_all x1, waiting for transfers between devices: 5.13 us -> 2.02 us  [per_device(): result = merge(exchanged(parts, axis_index_groups=line_y), True)]
    all_to_all x1, starting transfers between devices: 6.8 us -> 4.19 us  [per_device(): result = merge(exchanged(parts, axis_index_groups=line_y), True)]
    ppermute x1, starting transfers between devices: 2.64 us -> 4.14 us  [per_device(): result = spread(result, lax.ppermute(result, 'dec', sibling))]
  transfers between devices with their start and end apart: 10 -> 10, of which waited for: 2 -> 2; matrix products, arithmetic and copies ran while one was open for 0% -> 0% of each run, Pallas kernels for 17% -> 15%
where the time goes in v4:
time: 74.1 us; the launch traced here: 73.7 us
  starting transfers between devices  27.4 us (37%)
  Pallas kernels  20.7 us (28%)
  blocking collectives  17.8 us (24%)
  waiting for transfers between devices  5.96 us (8%)
  local copies, waits for them, and re-layouts  0.98 us (1%)
  between operations  0.79 us (1%)
    all_to_all x1, blocking collectives, per_device(): parts = exchanged(parts, axis_index_groups=line_x)  10.6 us
    ppermute x5, starting transfers between devices, exchange(): return lax.ppermute(piece, 'pre', [(i, i ^ turn) for i in range(groups)])  8.48 us
    all_to_all x1, starting transfers between devices, per_device(): arrived = exchanged(packed)  8.07 us
    pallas_call x1, Pallas kernels, attend(): pl.pallas_call(attend_kernel, in_specs=[vmem] * 8 + [pl.BlockSpec(memory_...  7.46 us
    all_to_all x1, blocking collectives, per_device(): result = exchanged(result, axis_index_groups=line_x)  7.21 us
    pallas_call x1, Pallas kernels, produce(): pl.pallas_call(functools.partial(produce_kernel, groups, owners), in_spec...  6.94 us
    all_to_all x1, starting transfers between devices, per_device(): result = merge(exchanged(parts, axis_index_groups=line_y), True)  4.19 us
    ppermute x1, starting transfers between devices, per_device(): result = spread(result, lax.ppermute(result, 'dec', sibling))  4.14 us
  transfers between devices with their start and end apart: 10, of which 2 were waited for; matrix products, arithmetic and copies ran while one was open for 0% of the time, Pallas kernels for 15%

profile of v4, /device:TPU:1, one launch (start us, length us, event | category | flops | bytes accessed | tf_op | source)
XLA Modules:
  0.0 73.7 jit_solution(12216713678421184529)
XLA Ops:
  0.7 6.9 %produce.1 = (bf16[576,256]{1,0:T(8,128)(2,1)}, bf16[64,8,640]{2,1,0:T(8,128)(2,1)}) custom-call(s32[4]{0:T(128)} %lengths_ref, s32[4096]{0:T(1024)} %dest_hbm.1, bf16[256,7168]{1,0:T(8,128)(2,1)} %hidden_hbm.1, bf16[576,7168]{1,0:T(8,128)(2,1)} %bitcast.13, f32[1,512]{1,0:T(1,128)} %bitcast.16, f32[32,128]{1,0:T(8,128)} %constant.20.clone.freq_hbm), custom_call_target="tpu_custom_call" | custom-call | tf_op jit(solution)/shard_map/produce/pallas_call | solution.py:159
  7.6 4.6 %collective-permute-start = (bf16[576,256]{1,0:T(8,128)(2,1)}, bf16[576,256]{1,0:T(8,128)(2,1)S(1)}, u32[]{:S(2)}, u32[]{:S(2)}) collective-permute-start(bf16[576,256]{1,0:T(8,128)(2,1)} %get-tuple-element.12.own_hbm), channel_id=1, source_target_pairs={{0,96},{32,64},{64,32},{96,0},{1,97},{33,65},{65,33},{97,1},{2,98}... | collective-permute-start | bytes 884744 | tf_op jit(solution)/shard_map/ppermute | solution.py:525
  12.2 8.1 %all-to-all-start = ((bf16[64,8,640]{2,1,0:T(8,128)(2,1)}), bf16[64,8,640]{2,1,0:T(8,128)(2,1)S(1)}, u32[]{:S(2)}, u32[]{:S(2)}) async-start(bf16[64,8,640]{2,1,0:T(8,128)(2,1)} %get-tuple-element.18), calls=%async_computation | async-start | bytes 1310720 | tf_op jit(solution)/shard_map/all_to_all | solution.py:586
  20.3 0.0 collective-permute-done.1.k2
  20.4 1.2 %collective-permute-start.2 = (bf16[576,256]{1,0:T(8,128)(2,1)S(1)}, bf16[576,256]{1,0:T(8,128)(2,1)S(1)}, u32[]{:S(2)}, u32[]{:S(2)}) collective-permute-start(bf16[576,256]{1,0:T(8,128)(2,1)S(1)} %broadcast_select_fusion), channel_id=1, source_target_pairs={{0,32},{1,97},{2,34},{3,99},{4,36},{5,101},{6,38},{7,103},{8,40},{... | collective-permute-start | bytes 884744 | tf_op jit(solution)/shard_map/ppermute | solution.py:538
  21.7 1.0 %copy-done.1 = bf16[576,256]{1,0:T(8,128)(2,1)S(1)} copy-done((bf16[576,256]{1,0:T(8,128)(2,1)S(1)}, bf16[576,256]{1,0:T(8,128)(2,1)}, u32[]{:S(2)}) %copy-start.1) | copy-done | bytes 294936
  22.6 1.0 %prepare.1 = (f32[256,1024]{1,0:T(8,128)S(1)}, s32[256,128]{1,0:T(8,128)S(1)}, bf16[576,256]{1,0:T(8,128)(2,1)S(1)}) custom-call(s32[4]{0:T(128)S(1)} %copy-done.4, s32[8]{0:T(128)S(1)} %copy-done.5, s32[4,8]{1,0:T(4,128)S(1)} %copy-done.3, bf16[576,256]{1,0:T(8,128)(2,1)S(1)} %copy-done.1), custom_call_target="tpu_custom_call" | custom-call | tf_op jit(solution)/shard_map/prepare/pallas_call | solution.py:300
  23.6 3.9 %collective-permute-done.2.k3 = bf16[576,256]{1,0:T(8,128)(2,1)S(1)} collective-permute-done((bf16[576,256]{1,0:T(8,128)(2,1)S(1)}, bf16[576,256]{1,0:T(8,128)(2,1)S(1)}, u32[]{:S(2)}, u32[]{:S(2)}) %collective-permute-start.2) | collective-permute-done | bytes 294944 | tf_op jit(solution)/shard_map/ppermute | solution.py:538
  27.6 7.5 %attend.1 = (f32[16,40,128]{2,1,0:T(8,128)S(1)}, f32[16,40,128]{2,1,0:T(8,128)S(1)}) custom-call(f32[256,1024]{1,0:T(8,128)S(1)} %get-tuple-element.14.bias_ref, s32[256,128]{1,0:T(8,128)S(1)} %get-tuple-element.15.valid_ref, bf16[32,4,8,512]{3,2,1,0:T(8,128)(2,1)S(1)} %bitcast.9, bf16[32,4,8,64]{3,2,1,0:T(8,128)(2,1)S(1)} %bitcast.12, ...), custom_call_target="tpu_custom_call" | custom-call | tf_op jit(solution)/shard_map/attend/pallas_call | solution.py:393
  35.0 1.2 %collective-permute-start.3 = (f32[16,40,128]{2,1,0:T(8,128)S(1)}, f32[16,40,128]{2,1,0:T(8,128)S(1)}, u32[]{:S(2)}, u32[]{:S(2)}) collective-permute-start(f32[16,40,128]{2,1,0:T(8,128)S(1)} %get-tuple-element.20), channel_id=1, source_target_pairs={{0,1},{1,0},{2,3},{3,2},{4,5},{5,4},{6,7},{7,6},{8,9},{9,8},{10,11... | collective-permute-start | bytes 983048 | tf_op jit(solution)/shard_map/ppermute | solution.py:589
  36.3 0.0 all-to-all-done.arrived_ref
  36.3 1.5 %place.1.refs_0_ = bf16[576,256]{1,0:T(8,128)(2,1)S(1)} custom-call(bf16[64,8,640]{2,1,0:T(8,128)(2,1)S(1)} %all-to-all-done.arrived_ref), custom_call_target="tpu_custom_call" | custom-call | tf_op jit(solution)/shard_map/place/pallas_call | solution.py:221
  37.8 0.5 merge_pair.1
  38.3 10.6 %all_to_all.20 = f32[16,40,128]{2,1,0:T(8,128)S(1)} all-to-all(f32[16,40,128]{2,1,0:T(8,128)S(1)} %merge_pair.1), channel_id=1, replica_groups={{0,2,4,6},{1,3,5,7},{8,10,12,14},{9,11,13,15},{16,18,20,22},{17,19,21,2..., dimensions={0} | all-to-all | bytes 655360 | tf_op jit(solution)/shard_map/all_to_all | solution.py:590
  48.9 0.9 %merge.2 = f32[4,4,40,128]{3,2,1,0:T(8,128)} custom-call(f32[4,4,40,128]{3,2,1,0:T(8,128)S(1)} %bitcast.8), custom_call_target="tpu_custom_call" | custom-call | tf_op jit(solution)/shard_map/merge/pallas_call | solution.py:483
  49.8 4.2 %all-to-all-start.2 = ((f32[4,4,40,128]{3,2,1,0:T(8,128)}), f32[4,4,40,128]{3,2,1,0:T(8,128)S(1)}, u32[]{:S(2)}, u32[]{:S(2)}) async-start(f32[4,4,40,128]{3,2,1,0:T(8,128)} %merge.2), calls=%async_computation.2 | async-start | bytes 655360 | tf_op jit(solution)/shard_map/all_to_all | solution.py:593
  54.0 1.2 %collective-permute-start.5 = (bf16[576,256]{1,0:T(8,128)(2,1)S(1)}, bf16[576,256]{1,0:T(8,128)(2,1)S(1)}, u32[]{:S(2)}, u32[]{:S(2)}) collective-permute-start(bf16[576,256]{1,0:T(8,128)(2,1)S(1)} %place.1.refs_0_), channel_id=1, source_target_pairs={{0,96},{32,64},{64,32},{96,0},{1,97},{33,65},{65,33},{97,1},{2,98}... | collective-permute-start | bytes 884744 | tf_op jit(solution)/shard_map/ppermute | solution.py:525
  55.2 2.6 %collective-permute-start.7 = (bf16[576,256]{1,0:T(8,128)(2,1)S(1)}, bf16[576,256]{1,0:T(8,128)(2,1)S(1)}, u32[]{:S(2)}, u32[]{:S(2)}) collective-permute-start(bf16[576,256]{1,0:T(8,128)(2,1)S(1)} %place.1.refs_0_), channel_id=1, source_target_pairs={{0,64},{32,96},{64,0},{96,32},{1,65},{33,97},{65,1},{97,33},{2,66}... | collective-permute-start | bytes 884744 | tf_op jit(solution)/shard_map/ppermute | solution.py:525
  57.9 2.0 %all-to-all-done.2.parts_ref = f32[4,4,40,128]{3,2,1,0:T(8,128)S(1)} async-done(((f32[4,4,40,128]{3,2,1,0:T(8,128)}), f32[4,4,40,128]{3,2,1,0:T(8,128)S(1)}, u32[]{:S(2)}, u32[]{:S(2)}) %all-to-all-start.2) | async-done | bytes 327712 | tf_op jit(solution)/shard_map/all_to_all | solution.py:593
  59.9 0.2 merge.3
  60.0 7.2 %all_to_all.21 = bf16[4,4,32,128]{3,2,1,0:T(8,128)(2,1)S(1)} all-to-all(bf16[4,4,32,128]{3,2,1,0:T(8,128)(2,1)S(1)} %merge.3), channel_id=1, replica_groups={{0,2,4,6},{1,3,5,7},{8,10,12,14},{9,11,13,15},{16,18,20,22},{17,19,21,2..., dimensions={0} | all-to-all | bytes 262144 | tf_op jit(solution)/shard_map/all_to_all | solution.py:594
  67.3 4.1 %collective-permute-start.4 = (bf16[16,32,128]{2,1,0:T(8,128)(2,1)S(1)}, bf16[16,32,128]{2,1,0:T(8,128)(2,1)S(1)}, u32[]{:S(2)}, u32[]{:S(2)}) collective-permute-start(bf16[16,32,128]{2,1,0:T(8,128)(2,1)S(1)} %bitcast.10), channel_id=1, source_target_pairs={{0,1},{1,0},{2,3},{3,2},{4,5},{5,4},{6,7},{7,6},{8,9},{9,8},{10,11... | collective-permute-start | bytes 393224 | tf_op jit(solution)/shard_map/ppermute | solution.py:596
  71.4 1.2 %assemble.1 = bf16[576,1024]{1,0:T(8,128)(2,1)} custom-call(bf16[576,256]{1,0:T(8,128)(2,1)S(1)} %place.1.refs_0_, bf16[576,256]{1,0:T(8,128)(2,1)S(1)} %collective-permute-done.5.refs_1_, bf16[576,256]{1,0:T(8,128)(2,1)S(1)} %collective-permute-done.6.refs_2_, bf16[576,256]{1,0:T(8,128)(2,1)S(1)} %collective-permute-done.7.refs_3_), custom_call_target="tpu_custom_call" | custom-call | tf_op jit(solution)/shard_map/assemble/pallas_call | solution.py:252
  72.6 1.1 %spread.1 = bf16[32,4096]{1,0:T(8,128)(2,1)} custom-call(bf16[16,32,128]{2,1,0:T(8,128)(2,1)S(1)} %bitcast.11, bf16[16,32,128]{2,1,0:T(8,128)(2,1)S(1)} %collective-permute-done.4.other_ref), custom_call_target="tpu_custom_call" | custom-call | tf_op jit(solution)/shard_map/spread/pallas_call | solution.py:513
  (20 shorter events, 0.1 us)
Async XLA Ops:
  0.6 21.0 %copy-start.3 = (s32[4,8]{1,0:T(4,128)S(1)}, s32[4,8]{1,0:T(4,128)}, u32[]{:S(2)}) copy-start(s32[4,8]{1,0:T(4,128)} %position_ref.1) | copy-start | bytes 388
  0.6 21.0 %copy-start.4 = (s32[4]{0:T(128)S(1)}, s32[4]{0:T(128)}, u32[]{:S(2)}) copy-start(s32[4]{0:T(128)} %lengths_ref) | copy-start | bytes 52
  0.7 21.0 %copy-start.5 = (s32[8]{0:T(128)S(1)}, s32[8]{0:T(128)}, u32[]{:S(2)}) copy-start(s32[8]{0:T(128)} %request_ref.1) | copy-start | bytes 100
  0.7 26.9 %copy-start = (bf16[4,8,32,512]{3,2,1,0:T(8,128)(2,1)S(1)}, bf16[4,8,32,512]{3,2,1,0:T(8,128)(2,1)}, u32[]{:S(2)}) copy-start(bf16[4,8,32,512]{3,2,1,0:T(8,128)(2,1)} %param.14) | copy-start | bytes 3145732
  0.7 26.9 %copy-start.2 = (bf16[4,8,32,64]{3,2,1,0:T(8,128)(2,1)S(1)}, bf16[4,8,32,64]{3,2,1,0:T(8,128)(2,1)}, u32[]{:S(2)}) copy-start(bf16[4,8,32,64]{3,2,1,0:T(8,128)(2,1)} %param.15) | copy-start | bytes 393220
  7.6 12.7 %collective-permute-start = (bf16[576,256]{1,0:T(8,128)(2,1)}, bf16[576,256]{1,0:T(8,128)(2,1)S(1)}, u32[]{:S(2)}, u32[]{:S(2)}) collective-permute-start(bf16[576,256]{1,0:T(8,128)(2,1)} %get-tuple-element.12.own_hbm), channel_id=1, source_target_pairs={{0,96},{32,64},{64,32},{96,0},{1,97},{33,65},{65,33},{97,1},{2,98}... | collective-permute-start | bytes 884744 | tf_op jit(solution)/shard_map/ppermute | solution.py:525
  12.2 8.1 %collective-permute-start.1 = (bf16[576,256]{1,0:T(8,128)(2,1)}, bf16[576,256]{1,0:T(8,128)(2,1)S(1)}, u32[]{:S(2)}, u32[]{:S(2)}) collective-permute-start(bf16[576,256]{1,0:T(8,128)(2,1)} %get-tuple-element.12.own_hbm), channel_id=1, source_target_pairs={{0,32},{32,0},{64,96},{96,64},{1,33},{33,1},{65,97},{97,65},{2,34}... | collective-permute-start | bytes 884744 | tf_op jit(solution)/shard_map/ppermute | solution.py:525
  12.2 24.0 %all-to-all-start = ((bf16[64,8,640]{2,1,0:T(8,128)(2,1)}), bf16[64,8,640]{2,1,0:T(8,128)(2,1)S(1)}, u32[]{:S(2)}, u32[]{:S(2)}) async-start(bf16[64,8,640]{2,1,0:T(8,128)(2,1)} %get-tuple-element.18), calls=%async_computation | async-start | bytes 1310720 | tf_op jit(solution)/shard_map/all_to_all | solution.py:586
  20.4 7.2 %collective-permute-start.2 = (bf16[576,256]{1,0:T(8,128)(2,1)S(1)}, bf16[576,256]{1,0:T(8,128)(2,1)S(1)}, u32[]{:S(2)}, u32[]{:S(2)}) collective-permute-start(bf16[576,256]{1,0:T(8,128)(2,1)S(1)} %broadcast_select_fusion), channel_id=1, source_target_pairs={{0,32},{1,97},{2,34},{3,99},{4,36},{5,101},{6,38},{7,103},{8,40},{... | collective-permute-start | bytes 884744 | tf_op jit(solution)/shard_map/ppermute | solution.py:538
  21.7 1.0 %copy-start.1 = (bf16[576,256]{1,0:T(8,128)(2,1)S(1)}, bf16[576,256]{1,0:T(8,128)(2,1)}, u32[]{:S(2)}) copy-start(bf16[576,256]{1,0:T(8,128)(2,1)} %get-tuple-element.12.own_hbm) | copy-start | bytes 884740
  35.0 2.7 %collective-permute-start.3 = (f32[16,40,128]{2,1,0:T(8,128)S(1)}, f32[16,40,128]{2,1,0:T(8,128)S(1)}, u32[]{:S(2)}, u32[]{:S(2)}) collective-permute-start(f32[16,40,128]{2,1,0:T(8,128)S(1)} %get-tuple-element.20), channel_id=1, source_target_pairs={{0,1},{1,0},{2,3},{3,2},{4,5},{5,4},{6,7},{7,6},{8,9},{9,8},{10,11... | collective-permute-start | bytes 983048 | tf_op jit(solution)/shard_map/ppermute | solution.py:589
  49.8 10.1 %all-to-all-start.2 = ((f32[4,4,40,128]{3,2,1,0:T(8,128)}), f32[4,4,40,128]{3,2,1,0:T(8,128)S(1)}, u32[]{:S(2)}, u32[]{:S(2)}) async-start(f32[4,4,40,128]{3,2,1,0:T(8,128)} %merge.2), calls=%async_computation.2 | async-start | bytes 655360 | tf_op jit(solution)/shard_map/all_to_all | solution.py:593
  54.0 17.4 %collective-permute-start.5 = (bf16[576,256]{1,0:T(8,128)(2,1)S(1)}, bf16[576,256]{1,0:T(8,128)(2,1)S(1)}, u32[]{:S(2)}, u32[]{:S(2)}) collective-permute-start(bf16[576,256]{1,0:T(8,128)(2,1)S(1)} %place.1.refs_0_), channel_id=1, source_target_pairs={{0,96},{32,64},{64,32},{96,0},{1,97},{33,65},{65,33},{97,1},{2,98}... | collective-permute-start | bytes 884744 | tf_op jit(solution)/shard_map/ppermute | solution.py:525
  55.2 16.2 %collective-permute-start.6 = (bf16[576,256]{1,0:T(8,128)(2,1)S(1)}, bf16[576,256]{1,0:T(8,128)(2,1)S(1)}, u32[]{:S(2)}, u32[]{:S(2)}) collective-permute-start(bf16[576,256]{1,0:T(8,128)(2,1)S(1)} %place.1.refs_0_), channel_id=1, source_target_pairs={{0,32},{32,0},{64,96},{96,64},{1,33},{33,1},{65,97},{97,65},{2,34}... | collective-permute-start | bytes 884744 | tf_op jit(solution)/shard_map/ppermute | solution.py:525
  55.2 16.2 %collective-permute-start.7 = (bf16[576,256]{1,0:T(8,128)(2,1)S(1)}, bf16[576,256]{1,0:T(8,128)(2,1)S(1)}, u32[]{:S(2)}, u32[]{:S(2)}) collective-permute-start(bf16[576,256]{1,0:T(8,128)(2,1)S(1)} %place.1.refs_0_), channel_id=1, source_target_pairs={{0,64},{32,96},{64,0},{96,32},{1,65},{33,97},{65,1},{97,33},{2,66}... | collective-permute-start | bytes 884744 | tf_op jit(solution)/shard_map/ppermute | solution.py:525
  67.3 5.3 %collective-permute-start.4 = (bf16[16,32,128]{2,1,0:T(8,128)(2,1)S(1)}, bf16[16,32,128]{2,1,0:T(8,128)(2,1)S(1)}, u32[]{:S(2)}, u32[]{:S(2)}) collective-permute-start(bf16[16,32,128]{2,1,0:T(8,128)(2,1)S(1)} %bitcast.10), channel_id=1, source_target_pairs={{0,1},{1,0},{2,3},{3,2},{4,5},{5,4},{6,7},{7,6},{8,9},{9,8},{10,11... | collective-permute-start | bytes 393224 | tf_op jit(solution)/shard_map/ppermute | solution.py:596

commit v5 on v3

--- a/solution.py
+++ b/solution.py
@@ -16,7 +16,7 @@
 SIDE = 4
 TURNS = (0, 3, 1, 2)
 CUT_HEADS = 8
-DEPTH = 1024
+DEPTH = 1792
 
 score_scale = 0.07216878364870323
 mask_value = -1e30
@@ -229,36 +229,6 @@
     )(arrived)
 
 
-def assemble_kernel(*refs):
-    pieces, out_ref = refs[:-1], refs[-1]
-    groups = len(pieces)
-    group = lax.axis_index("pre")
-    width, rows = pieces[0].shape
-    step = 64
-
-    def body(k, carry):
-        part = pl.ds(pl.multiple_of(k * step, step), step)
-        for turn, piece in zip(TURNS, pieces):
-            at = pl.multiple_of((group ^ turn) * rows, rows)
-            out_ref[part, pl.ds(at, rows)] = piece[part, :]
-        return carry
-
-    lax.fori_loop(0, width // step, body, 0)
-
-
-def assemble(pieces):
-    width, rows = pieces[0].shape
-    vmem = pl.BlockSpec(memory_space=pltpu.VMEM)
-    return pl.pallas_call(
-        assemble_kernel,
-        in_specs=[vmem] * len(pieces),
-        out_specs=vmem,
-        out_shape=jax.ShapeDtypeStruct((width, rows * len(pieces)), pieces[0].dtype),
-        compiler_params=params(4),
-        name="assemble",
-    )(*pieces)
-
-
 def prepare_kernel(
     owners, groups, lengths_ref, request_ref, position_ref, own_hbm,
     bias_ref, valid_ref, own_ref, sem,
@@ -359,10 +329,11 @@
         lower = (mixed - upper.astype(jnp.float32)).astype(jnp.bfloat16)
         weights_of(cut).wait()
         result = jnp.zeros((rows, 128), jnp.float32)
+        both = jnp.concatenate([upper, lower], axis=0)
         for h in range(0, heads, 2):
             pair = jnp.concatenate([w_ref[cut * heads + h], w_ref[cut * heads + h + 1]], axis=1)
-            y = jnp.dot(upper, pair, preferred_element_type=jnp.float32)
-            y += jnp.dot(lower, pair, preferred_element_type=jnp.float32)
+            y = jnp.dot(both, pair, preferred_element_type=jnp.float32)
+            y = y[:rows] + y[rows:]
             result = jnp.where(head == h, y[:, :128], result)
             result = jnp.where(head == h + 1, y[:, 128:], result)
         at = pl.multiple_of(cut * heads, heads)
@@ -372,13 +343,13 @@
         out_ref[:, all_heads:, :] += jnp.broadcast_to(lines, (items, PAD, 128))
         return carry
 
-    lax.fori_loop(0, cuts, body, 0)
+    lax.fori_loop(0, cuts, body, 0, unroll=2)
     half = items // 2
     core = lax.axis_index("dec") & 1
 
     def hand(i, carry):
-        keep_ref[i] = out_ref[core * half + i]
-        send_ref[i] = out_ref[(1 - core) * half + i]
+        keep_ref[i] = out_ref[core * half + half - 1 - i]
+        send_ref[i] = out_ref[(1 - core) * half + half - 1 - i]
         return carry
 
     lax.fori_loop(0, half, hand, 0)
@@ -489,14 +460,28 @@
     )(parts)
 
 
-def spread_kernel(mine_ref, other_ref, out_ref, wide_ref):
+def finish_kernel(mine_ref, other_ref, p0, p1, p2, p3, out_ref, cache_hbm, wide_ref, sems):
+    group = lax.axis_index("pre")
+    copies = []
+    for k, (turn, piece) in enumerate(zip(TURNS, (p0, p1, p2, p3))):
+        rows = piece.shape[1]
+        at = pl.multiple_of((group ^ turn) * rows, rows)
+        copies.append(
+            pltpu.make_async_copy(piece, cache_hbm.at[:, pl.ds(at, rows)], sems.at[k])
+        )
+    for copy in copies:
+        copy.start()
     half, heads, lanes = mine_ref.shape
     core = lax.axis_index("dec") & 1
-    rows = half * heads
-    for place_at, ref in ((core, mine_ref), (1 - core, other_ref)):
-        for k in range(half):
-            at = pl.ds(pl.multiple_of(place_at * rows + (half - 1 - k) * heads, heads), heads)
+
+    def widen(k, carry):
+        for place_at, ref in ((core, mine_ref), (1 - core, other_ref)):
+            item = place_at * half + half - 1 - k
+            at = pl.ds(pl.multiple_of(item * heads, heads), heads)
             wide_ref[at, :] = ref[k].astype(jnp.float32)
+        return carry
+
+    lax.fori_loop(0, half, widen, 0, unroll=4)
 
     def body(h, carry):
         piece = wide_ref[pl.ds(h, 2 * half, stride=heads), :]
@@ -505,20 +490,29 @@
         return carry
 
     lax.fori_loop(0, heads, body, 0, unroll=4)
-
-
-def spread(mine, other):
+    for copy in copies:
+        copy.wait()
+
+
+def finish(mine, other, pieces):
     half, heads, lanes = mine.shape
+    width, rows = pieces[0].shape
     vmem = pl.BlockSpec(memory_space=pltpu.VMEM)
     return pl.pallas_call(
-        spread_kernel,
-        in_specs=[vmem] * 2,
-        out_specs=vmem,
-        out_shape=jax.ShapeDtypeStruct((2 * half, heads * lanes), mine.dtype),
-        scratch_shapes=[pltpu.VMEM((2 * half * heads, lanes), jnp.float32)],
-        compiler_params=params(4),
-        name="spread",
-    )(mine, other)
+        finish_kernel,
+        in_specs=[vmem] * 6,
+        out_specs=[vmem, pl.BlockSpec(memory_space=pl.ANY)],
+        out_shape=[
+            jax.ShapeDtypeStruct((2 * half, heads * lanes), mine.dtype),
+            jax.ShapeDtypeStruct((width, rows * len(pieces)), pieces[0].dtype),
+        ],
+        scratch_shapes=[
+            pltpu.VMEM((2 * half * heads, lanes), jnp.float32),
+            pltpu.SemaphoreType.DMA((len(pieces),)),
+        ],
+        compiler_params=params(6),
+        name="finish",
+    )(mine, other, *pieces)
 
 
 def exchange(piece, groups, turn):
@@ -555,8 +549,7 @@
     owners = lax.axis_size("dec")
     steps, batch, heads, _ = query_latent.shape
     items = steps * batch
-    plane = [[2 * k + core for k in range(SIDE * SIDE)] for core in range(2)]
-    reverse = [group[::-1] for group in plane]
+    plane = [[2 * k + core for k in reversed(range(SIDE * SIDE))] for core in range(2)]
     sibling = [(d, d ^ 1) for d in range(owners)]
 
     produced, packed = produce(
@@ -582,14 +575,14 @@
     arrived = exchanged(packed)
     quarter = place(arrived, *produced.shape)
     pieces = [quarter] + [exchange(quarter, groups, turn) for turn in TURNS[1:]]
-    kv_cache = assemble(pieces).T
 
     keep, _ = lax.optimization_barrier((keep, quarter))
     parts = merge_pair(keep, lax.ppermute(send, "dec", sibling))
     result = merge(exchanged(parts, axis_index_groups=plane))
-    result = exchanged(result, axis_index_groups=reverse)
-    result = spread(result, lax.ppermute(result, "dec", sibling))
+    result = exchanged(result, axis_index_groups=plane)
+    result, kv_cache = finish(result, lax.ppermute(result, "dec", sibling), pieces)
     attention_out = result.reshape(steps, batch, -1)
+    kv_cache = kv_cache.T
     return (attention_out, kv_cache)
 
 

time: 70 us -> 68.3 us (0.976)
  waiting for transfers between devices: 9.07 us -> 6.58 us
  starting transfers between devices: 28.6 us -> 29.8 us
  Pallas kernels: 20.8 us -> 19.9 us
    all_to_all x1, waiting for transfers between devices: 5.13 us -> 1.71 us  [per_device(): result = merge(exchanged(parts, axis_index_groups=plane))]
    all_to_all x1, starting transfers between devices: 6.8 us -> 8.35 us  [per_device(): result = merge(exchanged(parts, axis_index_groups=plane))]
    ppermute x1, waiting for transfers between devices: 0.01 us -> 0.97 us  [per_device(): lax.ppermute(result, 'dec', sibling)]
    pallas_call x2 -> x1, Pallas kernels: 2.27 us -> 1.74 us  [finish(): pl.pallas_call(finish_kernel, in_specs=[vmem] * 6, out_specs=[vmem, pl.Bl...]
  transfers between devices with their start and end apart: 10 -> 10, of which waited for: 2 -> 3; matrix products, arithmetic and copies ran while one was open for 0% -> 0% of each run, Pallas kernels for 17% -> 15%
where the time goes in v5:
time: 68.3 us; the launch traced here: 68 us
  starting transfers between devices  29.8 us (44%)
  Pallas kernels  19.9 us (29%)
  blocking collectives  9.84 us (14%)
  waiting for transfers between devices  6.58 us (10%)
  local copies, waits for them, and re-layouts  0.98 us (1%)
  between operations  0.78 us (1%)
    all_to_all x1, blocking collectives, per_device(): result = exchanged(result, axis_index_groups=plane)  9.84 us
    ppermute x5, starting transfers between devices, exchange(): return lax.ppermute(piece, 'pre', [(i, i ^ turn) for i in range(groups)])  8.53 us
    all_to_all x1, starting transfers between devices, per_device(): result = merge(exchanged(parts, axis_index_groups=plane))  8.35 us
    all_to_all x1, starting transfers between devices, per_device(): arrived = exchanged(packed)  8.03 us
    pallas_call x1, Pallas kernels, attend(): pl.pallas_call(attend_kernel, in_specs=[vmem] * 8 + [pl.BlockSpec(memory_...  7.22 us
    pallas_call x1, Pallas kernels, produce(): pl.pallas_call(functools.partial(produce_kernel, groups, owners), in_spec...  6.79 us
    ppermute x1, waiting for transfers between devices, around(): far = lax.ppermute(chosen, ('pre', 'dec'), forward)  3.87 us
    ppermute x1, starting transfers between devices, per_device(): lax.ppermute(result, 'dec', sibling)  2.33 us
  transfers between devices with their start and end apart: 10, of which 3 were waited for; matrix products, arithmetic and copies ran while one was open for 0% of the time, Pallas kernels for 15%

profile of v5, /device:TPU:1, one launch (start us, length us, event | category | flops | bytes accessed | tf_op | source)
XLA Modules:
  0.0 68.0 jit_solution(15247864297674702538)
XLA Ops:
  0.7 6.8 %produce.1 = (bf16[576,256]{1,0:T(8,128)(2,1)}, bf16[64,8,640]{2,1,0:T(8,128)(2,1)}) custom-call(s32[4]{0:T(128)} %lengths_ref, s32[4096]{0:T(1024)} %dest_hbm.1, bf16[256,7168]{1,0:T(8,128)(2,1)} %hidden_hbm.1, bf16[576,7168]{1,0:T(8,128)(2,1)} %bitcast.8, f32[1,512]{1,0:T(1,128)} %bitcast.9, f32[32,128]{1,0:T(8,128)} %constant.20.clone.freq_hbm), custom_call_target="tpu_custom_call" | custom-call | tf_op jit(solution)/shard_map/produce/pallas_call | solution.py:159
  7.5 4.7 %collective-permute-start = (bf16[576,256]{1,0:T(8,128)(2,1)}, bf16[576,256]{1,0:T(8,128)(2,1)S(1)}, u32[]{:S(2)}, u32[]{:S(2)}) collective-permute-start(bf16[576,256]{1,0:T(8,128)(2,1)} %get-tuple-element.13.own_hbm), channel_id=1, source_target_pairs={{0,96},{32,64},{64,32},{96,0},{1,97},{33,65},{65,33},{97,1},{2,98}... | collective-permute-start | bytes 884744 | tf_op jit(solution)/shard_map/ppermute | solution.py:519
  12.1 0.0 collective-permute-start.1
  12.2 8.0 %all-to-all-start = ((bf16[64,8,640]{2,1,0:T(8,128)(2,1)}), bf16[64,8,640]{2,1,0:T(8,128)(2,1)S(1)}, u32[]{:S(2)}, u32[]{:S(2)}) async-start(bf16[64,8,640]{2,1,0:T(8,128)(2,1)} %get-tuple-element.19), calls=%async_computation | async-start | bytes 1310720 | tf_op jit(solution)/shard_map/all_to_all | solution.py:575
  20.2 0.0 collective-permute-done.1.k2
  20.3 1.3 %collective-permute-start.2 = (bf16[576,256]{1,0:T(8,128)(2,1)S(1)}, bf16[576,256]{1,0:T(8,128)(2,1)S(1)}, u32[]{:S(2)}, u32[]{:S(2)}) collective-permute-start(bf16[576,256]{1,0:T(8,128)(2,1)S(1)} %broadcast_select_fusion), channel_id=1, source_target_pairs={{0,32},{1,97},{2,34},{3,99},{4,36},{5,101},{6,38},{7,103},{8,40},{... | collective-permute-start | bytes 884744 | tf_op jit(solution)/shard_map/ppermute | solution.py:532
  21.6 1.0 %copy-done.1 = bf16[576,256]{1,0:T(8,128)(2,1)S(1)} copy-done((bf16[576,256]{1,0:T(8,128)(2,1)S(1)}, bf16[576,256]{1,0:T(8,128)(2,1)}, u32[]{:S(2)}) %copy-start.1) | copy-done | bytes 294936
  22.5 1.0 %prepare.1 = (f32[256,1024]{1,0:T(8,128)S(1)}, s32[256,128]{1,0:T(8,128)S(1)}, bf16[576,256]{1,0:T(8,128)(2,1)S(1)}) custom-call(s32[4]{0:T(128)S(1)} %copy-done.4, s32[8]{0:T(128)S(1)} %copy-done.5, s32[4,8]{1,0:T(4,128)S(1)} %copy-done.3, bf16[576,256]{1,0:T(8,128)(2,1)S(1)} %copy-done.1), custom_call_target="tpu_custom_call" | custom-call | tf_op jit(solution)/shard_map/prepare/pallas_call | solution.py:270
  23.6 3.9 %collective-permute-done.2.k3 = bf16[576,256]{1,0:T(8,128)(2,1)S(1)} collective-permute-done((bf16[576,256]{1,0:T(8,128)(2,1)S(1)}, bf16[576,256]{1,0:T(8,128)(2,1)S(1)}, u32[]{:S(2)}, u32[]{:S(2)}) %collective-permute-start.2) | collective-permute-done | bytes 294944 | tf_op jit(solution)/shard_map/ppermute | solution.py:532
  27.4 7.2 %attend.1 = (f32[16,40,128]{2,1,0:T(8,128)S(1)}, f32[16,40,128]{2,1,0:T(8,128)S(1)}) custom-call(f32[256,1024]{1,0:T(8,128)S(1)} %get-tuple-element.15.bias_ref, s32[256,128]{1,0:T(8,128)S(1)} %get-tuple-element.16.valid_ref, bf16[32,4,8,512]{3,2,1,0:T(8,128)(2,1)S(1)} %bitcast.6, bf16[32,4,8,64]{3,2,1,0:T(8,128)(2,1)S(1)} %bitcast.7, ...), custom_call_target="tpu_custom_call" | custom-call | tf_op jit(solution)/shard_map/attend/pallas_call | solution.py:363
  34.7 1.3 %collective-permute-start.3 = (f32[16,40,128]{2,1,0:T(8,128)S(1)}, f32[16,40,128]{2,1,0:T(8,128)S(1)}, u32[]{:S(2)}, u32[]{:S(2)}) collective-permute-start(f32[16,40,128]{2,1,0:T(8,128)S(1)} %get-tuple-element.21), channel_id=1, source_target_pairs={{0,1},{1,0},{2,3},{3,2},{4,5},{5,4},{6,7},{7,6},{8,9},{9,8},{10,11... | collective-permute-start | bytes 983048 | tf_op jit(solution)/shard_map/ppermute | solution.py:580
  35.9 1.5 %place.1.p0 = bf16[576,256]{1,0:T(8,128)(2,1)S(1)} custom-call(bf16[64,8,640]{2,1,0:T(8,128)(2,1)S(1)} %all-to-all-done.arrived_ref), custom_call_target="tpu_custom_call" | custom-call | tf_op jit(solution)/shard_map/place/pallas_call | solution.py:221
  37.4 1.2 %merge_pair.1 = f32[16,40,128]{2,1,0:T(8,128)} custom-call(f32[16,40,128]{2,1,0:T(8,128)S(1)} %get-tuple-element.20.mine_ref, f32[16,40,128]{2,1,0:T(8,128)S(1)} %collective-permute-done.3.other_ref), custom_call_target="tpu_custom_call" | custom-call | tf_op jit(solution)/shard_map/merge_pair/pallas_call | solution.py:422
  38.7 8.4 %all-to-all-start.1 = ((f32[16,40,128]{2,1,0:T(8,128)}), f32[16,40,128]{2,1,0:T(8,128)S(1)}, u32[]{:S(2)}, u32[]{:S(2)}) async-start(f32[16,40,128]{2,1,0:T(8,128)} %merge_pair.1), calls=%async_computation.1 | async-start | bytes 655360 | tf_op jit(solution)/shard_map/all_to_all | solution.py:581
  47.0 1.2 %collective-permute-start.5 = (bf16[576,256]{1,0:T(8,128)(2,1)S(1)}, bf16[576,256]{1,0:T(8,128)(2,1)S(1)}, u32[]{:S(2)}, u32[]{:S(2)}) collective-permute-start(bf16[576,256]{1,0:T(8,128)(2,1)S(1)} %place.1.p0), channel_id=1, source_target_pairs={{0,96},{32,64},{64,32},{96,0},{1,97},{33,65},{65,33},{97,1},{2,98}... | collective-permute-start | bytes 884744 | tf_op jit(solution)/shard_map/ppermute | solution.py:519
  48.3 0.0 collective-permute-start.6
  48.3 2.6 %collective-permute-start.7 = (bf16[576,256]{1,0:T(8,128)(2,1)S(1)}, bf16[576,256]{1,0:T(8,128)(2,1)S(1)}, u32[]{:S(2)}, u32[]{:S(2)}) collective-permute-start(bf16[576,256]{1,0:T(8,128)(2,1)S(1)} %place.1.p0), channel_id=1, source_target_pairs={{0,64},{32,96},{64,0},{96,32},{1,65},{33,97},{65,1},{97,33},{2,66}... | collective-permute-start | bytes 884744 | tf_op jit(solution)/shard_map/ppermute | solution.py:519
  50.9 1.7 %all-to-all-done.1.parts_ref = f32[16,40,128]{2,1,0:T(8,128)S(1)} async-done(((f32[16,40,128]{2,1,0:T(8,128)}), f32[16,40,128]{2,1,0:T(8,128)S(1)}, u32[]{:S(2)}, u32[]{:S(2)}) %all-to-all-start.1) | async-done | bytes 327712 | tf_op jit(solution)/shard_map/all_to_all | solution.py:581
  52.6 0.4 merge.1
  53.1 9.8 %all_to_all.15.mine_ref = bf16[16,32,128]{2,1,0:T(8,128)(2,1)S(1)} all-to-all(bf16[16,32,128]{2,1,0:T(8,128)(2,1)S(1)} %merge.1), channel_id=1, replica_groups={{30,28,26,24,22,20,18,16,14,12,10,8,6,4,2,0},{31,29,27,25,23,21,19,17,1..., dimensions={0} | all-to-all | bytes 262144 | tf_op jit(solution)/shard_map/all_to_all | solution.py:582
  62.9 2.3 %collective-permute-start.4 = (bf16[16,32,128]{2,1,0:T(8,128)(2,1)S(1)}, bf16[16,32,128]{2,1,0:T(8,128)(2,1)S(1)}, u32[]{:S(2)}, u32[]{:S(2)}) collective-permute-start(bf16[16,32,128]{2,1,0:T(8,128)(2,1)S(1)} %all_to_all.15.mine_ref), channel_id=1, source_target_pairs={{0,1},{1,0},{2,3},{3,2},{4,5},{5,4},{6,7},{7,6},{8,9},{9,8},{10,11... | collective-permute-start | bytes 393224 | tf_op jit(solution)/shard_map/ppermute | solution.py:583
  65.2 0.0 collective-permute-done.5.p1
  65.2 1.0 %collective-permute-done.4.other_ref = bf16[16,32,128]{2,1,0:T(8,128)(2,1)S(1)} collective-permute-done((bf16[16,32,128]{2,1,0:T(8,128)(2,1)S(1)}, bf16[16,32,128]{2,1,0:T(8,128)(2,1)S(1)}, u32[]{:S(2)}, u32[]{:S(2)}) %collective-permute-start.4) | collective-permute-done | bytes 131104 | tf_op jit(solution)/shard_map/ppermute | solution.py:583
  66.2 1.7 %finish.1 = (bf16[32,4096]{1,0:T(8,128)(2,1)}, bf16[576,1024]{1,0:T(8,128)(2,1)}) custom-call(bf16[16,32,128]{2,1,0:T(8,128)(2,1)S(1)} %all_to_all.15.mine_ref, bf16[16,32,128]{2,1,0:T(8,128)(2,1)S(1)} %collective-permute-done.4.other_ref, bf16[576,256]{1,0:T(8,128)(2,1)S(1)} %place.1.p0, bf16[576,256]{1,0:T(8,128)(2,1)S(1)} %collective-permute-done.5.p1, ...), custom_call_target="tpu_custom_call" | custom-call | tf_op jit(solution)/shard_map/finish/pallas_call | solution.py:501
  (17 shorter events, 0.1 us)
Async XLA Ops:
  0.6 20.9 %copy-start.3 = (s32[4,8]{1,0:T(4,128)S(1)}, s32[4,8]{1,0:T(4,128)}, u32[]{:S(2)}) copy-start(s32[4,8]{1,0:T(4,128)} %position_ref.1) | copy-start | bytes 388
  0.6 20.9 %copy-start.4 = (s32[4]{0:T(128)S(1)}, s32[4]{0:T(128)}, u32[]{:S(2)}) copy-start(s32[4]{0:T(128)} %lengths_ref) | copy-start | bytes 52
  0.7 20.9 %copy-start.5 = (s32[8]{0:T(128)S(1)}, s32[8]{0:T(128)}, u32[]{:S(2)}) copy-start(s32[8]{0:T(128)} %request_ref.1) | copy-start | bytes 100
  0.7 26.8 %copy-start = (bf16[4,8,32,512]{3,2,1,0:T(8,128)(2,1)S(1)}, bf16[4,8,32,512]{3,2,1,0:T(8,128)(2,1)}, u32[]{:S(2)}) copy-start(bf16[4,8,32,512]{3,2,1,0:T(8,128)(2,1)} %param.14) | copy-start | bytes 3145732
  0.7 26.8 %copy-start.2 = (bf16[4,8,32,64]{3,2,1,0:T(8,128)(2,1)S(1)}, bf16[4,8,32,64]{3,2,1,0:T(8,128)(2,1)}, u32[]{:S(2)}) copy-start(bf16[4,8,32,64]{3,2,1,0:T(8,128)(2,1)} %param.15) | copy-start | bytes 393220
  7.5 12.7 %collective-permute-start = (bf16[576,256]{1,0:T(8,128)(2,1)}, bf16[576,256]{1,0:T(8,128)(2,1)S(1)}, u32[]{:S(2)}, u32[]{:S(2)}) collective-permute-start(bf16[576,256]{1,0:T(8,128)(2,1)} %get-tuple-element.13.own_hbm), channel_id=1, source_target_pairs={{0,96},{32,64},{64,32},{96,0},{1,97},{33,65},{65,33},{97,1},{2,98}... | collective-permute-start | bytes 884744 | tf_op jit(solution)/shard_map/ppermute | solution.py:519
  12.1 8.1 %collective-permute-start.1 = (bf16[576,256]{1,0:T(8,128)(2,1)}, bf16[576,256]{1,0:T(8,128)(2,1)S(1)}, u32[]{:S(2)}, u32[]{:S(2)}) collective-permute-start(bf16[576,256]{1,0:T(8,128)(2,1)} %get-tuple-element.13.own_hbm), channel_id=1, source_target_pairs={{0,32},{32,0},{64,96},{96,64},{1,33},{33,1},{65,97},{97,65},{2,34}... | collective-permute-start | bytes 884744 | tf_op jit(solution)/shard_map/ppermute | solution.py:519
  12.2 23.8 %all-to-all-start = ((bf16[64,8,640]{2,1,0:T(8,128)(2,1)}), bf16[64,8,640]{2,1,0:T(8,128)(2,1)S(1)}, u32[]{:S(2)}, u32[]{:S(2)}) async-start(bf16[64,8,640]{2,1,0:T(8,128)(2,1)} %get-tuple-element.19), calls=%async_computation | async-start | bytes 1310720 | tf_op jit(solution)/shard_map/all_to_all | solution.py:575
  20.3 7.2 %collective-permute-start.2 = (bf16[576,256]{1,0:T(8,128)(2,1)S(1)}, bf16[576,256]{1,0:T(8,128)(2,1)S(1)}, u32[]{:S(2)}, u32[]{:S(2)}) collective-permute-start(bf16[576,256]{1,0:T(8,128)(2,1)S(1)} %broadcast_select_fusion), channel_id=1, source_target_pairs={{0,32},{1,97},{2,34},{3,99},{4,36},{5,101},{6,38},{7,103},{8,40},{... | collective-permute-start | bytes 884744 | tf_op jit(solution)/shard_map/ppermute | solution.py:532
  21.6 1.0 %copy-start.1 = (bf16[576,256]{1,0:T(8,128)(2,1)S(1)}, bf16[576,256]{1,0:T(8,128)(2,1)}, u32[]{:S(2)}) copy-start(bf16[576,256]{1,0:T(8,128)(2,1)} %get-tuple-element.13.own_hbm) | copy-start | bytes 884740
  34.7 2.8 %collective-permute-start.3 = (f32[16,40,128]{2,1,0:T(8,128)S(1)}, f32[16,40,128]{2,1,0:T(8,128)S(1)}, u32[]{:S(2)}, u32[]{:S(2)}) collective-permute-start(f32[16,40,128]{2,1,0:T(8,128)S(1)} %get-tuple-element.21), channel_id=1, source_target_pairs={{0,1},{1,0},{2,3},{3,2},{4,5},{5,4},{6,7},{7,6},{8,9},{9,8},{10,11... | collective-permute-start | bytes 983048 | tf_op jit(solution)/shard_map/ppermute | solution.py:580
  38.7 13.9 %all-to-all-start.1 = ((f32[16,40,128]{2,1,0:T(8,128)}), f32[16,40,128]{2,1,0:T(8,128)S(1)}, u32[]{:S(2)}, u32[]{:S(2)}) async-start(f32[16,40,128]{2,1,0:T(8,128)} %merge_pair.1), calls=%async_computation.1 | async-start | bytes 655360 | tf_op jit(solution)/shard_map/all_to_all | solution.py:581
  47.0 18.2 %collective-permute-start.5 = (bf16[576,256]{1,0:T(8,128)(2,1)S(1)}, bf16[576,256]{1,0:T(8,128)(2,1)S(1)}, u32[]{:S(2)}, u32[]{:S(2)}) collective-permute-start(bf16[576,256]{1,0:T(8,128)(2,1)S(1)} %place.1.p0), channel_id=1, source_target_pairs={{0,96},{32,64},{64,32},{96,0},{1,97},{33,65},{65,33},{97,1},{2,98}... | collective-permute-start | bytes 884744 | tf_op jit(solution)/shard_map/ppermute | solution.py:519
  48.3 17.0 %collective-permute-start.6 = (bf16[576,256]{1,0:T(8,128)(2,1)S(1)}, bf16[576,256]{1,0:T(8,128)(2,1)S(1)}, u32[]{:S(2)}, u32[]{:S(2)}) collective-permute-start(bf16[576,256]{1,0:T(8,128)(2,1)S(1)} %place.1.p0), channel_id=1, source_target_pairs={{0,32},{32,0},{64,96},{96,64},{1,33},{33,1},{65,97},{97,65},{2,34}... | collective-permute-start | bytes 884744 | tf_op jit(solution)/shard_map/ppermute | solution.py:519
  48.3 17.0 %collective-permute-start.7 = (bf16[576,256]{1,0:T(8,128)(2,1)S(1)}, bf16[576,256]{1,0:T(8,128)(2,1)S(1)}, u32[]{:S(2)}, u32[]{:S(2)}) collective-permute-start(bf16[576,256]{1,0:T(8,128)(2,1)S(1)} %place.1.p0), channel_id=1, source_target_pairs={{0,64},{32,96},{64,0},{96,32},{1,65},{33,97},{65,1},{97,33},{2,66}... | collective-permute-start | bytes 884744 | tf_op jit(solution)/shard_map/ppermute | solution.py:519
  62.9 3.3 %collective-permute-start.4 = (bf16[16,32,128]{2,1,0:T(8,128)(2,1)S(1)}, bf16[16,32,128]{2,1,0:T(8,128)(2,1)S(1)}, u32[]{:S(2)}, u32[]{:S(2)}) collective-permute-start(bf16[16,32,128]{2,1,0:T(8,128)(2,1)S(1)} %all_to_all.15.mine_ref), channel_id=1, source_target_pairs={{0,1},{1,0},{2,3},{3,2},{4,5},{5,4},{6,7},{7,6},{8,9},{9,8},{10,11... | collective-permute-start | bytes 393224 | tf_op jit(solution)/shard_map/ppermute | solution.py:583

commit v6 on v5

--- a/solution.py
+++ b/solution.py
@@ -230,8 +230,8 @@
 
 
 def prepare_kernel(
-    owners, groups, lengths_ref, request_ref, position_ref, own_hbm,
-    bias_ref, valid_ref, own_ref, sem,
+    owners, lengths_ref, request_ref, position_ref, own_hbm,
+    near_ref, far_ref, valid_ref, own_ref, sem,
 ):
     copy = pltpu.make_async_copy(own_hbm, own_ref, sem)
     copy.start()
@@ -252,9 +252,11 @@
             at = pl.ds(pl.multiple_of((s * batch + b) * heads, heads), heads)
             seen = jnp.int32(0)
             for c, base in enumerate(bases):
-                bias_ref[at, c * count : (c + 1) * count] = jnp.where(
-                    (row >= start - base) & (row < stop - base), 0.0, mask_value
-                )
+                bias = jnp.where((row >= start - base) & (row < stop - base), 0.0, mask_value)
+                if c < len(bases) - 1:
+                    near_ref[at, c * count : (c + 1) * count] = bias
+                else:
+                    far_ref[at, :] = bias
                 seen = seen + jnp.where((start < base + count) & (stop > base), 1, 0)
             valid_ref[at, :] = jnp.full((heads, 128), seen, jnp.int32)
         return carry
@@ -268,11 +270,12 @@
     smem = pl.BlockSpec(memory_space=pltpu.SMEM)
     vmem = pl.BlockSpec(memory_space=pltpu.VMEM)
     return pl.pallas_call(
-        functools.partial(prepare_kernel, owners, groups),
+        functools.partial(prepare_kernel, owners),
         in_specs=[smem] * 3 + [pl.BlockSpec(memory_space=pl.ANY)],
-        out_specs=[vmem] * 3,
+        out_specs=[vmem] * 4,
         out_shape=[
-            jax.ShapeDtypeStruct((rows, groups * own.shape[1]), jnp.float32),
+            jax.ShapeDtypeStruct((rows, (groups - 1) * own.shape[1]), jnp.float32),
+            jax.ShapeDtypeStruct((rows, own.shape[1]), jnp.float32),
             jax.ShapeDtypeStruct((rows, 128), jnp.int32),
             jax.ShapeDtypeStruct(own.shape, own.dtype),
         ],
@@ -282,15 +285,58 @@
     )(lengths, row_request, step_position, own)
 
 
-def attend_kernel(
-    bias_ref, valid_ref, latent_ref, rope_ref, k0, k1, k2, k3, w_hbm,
+def scores_of(latent_ref, rope_ref, cut, chunk_refs, bias_ref):
+    items, _, heads, _ = latent_ref.shape
+    rows = items * heads
+    latent = latent_ref[:, cut].reshape(rows, LAT)
+    rope = rope_ref[:, cut].reshape(rows, ROPE)
+    scores = []
+    for c, chunk_ref in enumerate(chunk_refs):
+        count = chunk_ref.shape[1]
+        s = jnp.dot(latent, chunk_ref[:LAT, :], preferred_element_type=jnp.float32)
+        s += jnp.dot(rope, chunk_ref[LAT:, :], preferred_element_type=jnp.float32)
+        scores.append(s + bias_ref[:, c * count : (c + 1) * count])
+    return scores
+
+
+def weigh(scores, peak, chunk_refs):
+    weights = [jnp.exp2((s - peak) * (score_scale * log2_e)) for s in scores]
+    total = jnp.sum(functools.reduce(jnp.add, weights), axis=1, keepdims=True)
+    mixed = sum(
+        lax.dot_general(
+            p.astype(jnp.bfloat16),
+            chunk_ref[:LAT, :],
+            (((1,), (1,)), ((), ())),
+            preferred_element_type=jnp.float32,
+        )
+        for p, chunk_ref in zip(weights, chunk_refs)
+    )
+    return total, mixed
+
+
+def near_kernel(bias_ref, latent_ref, rope_ref, k0, k1, k2, mixed_ref, stat_ref):
+    chunk_refs = (k0, k1, k2)
+    cuts, rows, _ = mixed_ref.shape
+    lane = lax.broadcasted_iota(jnp.int32, (rows, 128), 1)
+
+    def body(cut, carry):
+        scores = scores_of(latent_ref, rope_ref, cut, chunk_refs, bias_ref)
+        peak = jnp.max(functools.reduce(jnp.maximum, scores), axis=1, keepdims=True)
+        total, mixed = weigh(scores, peak, chunk_refs)
+        mixed_ref[cut] = mixed
+        stat_ref[cut] = jnp.where(lane == 0, peak, total)
+        return carry
+
+    lax.fori_loop(0, cuts, body, 0, unroll=2)
+
+
+def far_kernel(
+    bias_ref, valid_ref, latent_ref, rope_ref, k3, mixed_ref, stat_ref, w_hbm,
     keep_ref, send_ref, out_ref, w_ref, sems,
 ):
-    chunk_refs = (k0, k1, k2, k3)
     items, cuts, heads, _ = latent_ref.shape
     rows = items * heads
     all_heads = cuts * heads
-    count = k0.shape[1]
 
     def weights_of(cut):
         part = pl.ds(cut * heads, heads)
@@ -303,27 +349,15 @@
     lane = lax.broadcasted_iota(jnp.int32, (rows, 128), 1)
 
     def body(cut, carry):
-        latent = latent_ref[:, cut].reshape(rows, LAT)
-        rope = rope_ref[:, cut].reshape(rows, ROPE)
-        scores = []
-        for c, chunk_ref in enumerate(chunk_refs):
-            s = jnp.dot(latent, chunk_ref[:LAT, :], preferred_element_type=jnp.float32)
-            s += jnp.dot(rope, chunk_ref[LAT:, :], preferred_element_type=jnp.float32)
-            scores.append(s + bias_ref[:, c * count : (c + 1) * count])
-        peak = jnp.max(functools.reduce(jnp.maximum, scores), axis=1, keepdims=True)
-        weights = [jnp.exp2((s - peak) * (score_scale * log2_e)) for s in scores]
-        total = jnp.sum(functools.reduce(jnp.add, weights), axis=1, keepdims=True)
-        mixed = sum(
-            lax.dot_general(
-                p.astype(jnp.bfloat16),
-                chunk_ref[:LAT, :],
-                (((1,), (1,)), ((), ())),
-                preferred_element_type=jnp.float32,
-            )
-            for p, chunk_ref in zip(weights, chunk_refs)
-        )
+        scores = scores_of(latent_ref, rope_ref, cut, (k3,), bias_ref)
+        old_peak, old_total = stat_ref[cut, :, 0:1], stat_ref[cut, :, 1:2]
+        peak = jnp.maximum(old_peak, jnp.max(scores[0], axis=1, keepdims=True))
+        factor = jnp.exp2((old_peak - peak) * (score_scale * log2_e))
+        total, mixed = weigh(scores, peak, (k3,))
+        total += old_total * factor
         valid = valid_ref[:, 0:1] > 0
-        mixed = mixed * jnp.where(valid, 1.0 / total, 0.0)
+        inverse = jnp.where(valid, 1.0 / total, 0.0)
+        mixed = mixed * inverse + mixed_ref[cut] * (factor * inverse)
         level = jnp.where(valid, peak * score_scale + jnp.log(total), mask_value)
         upper = mixed.astype(jnp.bfloat16)
         lower = (mixed - upper.astype(jnp.float32)).astype(jnp.bfloat16)
@@ -355,14 +389,28 @@
     lax.fori_loop(0, half, hand, 0)
 
 
-def attend(bias, valid, latent, rope, chunks, w_up):
+def attend(near_bias, far_bias, valid, latent, rope, chunks, w_up):
     items, heads, _ = latent.shape
     cuts = heads // CUT_HEADS
+    rows = items * CUT_HEADS
+    latent = latent.reshape(items, cuts, CUT_HEADS, -1)
+    rope = rope.reshape(items, cuts, CUT_HEADS, -1)
     vmem = pl.BlockSpec(memory_space=pltpu.VMEM)
+    mixed, stat = pl.pallas_call(
+        near_kernel,
+        in_specs=[vmem] * 6,
+        out_specs=[vmem] * 2,
+        out_shape=[
+            jax.ShapeDtypeStruct((cuts, rows, LAT), jnp.float32),
+            jax.ShapeDtypeStruct((cuts, rows, 128), jnp.float32),
+        ],
+        compiler_params=params(20),
+        name="attend_near",
+    )(near_bias, latent, rope, *chunks[:3])
     out_shape = jax.ShapeDtypeStruct((items // 2, heads + PAD, 128), jnp.float32)
     return pl.pallas_call(
-        attend_kernel,
-        in_specs=[vmem] * 8 + [pl.BlockSpec(memory_space=pl.ANY)],
+        far_kernel,
+        in_specs=[vmem] * 7 + [pl.BlockSpec(memory_space=pl.ANY)],
         out_specs=[vmem] * 2,
         out_shape=[out_shape] * 2,
         scratch_shapes=[
@@ -370,16 +418,9 @@
             pltpu.VMEM(w_up.shape, w_up.dtype),
             pltpu.SemaphoreType.DMA((cuts,)),
         ],
-        compiler_params=params(48),
-        name="attend",
-    )(
-        bias,
-        valid,
-        latent.reshape(items, cuts, CUT_HEADS, -1),
-        rope.reshape(items, cuts, CUT_HEADS, -1),
-        *chunks,
-        w_up,
-    )
+        compiler_params=params(47),
+        name="attend_far",
+    )(far_bias, valid, latent, rope, chunks[3], mixed, stat, w_up)
 
 
 def merge_step(levels):
@@ -561,11 +602,12 @@
         lax.all_to_all, axis_name="dec", split_axis=0, concat_axis=0, tiled=True
     )
     lengths, _ = lax.optimization_barrier((request_rows, chosen))
-    bias, valid, chunks[0] = prepare(
+    near_bias, far_bias, valid, chunks[0] = prepare(
         owners, groups, lengths, row_request, step_position, produced
     )
     keep, send = attend(
-        bias,
+        near_bias,
+        far_bias,
         valid,
         query_latent.reshape(items, heads, -1),
         query_rope.reshape(items, heads, -1),

time: 68.3 us -> 67.5 us (0.988)
  waiting for transfers between devices: 6.58 us -> 3.05 us
  Pallas kernels: 19.9 us -> 22.6 us
    ppermute x1, waiting for transfers between devices: 3.87 us -> 0.34 us  [around(): far = lax.ppermute(chosen, ('pre', 'dec'), forward)]
    pallas_call x2 -> x3, Pallas kernels: 8.23 us -> 10.9 us  [the longest x1 6.37 us: attend(): pl.pallas_call(far_kernel, in_specs=[vmem] * 7 + [pl.BlockSpec(memory_spa...]
  transfers between devices with their start and end apart: 10 -> 10, of which waited for: 3 -> 3; matrix products, arithmetic and copies ran while one was open for 0% -> 0% of each run, Pallas kernels for 15% -> 19%
where the time goes in v6:
time: 67.5 us; the launch traced here: 67.1 us
  starting transfers between devices  29.8 us (44%)
  Pallas kernels  22.6 us (33%)
  blocking collectives  9.84 us (15%)
  waiting for transfers between devices  3.05 us (5%)
  local copies, waits for them, and re-layouts  0.98 us (1%)
  between operations  0.8 us (1%)
    all_to_all x1, blocking collectives, per_device(): result = exchanged(result, axis_index_groups=plane)  9.84 us
    ppermute x5, starting transfers between devices, exchange(): return lax.ppermute(piece, 'pre', [(i, i ^ turn) for i in range(groups)])  8.53 us
    all_to_all x1, starting transfers between devices, per_device(): result = merge(exchanged(parts, axis_index_groups=plane))  8.35 us
    all_to_all x1, starting transfers between devices, per_device(): arrived = exchanged(packed)  8.03 us
    pallas_call x1, Pallas kernels, produce(): pl.pallas_call(functools.partial(produce_kernel, groups, owners), in_spec...  6.79 us
    pallas_call x1, Pallas kernels, attend(): pl.pallas_call(far_kernel, in_specs=[vmem] * 7 + [pl.BlockSpec(memory_spa...  6.37 us
    pallas_call x1, Pallas kernels, attend(): pl.pallas_call(near_kernel, in_specs=[vmem] * 6, out_specs=[vmem] * 2, ou...  3.48 us
    ppermute x1, starting transfers between devices, per_device(): lax.ppermute(result, 'dec', sibling)  2.33 us
  transfers between devices with their start and end apart: 10, of which 3 were waited for; matrix products, arithmetic and copies ran while one was open for 0% of the time, Pallas kernels for 19%

profile of v6, /device:TPU:1, one launch (start us, length us, event | category | flops | bytes accessed | tf_op | source)
XLA Modules:
  0.0 67.1 jit_solution(4840557315361216517)
XLA Ops:
  0.7 6.8 %produce.1 = (bf16[576,256]{1,0:T(8,128)(2,1)}, bf16[64,8,640]{2,1,0:T(8,128)(2,1)}) custom-call(s32[4]{0:T(128)} %lengths_ref, s32[4096]{0:T(1024)} %dest_hbm.1, bf16[256,7168]{1,0:T(8,128)(2,1)} %hidden_hbm.1, bf16[576,7168]{1,0:T(8,128)(2,1)} %bitcast.10, f32[1,512]{1,0:T(1,128)} %bitcast.11, f32[32,128]{1,0:T(8,128)} %constant.20.clone.freq_hbm), custom_call_target="tpu_custom_call" | custom-call | tf_op jit(solution)/shard_map/produce/pallas_call | solution.py:159
  7.5 4.7 %collective-permute-start = (bf16[576,256]{1,0:T(8,128)(2,1)}, bf16[576,256]{1,0:T(8,128)(2,1)S(1)}, u32[]{:S(2)}, u32[]{:S(2)}) collective-permute-start(bf16[576,256]{1,0:T(8,128)(2,1)} %get-tuple-element.16.own_hbm), channel_id=1, source_target_pairs={{0,96},{32,64},{64,32},{96,0},{1,97},{33,65},{65,33},{97,1},{2,98}... | collective-permute-start | bytes 884744 | tf_op jit(solution)/shard_map/ppermute | solution.py:560
  12.1 0.0 collective-permute-start.1
  12.2 8.0 %all-to-all-start = ((bf16[64,8,640]{2,1,0:T(8,128)(2,1)}), bf16[64,8,640]{2,1,0:T(8,128)(2,1)S(1)}, u32[]{:S(2)}, u32[]{:S(2)}) async-start(bf16[64,8,640]{2,1,0:T(8,128)(2,1)} %get-tuple-element.25), calls=%async_computation | async-start | bytes 1310720 | tf_op jit(solution)/shard_map/all_to_all | solution.py:617
  20.2 0.0 collective-permute-done.1.k2
  20.3 1.3 %collective-permute-start.2 = (bf16[576,256]{1,0:T(8,128)(2,1)S(1)}, bf16[576,256]{1,0:T(8,128)(2,1)S(1)}, u32[]{:S(2)}, u32[]{:S(2)}) collective-permute-start(bf16[576,256]{1,0:T(8,128)(2,1)S(1)} %broadcast_select_fusion), channel_id=1, source_target_pairs={{0,32},{1,97},{2,34},{3,99},{4,36},{5,101},{6,38},{7,103},{8,40},{... | collective-permute-start | bytes 884744 | tf_op jit(solution)/shard_map/ppermute | solution.py:573
  21.6 1.0 %copy-done.2 = bf16[576,256]{1,0:T(8,128)(2,1)S(1)} copy-done((bf16[576,256]{1,0:T(8,128)(2,1)S(1)}, bf16[576,256]{1,0:T(8,128)(2,1)}, u32[]{:S(2)}) %copy-start.2) | copy-done | bytes 294936
  22.5 1.0 %prepare.1 = (f32[256,768]{1,0:T(8,128)S(1)}, f32[256,256]{1,0:T(8,128)S(1)}, s32[256,128]{1,0:T(8,128)S(1)}, bf16[576,256]{1,0:T(8,128)(2,1)S(1)}) custom-call(s32[4]{0:T(128)S(1)} %copy-done.4, s32[8]{0:T(128)S(1)} %copy-done.5, s32[4,8]{1,0:T(4,128)S(1)} %copy-done.3, bf16[576,256]{1,0:T(8,128)(2,1)S(1)} %copy-done.2), custom_call_target="tpu_custom_call" | custom-call | tf_op jit(solution)/shard_map/prepare/pallas_call | solution.py:272
  23.6 3.5 %attend_near.1 = (f32[4,256,512]{2,1,0:T(8,128)S(1)}, f32[4,256,128]{2,1,0:T(8,128)S(1)}) custom-call(f32[256,768]{1,0:T(8,128)S(1)} %get-tuple-element.20.bias_ref, bf16[32,4,8,512]{3,2,1,0:T(8,128)(2,1)S(1)} %bitcast.6, bf16[32,4,8,64]{3,2,1,0:T(8,128)(2,1)S(1)} %bitcast.8, bf16[576,256]{1,0:T(8,128)(2,1)S(1)} %get-tuple-element.21.k0, ...), custom_call_target="tpu_custom_call" | custom-call | tf_op jit(solution)/shard_map/attend_near/pallas_call | solution.py:399
  27.1 0.3 collective-permute-done.2.k3
  27.4 6.4 %attend_far.1 = (f32[16,40,128]{2,1,0:T(8,128)S(1)}, f32[16,40,128]{2,1,0:T(8,128)S(1)}) custom-call(f32[256,256]{1,0:T(8,128)S(1)} %get-tuple-element.18.bias_ref, s32[256,128]{1,0:T(8,128)S(1)} %get-tuple-element.19.valid_ref, bf16[32,4,8,512]{3,2,1,0:T(8,128)(2,1)S(1)} %bitcast.7, bf16[32,4,8,64]{3,2,1,0:T(8,128)(2,1)S(1)} %bitcast.9, ...), custom_call_target="tpu_custom_call" | custom-call | tf_op jit(solution)/shard_map/attend_far/pallas_call | solution.py:411
  33.8 1.3 %collective-permute-start.3 = (f32[16,40,128]{2,1,0:T(8,128)S(1)}, f32[16,40,128]{2,1,0:T(8,128)S(1)}, u32[]{:S(2)}, u32[]{:S(2)}) collective-permute-start(f32[16,40,128]{2,1,0:T(8,128)S(1)} %get-tuple-element.27), channel_id=1, source_target_pairs={{0,1},{1,0},{2,3},{3,2},{4,5},{5,4},{6,7},{7,6},{8,9},{9,8},{10,11... | collective-permute-start | bytes 983048 | tf_op jit(solution)/shard_map/ppermute | solution.py:622
  35.1 1.5 %place.1.p0 = bf16[576,256]{1,0:T(8,128)(2,1)S(1)} custom-call(bf16[64,8,640]{2,1,0:T(8,128)(2,1)S(1)} %all-to-all-done.arrived_ref), custom_call_target="tpu_custom_call" | custom-call | tf_op jit(solution)/shard_map/place/pallas_call | solution.py:221
  36.6 0.0 collective-permute-done.3.other_ref
  36.6 1.2 %merge_pair.1 = f32[16,40,128]{2,1,0:T(8,128)} custom-call(f32[16,40,128]{2,1,0:T(8,128)S(1)} %get-tuple-element.26.mine_ref, f32[16,40,128]{2,1,0:T(8,128)S(1)} %collective-permute-done.3.other_ref), custom_call_target="tpu_custom_call" | custom-call | tf_op jit(solution)/shard_map/merge_pair/pallas_call | solution.py:463
  37.8 8.3 %all-to-all-start.1 = ((f32[16,40,128]{2,1,0:T(8,128)}), f32[16,40,128]{2,1,0:T(8,128)S(1)}, u32[]{:S(2)}, u32[]{:S(2)}) async-start(f32[16,40,128]{2,1,0:T(8,128)} %merge_pair.1), calls=%async_computation.1 | async-start | bytes 655360 | tf_op jit(solution)/shard_map/all_to_all | solution.py:623
  46.2 1.2 %collective-permute-start.5 = (bf16[576,256]{1,0:T(8,128)(2,1)S(1)}, bf16[576,256]{1,0:T(8,128)(2,1)S(1)}, u32[]{:S(2)}, u32[]{:S(2)}) collective-permute-start(bf16[576,256]{1,0:T(8,128)(2,1)S(1)} %place.1.p0), channel_id=1, source_target_pairs={{0,96},{32,64},{64,32},{96,0},{1,97},{33,65},{65,33},{97,1},{2,98}... | collective-permute-start | bytes 884744 | tf_op jit(solution)/shard_map/ppermute | solution.py:560
  47.4 2.6 %collective-permute-start.7 = (bf16[576,256]{1,0:T(8,128)(2,1)S(1)}, bf16[576,256]{1,0:T(8,128)(2,1)S(1)}, u32[]{:S(2)}, u32[]{:S(2)}) collective-permute-start(bf16[576,256]{1,0:T(8,128)(2,1)S(1)} %place.1.p0), channel_id=1, source_target_pairs={{0,64},{32,96},{64,0},{96,32},{1,65},{33,97},{65,1},{97,33},{2,66}... | collective-permute-start | bytes 884744 | tf_op jit(solution)/shard_map/ppermute | solution.py:560
  50.0 1.7 %all-to-all-done.1.parts_ref = f32[16,40,128]{2,1,0:T(8,128)S(1)} async-done(((f32[16,40,128]{2,1,0:T(8,128)}), f32[16,40,128]{2,1,0:T(8,128)S(1)}, u32[]{:S(2)}, u32[]{:S(2)}) %all-to-all-start.1) | async-done | bytes 327712 | tf_op jit(solution)/shard_map/all_to_all | solution.py:623
  51.7 0.4 merge.1
  52.2 9.8 %all_to_all.15.mine_ref = bf16[16,32,128]{2,1,0:T(8,128)(2,1)S(1)} all-to-all(bf16[16,32,128]{2,1,0:T(8,128)(2,1)S(1)} %merge.1), channel_id=1, replica_groups={{30,28,26,24,22,20,18,16,14,12,10,8,6,4,2,0},{31,29,27,25,23,21,19,17,1..., dimensions={0} | all-to-all | bytes 262144 | tf_op jit(solution)/shard_map/all_to_all | solution.py:624
  62.0 2.3 %collective-permute-start.4 = (bf16[16,32,128]{2,1,0:T(8,128)(2,1)S(1)}, bf16[16,32,128]{2,1,0:T(8,128)(2,1)S(1)}, u32[]{:S(2)}, u32[]{:S(2)}) collective-permute-start(bf16[16,32,128]{2,1,0:T(8,128)(2,1)S(1)} %all_to_all.15.mine_ref), channel_id=1, source_target_pairs={{0,1},{1,0},{2,3},{3,2},{4,5},{5,4},{6,7},{7,6},{8,9},{9,8},{10,11... | collective-permute-start | bytes 393224 | tf_op jit(solution)/shard_map/ppermute | solution.py:625
  64.4 1.0 %collective-permute-done.4.other_ref = bf16[16,32,128]{2,1,0:T(8,128)(2,1)S(1)} collective-permute-done((bf16[16,32,128]{2,1,0:T(8,128)(2,1)S(1)}, bf16[16,32,128]{2,1,0:T(8,128)(2,1)S(1)}, u32[]{:S(2)}, u32[]{:S(2)}) %collective-permute-start.4) | collective-permute-done | bytes 131104 | tf_op jit(solution)/shard_map/ppermute | solution.py:625
  65.4 1.7 %finish.1 = (bf16[32,4096]{1,0:T(8,128)(2,1)}, bf16[576,1024]{1,0:T(8,128)(2,1)}) custom-call(bf16[16,32,128]{2,1,0:T(8,128)(2,1)S(1)} %all_to_all.15.mine_ref, bf16[16,32,128]{2,1,0:T(8,128)(2,1)S(1)} %collective-permute-done.4.other_ref, bf16[576,256]{1,0:T(8,128)(2,1)S(1)} %place.1.p0, bf16[576,256]{1,0:T(8,128)(2,1)S(1)} %collective-permute-done.5.p1, ...), custom_call_target="tpu_custom_call" | custom-call | tf_op jit(solution)/shard_map/finish/pallas_call | solution.py:542
  (18 shorter events, 0.1 us)
Async XLA Ops:
  0.6 20.9 %copy-start.3 = (s32[4,8]{1,0:T(4,128)S(1)}, s32[4,8]{1,0:T(4,128)}, u32[]{:S(2)}) copy-start(s32[4,8]{1,0:T(4,128)} %position_ref.1) | copy-start | bytes 388
  0.6 20.9 %copy-start.4 = (s32[4]{0:T(128)S(1)}, s32[4]{0:T(128)}, u32[]{:S(2)}) copy-start(s32[4]{0:T(128)} %lengths_ref) | copy-start | bytes 52
  0.7 20.9 %copy-start.5 = (s32[8]{0:T(128)S(1)}, s32[8]{0:T(128)}, u32[]{:S(2)}) copy-start(s32[8]{0:T(128)} %request_ref.1) | copy-start | bytes 100
  0.7 22.9 %copy-start = (bf16[4,8,32,512]{3,2,1,0:T(8,128)(2,1)S(1)}, bf16[4,8,32,512]{3,2,1,0:T(8,128)(2,1)}, u32[]{:S(2)}) copy-start(bf16[4,8,32,512]{3,2,1,0:T(8,128)(2,1)} %param.14) | copy-start | bytes 3145732
  0.7 22.9 %copy-start.1 = (bf16[4,8,32,64]{3,2,1,0:T(8,128)(2,1)S(1)}, bf16[4,8,32,64]{3,2,1,0:T(8,128)(2,1)}, u32[]{:S(2)}) copy-start(bf16[4,8,32,64]{3,2,1,0:T(8,128)(2,1)} %param.15) | copy-start | bytes 393220
  7.5 12.7 %collective-permute-start = (bf16[576,256]{1,0:T(8,128)(2,1)}, bf16[576,256]{1,0:T(8,128)(2,1)S(1)}, u32[]{:S(2)}, u32[]{:S(2)}) collective-permute-start(bf16[576,256]{1,0:T(8,128)(2,1)} %get-tuple-element.16.own_hbm), channel_id=1, source_target_pairs={{0,96},{32,64},{64,32},{96,0},{1,97},{33,65},{65,33},{97,1},{2,98}... | collective-permute-start | bytes 884744 | tf_op jit(solution)/shard_map/ppermute | solution.py:560
  12.1 8.1 %collective-permute-start.1 = (bf16[576,256]{1,0:T(8,128)(2,1)}, bf16[576,256]{1,0:T(8,128)(2,1)S(1)}, u32[]{:S(2)}, u32[]{:S(2)}) collective-permute-start(bf16[576,256]{1,0:T(8,128)(2,1)} %get-tuple-element.16.own_hbm), channel_id=1, source_target_pairs={{0,32},{32,0},{64,96},{96,64},{1,33},{33,1},{65,97},{97,65},{2,34}... | collective-permute-start | bytes 884744 | tf_op jit(solution)/shard_map/ppermute | solution.py:560
  12.2 22.9 %all-to-all-start = ((bf16[64,8,640]{2,1,0:T(8,128)(2,1)}), bf16[64,8,640]{2,1,0:T(8,128)(2,1)S(1)}, u32[]{:S(2)}, u32[]{:S(2)}) async-start(bf16[64,8,640]{2,1,0:T(8,128)(2,1)} %get-tuple-element.25), calls=%async_computation | async-start | bytes 1310720 | tf_op jit(solution)/shard_map/all_to_all | solution.py:617
  20.3 7.2 %collective-permute-start.2 = (bf16[576,256]{1,0:T(8,128)(2,1)S(1)}, bf16[576,256]{1,0:T(8,128)(2,1)S(1)}, u32[]{:S(2)}, u32[]{:S(2)}) collective-permute-start(bf16[576,256]{1,0:T(8,128)(2,1)S(1)} %broadcast_select_fusion), channel_id=1, source_target_pairs={{0,32},{1,97},{2,34},{3,99},{4,36},{5,101},{6,38},{7,103},{8,40},{... | collective-permute-start | bytes 884744 | tf_op jit(solution)/shard_map/ppermute | solution.py:573
  21.6 1.0 %copy-start.2 = (bf16[576,256]{1,0:T(8,128)(2,1)S(1)}, bf16[576,256]{1,0:T(8,128)(2,1)}, u32[]{:S(2)}) copy-start(bf16[576,256]{1,0:T(8,128)(2,1)} %get-tuple-element.16.own_hbm) | copy-start | bytes 884740
  33.8 2.8 %collective-permute-start.3 = (f32[16,40,128]{2,1,0:T(8,128)S(1)}, f32[16,40,128]{2,1,0:T(8,128)S(1)}, u32[]{:S(2)}, u32[]{:S(2)}) collective-permute-start(f32[16,40,128]{2,1,0:T(8,128)S(1)} %get-tuple-element.27), channel_id=1, source_target_pairs={{0,1},{1,0},{2,3},{3,2},{4,5},{5,4},{6,7},{7,6},{8,9},{9,8},{10,11... | collective-permute-start | bytes 983048 | tf_op jit(solution)/shard_map/ppermute | solution.py:622
  37.8 13.9 %all-to-all-start.1 = ((f32[16,40,128]{2,1,0:T(8,128)}), f32[16,40,128]{2,1,0:T(8,128)S(1)}, u32[]{:S(2)}, u32[]{:S(2)}) async-start(f32[16,40,128]{2,1,0:T(8,128)} %merge_pair.1), calls=%async_computation.1 | async-start | bytes 655360 | tf_op jit(solution)/shard_map/all_to_all | solution.py:623
  46.2 18.2 %collective-permute-start.5 = (bf16[576,256]{1,0:T(8,128)(2,1)S(1)}, bf16[576,256]{1,0:T(8,128)(2,1)S(1)}, u32[]{:S(2)}, u32[]{:S(2)}) collective-permute-start(bf16[576,256]{1,0:T(8,128)(2,1)S(1)} %place.1.p0), channel_id=1, source_target_pairs={{0,96},{32,64},{64,32},{96,0},{1,97},{33,65},{65,33},{97,1},{2,98}... | collective-permute-start | bytes 884744 | tf_op jit(solution)/shard_map/ppermute | solution.py:560
  47.4 17.0 %collective-permute-start.6 = (bf16[576,256]{1,0:T(8,128)(2,1)S(1)}, bf16[576,256]{1,0:T(8,128)(2,1)S(1)}, u32[]{:S(2)}, u32[]{:S(2)}) collective-permute-start(bf16[576,256]{1,0:T(8,128)(2,1)S(1)} %place.1.p0), channel_id=1, source_target_pairs={{0,32},{32,0},{64,96},{96,64},{1,33},{33,1},{65,97},{97,65},{2,34}... | collective-permute-start | bytes 884744 | tf_op jit(solution)/shard_map/ppermute | solution.py:560
  47.4 17.0 %collective-permute-start.7 = (bf16[576,256]{1,0:T(8,128)(2,1)S(1)}, bf16[576,256]{1,0:T(8,128)(2,1)S(1)}, u32[]{:S(2)}, u32[]{:S(2)}) collective-permute-start(bf16[576,256]{1,0:T(8,128)(2,1)S(1)} %place.1.p0), channel_id=1, source_target_pairs={{0,64},{32,96},{64,0},{96,32},{1,65},{33,97},{65,1},{97,33},{2,66}... | collective-permute-start | bytes 884744 | tf_op jit(solution)/shard_map/ppermute | solution.py:560
  62.0 3.3 %collective-permute-start.4 = (bf16[16,32,128]{2,1,0:T(8,128)(2,1)S(1)}, bf16[16,32,128]{2,1,0:T(8,128)(2,1)S(1)}, u32[]{:S(2)}, u32[]{:S(2)}) collective-permute-start(bf16[16,32,128]{2,1,0:T(8,128)(2,1)S(1)} %all_to_all.15.mine_ref), channel_id=1, source_target_pairs={{0,1},{1,0},{2,3},{3,2},{4,5},{5,4},{6,7},{7,6},{8,9},{9,8},{10,11... | collective-permute-start | bytes 393224 | tf_op jit(solution)/shard_map/ppermute | solution.py:625

commit v7 on v6

--- a/solution.py
+++ b/solution.py
@@ -330,6 +330,26 @@
     lax.fori_loop(0, cuts, body, 0, unroll=2)
 
 
+def apart(value):
+    rows, width = value.shape
+    tiles = value.reshape(rows // 16, 2, 8, width)
+    first, second = tiles[:, 0], tiles[:, 1]
+    upper_part = lax.broadcasted_iota(jnp.int32, first.shape, 1) < 4
+    low = jnp.where(upper_part, first, pltpu.roll(second, 4, 1))
+    high = jnp.where(upper_part, pltpu.roll(first, 4, 1), second)
+    return low.reshape(rows // 2, width), high.reshape(rows // 2, width)
+
+
+def together(low, high):
+    rows, width = low.shape
+    low = low.reshape(rows // 8, 8, width)
+    high = high.reshape(rows // 8, 8, width)
+    upper_part = lax.broadcasted_iota(jnp.int32, low.shape, 1) < 4
+    first = jnp.where(upper_part, low, pltpu.roll(high, 4, 1))
+    second = jnp.where(upper_part, pltpu.roll(low, 4, 1), high)
+    return jnp.stack([first, second], axis=1).reshape(2 * rows, width)
+
+
 def far_kernel(
     bias_ref, valid_ref, latent_ref, rope_ref, k3, mixed_ref, stat_ref, w_hbm,
     keep_ref, send_ref, out_ref, w_ref, sems,
@@ -347,6 +367,8 @@
     out_ref[:, all_heads:, :] = jnp.zeros((items, PAD, 128), jnp.float32)
     head = lax.broadcasted_iota(jnp.int32, (rows, 128), 0) % heads
     lane = lax.broadcasted_iota(jnp.int32, (rows, 128), 1)
+    half_heads = heads // 2
+    head_of_half = lax.broadcasted_iota(jnp.int32, (rows // 2, 128), 0) % half_heads
 
     def body(cut, carry):
         scores = scores_of(latent_ref, rope_ref, cut, (k3,), bias_ref)
@@ -359,17 +381,23 @@
         inverse = jnp.where(valid, 1.0 / total, 0.0)
         mixed = mixed * inverse + mixed_ref[cut] * (factor * inverse)
         level = jnp.where(valid, peak * score_scale + jnp.log(total), mask_value)
-        upper = mixed.astype(jnp.bfloat16)
-        lower = (mixed - upper.astype(jnp.float32)).astype(jnp.bfloat16)
+        low, high = apart(mixed)
         weights_of(cut).wait()
-        result = jnp.zeros((rows, 128), jnp.float32)
-        both = jnp.concatenate([upper, lower], axis=0)
-        for h in range(0, heads, 2):
-            pair = jnp.concatenate([w_ref[cut * heads + h], w_ref[cut * heads + h + 1]], axis=1)
-            y = jnp.dot(both, pair, preferred_element_type=jnp.float32)
-            y = y[:rows] + y[rows:]
-            result = jnp.where(head == h, y[:, :128], result)
-            result = jnp.where(head == h + 1, y[:, 128:], result)
+        pieces = []
+        for first, part in ((0, low), (half_heads, high)):
+            upper = part.astype(jnp.bfloat16)
+            lower = (part - upper.astype(jnp.float32)).astype(jnp.bfloat16)
+            both = jnp.concatenate([upper, lower], axis=0)
+            piece = jnp.zeros((rows // 2, 128), jnp.float32)
+            for h in range(0, half_heads, 2):
+                at = cut * heads + first + h
+                pair = jnp.concatenate([w_ref[at], w_ref[at + 1]], axis=1)
+                y = jnp.dot(both, pair, preferred_element_type=jnp.float32)
+                y = y[: rows // 2] + y[rows // 2 :]
+                piece = jnp.where(head_of_half == h, y[:, :128], piece)
+                piece = jnp.where(head_of_half == h + 1, y[:, 128:], piece)
+            pieces.append(piece)
+        result = together(*pieces)
         at = pl.multiple_of(cut * heads, heads)
         out_ref[:, pl.ds(at, heads), :] = result.reshape(items, heads, 128)
         lines = jnp.where(lane == head + at, level, 0.0).reshape(items, heads, 128)

time: 67.5 us -> 66.3 us (0.982)
  Pallas kernels: 22.6 us -> 21.5 us
    pallas_call x1, Pallas kernels: 6.37 us -> 5.26 us  [attend(): pl.pallas_call(far_kernel, in_specs=[vmem] * 7 + [pl.BlockSpec(memory_spa...]
  transfers between devices with their start and end apart: 10 -> 10, of which waited for: 3 -> 3; matrix products, arithmetic and copies ran while one was open for 0% -> 0% of each run, Pallas kernels for 19% -> 18%
where the time goes in v7:
time: 66.3 us; the launch traced here: 66 us
  starting transfers between devices  29.8 us (45%)
  Pallas kernels  21.5 us (32%)
  blocking collectives  9.84 us (15%)
  waiting for transfers between devices  3.05 us (5%)
  local copies, waits for them, and re-layouts  0.98 us (1%)
  between operations  0.8 us (1%)
    all_to_all x1, blocking collectives, per_device(): result = exchanged(result, axis_index_groups=plane)  9.84 us
    ppermute x5, starting transfers between devices, exchange(): return lax.ppermute(piece, 'pre', [(i, i ^ turn) for i in range(groups)])  8.53 us
    all_to_all x1, starting transfers between devices, per_device(): result = merge(exchanged(parts, axis_index_groups=plane))  8.35 us
    all_to_all x1, starting transfers between devices, per_device(): arrived = exchanged(packed)  8.03 us
    pallas_call x1, Pallas kernels, produce(): pl.pallas_call(functools.partial(produce_kernel, groups, owners), in_spec...  6.79 us
    pallas_call x1, Pallas kernels, attend(): pl.pallas_call(far_kernel, in_specs=[vmem] * 7 + [pl.BlockSpec(memory_spa...  5.26 us
    pallas_call x1, Pallas kernels, attend(): pl.pallas_call(near_kernel, in_specs=[vmem] * 6, out_specs=[vmem] * 2, ou...  3.48 us
    ppermute x1, starting transfers between devices, per_device(): lax.ppermute(result, 'dec', sibling)  2.33 us
  transfers between devices with their start and end apart: 10, of which 3 were waited for; matrix products, arithmetic and copies ran while one was open for 0% of the time, Pallas kernels for 18%

profile of v7, /device:TPU:1, one launch (start us, length us, event | category | flops | bytes accessed | tf_op | source)
XLA Modules:
  0.0 66.0 jit_solution(9318189462195574838)
XLA Ops:
  0.7 6.8 %produce.1 = (bf16[576,256]{1,0:T(8,128)(2,1)}, bf16[64,8,640]{2,1,0:T(8,128)(2,1)}) custom-call(s32[4]{0:T(128)} %lengths_ref, s32[4096]{0:T(1024)} %dest_hbm.1, bf16[256,7168]{1,0:T(8,128)(2,1)} %hidden_hbm.1, bf16[576,7168]{1,0:T(8,128)(2,1)} %bitcast.10, f32[1,512]{1,0:T(1,128)} %bitcast.11, f32[32,128]{1,0:T(8,128)} %constant.20.clone.freq_hbm), custom_call_target="tpu_custom_call" | custom-call | tf_op jit(solution)/shard_map/produce/pallas_call | solution.py:159
  7.5 4.7 %collective-permute-start = (bf16[576,256]{1,0:T(8,128)(2,1)}, bf16[576,256]{1,0:T(8,128)(2,1)S(1)}, u32[]{:S(2)}, u32[]{:S(2)}) collective-permute-start(bf16[576,256]{1,0:T(8,128)(2,1)} %get-tuple-element.16.own_hbm), channel_id=1, source_target_pairs={{0,96},{32,64},{64,32},{96,0},{1,97},{33,65},{65,33},{97,1},{2,98}... | collective-permute-start | bytes 884744 | tf_op jit(solution)/shard_map/ppermute | solution.py:588
  12.1 0.0 collective-permute-start.1
  12.2 8.0 %all-to-all-start = ((bf16[64,8,640]{2,1,0:T(8,128)(2,1)}), bf16[64,8,640]{2,1,0:T(8,128)(2,1)S(1)}, u32[]{:S(2)}, u32[]{:S(2)}) async-start(bf16[64,8,640]{2,1,0:T(8,128)(2,1)} %get-tuple-element.25), calls=%async_computation | async-start | bytes 1310720 | tf_op jit(solution)/shard_map/all_to_all | solution.py:645
  20.2 0.0 collective-permute-done.1.k2
  20.3 1.3 %collective-permute-start.2 = (bf16[576,256]{1,0:T(8,128)(2,1)S(1)}, bf16[576,256]{1,0:T(8,128)(2,1)S(1)}, u32[]{:S(2)}, u32[]{:S(2)}) collective-permute-start(bf16[576,256]{1,0:T(8,128)(2,1)S(1)} %broadcast_select_fusion), channel_id=1, source_target_pairs={{0,32},{1,97},{2,34},{3,99},{4,36},{5,101},{6,38},{7,103},{8,40},{... | collective-permute-start | bytes 884744 | tf_op jit(solution)/shard_map/ppermute | solution.py:601
  21.6 1.0 %copy-done.2 = bf16[576,256]{1,0:T(8,128)(2,1)S(1)} copy-done((bf16[576,256]{1,0:T(8,128)(2,1)S(1)}, bf16[576,256]{1,0:T(8,128)(2,1)}, u32[]{:S(2)}) %copy-start.2) | copy-done | bytes 294936
  22.5 1.0 %prepare.1 = (f32[256,768]{1,0:T(8,128)S(1)}, f32[256,256]{1,0:T(8,128)S(1)}, s32[256,128]{1,0:T(8,128)S(1)}, bf16[576,256]{1,0:T(8,128)(2,1)S(1)}) custom-call(s32[4]{0:T(128)S(1)} %copy-done.4, s32[8]{0:T(128)S(1)} %copy-done.5, s32[4,8]{1,0:T(4,128)S(1)} %copy-done.3, bf16[576,256]{1,0:T(8,128)(2,1)S(1)} %copy-done.2), custom_call_target="tpu_custom_call" | custom-call | tf_op jit(solution)/shard_map/prepare/pallas_call | solution.py:272
  23.6 3.5 %attend_near.1 = (f32[4,256,512]{2,1,0:T(8,128)S(1)}, f32[4,256,128]{2,1,0:T(8,128)S(1)}) custom-call(f32[256,768]{1,0:T(8,128)S(1)} %get-tuple-element.20.bias_ref, bf16[32,4,8,512]{3,2,1,0:T(8,128)(2,1)S(1)} %bitcast.6, bf16[32,4,8,64]{3,2,1,0:T(8,128)(2,1)S(1)} %bitcast.8, bf16[576,256]{1,0:T(8,128)(2,1)S(1)} %get-tuple-element.21.k0, ...), custom_call_target="tpu_custom_call" | custom-call | tf_op jit(solution)/shard_map/attend_near/pallas_call | solution.py:427
  27.1 0.3 collective-permute-done.2.k3
  27.4 5.3 %attend_far.1 = (f32[16,40,128]{2,1,0:T(8,128)S(1)}, f32[16,40,128]{2,1,0:T(8,128)S(1)}) custom-call(f32[256,256]{1,0:T(8,128)S(1)} %get-tuple-element.18.bias_ref, s32[256,128]{1,0:T(8,128)S(1)} %get-tuple-element.19.valid_ref, bf16[32,4,8,512]{3,2,1,0:T(8,128)(2,1)S(1)} %bitcast.7, bf16[32,4,8,64]{3,2,1,0:T(8,128)(2,1)S(1)} %bitcast.9, ...), custom_call_target="tpu_custom_call" | custom-call | tf_op jit(solution)/shard_map/attend_far/pallas_call | solution.py:439
  32.7 1.3 %collective-permute-start.3 = (f32[16,40,128]{2,1,0:T(8,128)S(1)}, f32[16,40,128]{2,1,0:T(8,128)S(1)}, u32[]{:S(2)}, u32[]{:S(2)}) collective-permute-start(f32[16,40,128]{2,1,0:T(8,128)S(1)} %get-tuple-element.27), channel_id=1, source_target_pairs={{0,1},{1,0},{2,3},{3,2},{4,5},{5,4},{6,7},{7,6},{8,9},{9,8},{10,11... | collective-permute-start | bytes 983048 | tf_op jit(solution)/shard_map/ppermute | solution.py:650
  34.0 0.0 all-to-all-done.arrived_ref
  34.0 1.5 %place.1.p0 = bf16[576,256]{1,0:T(8,128)(2,1)S(1)} custom-call(bf16[64,8,640]{2,1,0:T(8,128)(2,1)S(1)} %all-to-all-done.arrived_ref), custom_call_target="tpu_custom_call" | custom-call | tf_op jit(solution)/shard_map/place/pallas_call | solution.py:221
  35.5 1.2 %merge_pair.1 = f32[16,40,128]{2,1,0:T(8,128)} custom-call(f32[16,40,128]{2,1,0:T(8,128)S(1)} %get-tuple-element.26.mine_ref, f32[16,40,128]{2,1,0:T(8,128)S(1)} %collective-permute-done.3.other_ref), custom_call_target="tpu_custom_call" | custom-call | tf_op jit(solution)/shard_map/merge_pair/pallas_call | solution.py:491
  36.7 8.4 %all-to-all-start.1 = ((f32[16,40,128]{2,1,0:T(8,128)}), f32[16,40,128]{2,1,0:T(8,128)S(1)}, u32[]{:S(2)}, u32[]{:S(2)}) async-start(f32[16,40,128]{2,1,0:T(8,128)} %merge_pair.1), calls=%async_computation.1 | async-start | bytes 655360 | tf_op jit(solution)/shard_map/all_to_all | solution.py:651
  45.1 1.2 %collective-permute-start.5 = (bf16[576,256]{1,0:T(8,128)(2,1)S(1)}, bf16[576,256]{1,0:T(8,128)(2,1)S(1)}, u32[]{:S(2)}, u32[]{:S(2)}) collective-permute-start(bf16[576,256]{1,0:T(8,128)(2,1)S(1)} %place.1.p0), channel_id=1, source_target_pairs={{0,96},{32,64},{64,32},{96,0},{1,97},{33,65},{65,33},{97,1},{2,98}... | collective-permute-start | bytes 884744 | tf_op jit(solution)/shard_map/ppermute | solution.py:588
  46.3 2.6 %collective-permute-start.7 = (bf16[576,256]{1,0:T(8,128)(2,1)S(1)}, bf16[576,256]{1,0:T(8,128)(2,1)S(1)}, u32[]{:S(2)}, u32[]{:S(2)}) collective-permute-start(bf16[576,256]{1,0:T(8,128)(2,1)S(1)} %place.1.p0), channel_id=1, source_target_pairs={{0,64},{32,96},{64,0},{96,32},{1,65},{33,97},{65,1},{97,33},{2,66}... | collective-permute-start | bytes 884744 | tf_op jit(solution)/shard_map/ppermute | solution.py:588
  48.9 1.7 %all-to-all-done.1.parts_ref = f32[16,40,128]{2,1,0:T(8,128)S(1)} async-done(((f32[16,40,128]{2,1,0:T(8,128)}), f32[16,40,128]{2,1,0:T(8,128)S(1)}, u32[]{:S(2)}, u32[]{:S(2)}) %all-to-all-start.1) | async-done | bytes 327712 | tf_op jit(solution)/shard_map/all_to_all | solution.py:651
  50.6 0.4 merge.1
  51.1 9.8 %all_to_all.15.mine_ref = bf16[16,32,128]{2,1,0:T(8,128)(2,1)S(1)} all-to-all(bf16[16,32,128]{2,1,0:T(8,128)(2,1)S(1)} %merge.1), channel_id=1, replica_groups={{30,28,26,24,22,20,18,16,14,12,10,8,6,4,2,0},{31,29,27,25,23,21,19,17,1..., dimensions={0} | all-to-all | bytes 262144 | tf_op jit(solution)/shard_map/all_to_all | solution.py:652
  60.9 2.3 %collective-permute-start.4 = (bf16[16,32,128]{2,1,0:T(8,128)(2,1)S(1)}, bf16[16,32,128]{2,1,0:T(8,128)(2,1)S(1)}, u32[]{:S(2)}, u32[]{:S(2)}) collective-permute-start(bf16[16,32,128]{2,1,0:T(8,128)(2,1)S(1)} %all_to_all.15.mine_ref), channel_id=1, source_target_pairs={{0,1},{1,0},{2,3},{3,2},{4,5},{5,4},{6,7},{7,6},{8,9},{9,8},{10,11... | collective-permute-start | bytes 393224 | tf_op jit(solution)/shard_map/ppermute | solution.py:653
  63.3 1.0 %collective-permute-done.4.other_ref = bf16[16,32,128]{2,1,0:T(8,128)(2,1)S(1)} collective-permute-done((bf16[16,32,128]{2,1,0:T(8,128)(2,1)S(1)}, bf16[16,32,128]{2,1,0:T(8,128)(2,1)S(1)}, u32[]{:S(2)}, u32[]{:S(2)}) %collective-permute-start.4) | collective-permute-done | bytes 131104 | tf_op jit(solution)/shard_map/ppermute | solution.py:653
  64.2 1.7 %finish.1 = (bf16[32,4096]{1,0:T(8,128)(2,1)}, bf16[576,1024]{1,0:T(8,128)(2,1)}) custom-call(bf16[16,32,128]{2,1,0:T(8,128)(2,1)S(1)} %all_to_all.15.mine_ref, bf16[16,32,128]{2,1,0:T(8,128)(2,1)S(1)} %collective-permute-done.4.other_ref, bf16[576,256]{1,0:T(8,128)(2,1)S(1)} %place.1.p0, bf16[576,256]{1,0:T(8,128)(2,1)S(1)} %collective-permute-done.5.p1, ...), custom_call_target="tpu_custom_call" | custom-call | tf_op jit(solution)/shard_map/finish/pallas_call | solution.py:570
  (18 shorter events, 0.1 us)
Async XLA Ops:
  0.6 20.9 %copy-start.3 = (s32[4,8]{1,0:T(4,128)S(1)}, s32[4,8]{1,0:T(4,128)}, u32[]{:S(2)}) copy-start(s32[4,8]{1,0:T(4,128)} %position_ref.1) | copy-start | bytes 388
  0.6 20.9 %copy-start.4 = (s32[4]{0:T(128)S(1)}, s32[4]{0:T(128)}, u32[]{:S(2)}) copy-start(s32[4]{0:T(128)} %lengths_ref) | copy-start | bytes 52
  0.7 20.9 %copy-start.5 = (s32[8]{0:T(128)S(1)}, s32[8]{0:T(128)}, u32[]{:S(2)}) copy-start(s32[8]{0:T(128)} %request_ref.1) | copy-start | bytes 100
  0.7 22.9 %copy-start = (bf16[4,8,32,512]{3,2,1,0:T(8,128)(2,1)S(1)}, bf16[4,8,32,512]{3,2,1,0:T(8,128)(2,1)}, u32[]{:S(2)}) copy-start(bf16[4,8,32,512]{3,2,1,0:T(8,128)(2,1)} %param.14) | copy-start | bytes 3145732
  0.7 22.9 %copy-start.1 = (bf16[4,8,32,64]{3,2,1,0:T(8,128)(2,1)S(1)}, bf16[4,8,32,64]{3,2,1,0:T(8,128)(2,1)}, u32[]{:S(2)}) copy-start(bf16[4,8,32,64]{3,2,1,0:T(8,128)(2,1)} %param.15) | copy-start | bytes 393220
  7.5 12.7 %collective-permute-start = (bf16[576,256]{1,0:T(8,128)(2,1)}, bf16[576,256]{1,0:T(8,128)(2,1)S(1)}, u32[]{:S(2)}, u32[]{:S(2)}) collective-permute-start(bf16[576,256]{1,0:T(8,128)(2,1)} %get-tuple-element.16.own_hbm), channel_id=1, source_target_pairs={{0,96},{32,64},{64,32},{96,0},{1,97},{33,65},{65,33},{97,1},{2,98}... | collective-permute-start | bytes 884744 | tf_op jit(solution)/shard_map/ppermute | solution.py:588
  12.1 8.1 %collective-permute-start.1 = (bf16[576,256]{1,0:T(8,128)(2,1)}, bf16[576,256]{1,0:T(8,128)(2,1)S(1)}, u32[]{:S(2)}, u32[]{:S(2)}) collective-permute-start(bf16[576,256]{1,0:T(8,128)(2,1)} %get-tuple-element.16.own_hbm), channel_id=1, source_target_pairs={{0,32},{32,0},{64,96},{96,64},{1,33},{33,1},{65,97},{97,65},{2,34}... | collective-permute-start | bytes 884744 | tf_op jit(solution)/shard_map/ppermute | solution.py:588
  12.2 21.8 %all-to-all-start = ((bf16[64,8,640]{2,1,0:T(8,128)(2,1)}), bf16[64,8,640]{2,1,0:T(8,128)(2,1)S(1)}, u32[]{:S(2)}, u32[]{:S(2)}) async-start(bf16[64,8,640]{2,1,0:T(8,128)(2,1)} %get-tuple-element.25), calls=%async_computation | async-start | bytes 1310720 | tf_op jit(solution)/shard_map/all_to_all | solution.py:645
  20.3 7.2 %collective-permute-start.2 = (bf16[576,256]{1,0:T(8,128)(2,1)S(1)}, bf16[576,256]{1,0:T(8,128)(2,1)S(1)}, u32[]{:S(2)}, u32[]{:S(2)}) collective-permute-start(bf16[576,256]{1,0:T(8,128)(2,1)S(1)} %broadcast_select_fusion), channel_id=1, source_target_pairs={{0,32},{1,97},{2,34},{3,99},{4,36},{5,101},{6,38},{7,103},{8,40},{... | collective-permute-start | bytes 884744 | tf_op jit(solution)/shard_map/ppermute | solution.py:601
  21.6 1.0 %copy-start.2 = (bf16[576,256]{1,0:T(8,128)(2,1)S(1)}, bf16[576,256]{1,0:T(8,128)(2,1)}, u32[]{:S(2)}) copy-start(bf16[576,256]{1,0:T(8,128)(2,1)} %get-tuple-element.16.own_hbm) | copy-start | bytes 884740
  32.7 2.8 %collective-permute-start.3 = (f32[16,40,128]{2,1,0:T(8,128)S(1)}, f32[16,40,128]{2,1,0:T(8,128)S(1)}, u32[]{:S(2)}, u32[]{:S(2)}) collective-permute-start(f32[16,40,128]{2,1,0:T(8,128)S(1)} %get-tuple-element.27), channel_id=1, source_target_pairs={{0,1},{1,0},{2,3},{3,2},{4,5},{5,4},{6,7},{7,6},{8,9},{9,8},{10,11... | collective-permute-start | bytes 983048 | tf_op jit(solution)/shard_map/ppermute | solution.py:650
  36.7 13.9 %all-to-all-start.1 = ((f32[16,40,128]{2,1,0:T(8,128)}), f32[16,40,128]{2,1,0:T(8,128)S(1)}, u32[]{:S(2)}, u32[]{:S(2)}) async-start(f32[16,40,128]{2,1,0:T(8,128)} %merge_pair.1), calls=%async_computation.1 | async-start | bytes 655360 | tf_op jit(solution)/shard_map/all_to_all | solution.py:651
  45.1 18.2 %collective-permute-start.5 = (bf16[576,256]{1,0:T(8,128)(2,1)S(1)}, bf16[576,256]{1,0:T(8,128)(2,1)S(1)}, u32[]{:S(2)}, u32[]{:S(2)}) collective-permute-start(bf16[576,256]{1,0:T(8,128)(2,1)S(1)} %place.1.p0), channel_id=1, source_target_pairs={{0,96},{32,64},{64,32},{96,0},{1,97},{33,65},{65,33},{97,1},{2,98}... | collective-permute-start | bytes 884744 | tf_op jit(solution)/shard_map/ppermute | solution.py:588
  46.3 17.0 %collective-permute-start.6 = (bf16[576,256]{1,0:T(8,128)(2,1)S(1)}, bf16[576,256]{1,0:T(8,128)(2,1)S(1)}, u32[]{:S(2)}, u32[]{:S(2)}) collective-permute-start(bf16[576,256]{1,0:T(8,128)(2,1)S(1)} %place.1.p0), channel_id=1, source_target_pairs={{0,32},{32,0},{64,96},{96,64},{1,33},{33,1},{65,97},{97,65},{2,34}... | collective-permute-start | bytes 884744 | tf_op jit(solution)/shard_map/ppermute | solution.py:588
  46.3 17.0 %collective-permute-start.7 = (bf16[576,256]{1,0:T(8,128)(2,1)S(1)}, bf16[576,256]{1,0:T(8,128)(2,1)S(1)}, u32[]{:S(2)}, u32[]{:S(2)}) collective-permute-start(bf16[576,256]{1,0:T(8,128)(2,1)S(1)} %place.1.p0), channel_id=1, source_target_pairs={{0,64},{32,96},{64,0},{96,32},{1,65},{33,97},{65,1},{97,33},{2,66}... | collective-permute-start | bytes 884744 | tf_op jit(solution)/shard_map/ppermute | solution.py:588
  60.9 3.3 %collective-permute-start.4 = (bf16[16,32,128]{2,1,0:T(8,128)(2,1)S(1)}, bf16[16,32,128]{2,1,0:T(8,128)(2,1)S(1)}, u32[]{:S(2)}, u32[]{:S(2)}) collective-permute-start(bf16[16,32,128]{2,1,0:T(8,128)(2,1)S(1)} %all_to_all.15.mine_ref), channel_id=1, source_target_pairs={{0,1},{1,0},{2,3},{3,2},{4,5},{5,4},{6,7},{7,6},{8,9},{9,8},{10,11... | collective-permute-start | bytes 393224 | tf_op jit(solution)/shard_map/ppermute | solution.py:653

commit v8 on v7

--- a/solution.py
+++ b/solution.py
@@ -314,7 +314,11 @@
     return total, mixed
 
 
-def near_kernel(bias_ref, latent_ref, rope_ref, k0, k1, k2, mixed_ref, stat_ref):
+def near_kernel(
+    bias_ref, latent_ref, rope_ref, k0, k1, k2, w_hbm, mixed_ref, stat_ref, w_ref, sem
+):
+    copy = pltpu.make_async_copy(w_hbm, w_ref, sem)
+    copy.start()
     chunk_refs = (k0, k1, k2)
     cuts, rows, _ = mixed_ref.shape
     lane = lax.broadcasted_iota(jnp.int32, (rows, 128), 1)
@@ -328,6 +332,7 @@
         return carry
 
     lax.fori_loop(0, cuts, body, 0, unroll=2)
+    copy.wait()
 
 
 def apart(value):
@@ -351,19 +356,13 @@
 
 
 def far_kernel(
-    bias_ref, valid_ref, latent_ref, rope_ref, k3, mixed_ref, stat_ref, w_hbm,
-    keep_ref, send_ref, out_ref, w_ref, sems,
+    bias_ref, valid_ref, latent_ref, rope_ref, k3, mixed_ref, stat_ref, w_ref,
+    keep_ref, send_ref, out_ref,
 ):
     items, cuts, heads, _ = latent_ref.shape
     rows = items * heads
     all_heads = cuts * heads
 
-    def weights_of(cut):
-        part = pl.ds(cut * heads, heads)
-        return pltpu.make_async_copy(w_hbm.at[part], w_ref.at[part], sems.at[cut])
-
-    for cut in range(cuts):
-        weights_of(cut).start()
     out_ref[:, all_heads:, :] = jnp.zeros((items, PAD, 128), jnp.float32)
     head = lax.broadcasted_iota(jnp.int32, (rows, 128), 0) % heads
     lane = lax.broadcasted_iota(jnp.int32, (rows, 128), 1)
@@ -382,7 +381,6 @@
         mixed = mixed * inverse + mixed_ref[cut] * (factor * inverse)
         level = jnp.where(valid, peak * score_scale + jnp.log(total), mask_value)
         low, high = apart(mixed)
-        weights_of(cut).wait()
         pieces = []
         for first, part in ((0, low), (half_heads, high)):
             upper = part.astype(jnp.bfloat16)
@@ -424,31 +422,29 @@
     latent = latent.reshape(items, cuts, CUT_HEADS, -1)
     rope = rope.reshape(items, cuts, CUT_HEADS, -1)
     vmem = pl.BlockSpec(memory_space=pltpu.VMEM)
-    mixed, stat = pl.pallas_call(
+    mixed, stat, w_near = pl.pallas_call(
         near_kernel,
-        in_specs=[vmem] * 6,
-        out_specs=[vmem] * 2,
+        in_specs=[vmem] * 6 + [pl.BlockSpec(memory_space=pl.ANY)],
+        out_specs=[vmem] * 3,
         out_shape=[
             jax.ShapeDtypeStruct((cuts, rows, LAT), jnp.float32),
             jax.ShapeDtypeStruct((cuts, rows, 128), jnp.float32),
+            jax.ShapeDtypeStruct(w_up.shape, w_up.dtype),
         ],
-        compiler_params=params(20),
+        scratch_shapes=[pltpu.SemaphoreType.DMA(())],
+        compiler_params=params(42),
         name="attend_near",
-    )(near_bias, latent, rope, *chunks[:3])
+    )(near_bias, latent, rope, *chunks[:3], w_up)
     out_shape = jax.ShapeDtypeStruct((items // 2, heads + PAD, 128), jnp.float32)
     return pl.pallas_call(
         far_kernel,
-        in_specs=[vmem] * 7 + [pl.BlockSpec(memory_space=pl.ANY)],
+        in_specs=[vmem] * 8,
         out_specs=[vmem] * 2,
         out_shape=[out_shape] * 2,
-        scratch_shapes=[
-            pltpu.VMEM((items, heads + PAD, 128), jnp.float32),
-            pltpu.VMEM(w_up.shape, w_up.dtype),
-            pltpu.SemaphoreType.DMA((cuts,)),
-        ],
-        compiler_params=params(47),
+        scratch_shapes=[pltpu.VMEM((items, heads + PAD, 128), jnp.float32)],
+        compiler_params=params(20),
         name="attend_far",
-    )(far_bias, valid, latent, rope, chunks[3], mixed, stat, w_up)
+    )(far_bias, valid, latent, rope, chunks[3], mixed, stat, w_near)
 
 
 def merge_step(levels):
@@ -646,7 +642,6 @@
     quarter = place(arrived, *produced.shape)
     pieces = [quarter] + [exchange(quarter, groups, turn) for turn in TURNS[1:]]
 
-    keep, _ = lax.optimization_barrier((keep, quarter))
     parts = merge_pair(keep, lax.ppermute(send, "dec", sibling))
     result = merge(exchanged(parts, axis_index_groups=plane))
     result = exchanged(result, axis_index_groups=plane)

time: 66.3 us -> 65.8 us (level)
  Pallas kernels: 21.5 us -> 20.8 us
    all_to_all x1, waiting for transfers between devices: 1.71 us -> 0.01 us  [per_device(): result = merge(exchanged(parts, axis_index_groups=plane))]
    ppermute x1, waiting for transfers between devices: 0.01 us -> 1.26 us  [per_device(): parts = merge_pair(keep, lax.ppermute(send, 'dec', sibling))]
    pallas_call x2, Pallas kernels: 8.73 us -> 8.04 us  [the longest x1 4.54 us: attend(): pl.pallas_call(far_kernel, in_specs=[vmem] * 8, out_specs=[vmem] * 2, out...]
  transfers between devices with their start and end apart: 10 -> 10, of which waited for: 3 -> 3; matrix products, arithmetic and copies ran while one was open for 0% -> 0% of each run, Pallas kernels for 18% -> 19%
where the time goes in v8:
time: 65.8 us; the launch traced here: 65.5 us
  starting transfers between devices  30.4 us (46%)
  Pallas kernels  20.8 us (32%)
  blocking collectives  9.89 us (15%)
  waiting for transfers between devices  2.57 us (4%)
  local copies, waits for them, and re-layouts  0.98 us (1%)
  between operations  0.79 us (1%)
    all_to_all x1, blocking collectives, per_device(): result = exchanged(result, axis_index_groups=plane)  9.89 us
    ppermute x5, starting transfers between devices, exchange(): return lax.ppermute(piece, 'pre', [(i, i ^ turn) for i in range(groups)])  8.61 us
    all_to_all x1, starting transfers between devices, per_device(): result = merge(exchanged(parts, axis_index_groups=plane))  8.37 us
    all_to_all x1, starting transfers between devices, per_device(): arrived = exchanged(packed)  8.03 us
    pallas_call x1, Pallas kernels, produce(): pl.pallas_call(functools.partial(produce_kernel, groups, owners), in_spec...  6.79 us
    pallas_call x1, Pallas kernels, attend(): pl.pallas_call(far_kernel, in_specs=[vmem] * 8, out_specs=[vmem] * 2, out...  4.54 us
    pallas_call x1, Pallas kernels, attend(): pl.pallas_call(near_kernel, in_specs=[vmem] * 6 + [pl.BlockSpec(memory_sp...  3.5 us
    ppermute x1, starting transfers between devices, per_device(): lax.ppermute(result, 'dec', sibling)  2.87 us
  transfers between devices with their start and end apart: 10, of which 3 were waited for; matrix products, arithmetic and copies ran while one was open for 0% of the time, Pallas kernels for 19%

profile of v8, /device:TPU:1, one launch (start us, length us, event | category | flops | bytes accessed | tf_op | source)
XLA Modules:
  0.0 65.5 jit_solution(15376702413051061436)
XLA Ops:
  0.7 6.8 %produce.1 = (bf16[576,256]{1,0:T(8,128)(2,1)}, bf16[64,8,640]{2,1,0:T(8,128)(2,1)}) custom-call(s32[4]{0:T(128)} %lengths_ref, s32[4096]{0:T(1024)} %dest_hbm.1, bf16[256,7168]{1,0:T(8,128)(2,1)} %hidden_hbm.1, bf16[576,7168]{1,0:T(8,128)(2,1)} %bitcast.10, f32[1,512]{1,0:T(1,128)} %bitcast.11, f32[32,128]{1,0:T(8,128)} %constant.20.clone.freq_hbm), custom_call_target="tpu_custom_call" | custom-call | tf_op jit(solution)/shard_map/produce/pallas_call | solution.py:159
  7.5 4.7 %collective-permute-start = (bf16[576,256]{1,0:T(8,128)(2,1)}, bf16[576,256]{1,0:T(8,128)(2,1)S(1)}, u32[]{:S(2)}, u32[]{:S(2)}) collective-permute-start(bf16[576,256]{1,0:T(8,128)(2,1)} %get-tuple-element.16.own_hbm), channel_id=1, source_target_pairs={{0,96},{32,64},{64,32},{96,0},{1,97},{33,65},{65,33},{97,1},{2,98}... | collective-permute-start | bytes 884744 | tf_op jit(solution)/shard_map/ppermute | solution.py:584
  12.1 0.0 collective-permute-start.1
  12.2 8.0 %all-to-all-start.2 = ((bf16[64,8,640]{2,1,0:T(8,128)(2,1)}), bf16[64,8,640]{2,1,0:T(8,128)(2,1)S(1)}, u32[]{:S(2)}, u32[]{:S(2)}) async-start(bf16[64,8,640]{2,1,0:T(8,128)(2,1)} %get-tuple-element.27), calls=%async_computation.2 | async-start | bytes 1310720 | tf_op jit(solution)/shard_map/all_to_all | solution.py:641
  20.2 0.0 collective-permute-done.1.k2
  20.3 1.3 %collective-permute-start.2 = (bf16[576,256]{1,0:T(8,128)(2,1)S(1)}, bf16[576,256]{1,0:T(8,128)(2,1)S(1)}, u32[]{:S(2)}, u32[]{:S(2)}) collective-permute-start(bf16[576,256]{1,0:T(8,128)(2,1)S(1)} %broadcast_select_fusion), channel_id=1, source_target_pairs={{0,32},{1,97},{2,34},{3,99},{4,36},{5,101},{6,38},{7,103},{8,40},{... | collective-permute-start | bytes 884744 | tf_op jit(solution)/shard_map/ppermute | solution.py:597
  21.6 1.0 %copy-done.2 = bf16[576,256]{1,0:T(8,128)(2,1)S(1)} copy-done((bf16[576,256]{1,0:T(8,128)(2,1)S(1)}, bf16[576,256]{1,0:T(8,128)(2,1)}, u32[]{:S(2)}) %copy-start.2) | copy-done | bytes 294936
  22.5 1.0 %prepare.1 = (f32[256,768]{1,0:T(8,128)S(1)}, f32[256,256]{1,0:T(8,128)S(1)}, s32[256,128]{1,0:T(8,128)S(1)}, bf16[576,256]{1,0:T(8,128)(2,1)S(1)}) custom-call(s32[4]{0:T(128)S(1)} %copy-done.4, s32[8]{0:T(128)S(1)} %copy-done.5, s32[4,8]{1,0:T(4,128)S(1)} %copy-done.3, bf16[576,256]{1,0:T(8,128)(2,1)S(1)} %copy-done.2), custom_call_target="tpu_custom_call" | custom-call | tf_op jit(solution)/shard_map/prepare/pallas_call | solution.py:272
  23.6 3.5 %attend_near.1 = (f32[4,256,512]{2,1,0:T(8,128)S(1)}, f32[4,256,128]{2,1,0:T(8,128)S(1)}, bf16[32,512,128]{2,1,0:T(8,128)(2,1)S(1)}) custom-call(f32[256,768]{1,0:T(8,128)S(1)} %get-tuple-element.20.bias_ref, bf16[32,4,8,512]{3,2,1,0:T(8,128)(2,1)S(1)} %bitcast.6, bf16[32,4,8,64]{3,2,1,0:T(8,128)(2,1)S(1)} %bitcast.8, ...), custom_call_target="tpu_custom_call" | custom-call | tf_op jit(solution)/shard_map/attend_near/pallas_call | solution.py:425
  27.1 0.3 collective-permute-done.2.k3
  27.4 4.5 %attend_far.1 = (f32[16,40,128]{2,1,0:T(8,128)S(1)}, f32[16,40,128]{2,1,0:T(8,128)S(1)}) custom-call(f32[256,256]{1,0:T(8,128)S(1)} %get-tuple-element.18.bias_ref, s32[256,128]{1,0:T(8,128)S(1)} %get-tuple-element.19.valid_ref, bf16[32,4,8,512]{3,2,1,0:T(8,128)(2,1)S(1)} %bitcast.7, bf16[32,4,8,64]{3,2,1,0:T(8,128)(2,1)S(1)} %bitcast.9, ...), custom_call_target="tpu_custom_call" | custom-call | tf_op jit(solution)/shard_map/attend_far/pallas_call | solution.py:439
  32.0 1.3 %collective-permute-start.3 = (f32[16,40,128]{2,1,0:T(8,128)S(1)}, f32[16,40,128]{2,1,0:T(8,128)S(1)}, u32[]{:S(2)}, u32[]{:S(2)}) collective-permute-start(f32[16,40,128]{2,1,0:T(8,128)S(1)} %get-tuple-element.26), channel_id=1, source_target_pairs={{0,1},{1,0},{2,3},{3,2},{4,5},{5,4},{6,7},{7,6},{8,9},{9,8},{10,11... | collective-permute-start | bytes 983048 | tf_op jit(solution)/shard_map/ppermute | solution.py:645
  33.3 1.3 %collective-permute-done.3.other_ref = f32[16,40,128]{2,1,0:T(8,128)S(1)} collective-permute-done((f32[16,40,128]{2,1,0:T(8,128)S(1)}, f32[16,40,128]{2,1,0:T(8,128)S(1)}, u32[]{:S(2)}, u32[]{:S(2)}) %collective-permute-start.3) | collective-permute-done | bytes 327712 | tf_op jit(solution)/shard_map/ppermute | solution.py:645
  34.5 1.2 %merge_pair.1 = f32[16,40,128]{2,1,0:T(8,128)} custom-call(f32[16,40,128]{2,1,0:T(8,128)S(1)} %get-tuple-element.25.mine_ref, f32[16,40,128]{2,1,0:T(8,128)S(1)} %collective-permute-done.3.other_ref), custom_call_target="tpu_custom_call" | custom-call | tf_op jit(solution)/shard_map/merge_pair/pallas_call | solution.py:487
  35.8 8.4 %all-to-all-start = ((f32[16,40,128]{2,1,0:T(8,128)}), f32[16,40,128]{2,1,0:T(8,128)S(1)}, u32[]{:S(2)}, u32[]{:S(2)}) async-start(f32[16,40,128]{2,1,0:T(8,128)} %merge_pair.1), calls=%async_computation | async-start | bytes 655360 | tf_op jit(solution)/shard_map/all_to_all | solution.py:646
  44.1 1.5 %place.1.p0 = bf16[576,256]{1,0:T(8,128)(2,1)S(1)} custom-call(bf16[64,8,640]{2,1,0:T(8,128)(2,1)S(1)} %all-to-all-done.2.arrived_ref), custom_call_target="tpu_custom_call" | custom-call | tf_op jit(solution)/shard_map/place/pallas_call | solution.py:221
  45.6 1.3 %collective-permute-start.5 = (bf16[576,256]{1,0:T(8,128)(2,1)S(1)}, bf16[576,256]{1,0:T(8,128)(2,1)S(1)}, u32[]{:S(2)}, u32[]{:S(2)}) collective-permute-start(bf16[576,256]{1,0:T(8,128)(2,1)S(1)} %place.1.p0), channel_id=1, source_target_pairs={{0,96},{32,64},{64,32},{96,0},{1,97},{33,65},{65,33},{97,1},{2,98}... | collective-permute-start | bytes 884744 | tf_op jit(solution)/shard_map/ppermute | solution.py:584
  46.9 0.0 collective-permute-start.6
  46.9 2.7 %collective-permute-start.7 = (bf16[576,256]{1,0:T(8,128)(2,1)S(1)}, bf16[576,256]{1,0:T(8,128)(2,1)S(1)}, u32[]{:S(2)}, u32[]{:S(2)}) collective-permute-start(bf16[576,256]{1,0:T(8,128)(2,1)S(1)} %place.1.p0), channel_id=1, source_target_pairs={{0,64},{32,96},{64,0},{96,32},{1,65},{33,97},{65,1},{97,33},{2,66}... | collective-permute-start | bytes 884744 | tf_op jit(solution)/shard_map/ppermute | solution.py:584
  49.5 0.4 merge.1
  50.0 9.9 %all_to_all.15.mine_ref = bf16[16,32,128]{2,1,0:T(8,128)(2,1)S(1)} all-to-all(bf16[16,32,128]{2,1,0:T(8,128)(2,1)S(1)} %merge.1), channel_id=1, replica_groups={{30,28,26,24,22,20,18,16,14,12,10,8,6,4,2,0},{31,29,27,25,23,21,19,17,1..., dimensions={0} | all-to-all | bytes 262144 | tf_op jit(solution)/shard_map/all_to_all | solution.py:647
  59.9 2.9 %collective-permute-start.4 = (bf16[16,32,128]{2,1,0:T(8,128)(2,1)S(1)}, bf16[16,32,128]{2,1,0:T(8,128)(2,1)S(1)}, u32[]{:S(2)}, u32[]{:S(2)}) collective-permute-start(bf16[16,32,128]{2,1,0:T(8,128)(2,1)S(1)} %all_to_all.15.mine_ref), channel_id=1, source_target_pairs={{0,1},{1,0},{2,3},{3,2},{4,5},{5,4},{6,7},{7,6},{8,9},{9,8},{10,11... | collective-permute-start | bytes 393224 | tf_op jit(solution)/shard_map/ppermute | solution.py:648
  62.8 1.0 %collective-permute-done.4.other_ref = bf16[16,32,128]{2,1,0:T(8,128)(2,1)S(1)} collective-permute-done((bf16[16,32,128]{2,1,0:T(8,128)(2,1)S(1)}, bf16[16,32,128]{2,1,0:T(8,128)(2,1)S(1)}, u32[]{:S(2)}, u32[]{:S(2)}) %collective-permute-start.4) | collective-permute-done | bytes 131104 | tf_op jit(solution)/shard_map/ppermute | solution.py:648
  63.7 1.7 %finish.1 = (bf16[32,4096]{1,0:T(8,128)(2,1)}, bf16[576,1024]{1,0:T(8,128)(2,1)}) custom-call(bf16[16,32,128]{2,1,0:T(8,128)(2,1)S(1)} %all_to_all.15.mine_ref, bf16[16,32,128]{2,1,0:T(8,128)(2,1)S(1)} %collective-permute-done.4.other_ref, bf16[576,256]{1,0:T(8,128)(2,1)S(1)} %place.1.p0, bf16[576,256]{1,0:T(8,128)(2,1)S(1)} %collective-permute-done.5.p1, ...), custom_call_target="tpu_custom_call" | custom-call | tf_op jit(solution)/shard_map/finish/pallas_call | solution.py:566
  (18 shorter events, 0.1 us)
Async XLA Ops:
  0.6 20.9 %copy-start.3 = (s32[4,8]{1,0:T(4,128)S(1)}, s32[4,8]{1,0:T(4,128)}, u32[]{:S(2)}) copy-start(s32[4,8]{1,0:T(4,128)} %position_ref.1) | copy-start | bytes 388
  0.6 20.9 %copy-start.4 = (s32[4]{0:T(128)S(1)}, s32[4]{0:T(128)}, u32[]{:S(2)}) copy-start(s32[4]{0:T(128)} %lengths_ref) | copy-start | bytes 52
  0.7 20.9 %copy-start.5 = (s32[8]{0:T(128)S(1)}, s32[8]{0:T(128)}, u32[]{:S(2)}) copy-start(s32[8]{0:T(128)} %request_ref.1) | copy-start | bytes 100
  0.7 22.9 %copy-start = (bf16[4,8,32,512]{3,2,1,0:T(8,128)(2,1)S(1)}, bf16[4,8,32,512]{3,2,1,0:T(8,128)(2,1)}, u32[]{:S(2)}) copy-start(bf16[4,8,32,512]{3,2,1,0:T(8,128)(2,1)} %param.14) | copy-start | bytes 3145732
  0.7 22.9 %copy-start.1 = (bf16[4,8,32,64]{3,2,1,0:T(8,128)(2,1)S(1)}, bf16[4,8,32,64]{3,2,1,0:T(8,128)(2,1)}, u32[]{:S(2)}) copy-start(bf16[4,8,32,64]{3,2,1,0:T(8,128)(2,1)} %param.15) | copy-start | bytes 393220
  7.5 12.7 %collective-permute-start = (bf16[576,256]{1,0:T(8,128)(2,1)}, bf16[576,256]{1,0:T(8,128)(2,1)S(1)}, u32[]{:S(2)}, u32[]{:S(2)}) collective-permute-start(bf16[576,256]{1,0:T(8,128)(2,1)} %get-tuple-element.16.own_hbm), channel_id=1, source_target_pairs={{0,96},{32,64},{64,32},{96,0},{1,97},{33,65},{65,33},{97,1},{2,98}... | collective-permute-start | bytes 884744 | tf_op jit(solution)/shard_map/ppermute | solution.py:584
  12.1 8.1 %collective-permute-start.1 = (bf16[576,256]{1,0:T(8,128)(2,1)}, bf16[576,256]{1,0:T(8,128)(2,1)S(1)}, u32[]{:S(2)}, u32[]{:S(2)}) collective-permute-start(bf16[576,256]{1,0:T(8,128)(2,1)} %get-tuple-element.16.own_hbm), channel_id=1, source_target_pairs={{0,32},{32,0},{64,96},{96,64},{1,33},{33,1},{65,97},{97,65},{2,34}... | collective-permute-start | bytes 884744 | tf_op jit(solution)/shard_map/ppermute | solution.py:584
  12.2 23.6 %all-to-all-start.2 = ((bf16[64,8,640]{2,1,0:T(8,128)(2,1)}), bf16[64,8,640]{2,1,0:T(8,128)(2,1)S(1)}, u32[]{:S(2)}, u32[]{:S(2)}) async-start(bf16[64,8,640]{2,1,0:T(8,128)(2,1)} %get-tuple-element.27), calls=%async_computation.2 | async-start | bytes 1310720 | tf_op jit(solution)/shard_map/all_to_all | solution.py:641
  20.3 7.2 %collective-permute-start.2 = (bf16[576,256]{1,0:T(8,128)(2,1)S(1)}, bf16[576,256]{1,0:T(8,128)(2,1)S(1)}, u32[]{:S(2)}, u32[]{:S(2)}) collective-permute-start(bf16[576,256]{1,0:T(8,128)(2,1)S(1)} %broadcast_select_fusion), channel_id=1, source_target_pairs={{0,32},{1,97},{2,34},{3,99},{4,36},{5,101},{6,38},{7,103},{8,40},{... | collective-permute-start | bytes 884744 | tf_op jit(solution)/shard_map/ppermute | solution.py:597
  21.6 1.0 %copy-start.2 = (bf16[576,256]{1,0:T(8,128)(2,1)S(1)}, bf16[576,256]{1,0:T(8,128)(2,1)}, u32[]{:S(2)}) copy-start(bf16[576,256]{1,0:T(8,128)(2,1)} %get-tuple-element.16.own_hbm) | copy-start | bytes 884740
  32.0 2.5 %collective-permute-start.3 = (f32[16,40,128]{2,1,0:T(8,128)S(1)}, f32[16,40,128]{2,1,0:T(8,128)S(1)}, u32[]{:S(2)}, u32[]{:S(2)}) collective-permute-start(f32[16,40,128]{2,1,0:T(8,128)S(1)} %get-tuple-element.26), channel_id=1, source_target_pairs={{0,1},{1,0},{2,3},{3,2},{4,5},{5,4},{6,7},{7,6},{8,9},{9,8},{10,11... | collective-permute-start | bytes 983048 | tf_op jit(solution)/shard_map/ppermute | solution.py:645
  35.8 13.8 %all-to-all-start = ((f32[16,40,128]{2,1,0:T(8,128)}), f32[16,40,128]{2,1,0:T(8,128)S(1)}, u32[]{:S(2)}, u32[]{:S(2)}) async-start(f32[16,40,128]{2,1,0:T(8,128)} %merge_pair.1), calls=%async_computation | async-start | bytes 655360 | tf_op jit(solution)/shard_map/all_to_all | solution.py:646
  45.6 17.1 %collective-permute-start.5 = (bf16[576,256]{1,0:T(8,128)(2,1)S(1)}, bf16[576,256]{1,0:T(8,128)(2,1)S(1)}, u32[]{:S(2)}, u32[]{:S(2)}) collective-permute-start(bf16[576,256]{1,0:T(8,128)(2,1)S(1)} %place.1.p0), channel_id=1, source_target_pairs={{0,96},{32,64},{64,32},{96,0},{1,97},{33,65},{65,33},{97,1},{2,98}... | collective-permute-start | bytes 884744 | tf_op jit(solution)/shard_map/ppermute | solution.py:584
  46.9 15.9 %collective-permute-start.6 = (bf16[576,256]{1,0:T(8,128)(2,1)S(1)}, bf16[576,256]{1,0:T(8,128)(2,1)S(1)}, u32[]{:S(2)}, u32[]{:S(2)}) collective-permute-start(bf16[576,256]{1,0:T(8,128)(2,1)S(1)} %place.1.p0), channel_id=1, source_target_pairs={{0,32},{32,0},{64,96},{96,64},{1,33},{33,1},{65,97},{97,65},{2,34}... | collective-permute-start | bytes 884744 | tf_op jit(solution)/shard_map/ppermute | solution.py:584
  46.9 15.9 %collective-permute-start.7 = (bf16[576,256]{1,0:T(8,128)(2,1)S(1)}, bf16[576,256]{1,0:T(8,128)(2,1)S(1)}, u32[]{:S(2)}, u32[]{:S(2)}) collective-permute-start(bf16[576,256]{1,0:T(8,128)(2,1)S(1)} %place.1.p0), channel_id=1, source_target_pairs={{0,64},{32,96},{64,0},{96,32},{1,65},{33,97},{65,1},{97,33},{2,66}... | collective-permute-start | bytes 884744 | tf_op jit(solution)/shard_map/ppermute | solution.py:584
  59.9 3.9 %collective-permute-start.4 = (bf16[16,32,128]{2,1,0:T(8,128)(2,1)S(1)}, bf16[16,32,128]{2,1,0:T(8,128)(2,1)S(1)}, u32[]{:S(2)}, u32[]{:S(2)}) collective-permute-start(bf16[16,32,128]{2,1,0:T(8,128)(2,1)S(1)} %all_to_all.15.mine_ref), channel_id=1, source_target_pairs={{0,1},{1,0},{2,3},{3,2},{4,5},{5,4},{6,7},{7,6},{8,9},{9,8},{10,11... | collective-permute-start | bytes 393224 | tf_op jit(solution)/shard_map/ppermute | solution.py:648

commit v9 on v8

--- a/solution.py
+++ b/solution.py
@@ -94,7 +94,7 @@
         owner = lax.shift_right_logical(dest_ref[device * blocks + b], shift_of(groups * owners))
         rank = count_ref[owner]
         count_ref[owner] = rank + 1
-        slot_ref[b] = owner * MOST + rank
+        slot_ref[b] = (owners - 1 - owner) * MOST + rank
         return carry
 
     lax.fori_loop(0, owners, clear, 0)
@@ -194,22 +194,20 @@
 def place_kernel(arrived_ref, out_ref, rows_ref):
     blocks, block_rows, _ = arrived_ref.shape
     width, rows = out_ref.shape
-    part = 128 // block_rows
-    row = lax.broadcasted_iota(jnp.int32, (rows, 128), 0).astype(jnp.float32)
-    lane = lax.broadcasted_iota(jnp.int32, (1, 128), 1)
+    depth = 256
+    part = depth // block_rows
+    row = lax.broadcasted_iota(jnp.int32, (rows, depth), 0).astype(jnp.float32)
+    lane = lax.broadcasted_iota(jnp.int32, (1, depth), 1)
     within = lax.rem(lane, block_rows).astype(jnp.float32)
-    rows_ref[...] = jnp.zeros_like(rows_ref)
-
-    def body(k, carry):
-        source = arrived_ref[pl.ds(k * part, part)].astype(jnp.float32).reshape(128, WIDE)
+    for k in range(blocks // part):
+        source = arrived_ref[k * part : (k + 1) * part].astype(jnp.float32).reshape(depth, WIDE)
         slot = jnp.transpose(source[:, WIDE - 128 :])[127:128, :]
         select = jnp.where(row == slot * block_rows + within, 1.0, 0.0).astype(jnp.bfloat16)
-        rows_ref[...] += jnp.dot(
-            select, source.astype(jnp.bfloat16), preferred_element_type=jnp.float32
-        )
-        return carry
-
-    lax.fori_loop(0, blocks // part, body, 0)
+        placed = jnp.dot(select, source.astype(jnp.bfloat16), preferred_element_type=jnp.float32)
+        if k == 0:
+            rows_ref[...] = placed
+        else:
+            rows_ref[...] += placed
     for at in range(0, width, 128):
         count = min(128, width - at)
         turned = jnp.transpose(rows_ref[:, at : at + 128])
@@ -638,7 +636,7 @@
         chunks,
         w_up_value,
     )
-    arrived = exchanged(packed)
+    arrived = exchanged(packed, axis_index_groups=[list(reversed(range(owners)))])
     quarter = place(arrived, *produced.shape)
     pieces = [quarter] + [exchange(quarter, groups, turn) for turn in TURNS[1:]]
 

time: 65.8 us -> 65.4 us (level)
  waiting for transfers between devices: 2.57 us -> 4.31 us
  starting transfers between devices: 30.4 us -> 29 us
  Pallas kernels: 20.8 us -> 19.8 us
    all_to_all x1, starting transfers between devices: 8.03 us -> 9.08 us  [per_device(): exchanged(packed, axis_index_groups=[list(reversed(range(owners)))])]
    ppermute x1, waiting for transfers between devices: 0.32 us -> 1.33 us  [around(): far = lax.ppermute(chosen, ('pre', 'dec'), forward)]
    ppermute x1, starting transfers between devices: 1.3 us -> 0.31 us  [around(): far = lax.ppermute(chosen, ('pre', 'dec'), forward)]
    pallas_call x1, Pallas kernels: 1.48 us -> 0.55 us  [place(): pl.pallas_call(place_kernel, in_specs=[vmem], out_specs=vmem, out_shape=j...]
    all_to_all x1, starting transfers between devices: 8.37 us -> 7.6 us  [per_device(): result = merge(exchanged(parts, axis_index_groups=plane))]
    all_to_all x1, waiting for transfers between devices: 0.01 us -> 0.74 us  [per_device(): result = merge(exchanged(parts, axis_index_groups=plane))]
  transfers between devices with their start and end apart: 10 -> 10, of which waited for: 3 -> 4; matrix products, arithmetic and copies ran while one was open for 0% -> 0% of each run, Pallas kernels for 19% -> 17%
where the time goes in v9:
time: 65.4 us; the launch traced here: 65 us
  starting transfers between devices  29 us (44%)
  Pallas kernels  19.8 us (30%)
  blocking collectives  10.1 us (15%)
  waiting for transfers between devices  4.31 us (7%)
  local copies, waits for them, and re-layouts  0.98 us (1%)
  between operations  0.79 us (1%)
    all_to_all x1, blocking collectives, per_device(): result = exchanged(result, axis_index_groups=plane)  10.1 us
    all_to_all x1, starting transfers between devices, per_device(): exchanged(packed, axis_index_groups=[list(reversed(range(owners)))])  9.08 us
    ppermute x5, starting transfers between devices, exchange(): return lax.ppermute(piece, 'pre', [(i, i ^ turn) for i in range(groups)])  8.61 us
    all_to_all x1, starting transfers between devices, per_device(): result = merge(exchanged(parts, axis_index_groups=plane))  7.6 us
    pallas_call x1, Pallas kernels, produce(): pl.pallas_call(functools.partial(produce_kernel, groups, owners), in_spec...  6.79 us
    pallas_call x1, Pallas kernels, attend(): pl.pallas_call(far_kernel, in_specs=[vmem] * 8, out_specs=[vmem] * 2, out...  4.56 us
    pallas_call x1, Pallas kernels, attend(): pl.pallas_call(near_kernel, in_specs=[vmem] * 6 + [pl.BlockSpec(memory_sp...  3.48 us
    ppermute x1, starting transfers between devices, per_device(): lax.ppermute(result, 'dec', sibling)  2.44 us
  transfers between devices with their start and end apart: 10, of which 4 were waited for; matrix products, arithmetic and copies ran while one was open for 0% of the time, Pallas kernels for 17%

profile of v9, /device:TPU:1, one launch (start us, length us, event | category | flops | bytes accessed | tf_op | source)
XLA Modules:
  0.0 65.0 jit_solution(15978642852631866953)
XLA Ops:
  0.7 6.8 %produce.1 = (bf16[576,256]{1,0:T(8,128)(2,1)}, bf16[64,8,640]{2,1,0:T(8,128)(2,1)}) custom-call(s32[4]{0:T(128)} %lengths_ref, s32[4096]{0:T(1024)} %dest_hbm.1, bf16[256,7168]{1,0:T(8,128)(2,1)} %hidden_hbm.1, bf16[576,7168]{1,0:T(8,128)(2,1)} %bitcast.10, f32[1,512]{1,0:T(1,128)} %bitcast.11, f32[32,128]{1,0:T(8,128)} %constant.20.clone.freq_hbm), custom_call_target="tpu_custom_call" | custom-call | tf_op jit(solution)/shard_map/produce/pallas_call | solution.py:159
  7.5 4.7 %collective-permute-start = (bf16[576,256]{1,0:T(8,128)(2,1)}, bf16[576,256]{1,0:T(8,128)(2,1)S(1)}, u32[]{:S(2)}, u32[]{:S(2)}) collective-permute-start(bf16[576,256]{1,0:T(8,128)(2,1)} %get-tuple-element.16.own_hbm), channel_id=1, source_target_pairs={{0,96},{32,64},{64,32},{96,0},{1,97},{33,65},{65,33},{97,1},{2,98}... | collective-permute-start | bytes 884744 | tf_op jit(solution)/shard_map/ppermute | solution.py:582
  12.1 0.0 collective-permute-start.1
  12.2 9.1 %all-to-all-start.2 = ((bf16[64,8,640]{2,1,0:T(8,128)(2,1)}), bf16[64,8,640]{2,1,0:T(8,128)(2,1)S(1)}, u32[]{:S(2)}, u32[]{:S(2)}) async-start(bf16[64,8,640]{2,1,0:T(8,128)(2,1)} %get-tuple-element.27), calls=%async_computation.2 | async-start | bytes 1310720 | tf_op jit(solution)/shard_map/all_to_all | solution.py:639
  21.3 0.0 collective-permute-done.1.k2
  21.3 0.3 collective-permute-start.2
  21.6 1.0 %copy-done.2 = bf16[576,256]{1,0:T(8,128)(2,1)S(1)} copy-done((bf16[576,256]{1,0:T(8,128)(2,1)S(1)}, bf16[576,256]{1,0:T(8,128)(2,1)}, u32[]{:S(2)}) %copy-start.2) | copy-done | bytes 294936
  22.6 1.0 %prepare.1 = (f32[256,768]{1,0:T(8,128)S(1)}, f32[256,256]{1,0:T(8,128)S(1)}, s32[256,128]{1,0:T(8,128)S(1)}, bf16[576,256]{1,0:T(8,128)(2,1)S(1)}) custom-call(s32[4]{0:T(128)S(1)} %copy-done.4, s32[8]{0:T(128)S(1)} %copy-done.5, s32[4,8]{1,0:T(4,128)S(1)} %copy-done.3, bf16[576,256]{1,0:T(8,128)(2,1)S(1)} %copy-done.2), custom_call_target="tpu_custom_call" | custom-call | tf_op jit(solution)/shard_map/prepare/pallas_call | solution.py:270
  23.7 3.5 %attend_near.1 = (f32[4,256,512]{2,1,0:T(8,128)S(1)}, f32[4,256,128]{2,1,0:T(8,128)S(1)}, bf16[32,512,128]{2,1,0:T(8,128)(2,1)S(1)}) custom-call(f32[256,768]{1,0:T(8,128)S(1)} %get-tuple-element.20.bias_ref, bf16[32,4,8,512]{3,2,1,0:T(8,128)(2,1)S(1)} %bitcast.6, bf16[32,4,8,64]{3,2,1,0:T(8,128)(2,1)S(1)} %bitcast.8, ...), custom_call_target="tpu_custom_call" | custom-call | tf_op jit(solution)/shard_map/attend_near/pallas_call | solution.py:423
  27.1 1.3 %collective-permute-done.2.k3 = bf16[576,256]{1,0:T(8,128)(2,1)S(1)} collective-permute-done((bf16[576,256]{1,0:T(8,128)(2,1)S(1)}, bf16[576,256]{1,0:T(8,128)(2,1)S(1)}, u32[]{:S(2)}, u32[]{:S(2)}) %collective-permute-start.2) | collective-permute-done | bytes 294944 | tf_op jit(solution)/shard_map/ppermute | solution.py:595
  28.5 4.6 %attend_far.1 = (f32[16,40,128]{2,1,0:T(8,128)S(1)}, f32[16,40,128]{2,1,0:T(8,128)S(1)}) custom-call(f32[256,256]{1,0:T(8,128)S(1)} %get-tuple-element.18.bias_ref, s32[256,128]{1,0:T(8,128)S(1)} %get-tuple-element.19.valid_ref, bf16[32,4,8,512]{3,2,1,0:T(8,128)(2,1)S(1)} %bitcast.7, bf16[32,4,8,64]{3,2,1,0:T(8,128)(2,1)S(1)} %bitcast.9, ...), custom_call_target="tpu_custom_call" | custom-call | tf_op jit(solution)/shard_map/attend_far/pallas_call | solution.py:437
  33.0 1.0 %collective-permute-start.3 = (f32[16,40,128]{2,1,0:T(8,128)S(1)}, f32[16,40,128]{2,1,0:T(8,128)S(1)}, u32[]{:S(2)}, u32[]{:S(2)}) collective-permute-start(f32[16,40,128]{2,1,0:T(8,128)S(1)} %get-tuple-element.26), channel_id=1, source_target_pairs={{0,1},{1,0},{2,3},{3,2},{4,5},{5,4},{6,7},{7,6},{8,9},{9,8},{10,11... | collective-permute-start | bytes 983048 | tf_op jit(solution)/shard_map/ppermute | solution.py:643
  34.0 1.3 %collective-permute-done.3.other_ref = f32[16,40,128]{2,1,0:T(8,128)S(1)} collective-permute-done((f32[16,40,128]{2,1,0:T(8,128)S(1)}, f32[16,40,128]{2,1,0:T(8,128)S(1)}, u32[]{:S(2)}, u32[]{:S(2)}) %collective-permute-start.3) | collective-permute-done | bytes 327712 | tf_op jit(solution)/shard_map/ppermute | solution.py:643
  35.3 1.2 %merge_pair.1 = f32[16,40,128]{2,1,0:T(8,128)} custom-call(f32[16,40,128]{2,1,0:T(8,128)S(1)} %get-tuple-element.25.mine_ref, f32[16,40,128]{2,1,0:T(8,128)S(1)} %collective-permute-done.3.other_ref), custom_call_target="tpu_custom_call" | custom-call | tf_op jit(solution)/shard_map/merge_pair/pallas_call | solution.py:485
  36.5 7.6 %all-to-all-start = ((f32[16,40,128]{2,1,0:T(8,128)}), f32[16,40,128]{2,1,0:T(8,128)S(1)}, u32[]{:S(2)}, u32[]{:S(2)}) async-start(f32[16,40,128]{2,1,0:T(8,128)} %merge_pair.1), calls=%async_computation | async-start | bytes 655360 | tf_op jit(solution)/shard_map/all_to_all | solution.py:644
  44.1 0.5 place.1.p0
  44.7 1.3 %collective-permute-start.5 = (bf16[576,256]{1,0:T(8,128)(2,1)S(1)}, bf16[576,256]{1,0:T(8,128)(2,1)S(1)}, u32[]{:S(2)}, u32[]{:S(2)}) collective-permute-start(bf16[576,256]{1,0:T(8,128)(2,1)S(1)} %place.1.p0), channel_id=1, source_target_pairs={{0,96},{32,64},{64,32},{96,0},{1,97},{33,65},{65,33},{97,1},{2,98}... | collective-permute-start | bytes 884744 | tf_op jit(solution)/shard_map/ppermute | solution.py:582
  46.0 2.7 %collective-permute-start.7 = (bf16[576,256]{1,0:T(8,128)(2,1)S(1)}, bf16[576,256]{1,0:T(8,128)(2,1)S(1)}, u32[]{:S(2)}, u32[]{:S(2)}) collective-permute-start(bf16[576,256]{1,0:T(8,128)(2,1)S(1)} %place.1.p0), channel_id=1, source_target_pairs={{0,64},{32,96},{64,0},{96,32},{1,65},{33,97},{65,1},{97,33},{2,66}... | collective-permute-start | bytes 884744 | tf_op jit(solution)/shard_map/ppermute | solution.py:582
  48.6 0.7 %all-to-all-done.parts_ref = f32[16,40,128]{2,1,0:T(8,128)S(1)} async-done(((f32[16,40,128]{2,1,0:T(8,128)}), f32[16,40,128]{2,1,0:T(8,128)S(1)}, u32[]{:S(2)}, u32[]{:S(2)}) %all-to-all-start) | async-done | bytes 327712 | tf_op jit(solution)/shard_map/all_to_all | solution.py:644
  49.4 0.4 merge.1
  49.8 10.1 %all_to_all.15.mine_ref = bf16[16,32,128]{2,1,0:T(8,128)(2,1)S(1)} all-to-all(bf16[16,32,128]{2,1,0:T(8,128)(2,1)S(1)} %merge.1), channel_id=1, replica_groups={{30,28,26,24,22,20,18,16,14,12,10,8,6,4,2,0},{31,29,27,25,23,21,19,17,1..., dimensions={0} | all-to-all | bytes 262144 | tf_op jit(solution)/shard_map/all_to_all | solution.py:645
  59.9 2.4 %collective-permute-start.4 = (bf16[16,32,128]{2,1,0:T(8,128)(2,1)S(1)}, bf16[16,32,128]{2,1,0:T(8,128)(2,1)S(1)}, u32[]{:S(2)}, u32[]{:S(2)}) collective-permute-start(bf16[16,32,128]{2,1,0:T(8,128)(2,1)S(1)} %all_to_all.15.mine_ref), channel_id=1, source_target_pairs={{0,1},{1,0},{2,3},{3,2},{4,5},{5,4},{6,7},{7,6},{8,9},{9,8},{10,11... | collective-permute-start | bytes 393224 | tf_op jit(solution)/shard_map/ppermute | solution.py:646
  62.3 1.0 %collective-permute-done.4.other_ref = bf16[16,32,128]{2,1,0:T(8,128)(2,1)S(1)} collective-permute-done((bf16[16,32,128]{2,1,0:T(8,128)(2,1)S(1)}, bf16[16,32,128]{2,1,0:T(8,128)(2,1)S(1)}, u32[]{:S(2)}, u32[]{:S(2)}) %collective-permute-start.4) | collective-permute-done | bytes 131104 | tf_op jit(solution)/shard_map/ppermute | solution.py:646
  63.3 1.7 %finish.1 = (bf16[32,4096]{1,0:T(8,128)(2,1)}, bf16[576,1024]{1,0:T(8,128)(2,1)}) custom-call(bf16[16,32,128]{2,1,0:T(8,128)(2,1)S(1)} %all_to_all.15.mine_ref, bf16[16,32,128]{2,1,0:T(8,128)(2,1)S(1)} %collective-permute-done.4.other_ref, bf16[576,256]{1,0:T(8,128)(2,1)S(1)} %place.1.p0, bf16[576,256]{1,0:T(8,128)(2,1)S(1)} %collective-permute-done.5.p1, ...), custom_call_target="tpu_custom_call" | custom-call | tf_op jit(solution)/shard_map/finish/pallas_call | solution.py:564
  (18 shorter events, 0.1 us)
Async XLA Ops:
  0.6 21.0 %copy-start.3 = (s32[4,8]{1,0:T(4,128)S(1)}, s32[4,8]{1,0:T(4,128)}, u32[]{:S(2)}) copy-start(s32[4,8]{1,0:T(4,128)} %position_ref.1) | copy-start | bytes 388
  0.6 21.0 %copy-start.4 = (s32[4]{0:T(128)S(1)}, s32[4]{0:T(128)}, u32[]{:S(2)}) copy-start(s32[4]{0:T(128)} %lengths_ref) | copy-start | bytes 52
  0.7 21.0 %copy-start.5 = (s32[8]{0:T(128)S(1)}, s32[8]{0:T(128)}, u32[]{:S(2)}) copy-start(s32[8]{0:T(128)} %request_ref.1) | copy-start | bytes 100
  0.7 23.0 %copy-start = (bf16[4,8,32,512]{3,2,1,0:T(8,128)(2,1)S(1)}, bf16[4,8,32,512]{3,2,1,0:T(8,128)(2,1)}, u32[]{:S(2)}) copy-start(bf16[4,8,32,512]{3,2,1,0:T(8,128)(2,1)} %param.14) | copy-start | bytes 3145732
  0.7 23.0 %copy-start.1 = (bf16[4,8,32,64]{3,2,1,0:T(8,128)(2,1)S(1)}, bf16[4,8,32,64]{3,2,1,0:T(8,128)(2,1)}, u32[]{:S(2)}) copy-start(bf16[4,8,32,64]{3,2,1,0:T(8,128)(2,1)} %param.15) | copy-start | bytes 393220
  7.5 13.8 %collective-permute-start = (bf16[576,256]{1,0:T(8,128)(2,1)}, bf16[576,256]{1,0:T(8,128)(2,1)S(1)}, u32[]{:S(2)}, u32[]{:S(2)}) collective-permute-start(bf16[576,256]{1,0:T(8,128)(2,1)} %get-tuple-element.16.own_hbm), channel_id=1, source_target_pairs={{0,96},{32,64},{64,32},{96,0},{1,97},{33,65},{65,33},{97,1},{2,98}... | collective-permute-start | bytes 884744 | tf_op jit(solution)/shard_map/ppermute | solution.py:582
  12.1 9.1 %collective-permute-start.1 = (bf16[576,256]{1,0:T(8,128)(2,1)}, bf16[576,256]{1,0:T(8,128)(2,1)S(1)}, u32[]{:S(2)}, u32[]{:S(2)}) collective-permute-start(bf16[576,256]{1,0:T(8,128)(2,1)} %get-tuple-element.16.own_hbm), channel_id=1, source_target_pairs={{0,32},{32,0},{64,96},{96,64},{1,33},{33,1},{65,97},{97,65},{2,34}... | collective-permute-start | bytes 884744 | tf_op jit(solution)/shard_map/ppermute | solution.py:582
  12.2 24.4 %all-to-all-start.2 = ((bf16[64,8,640]{2,1,0:T(8,128)(2,1)}), bf16[64,8,640]{2,1,0:T(8,128)(2,1)S(1)}, u32[]{:S(2)}, u32[]{:S(2)}) async-start(bf16[64,8,640]{2,1,0:T(8,128)(2,1)} %get-tuple-element.27), calls=%async_computation.2 | async-start | bytes 1310720 | tf_op jit(solution)/shard_map/all_to_all | solution.py:639
  21.3 7.2 %collective-permute-start.2 = (bf16[576,256]{1,0:T(8,128)(2,1)S(1)}, bf16[576,256]{1,0:T(8,128)(2,1)S(1)}, u32[]{:S(2)}, u32[]{:S(2)}) collective-permute-start(bf16[576,256]{1,0:T(8,128)(2,1)S(1)} %broadcast_select_fusion), channel_id=1, source_target_pairs={{0,32},{1,97},{2,34},{3,99},{4,36},{5,101},{6,38},{7,103},{8,40},{... | collective-permute-start | bytes 884744 | tf_op jit(solution)/shard_map/ppermute | solution.py:595
  21.6 1.0 %copy-start.2 = (bf16[576,256]{1,0:T(8,128)(2,1)S(1)}, bf16[576,256]{1,0:T(8,128)(2,1)}, u32[]{:S(2)}) copy-start(bf16[576,256]{1,0:T(8,128)(2,1)} %get-tuple-element.16.own_hbm) | copy-start | bytes 884740
  33.0 2.2 %collective-permute-start.3 = (f32[16,40,128]{2,1,0:T(8,128)S(1)}, f32[16,40,128]{2,1,0:T(8,128)S(1)}, u32[]{:S(2)}, u32[]{:S(2)}) collective-permute-start(f32[16,40,128]{2,1,0:T(8,128)S(1)} %get-tuple-element.26), channel_id=1, source_target_pairs={{0,1},{1,0},{2,3},{3,2},{4,5},{5,4},{6,7},{7,6},{8,9},{9,8},{10,11... | collective-permute-start | bytes 983048 | tf_op jit(solution)/shard_map/ppermute | solution.py:643
  36.5 12.8 %all-to-all-start = ((f32[16,40,128]{2,1,0:T(8,128)}), f32[16,40,128]{2,1,0:T(8,128)S(1)}, u32[]{:S(2)}, u32[]{:S(2)}) async-start(f32[16,40,128]{2,1,0:T(8,128)} %merge_pair.1), calls=%async_computation | async-start | bytes 655360 | tf_op jit(solution)/shard_map/all_to_all | solution.py:644
  44.7 17.6 %collective-permute-start.5 = (bf16[576,256]{1,0:T(8,128)(2,1)S(1)}, bf16[576,256]{1,0:T(8,128)(2,1)S(1)}, u32[]{:S(2)}, u32[]{:S(2)}) collective-permute-start(bf16[576,256]{1,0:T(8,128)(2,1)S(1)} %place.1.p0), channel_id=1, source_target_pairs={{0,96},{32,64},{64,32},{96,0},{1,97},{33,65},{65,33},{97,1},{2,98}... | collective-permute-start | bytes 884744 | tf_op jit(solution)/shard_map/ppermute | solution.py:582
  46.0 16.4 %collective-permute-start.6 = (bf16[576,256]{1,0:T(8,128)(2,1)S(1)}, bf16[576,256]{1,0:T(8,128)(2,1)S(1)}, u32[]{:S(2)}, u32[]{:S(2)}) collective-permute-start(bf16[576,256]{1,0:T(8,128)(2,1)S(1)} %place.1.p0), channel_id=1, source_target_pairs={{0,32},{32,0},{64,96},{96,64},{1,33},{33,1},{65,97},{97,65},{2,34}... | collective-permute-start | bytes 884744 | tf_op jit(solution)/shard_map/ppermute | solution.py:582
  46.0 16.4 %collective-permute-start.7 = (bf16[576,256]{1,0:T(8,128)(2,1)S(1)}, bf16[576,256]{1,0:T(8,128)(2,1)S(1)}, u32[]{:S(2)}, u32[]{:S(2)}) collective-permute-start(bf16[576,256]{1,0:T(8,128)(2,1)S(1)} %place.1.p0), channel_id=1, source_target_pairs={{0,64},{32,96},{64,0},{96,32},{1,65},{33,97},{65,1},{97,33},{2,66}... | collective-permute-start | bytes 884744 | tf_op jit(solution)/shard_map/ppermute | solution.py:582
  59.9 3.4 %collective-permute-start.4 = (bf16[16,32,128]{2,1,0:T(8,128)(2,1)S(1)}, bf16[16,32,128]{2,1,0:T(8,128)(2,1)S(1)}, u32[]{:S(2)}, u32[]{:S(2)}) collective-permute-start(bf16[16,32,128]{2,1,0:T(8,128)(2,1)S(1)} %all_to_all.15.mine_ref), channel_id=1, source_target_pairs={{0,1},{1,0},{2,3},{3,2},{4,5},{5,4},{6,7},{7,6},{8,9},{9,8},{10,11... | collective-permute-start | bytes 393224 | tf_op jit(solution)/shard_map/ppermute | solution.py:646

commit v10 on v9

--- a/solution.py
+++ b/solution.py
@@ -44,21 +44,16 @@
 
 
 def produce_kernel(
-    groups, owners, lengths_hbm, dest_hbm, hidden_hbm, w_hbm, gain_hbm, freq_hbm,
-    out_ref, packed_ref, hidden_ref, w_ref, acc_ref, lengths_ref, dest_ref, gain_ref, freq_ref,
-    turn_ref, column_ref, rows_ref, count_ref, slot_ref, sems, small_sems,
+    owners, lengths_hbm, hidden_hbm, w_hbm, gain_hbm, freq_hbm,
+    out_ref, hidden_ref, w_ref, acc_ref, lengths_ref, gain_ref, freq_ref, turn_ref, column_ref,
+    sems, small_sems,
 ):
     pieces, rows, depth = hidden_ref.shape
     half = ROPE // 2
     small = [
         pltpu.make_async_copy(source, target, small_sems.at[k])
         for k, (source, target) in enumerate(
-            (
-                (lengths_hbm, lengths_ref),
-                (dest_hbm, dest_ref),
-                (gain_hbm, gain_ref),
-                (freq_hbm, freq_ref),
-            )
+            ((lengths_hbm, lengths_ref), (gain_hbm, gain_ref), (freq_hbm, freq_ref))
         )
     ]
 
@@ -78,27 +73,9 @@
         copy.start()
     lax.fori_loop(0, pieces, begin, 0)
     acc_ref[...] = jnp.zeros_like(acc_ref)
-    packed_ref[...] = jnp.full(packed_ref.shape, -1.0, packed_ref.dtype)
     for copy in small:
         copy.wait()
-    group = lax.axis_index("pre")
-    device = group * owners + lax.axis_index("dec")
-    block_rows = packed_ref.shape[1]
-    blocks = rows // block_rows
-
-    def clear(owner, carry):
-        count_ref[owner] = 0
-        return carry
-
-    def choose(b, carry):
-        owner = lax.shift_right_logical(dest_ref[device * blocks + b], shift_of(groups * owners))
-        rank = count_ref[owner]
-        count_ref[owner] = rank + 1
-        slot_ref[b] = (owners - 1 - owner) * MOST + rank
-        return carry
-
-    lax.fori_loop(0, owners, clear, 0)
-    lax.fori_loop(0, blocks, choose, 0)
+    device = lax.axis_index("pre") * owners + lax.axis_index("dec")
     row = device * rows + lax.broadcasted_iota(jnp.int32, (1, rows), 1)
     start = jnp.zeros((1, rows), jnp.int32)
     first_row = jnp.int32(0)
@@ -132,63 +109,98 @@
     out_ref[LAT : LAT + half, :] = turned.astype(out_ref.dtype)
     turned = second * cosine + first * sine
     out_ref[LAT + half :, :] = turned.astype(out_ref.dtype)
-    width = out_ref.shape[0]
-    for at in range(0, width, 128):
-        count = min(128, width - at)
-        wide = out_ref[at : at + count, :].astype(jnp.float32)
-        if count < 128:
-            wide = jnp.concatenate([wide, jnp.zeros((128 - count, rows), jnp.float32)], axis=0)
-        rows_ref[:, :, at : at + 128] = jnp.transpose(wide).reshape(blocks, block_rows, 128)
-    lane = lax.broadcasted_iota(jnp.int32, (block_rows, WIDE), 1)
-
-    def put(b, carry):
-        place_at = (dest_ref[device * blocks + b] & (groups * owners - 1)) - group * owners
-        block = jnp.where(lane < width, rows_ref[b], place_at.astype(jnp.float32))
-        packed_ref[slot_ref[b]] = block.astype(packed_ref.dtype)
-        return carry
-
-    lax.fori_loop(0, blocks, put, 0, unroll=4)
-
-
-def produce(groups, owners, lengths, destination, hidden, w_turned, gain):
+
+
+def produce(owners, lengths, hidden, w_turned, gain):
     rows, width = hidden.shape
     row_width = w_turned.shape[0]
     pieces = width // DEPTH
-    block_rows = rows // owners
-    vmem = pl.BlockSpec(memory_space=pltpu.VMEM)
-    return pl.pallas_call(
-        functools.partial(produce_kernel, groups, owners),
-        in_specs=[pl.BlockSpec(memory_space=pltpu.HBM)] * 6,
-        out_specs=[vmem, vmem],
-        out_shape=[
-            jax.ShapeDtypeStruct((row_width, rows), jnp.bfloat16),
-            jax.ShapeDtypeStruct((owners * MOST, block_rows, WIDE), jnp.bfloat16),
-        ],
+    return pl.pallas_call(
+        functools.partial(produce_kernel, owners),
+        in_specs=[pl.BlockSpec(memory_space=pltpu.HBM)] * 5,
+        out_specs=pl.BlockSpec(memory_space=pltpu.VMEM),
+        out_shape=jax.ShapeDtypeStruct((row_width, rows), jnp.bfloat16),
         scratch_shapes=[
             pltpu.VMEM((pieces, rows, DEPTH), jnp.bfloat16),
             pltpu.VMEM((pieces, row_width, DEPTH), jnp.bfloat16),
             pltpu.VMEM((row_width, rows), jnp.float32),
             pltpu.SMEM(lengths.shape, jnp.int32),
-            pltpu.SMEM(destination.shape, jnp.int32),
             pltpu.VMEM((1, LAT), jnp.float32),
             pltpu.VMEM((ROPE // 2, 128), jnp.float32),
             pltpu.VMEM((ROPE, rows), jnp.float32),
             pltpu.VMEM((LAT, 128), jnp.float32),
+            pltpu.SemaphoreType.DMA((2, pieces)),
+            pltpu.SemaphoreType.DMA((3,)),
+        ],
+        name="produce",
+    )(lengths, hidden, w_turned, gain.reshape(1, -1), jnp.asarray(frequencies()))
+
+
+def pack_kernel(
+    groups, owners, dest_hbm, rows_hbm, out_ref, turned_ref, dest_ref, rows_ref, count_ref, slot_ref,
+    sems,
+):
+    dest_copy = pltpu.make_async_copy(dest_hbm, dest_ref, sems.at[0])
+    rows_copy = pltpu.make_async_copy(rows_hbm, rows_ref, sems.at[1])
+    dest_copy.start()
+    rows_copy.start()
+    width, rows = rows_ref.shape
+    block_rows = out_ref.shape[1]
+    blocks = rows // block_rows
+    group = lax.axis_index("pre")
+    first = (group * owners + lax.axis_index("dec")) * blocks
+    out_ref[...] = jnp.full(out_ref.shape, -1.0, out_ref.dtype)
+
+    def clear(owner, carry):
+        count_ref[owner] = 0
+        return carry
+
+    def choose(b, carry):
+        owner = lax.shift_right_logical(dest_ref[first + b], shift_of(groups * owners))
+        rank = count_ref[owner]
+        count_ref[owner] = rank + 1
+        slot_ref[b] = (owners - 1 - owner) * MOST + rank
+        return carry
+
+    lax.fori_loop(0, owners, clear, 0)
+    dest_copy.wait()
+    lax.fori_loop(0, blocks, choose, 0)
+    rows_copy.wait()
+    for at in range(0, width, 128):
+        count = min(128, width - at)
+        wide = rows_ref[at : at + count, :].astype(jnp.float32)
+        if count < 128:
+            wide = jnp.concatenate([wide, jnp.zeros((128 - count, rows), jnp.float32)], axis=0)
+        turned_ref[:, :, at : at + 128] = jnp.transpose(wide).reshape(blocks, block_rows, 128)
+    lane = lax.broadcasted_iota(jnp.int32, (block_rows, WIDE), 1)
+
+    def put(b, carry):
+        place_at = (dest_ref[first + b] & (groups * owners - 1)) - group * owners
+        block = jnp.where(lane < width, turned_ref[b], place_at.astype(jnp.float32))
+        out_ref[slot_ref[b]] = block.astype(out_ref.dtype)
+        return carry
+
+    lax.fori_loop(0, blocks, put, 0, unroll=4)
+
+
+def pack(groups, owners, destination, produced):
+    width, rows = produced.shape
+    block_rows = rows // owners
+    return pl.pallas_call(
+        functools.partial(pack_kernel, groups, owners),
+        in_specs=[pl.BlockSpec(memory_space=pltpu.HBM)] * 2,
+        out_specs=pl.BlockSpec(memory_space=pltpu.VMEM),
+        out_shape=jax.ShapeDtypeStruct((owners * MOST, block_rows, WIDE), produced.dtype),
+        scratch_shapes=[
             pltpu.VMEM((owners, block_rows, WIDE), jnp.float32),
+            pltpu.SMEM(destination.shape, jnp.int32),
+            pltpu.VMEM(produced.shape, produced.dtype),
             pltpu.SMEM((owners,), jnp.int32),
             pltpu.SMEM((owners,), jnp.int32),
-            pltpu.SemaphoreType.DMA((2, pieces)),
-            pltpu.SemaphoreType.DMA((4,)),
+            pltpu.SemaphoreType.DMA((2,)),
         ],
-        name="produce",
-    )(
-        lengths,
-        destination,
-        hidden,
-        w_turned,
-        gain.reshape(1, -1),
-        jnp.asarray(frequencies()),
-    )
+        name="pack",
+    )(destination, produced)
 
 
 def place_kernel(arrived_ref, out_ref, rows_ref):
@@ -593,7 +605,7 @@
     ]
     chosen = jnp.where(core == 0, first, second)
     far = lax.ppermute(chosen, ("pre", "dec"), forward)
-    return [piece, first, second, far], chosen
+    return [piece, first, second, far]
 
 
 def per_device(
@@ -615,17 +627,14 @@
     plane = [[2 * k + core for k in reversed(range(SIDE * SIDE))] for core in range(2)]
     sibling = [(d, d ^ 1) for d in range(owners)]
 
-    produced, packed = produce(
-        groups, owners, request_rows, destination, hidden, w_down.T, kv_gain
-    )
-    chunks, chosen = around(produced, groups, owners)
+    produced = produce(owners, request_rows, hidden, w_down.T, kv_gain)
+    chunks = around(produced, groups, owners)
 
     exchanged = functools.partial(
         lax.all_to_all, axis_name="dec", split_axis=0, concat_axis=0, tiled=True
     )
-    lengths, _ = lax.optimization_barrier((request_rows, chosen))
     near_bias, far_bias, valid, chunks[0] = prepare(
-        owners, groups, lengths, row_request, step_position, produced
+        owners, groups, request_rows, row_request, step_position, produced
     )
     keep, send = attend(
         near_bias,
@@ -636,6 +645,7 @@
         chunks,
         w_up_value,
     )
+    packed = pack(groups, owners, destination, produced)
     arrived = exchanged(packed, axis_index_groups=[list(reversed(range(owners)))])
     quarter = place(arrived, *produced.shape)
     pieces = [quarter] + [exchange(quarter, groups, turn) for turn in TURNS[1:]]

time: 65.4 us -> 66.3 us (1.014)
  Pallas kernels: 19.8 us -> 21.7 us
  starting transfers between devices: 29 us -> 28.3 us
    pallas_call x1 -> x2, Pallas kernels: 6.79 us -> 8.61 us  [the longest x1 6.24 us: produce(): pl.pallas_call(functools.partial(produce_kernel, owners), in_specs=[pl.Bl...]
    all_to_all x1, starting transfers between devices: 7.6 us -> 6.62 us  [per_device(): result = merge(exchanged(parts, axis_index_groups=plane))]
  transfers between devices with their start and end apart: 10 -> 10, of which waited for: 4 -> 4; matrix products, arithmetic and copies ran while one was open for 0% -> 0% of each run, Pallas kernels for 17% -> 21%
where the time goes in v10:
time: 66.3 us; the launch traced here: 65.9 us
  starting transfers between devices  28.3 us (43%)
  Pallas kernels  21.7 us (33%)
  blocking collectives  10.1 us (15%)
  waiting for transfers between devices  4.07 us (6%)
  local copies, waits for them, and re-layouts  0.98 us (1%)
  between operations  0.8 us (1%)
    all_to_all x1, blocking collectives, per_device(): result = exchanged(result, axis_index_groups=plane)  10.1 us
    all_to_all x1, starting transfers between devices, per_device(): exchanged(packed, axis_index_groups=[list(reversed(range(owners)))])  9.09 us
    ppermute x5, starting transfers between devices, exchange(): return lax.ppermute(piece, 'pre', [(i, i ^ turn) for i in range(groups)])  8.61 us
    all_to_all x1, starting transfers between devices, per_device(): result = merge(exchanged(parts, axis_index_groups=plane))  6.62 us
    pallas_call x1, Pallas kernels, produce(): pl.pallas_call(functools.partial(produce_kernel, owners), in_specs=[pl.Bl...  6.24 us
    pallas_call x1, Pallas kernels, attend(): pl.pallas_call(far_kernel, in_specs=[vmem] * 8, out_specs=[vmem] * 2, out...  4.54 us
    pallas_call x1, Pallas kernels, attend(): pl.pallas_call(near_kernel, in_specs=[vmem] * 6 + [pl.BlockSpec(memory_sp...  3.5 us
    ppermute x1, starting transfers between devices, per_device(): lax.ppermute(result, 'dec', sibling)  2.67 us
  transfers between devices with their start and end apart: 10, of which 4 were waited for; matrix products, arithmetic and copies ran while one was open for 0% of the time, Pallas kernels for 21%

profile of v10, /device:TPU:1, one launch (start us, length us, event | category | flops | bytes accessed | tf_op | source)
XLA Modules:
  0.0 65.9 jit_solution(16886133156749828358)
XLA Ops:
  0.7 6.2 %produce.1.own_hbm.rows_hbm = bf16[576,256]{1,0:T(8,128)(2,1)} custom-call(s32[4]{0:T(128)} %lengths_ref.1, bf16[256,7168]{1,0:T(8,128)(2,1)} %hidden_hbm.1, bf16[576,7168]{1,0:T(8,128)(2,1)} %bitcast.10, f32[1,512]{1,0:T(1,128)} %bitcast.11, f32[32,128]{1,0:T(8,128)} %constant.20.clone.freq_hbm), custom_call_target="tpu_custom_call" | custom-call | tf_op jit(solution)/shard_map/produce/pallas_call | solution.py:118
  6.9 4.7 %collective-permute-start = (bf16[576,256]{1,0:T(8,128)(2,1)}, bf16[576,256]{1,0:T(8,128)(2,1)S(1)}, u32[]{:S(2)}, u32[]{:S(2)}) collective-permute-start(bf16[576,256]{1,0:T(8,128)(2,1)} %produce.1.own_hbm.rows_hbm), channel_id=1, source_target_pairs={{0,96},{32,64},{64,32},{96,0},{1,97},{33,65},{65,33},{97,1},{2,98}... | collective-permute-start | bytes 884744 | tf_op jit(solution)/shard_map/ppermute | solution.py:594
  11.6 2.4 %pack.1 = bf16[64,8,640]{2,1,0:T(8,128)(2,1)} custom-call(s32[4096]{0:T(1024)} %dest_hbm.1, bf16[576,256]{1,0:T(8,128)(2,1)} %produce.1.own_hbm.rows_hbm), custom_call_target="tpu_custom_call" | custom-call | tf_op jit(solution)/shard_map/pack/pallas_call | solution.py:189
  14.0 9.1 %all-to-all-start.2 = ((bf16[64,8,640]{2,1,0:T(8,128)(2,1)}), bf16[64,8,640]{2,1,0:T(8,128)(2,1)S(1)}, u32[]{:S(2)}, u32[]{:S(2)}) async-start(bf16[64,8,640]{2,1,0:T(8,128)(2,1)} %pack.1), calls=%async_computation.2 | async-start | bytes 1310720 | tf_op jit(solution)/shard_map/all_to_all | solution.py:649
  23.2 0.3 collective-permute-start.2
  23.5 1.0 %copy-done.1 = bf16[576,256]{1,0:T(8,128)(2,1)S(1)} copy-done((bf16[576,256]{1,0:T(8,128)(2,1)S(1)}, bf16[576,256]{1,0:T(8,128)(2,1)}, u32[]{:S(2)}) %copy-start.1) | copy-done | bytes 294936
  24.4 1.0 %prepare.1 = (f32[256,768]{1,0:T(8,128)S(1)}, f32[256,256]{1,0:T(8,128)S(1)}, s32[256,128]{1,0:T(8,128)S(1)}, bf16[576,256]{1,0:T(8,128)(2,1)S(1)}) custom-call(s32[4]{0:T(128)S(1)} %copy-done.4, s32[8]{0:T(128)S(1)} %copy-done.5, s32[4,8]{1,0:T(4,128)S(1)} %copy-done.3, bf16[576,256]{1,0:T(8,128)(2,1)S(1)} %copy-done.1), custom_call_target="tpu_custom_call" | custom-call | tf_op jit(solution)/shard_map/prepare/pallas_call | solution.py:282
  25.5 3.5 %attend_near.1 = (f32[4,256,512]{2,1,0:T(8,128)S(1)}, f32[4,256,128]{2,1,0:T(8,128)S(1)}, bf16[32,512,128]{2,1,0:T(8,128)(2,1)S(1)}) custom-call(f32[256,768]{1,0:T(8,128)S(1)} %get-tuple-element.15.bias_ref, bf16[32,4,8,512]{3,2,1,0:T(8,128)(2,1)S(1)} %bitcast.6, bf16[32,4,8,64]{3,2,1,0:T(8,128)(2,1)S(1)} %bitcast.8, ...), custom_call_target="tpu_custom_call" | custom-call | tf_op jit(solution)/shard_map/attend_near/pallas_call | solution.py:435
  29.0 1.3 %collective-permute-done.2.k3 = bf16[576,256]{1,0:T(8,128)(2,1)S(1)} collective-permute-done((bf16[576,256]{1,0:T(8,128)(2,1)S(1)}, bf16[576,256]{1,0:T(8,128)(2,1)S(1)}, u32[]{:S(2)}, u32[]{:S(2)}) %collective-permute-start.2) | collective-permute-done | bytes 294944 | tf_op jit(solution)/shard_map/ppermute | solution.py:607
  30.3 4.5 %attend_far.1 = (f32[16,40,128]{2,1,0:T(8,128)S(1)}, f32[16,40,128]{2,1,0:T(8,128)S(1)}) custom-call(f32[256,256]{1,0:T(8,128)S(1)} %get-tuple-element.13.bias_ref, s32[256,128]{1,0:T(8,128)S(1)} %get-tuple-element.14.valid_ref, bf16[32,4,8,512]{3,2,1,0:T(8,128)(2,1)S(1)} %bitcast.7, bf16[32,4,8,64]{3,2,1,0:T(8,128)(2,1)S(1)} %bitcast.9, ...), custom_call_target="tpu_custom_call" | custom-call | tf_op jit(solution)/shard_map/attend_far/pallas_call | solution.py:449
  34.9 1.0 %collective-permute-start.3 = (f32[16,40,128]{2,1,0:T(8,128)S(1)}, f32[16,40,128]{2,1,0:T(8,128)S(1)}, u32[]{:S(2)}, u32[]{:S(2)}) collective-permute-start(f32[16,40,128]{2,1,0:T(8,128)S(1)} %get-tuple-element.21), channel_id=1, source_target_pairs={{0,1},{1,0},{2,3},{3,2},{4,5},{5,4},{6,7},{7,6},{8,9},{9,8},{10,11... | collective-permute-start | bytes 983048 | tf_op jit(solution)/shard_map/ppermute | solution.py:653
  35.9 1.3 %collective-permute-done.3.other_ref = f32[16,40,128]{2,1,0:T(8,128)S(1)} collective-permute-done((f32[16,40,128]{2,1,0:T(8,128)S(1)}, f32[16,40,128]{2,1,0:T(8,128)S(1)}, u32[]{:S(2)}, u32[]{:S(2)}) %collective-permute-start.3) | collective-permute-done | bytes 327712 | tf_op jit(solution)/shard_map/ppermute | solution.py:653
  37.1 1.3 %merge_pair.1 = f32[16,40,128]{2,1,0:T(8,128)} custom-call(f32[16,40,128]{2,1,0:T(8,128)S(1)} %get-tuple-element.20.mine_ref, f32[16,40,128]{2,1,0:T(8,128)S(1)} %collective-permute-done.3.other_ref), custom_call_target="tpu_custom_call" | custom-call | tf_op jit(solution)/shard_map/merge_pair/pallas_call | solution.py:497
  38.4 6.6 %all-to-all-start = ((f32[16,40,128]{2,1,0:T(8,128)}), f32[16,40,128]{2,1,0:T(8,128)S(1)}, u32[]{:S(2)}, u32[]{:S(2)}) async-start(f32[16,40,128]{2,1,0:T(8,128)} %merge_pair.1), calls=%async_computation | async-start | bytes 655360 | tf_op jit(solution)/shard_map/all_to_all | solution.py:654
  45.0 0.5 place.1.p0
  45.5 0.7 %collective-permute-start.5 = (bf16[576,256]{1,0:T(8,128)(2,1)S(1)}, bf16[576,256]{1,0:T(8,128)(2,1)S(1)}, u32[]{:S(2)}, u32[]{:S(2)}) collective-permute-start(bf16[576,256]{1,0:T(8,128)(2,1)S(1)} %place.1.p0), channel_id=1, source_target_pairs={{0,96},{32,64},{64,32},{96,0},{1,97},{33,65},{65,33},{97,1},{2,98}... | collective-permute-start | bytes 884744 | tf_op jit(solution)/shard_map/ppermute | solution.py:594
  46.2 0.5 collective-permute-start.6
  46.7 2.7 %collective-permute-start.7 = (bf16[576,256]{1,0:T(8,128)(2,1)S(1)}, bf16[576,256]{1,0:T(8,128)(2,1)S(1)}, u32[]{:S(2)}, u32[]{:S(2)}) collective-permute-start(bf16[576,256]{1,0:T(8,128)(2,1)S(1)} %place.1.p0), channel_id=1, source_target_pairs={{0,64},{32,96},{64,0},{96,32},{1,65},{33,97},{65,1},{97,33},{2,66}... | collective-permute-start | bytes 884744 | tf_op jit(solution)/shard_map/ppermute | solution.py:594
  49.5 0.5 all-to-all-done.parts_ref
  50.0 0.4 merge.1
  50.4 10.1 %all_to_all.15.mine_ref = bf16[16,32,128]{2,1,0:T(8,128)(2,1)S(1)} all-to-all(bf16[16,32,128]{2,1,0:T(8,128)(2,1)S(1)} %merge.1), channel_id=1, replica_groups={{30,28,26,24,22,20,18,16,14,12,10,8,6,4,2,0},{31,29,27,25,23,21,19,17,1..., dimensions={0} | all-to-all | bytes 262144 | tf_op jit(solution)/shard_map/all_to_all | solution.py:655
  60.5 2.7 %collective-permute-start.4 = (bf16[16,32,128]{2,1,0:T(8,128)(2,1)S(1)}, bf16[16,32,128]{2,1,0:T(8,128)(2,1)S(1)}, u32[]{:S(2)}, u32[]{:S(2)}) collective-permute-start(bf16[16,32,128]{2,1,0:T(8,128)(2,1)S(1)} %all_to_all.15.mine_ref), channel_id=1, source_target_pairs={{0,1},{1,0},{2,3},{3,2},{4,5},{5,4},{6,7},{7,6},{8,9},{9,8},{10,11... | collective-permute-start | bytes 393224 | tf_op jit(solution)/shard_map/ppermute | solution.py:656
  63.2 1.0 %collective-permute-done.4.other_ref = bf16[16,32,128]{2,1,0:T(8,128)(2,1)S(1)} collective-permute-done((bf16[16,32,128]{2,1,0:T(8,128)(2,1)S(1)}, bf16[16,32,128]{2,1,0:T(8,128)(2,1)S(1)}, u32[]{:S(2)}, u32[]{:S(2)}) %collective-permute-start.4) | collective-permute-done | bytes 131104 | tf_op jit(solution)/shard_map/ppermute | solution.py:656
  64.2 1.7 %finish.1 = (bf16[32,4096]{1,0:T(8,128)(2,1)}, bf16[576,1024]{1,0:T(8,128)(2,1)}) custom-call(bf16[16,32,128]{2,1,0:T(8,128)(2,1)S(1)} %all_to_all.15.mine_ref, bf16[16,32,128]{2,1,0:T(8,128)(2,1)S(1)} %collective-permute-done.4.other_ref, bf16[576,256]{1,0:T(8,128)(2,1)S(1)} %place.1.p0, bf16[576,256]{1,0:T(8,128)(2,1)S(1)} %collective-permute-done.5.p1, ...), custom_call_target="tpu_custom_call" | custom-call | tf_op jit(solution)/shard_map/finish/pallas_call | solution.py:576
  (19 shorter events, 0.1 us)
Async XLA Ops:
  0.6 22.8 %copy-start.3 = (s32[4,8]{1,0:T(4,128)S(1)}, s32[4,8]{1,0:T(4,128)}, u32[]{:S(2)}) copy-start(s32[4,8]{1,0:T(4,128)} %position_ref.1) | copy-start | bytes 388
  0.6 22.8 %copy-start.4 = (s32[4]{0:T(128)S(1)}, s32[4]{0:T(128)}, u32[]{:S(2)}) copy-start(s32[4]{0:T(128)} %lengths_ref.1) | copy-start | bytes 52
  0.7 22.8 %copy-start.5 = (s32[8]{0:T(128)S(1)}, s32[8]{0:T(128)}, u32[]{:S(2)}) copy-start(s32[8]{0:T(128)} %request_ref.1) | copy-start | bytes 100
  0.7 24.8 %copy-start.2 = (bf16[4,8,32,64]{3,2,1,0:T(8,128)(2,1)S(1)}, bf16[4,8,32,64]{3,2,1,0:T(8,128)(2,1)}, u32[]{:S(2)}) copy-start(bf16[4,8,32,64]{3,2,1,0:T(8,128)(2,1)} %param.15) | copy-start | bytes 393220
  6.9 18.6 %copy-start = (bf16[4,8,32,512]{3,2,1,0:T(8,128)(2,1)S(1)}, bf16[4,8,32,512]{3,2,1,0:T(8,128)(2,1)}, u32[]{:S(2)}) copy-start(bf16[4,8,32,512]{3,2,1,0:T(8,128)(2,1)} %param.14) | copy-start | bytes 3145732
  6.9 16.2 %collective-permute-start = (bf16[576,256]{1,0:T(8,128)(2,1)}, bf16[576,256]{1,0:T(8,128)(2,1)S(1)}, u32[]{:S(2)}, u32[]{:S(2)}) collective-permute-start(bf16[576,256]{1,0:T(8,128)(2,1)} %produce.1.own_hbm.rows_hbm), channel_id=1, source_target_pairs={{0,96},{32,64},{64,32},{96,0},{1,97},{33,65},{65,33},{97,1},{2,98}... | collective-permute-start | bytes 884744 | tf_op jit(solution)/shard_map/ppermute | solution.py:594
  11.6 11.5 %collective-permute-start.1 = (bf16[576,256]{1,0:T(8,128)(2,1)}, bf16[576,256]{1,0:T(8,128)(2,1)S(1)}, u32[]{:S(2)}, u32[]{:S(2)}) collective-permute-start(bf16[576,256]{1,0:T(8,128)(2,1)} %produce.1.own_hbm.rows_hbm), channel_id=1, source_target_pairs={{0,32},{32,0},{64,96},{96,64},{1,33},{33,1},{65,97},{97,65},{2,34}... | collective-permute-start | bytes 884744 | tf_op jit(solution)/shard_map/ppermute | solution.py:594
  14.0 24.4 %all-to-all-start.2 = ((bf16[64,8,640]{2,1,0:T(8,128)(2,1)}), bf16[64,8,640]{2,1,0:T(8,128)(2,1)S(1)}, u32[]{:S(2)}, u32[]{:S(2)}) async-start(bf16[64,8,640]{2,1,0:T(8,128)(2,1)} %pack.1), calls=%async_computation.2 | async-start | bytes 1310720 | tf_op jit(solution)/shard_map/all_to_all | solution.py:649
  23.2 7.2 %collective-permute-start.2 = (bf16[576,256]{1,0:T(8,128)(2,1)S(1)}, bf16[576,256]{1,0:T(8,128)(2,1)S(1)}, u32[]{:S(2)}, u32[]{:S(2)}) collective-permute-start(bf16[576,256]{1,0:T(8,128)(2,1)S(1)} %broadcast_select_fusion), channel_id=1, source_target_pairs={{0,32},{1,97},{2,34},{3,99},{4,36},{5,101},{6,38},{7,103},{8,40},{... | collective-permute-start | bytes 884744 | tf_op jit(solution)/shard_map/ppermute | solution.py:607
  23.5 1.0 %copy-start.1 = (bf16[576,256]{1,0:T(8,128)(2,1)S(1)}, bf16[576,256]{1,0:T(8,128)(2,1)}, u32[]{:S(2)}) copy-start(bf16[576,256]{1,0:T(8,128)(2,1)} %produce.1.own_hbm.rows_hbm) | copy-start | bytes 884740
  34.9 2.2 %collective-permute-start.3 = (f32[16,40,128]{2,1,0:T(8,128)S(1)}, f32[16,40,128]{2,1,0:T(8,128)S(1)}, u32[]{:S(2)}, u32[]{:S(2)}) collective-permute-start(f32[16,40,128]{2,1,0:T(8,128)S(1)} %get-tuple-element.21), channel_id=1, source_target_pairs={{0,1},{1,0},{2,3},{3,2},{4,5},{5,4},{6,7},{7,6},{8,9},{9,8},{10,11... | collective-permute-start | bytes 983048 | tf_op jit(solution)/shard_map/ppermute | solution.py:653
  38.4 11.6 %all-to-all-start = ((f32[16,40,128]{2,1,0:T(8,128)}), f32[16,40,128]{2,1,0:T(8,128)S(1)}, u32[]{:S(2)}, u32[]{:S(2)}) async-start(f32[16,40,128]{2,1,0:T(8,128)} %merge_pair.1), calls=%async_computation | async-start | bytes 655360 | tf_op jit(solution)/shard_map/all_to_all | solution.py:654
  45.5 17.7 %collective-permute-start.5 = (bf16[576,256]{1,0:T(8,128)(2,1)S(1)}, bf16[576,256]{1,0:T(8,128)(2,1)S(1)}, u32[]{:S(2)}, u32[]{:S(2)}) collective-permute-start(bf16[576,256]{1,0:T(8,128)(2,1)S(1)} %place.1.p0), channel_id=1, source_target_pairs={{0,96},{32,64},{64,32},{96,0},{1,97},{33,65},{65,33},{97,1},{2,98}... | collective-permute-start | bytes 884744 | tf_op jit(solution)/shard_map/ppermute | solution.py:594
  46.2 17.0 %collective-permute-start.6 = (bf16[576,256]{1,0:T(8,128)(2,1)S(1)}, bf16[576,256]{1,0:T(8,128)(2,1)S(1)}, u32[]{:S(2)}, u32[]{:S(2)}) collective-permute-start(bf16[576,256]{1,0:T(8,128)(2,1)S(1)} %place.1.p0), channel_id=1, source_target_pairs={{0,32},{32,0},{64,96},{96,64},{1,33},{33,1},{65,97},{97,65},{2,34}... | collective-permute-start | bytes 884744 | tf_op jit(solution)/shard_map/ppermute | solution.py:594
  46.7 16.5 %collective-permute-start.7 = (bf16[576,256]{1,0:T(8,128)(2,1)S(1)}, bf16[576,256]{1,0:T(8,128)(2,1)S(1)}, u32[]{:S(2)}, u32[]{:S(2)}) collective-permute-start(bf16[576,256]{1,0:T(8,128)(2,1)S(1)} %place.1.p0), channel_id=1, source_target_pairs={{0,64},{32,96},{64,0},{96,32},{1,65},{33,97},{65,1},{97,33},{2,66}... | collective-permute-start | bytes 884744 | tf_op jit(solution)/shard_map/ppermute | solution.py:594
  60.5 3.7 %collective-permute-start.4 = (bf16[16,32,128]{2,1,0:T(8,128)(2,1)S(1)}, bf16[16,32,128]{2,1,0:T(8,128)(2,1)S(1)}, u32[]{:S(2)}, u32[]{:S(2)}) collective-permute-start(bf16[16,32,128]{2,1,0:T(8,128)(2,1)S(1)} %all_to_all.15.mine_ref), channel_id=1, source_target_pairs={{0,1},{1,0},{2,3},{3,2},{4,5},{5,4},{6,7},{7,6},{8,9},{9,8},{10,11... | collective-permute-start | bytes 393224 | tf_op jit(solution)/shard_map/ppermute | solution.py:656

commit v11 on v9

--- a/solution.py
+++ b/solution.py
@@ -582,18 +582,19 @@
     return lax.ppermute(piece, "pre", [(i, i ^ turn) for i in range(groups)])
 
 
-def around(piece, groups, owners):
+def around(piece, groups, owners, gate):
     core = lax.axis_index("dec") % 2
     first = exchange(piece, groups, 3)
     second = exchange(piece, groups, 1)
+    early_first, early_second, _ = lax.optimization_barrier((first, second, gate))
     forward = [
         (g * owners + d, (g ^ (1 if d % 2 == 0 else 3)) * owners + d)
         for g in range(groups)
         for d in range(owners)
     ]
-    chosen = jnp.where(core == 0, first, second)
+    chosen = jnp.where(core == 0, early_first, early_second)
     far = lax.ppermute(chosen, ("pre", "dec"), forward)
-    return [piece, first, second, far], chosen
+    return [piece, first, second, far]
 
 
 def per_device(
@@ -618,14 +619,14 @@
     produced, packed = produce(
         groups, owners, request_rows, destination, hidden, w_down.T, kv_gain
     )
-    chunks, chosen = around(produced, groups, owners)
+    near_bias, far_bias, valid, own = prepare(
+        owners, groups, request_rows, row_request, step_position, produced
+    )
+    chunks = around(produced, groups, owners, valid)
+    chunks[0] = own
 
     exchanged = functools.partial(
         lax.all_to_all, axis_name="dec", split_axis=0, concat_axis=0, tiled=True
-    )
-    lengths, _ = lax.optimization_barrier((request_rows, chosen))
-    near_bias, far_bias, valid, chunks[0] = prepare(
-        owners, groups, lengths, row_request, step_position, produced
     )
     keep, send = attend(
         near_bias,

time: 65.4 us -> 65.7 us (level)
  waiting for transfers between devices: 4.31 us -> 6.51 us
  starting transfers between devices: 29 us -> 27.2 us
    ppermute x1, waiting for transfers between devices: 1.33 us -> 3.35 us  [around(): far = lax.ppermute(chosen, ('pre', 'dec'), forward)]
    all_to_all x1, starting transfers between devices: 7.6 us -> 6.39 us  [per_device(): result = merge(exchanged(parts, axis_index_groups=plane))]
    ppermute x1, starting transfers between devices: 0.98 us -> 0.15 us  [per_device(): parts = merge_pair(keep, lax.ppermute(send, 'dec', sibling))]
where the time goes in v11:
time: 65.7 us; the launch traced here: 65.3 us
  starting transfers between devices  27.2 us (41%)
  Pallas kernels  19.8 us (30%)
  blocking collectives  10 us (15%)
  waiting for transfers between devices  6.51 us (10%)
  local copies, waits for them, and re-layouts  0.98 us (1%)
  between operations  0.81 us (1%)
    all_to_all x1, blocking collectives, per_device(): result = exchanged(result, axis_index_groups=plane)  10 us
    all_to_all x1, starting transfers between devices, per_device(): exchanged(packed, axis_index_groups=[list(reversed(range(owners)))])  9.08 us
    ppermute x5, starting transfers between devices, exchange(): return lax.ppermute(piece, 'pre', [(i, i ^ turn) for i in range(groups)])  8.61 us
    pallas_call x1, Pallas kernels, produce(): pl.pallas_call(functools.partial(produce_kernel, groups, owners), in_spec...  6.79 us
    all_to_all x1, starting transfers between devices, per_device(): result = merge(exchanged(parts, axis_index_groups=plane))  6.39 us
    pallas_call x1, Pallas kernels, attend(): pl.pallas_call(far_kernel, in_specs=[vmem] * 8, out_specs=[vmem] * 2, out...  4.54 us
    pallas_call x1, Pallas kernels, attend(): pl.pallas_call(near_kernel, in_specs=[vmem] * 6 + [pl.BlockSpec(memory_sp...  3.49 us
    ppermute x1, waiting for transfers between devices, around(): far = lax.ppermute(chosen, ('pre', 'dec'), forward)  3.35 us
  transfers between devices with their start and end apart: 10, of which 4 were waited for; matrix products, arithmetic and copies ran while one was open for 0% of the time, Pallas kernels for 17%

profile of v11, /device:TPU:1, one launch (start us, length us, event | category | flops | bytes accessed | tf_op | source)
XLA Modules:
  0.0 65.3 jit_solution(4494805947480754525)
XLA Ops:
  0.7 6.8 %produce.1 = (bf16[576,256]{1,0:T(8,128)(2,1)}, bf16[64,8,640]{2,1,0:T(8,128)(2,1)}) custom-call(s32[4]{0:T(128)} %lengths_ref.1, s32[4096]{0:T(1024)} %dest_hbm.1, bf16[256,7168]{1,0:T(8,128)(2,1)} %hidden_hbm.1, bf16[576,7168]{1,0:T(8,128)(2,1)} %bitcast.10, f32[1,512]{1,0:T(1,128)} %bitcast.11, f32[32,128]{1,0:T(8,128)} %constant.20.clone.freq_hbm), custom_call_target="tpu_custom_call" | custom-call | tf_op jit(solution)/shard_map/produce/pallas_call | solution.py:159
  7.5 4.7 %collective-permute-start = (bf16[576,256]{1,0:T(8,128)(2,1)}, bf16[576,256]{1,0:T(8,128)(2,1)S(1)}, u32[]{:S(2)}, u32[]{:S(2)}) collective-permute-start(bf16[576,256]{1,0:T(8,128)(2,1)} %get-tuple-element.17.own_hbm), channel_id=1, source_target_pairs={{0,96},{32,64},{64,32},{96,0},{1,97},{33,65},{65,33},{97,1},{2,98}... | collective-permute-start | bytes 884744 | tf_op jit(solution)/shard_map/ppermute | solution.py:582
  12.2 9.1 %all-to-all-start.2 = ((bf16[64,8,640]{2,1,0:T(8,128)(2,1)}), bf16[64,8,640]{2,1,0:T(8,128)(2,1)S(1)}, u32[]{:S(2)}, u32[]{:S(2)}) async-start(bf16[64,8,640]{2,1,0:T(8,128)(2,1)} %get-tuple-element.29), calls=%async_computation.2 | async-start | bytes 1310720 | tf_op jit(solution)/shard_map/all_to_all | solution.py:640
  21.3 1.0 %copy-done.2 = bf16[576,256]{1,0:T(8,128)(2,1)S(1)} copy-done((bf16[576,256]{1,0:T(8,128)(2,1)S(1)}, bf16[576,256]{1,0:T(8,128)(2,1)}, u32[]{:S(2)}) %copy-start.2) | copy-done | bytes 294936
  22.2 1.0 %prepare.1 = (f32[256,768]{1,0:T(8,128)S(1)}, f32[256,256]{1,0:T(8,128)S(1)}, s32[256,128]{1,0:T(8,128)S(1)}, bf16[576,256]{1,0:T(8,128)(2,1)S(1)}) custom-call(s32[4]{0:T(128)S(1)} %copy-done.4, s32[8]{0:T(128)S(1)} %copy-done.5, s32[4,8]{1,0:T(4,128)S(1)} %copy-done.3, bf16[576,256]{1,0:T(8,128)(2,1)S(1)} %copy-done.2), custom_call_target="tpu_custom_call" | custom-call | tf_op jit(solution)/shard_map/prepare/pallas_call | solution.py:270
  23.3 0.0 collective-permute-done.k1
  23.4 0.3 collective-permute-start.2
  23.7 3.5 %attend_near.1 = (f32[4,256,512]{2,1,0:T(8,128)S(1)}, f32[4,256,128]{2,1,0:T(8,128)S(1)}, bf16[32,512,128]{2,1,0:T(8,128)(2,1)S(1)}) custom-call(f32[256,768]{1,0:T(8,128)S(1)} %get-tuple-element.22.bias_ref, bf16[32,4,8,512]{3,2,1,0:T(8,128)(2,1)S(1)} %bitcast.6, bf16[32,4,8,64]{3,2,1,0:T(8,128)(2,1)S(1)} %bitcast.8, ...), custom_call_target="tpu_custom_call" | custom-call | tf_op jit(solution)/shard_map/attend_near/pallas_call | solution.py:423
  27.2 3.3 %collective-permute-done.2.k3 = bf16[576,256]{1,0:T(8,128)(2,1)S(1)} collective-permute-done((bf16[576,256]{1,0:T(8,128)(2,1)S(1)}, bf16[576,256]{1,0:T(8,128)(2,1)S(1)}, u32[]{:S(2)}, u32[]{:S(2)}) %collective-permute-start.2) | collective-permute-done | bytes 294944 | tf_op jit(solution)/shard_map/ppermute | solution.py:596
  30.5 4.5 %attend_far.1 = (f32[16,40,128]{2,1,0:T(8,128)S(1)}, f32[16,40,128]{2,1,0:T(8,128)S(1)}) custom-call(f32[256,256]{1,0:T(8,128)S(1)} %get-tuple-element.18.bias_ref, s32[256,128]{1,0:T(8,128)S(1)} %get-tuple-element.19.valid_ref, bf16[32,4,8,512]{3,2,1,0:T(8,128)(2,1)S(1)} %bitcast.7, bf16[32,4,8,64]{3,2,1,0:T(8,128)(2,1)S(1)} %bitcast.9, ...), custom_call_target="tpu_custom_call" | custom-call | tf_op jit(solution)/shard_map/attend_far/pallas_call | solution.py:437
  35.1 0.2 collective-permute-start.3
  35.2 1.6 %collective-permute-done.3.other_ref = f32[16,40,128]{2,1,0:T(8,128)S(1)} collective-permute-done((f32[16,40,128]{2,1,0:T(8,128)S(1)}, f32[16,40,128]{2,1,0:T(8,128)S(1)}, u32[]{:S(2)}, u32[]{:S(2)}) %collective-permute-start.3) | collective-permute-done | bytes 327712 | tf_op jit(solution)/shard_map/ppermute | solution.py:644
  36.8 1.2 %merge_pair.1 = f32[16,40,128]{2,1,0:T(8,128)} custom-call(f32[16,40,128]{2,1,0:T(8,128)S(1)} %get-tuple-element.27.mine_ref, f32[16,40,128]{2,1,0:T(8,128)S(1)} %collective-permute-done.3.other_ref), custom_call_target="tpu_custom_call" | custom-call | tf_op jit(solution)/shard_map/merge_pair/pallas_call | solution.py:485
  38.0 6.4 %all-to-all-start = ((f32[16,40,128]{2,1,0:T(8,128)}), f32[16,40,128]{2,1,0:T(8,128)S(1)}, u32[]{:S(2)}, u32[]{:S(2)}) async-start(f32[16,40,128]{2,1,0:T(8,128)} %merge_pair.1), calls=%async_computation | async-start | bytes 655360 | tf_op jit(solution)/shard_map/all_to_all | solution.py:645
  44.4 0.5 place.1.p0
  45.0 1.0 %collective-permute-start.5 = (bf16[576,256]{1,0:T(8,128)(2,1)S(1)}, bf16[576,256]{1,0:T(8,128)(2,1)S(1)}, u32[]{:S(2)}, u32[]{:S(2)}) collective-permute-start(bf16[576,256]{1,0:T(8,128)(2,1)S(1)} %place.1.p0), channel_id=1, source_target_pairs={{0,96},{32,64},{64,32},{96,0},{1,97},{33,65},{65,33},{97,1},{2,98}... | collective-permute-start | bytes 884744 | tf_op jit(solution)/shard_map/ppermute | solution.py:582
  46.0 0.8 %collective-permute-start.6 = (bf16[576,256]{1,0:T(8,128)(2,1)S(1)}, bf16[576,256]{1,0:T(8,128)(2,1)S(1)}, u32[]{:S(2)}, u32[]{:S(2)}) collective-permute-start(bf16[576,256]{1,0:T(8,128)(2,1)S(1)} %place.1.p0), channel_id=1, source_target_pairs={{0,32},{32,0},{64,96},{96,64},{1,33},{33,1},{65,97},{97,65},{2,34}... | collective-permute-start | bytes 884744 | tf_op jit(solution)/shard_map/ppermute | solution.py:582
  46.8 2.1 %collective-permute-start.7 = (bf16[576,256]{1,0:T(8,128)(2,1)S(1)}, bf16[576,256]{1,0:T(8,128)(2,1)S(1)}, u32[]{:S(2)}, u32[]{:S(2)}) collective-permute-start(bf16[576,256]{1,0:T(8,128)(2,1)S(1)} %place.1.p0), channel_id=1, source_target_pairs={{0,64},{32,96},{64,0},{96,32},{1,65},{33,97},{65,1},{97,33},{2,66}... | collective-permute-start | bytes 884744 | tf_op jit(solution)/shard_map/ppermute | solution.py:582
  48.9 0.6 all-to-all-done.parts_ref
  49.5 0.4 merge.1
  50.0 10.0 %all_to_all.15.mine_ref = bf16[16,32,128]{2,1,0:T(8,128)(2,1)S(1)} all-to-all(bf16[16,32,128]{2,1,0:T(8,128)(2,1)S(1)} %merge.1), channel_id=1, replica_groups={{30,28,26,24,22,20,18,16,14,12,10,8,6,4,2,0},{31,29,27,25,23,21,19,17,1..., dimensions={0} | all-to-all | bytes 262144 | tf_op jit(solution)/shard_map/all_to_all | solution.py:646
  60.0 2.6 %collective-permute-start.4 = (bf16[16,32,128]{2,1,0:T(8,128)(2,1)S(1)}, bf16[16,32,128]{2,1,0:T(8,128)(2,1)S(1)}, u32[]{:S(2)}, u32[]{:S(2)}) collective-permute-start(bf16[16,32,128]{2,1,0:T(8,128)(2,1)S(1)} %all_to_all.15.mine_ref), channel_id=1, source_target_pairs={{0,1},{1,0},{2,3},{3,2},{4,5},{5,4},{6,7},{7,6},{8,9},{9,8},{10,11... | collective-permute-start | bytes 393224 | tf_op jit(solution)/shard_map/ppermute | solution.py:647
  62.6 1.0 %collective-permute-done.4.other_ref = bf16[16,32,128]{2,1,0:T(8,128)(2,1)S(1)} collective-permute-done((bf16[16,32,128]{2,1,0:T(8,128)(2,1)S(1)}, bf16[16,32,128]{2,1,0:T(8,128)(2,1)S(1)}, u32[]{:S(2)}, u32[]{:S(2)}) %collective-permute-start.4) | collective-permute-done | bytes 131104 | tf_op jit(solution)/shard_map/ppermute | solution.py:647
  63.6 1.7 %finish.1 = (bf16[32,4096]{1,0:T(8,128)(2,1)}, bf16[576,1024]{1,0:T(8,128)(2,1)}) custom-call(bf16[16,32,128]{2,1,0:T(8,128)(2,1)S(1)} %all_to_all.15.mine_ref, bf16[16,32,128]{2,1,0:T(8,128)(2,1)S(1)} %collective-permute-done.4.other_ref, bf16[576,256]{1,0:T(8,128)(2,1)S(1)} %place.1.p0, bf16[576,256]{1,0:T(8,128)(2,1)S(1)} %collective-permute-done.5.p1, ...), custom_call_target="tpu_custom_call" | custom-call | tf_op jit(solution)/shard_map/finish/pallas_call | solution.py:564
  (18 shorter events, 0.1 us)
Async XLA Ops:
  0.6 20.6 %copy-start.3 = (s32[4,8]{1,0:T(4,128)S(1)}, s32[4,8]{1,0:T(4,128)}, u32[]{:S(2)}) copy-start(s32[4,8]{1,0:T(4,128)} %position_ref.1) | copy-start | bytes 388
  0.6 20.6 %copy-start.4 = (s32[4]{0:T(128)S(1)}, s32[4]{0:T(128)}, u32[]{:S(2)}) copy-start(s32[4]{0:T(128)} %lengths_ref.1) | copy-start | bytes 52
  0.7 20.6 %copy-start.5 = (s32[8]{0:T(128)S(1)}, s32[8]{0:T(128)}, u32[]{:S(2)}) copy-start(s32[8]{0:T(128)} %request_ref.1) | copy-start | bytes 100
  0.7 23.0 %copy-start = (bf16[4,8,32,512]{3,2,1,0:T(8,128)(2,1)S(1)}, bf16[4,8,32,512]{3,2,1,0:T(8,128)(2,1)}, u32[]{:S(2)}) copy-start(bf16[4,8,32,512]{3,2,1,0:T(8,128)(2,1)} %param.14) | copy-start | bytes 3145732
  0.7 23.0 %copy-start.1 = (bf16[4,8,32,64]{3,2,1,0:T(8,128)(2,1)S(1)}, bf16[4,8,32,64]{3,2,1,0:T(8,128)(2,1)}, u32[]{:S(2)}) copy-start(bf16[4,8,32,64]{3,2,1,0:T(8,128)(2,1)} %param.15) | copy-start | bytes 393220
  7.5 15.8 %collective-permute-start = (bf16[576,256]{1,0:T(8,128)(2,1)}, bf16[576,256]{1,0:T(8,128)(2,1)S(1)}, u32[]{:S(2)}, u32[]{:S(2)}) collective-permute-start(bf16[576,256]{1,0:T(8,128)(2,1)} %get-tuple-element.17.own_hbm), channel_id=1, source_target_pairs={{0,96},{32,64},{64,32},{96,0},{1,97},{33,65},{65,33},{97,1},{2,98}... | collective-permute-start | bytes 884744 | tf_op jit(solution)/shard_map/ppermute | solution.py:582
  12.1 11.2 %collective-permute-start.1 = (bf16[576,256]{1,0:T(8,128)(2,1)}, bf16[576,256]{1,0:T(8,128)(2,1)S(1)}, u32[]{:S(2)}, u32[]{:S(2)}) collective-permute-start(bf16[576,256]{1,0:T(8,128)(2,1)} %get-tuple-element.17.own_hbm), channel_id=1, source_target_pairs={{0,32},{32,0},{64,96},{96,64},{1,33},{33,1},{65,97},{97,65},{2,34}... | collective-permute-start | bytes 884744 | tf_op jit(solution)/shard_map/ppermute | solution.py:582
  12.2 25.9 %all-to-all-start.2 = ((bf16[64,8,640]{2,1,0:T(8,128)(2,1)}), bf16[64,8,640]{2,1,0:T(8,128)(2,1)S(1)}, u32[]{:S(2)}, u32[]{:S(2)}) async-start(bf16[64,8,640]{2,1,0:T(8,128)(2,1)} %get-tuple-element.29), calls=%async_computation.2 | async-start | bytes 1310720 | tf_op jit(solution)/shard_map/all_to_all | solution.py:640
  21.3 1.0 %copy-start.2 = (bf16[576,256]{1,0:T(8,128)(2,1)S(1)}, bf16[576,256]{1,0:T(8,128)(2,1)}, u32[]{:S(2)}) copy-start(bf16[576,256]{1,0:T(8,128)(2,1)} %get-tuple-element.17.own_hbm) | copy-start | bytes 884740
  23.4 7.2 %collective-permute-start.2 = (bf16[576,256]{1,0:T(8,128)(2,1)S(1)}, bf16[576,256]{1,0:T(8,128)(2,1)S(1)}, u32[]{:S(2)}, u32[]{:S(2)}) collective-permute-start(bf16[576,256]{1,0:T(8,128)(2,1)S(1)} %broadcast_select_fusion), channel_id=1, source_target_pairs={{0,32},{1,97},{2,34},{3,99},{4,36},{5,101},{6,38},{7,103},{8,40},{... | collective-permute-start | bytes 884744 | tf_op jit(solution)/shard_map/ppermute | solution.py:596
  35.1 1.7 %collective-permute-start.3 = (f32[16,40,128]{2,1,0:T(8,128)S(1)}, f32[16,40,128]{2,1,0:T(8,128)S(1)}, u32[]{:S(2)}, u32[]{:S(2)}) collective-permute-start(f32[16,40,128]{2,1,0:T(8,128)S(1)} %get-tuple-element.28), channel_id=1, source_target_pairs={{0,1},{1,0},{2,3},{3,2},{4,5},{5,4},{6,7},{7,6},{8,9},{9,8},{10,11... | collective-permute-start | bytes 983048 | tf_op jit(solution)/shard_map/ppermute | solution.py:644
  38.0 11.5 %all-to-all-start = ((f32[16,40,128]{2,1,0:T(8,128)}), f32[16,40,128]{2,1,0:T(8,128)S(1)}, u32[]{:S(2)}, u32[]{:S(2)}) async-start(f32[16,40,128]{2,1,0:T(8,128)} %merge_pair.1), calls=%async_computation | async-start | bytes 655360 | tf_op jit(solution)/shard_map/all_to_all | solution.py:645
  45.0 17.7 %collective-permute-start.5 = (bf16[576,256]{1,0:T(8,128)(2,1)S(1)}, bf16[576,256]{1,0:T(8,128)(2,1)S(1)}, u32[]{:S(2)}, u32[]{:S(2)}) collective-permute-start(bf16[576,256]{1,0:T(8,128)(2,1)S(1)} %place.1.p0), channel_id=1, source_target_pairs={{0,96},{32,64},{64,32},{96,0},{1,97},{33,65},{65,33},{97,1},{2,98}... | collective-permute-start | bytes 884744 | tf_op jit(solution)/shard_map/ppermute | solution.py:582
  46.0 16.7 %collective-permute-start.6 = (bf16[576,256]{1,0:T(8,128)(2,1)S(1)}, bf16[576,256]{1,0:T(8,128)(2,1)S(1)}, u32[]{:S(2)}, u32[]{:S(2)}) collective-permute-start(bf16[576,256]{1,0:T(8,128)(2,1)S(1)} %place.1.p0), channel_id=1, source_target_pairs={{0,32},{32,0},{64,96},{96,64},{1,33},{33,1},{65,97},{97,65},{2,34}... | collective-permute-start | bytes 884744 | tf_op jit(solution)/shard_map/ppermute | solution.py:582
  46.8 15.8 %collective-permute-start.7 = (bf16[576,256]{1,0:T(8,128)(2,1)S(1)}, bf16[576,256]{1,0:T(8,128)(2,1)S(1)}, u32[]{:S(2)}, u32[]{:S(2)}) collective-permute-start(bf16[576,256]{1,0:T(8,128)(2,1)S(1)} %place.1.p0), channel_id=1, source_target_pairs={{0,64},{32,96},{64,0},{96,32},{1,65},{33,97},{65,1},{97,33},{2,66}... | collective-permute-start | bytes 884744 | tf_op jit(solution)/shard_map/ppermute | solution.py:582
  60.0 3.6 %collective-permute-start.4 = (bf16[16,32,128]{2,1,0:T(8,128)(2,1)S(1)}, bf16[16,32,128]{2,1,0:T(8,128)(2,1)S(1)}, u32[]{:S(2)}, u32[]{:S(2)}) collective-permute-start(bf16[16,32,128]{2,1,0:T(8,128)(2,1)S(1)} %all_to_all.15.mine_ref), channel_id=1, source_target_pairs={{0,1},{1,0},{2,3},{3,2},{4,5},{5,4},{6,7},{7,6},{8,9},{9,8},{10,11... | collective-permute-start | bytes 393224 | tf_op jit(solution)/shard_map/ppermute | solution.py:647

commit v12 on v9

--- a/solution.py
+++ b/solution.py
@@ -516,14 +516,14 @@
         merge_kernel,
         in_specs=[vmem],
         out_specs=vmem,
-        out_shape=jax.ShapeDtypeStruct((sources, depth - PAD, lanes), jnp.bfloat16),
+        out_shape=jax.ShapeDtypeStruct((2 * sources, depth - PAD, lanes), jnp.bfloat16),
         scratch_shapes=[pltpu.VMEM((sources, PAD, lanes), jnp.float32)],
         compiler_params=params(4),
         name="merge",
     )(parts)
 
 
-def finish_kernel(mine_ref, other_ref, p0, p1, p2, p3, out_ref, cache_hbm, wide_ref, sems):
+def finish_kernel(result_ref, p0, p1, p2, p3, out_ref, cache_hbm, wide_ref, sems):
     group = lax.axis_index("pre")
     copies = []
     for k, (turn, piece) in enumerate(zip(TURNS, (p0, p1, p2, p3))):
@@ -534,20 +534,19 @@
         )
     for copy in copies:
         copy.start()
-    half, heads, lanes = mine_ref.shape
-    core = lax.axis_index("dec") & 1
+    items, heads, lanes = result_ref.shape
 
     def widen(k, carry):
-        for place_at, ref in ((core, mine_ref), (1 - core, other_ref)):
-            item = place_at * half + half - 1 - k
-            at = pl.ds(pl.multiple_of(item * heads, heads), heads)
-            wide_ref[at, :] = ref[k].astype(jnp.float32)
-        return carry
-
-    lax.fori_loop(0, half, widen, 0, unroll=4)
+        device = items - 1 - k
+        item = (device & 1) * (items // 2) + lax.shift_right_logical(device, 1)
+        at = pl.ds(pl.multiple_of(item * heads, heads), heads)
+        wide_ref[at, :] = result_ref[k].astype(jnp.float32)
+        return carry
+
+    lax.fori_loop(0, items, widen, 0, unroll=8)
 
     def body(h, carry):
-        piece = wide_ref[pl.ds(h, 2 * half, stride=heads), :]
+        piece = wide_ref[pl.ds(h, items, stride=heads), :]
         at = pl.multiple_of(h * lanes, lanes)
         out_ref[:, pl.ds(at, lanes)] = piece.astype(out_ref.dtype)
         return carry
@@ -557,25 +556,25 @@
         copy.wait()
 
 
-def finish(mine, other, pieces):
-    half, heads, lanes = mine.shape
+def finish(result, pieces):
+    items, heads, lanes = result.shape
     width, rows = pieces[0].shape
     vmem = pl.BlockSpec(memory_space=pltpu.VMEM)
     return pl.pallas_call(
         finish_kernel,
-        in_specs=[vmem] * 6,
+        in_specs=[vmem] * 5,
         out_specs=[vmem, pl.BlockSpec(memory_space=pl.ANY)],
         out_shape=[
-            jax.ShapeDtypeStruct((2 * half, heads * lanes), mine.dtype),
+            jax.ShapeDtypeStruct((items, heads * lanes), result.dtype),
             jax.ShapeDtypeStruct((width, rows * len(pieces)), pieces[0].dtype),
         ],
         scratch_shapes=[
-            pltpu.VMEM((2 * half * heads, lanes), jnp.float32),
+            pltpu.VMEM((items * heads, lanes), jnp.float32),
             pltpu.SemaphoreType.DMA((len(pieces),)),
         ],
         compiler_params=params(6),
         name="finish",
-    )(mine, other, *pieces)
+    )(result, *pieces)
 
 
 def exchange(piece, groups, turn):
@@ -613,6 +612,7 @@
     steps, batch, heads, _ = query_latent.shape
     items = steps * batch
     plane = [[2 * k + core for k in reversed(range(SIDE * SIDE))] for core in range(2)]
+    everyone = [list(reversed(range(owners)))]
     sibling = [(d, d ^ 1) for d in range(owners)]
 
     produced, packed = produce(
@@ -636,14 +636,13 @@
         chunks,
         w_up_value,
     )
-    arrived = exchanged(packed, axis_index_groups=[list(reversed(range(owners)))])
+    arrived = exchanged(packed, axis_index_groups=everyone)
     quarter = place(arrived, *produced.shape)
     pieces = [quarter] + [exchange(quarter, groups, turn) for turn in TURNS[1:]]
 
     parts = merge_pair(keep, lax.ppermute(send, "dec", sibling))
     result = merge(exchanged(parts, axis_index_groups=plane))
-    result = exchanged(result, axis_index_groups=plane)
-    result, kv_cache = finish(result, lax.ppermute(result, "dec", sibling), pieces)
+    result, kv_cache = finish(exchanged(result, axis_index_groups=everyone), pieces)
     attention_out = result.reshape(steps, batch, -1)
     kv_cache = kv_cache.T
     return (attention_out, kv_cache)

time: 65.4 us -> 65.9 us (level)
  blocking collectives: 10.1 us -> 0 us
  starting transfers between devices: 29 us -> 34.6 us
  waiting for transfers between devices: 4.31 us -> 8.61 us
  Pallas kernels: 19.8 us -> 20.5 us
    all_to_all x1 -> x0, blocking collectives: 10.1 us -> none  [per_device(): result = exchanged(result, axis_index_groups=plane)]
    all_to_all x1 -> x2, starting transfers between devices: 9.08 us -> 17.1 us  [the longest x1 9.08 us: per_device(): arrived = exchanged(packed, axis_index_groups=everyone)]
    all_to_all x1 -> x2, waiting for transfers between devices: 0.01 us -> 2.76 us  [the longest x1 2.76 us: per_device(): exchanged(result, axis_index_groups=everyone)]
    ppermute x5, waiting for transfers between devices: 0.01 us -> 2.53 us  [exchange(): return lax.ppermute(piece, 'pre', [(i, i ^ turn) for i in range(groups)])]
    ppermute x1 -> x0, starting transfers between devices: 2.44 us -> none  [per_device(): lax.ppermute(result, 'dec', sibling)]
    ppermute x1 -> x0, waiting for transfers between devices: 0.97 us -> none  [per_device(): lax.ppermute(result, 'dec', sibling)]
    pallas_call x1, Pallas kernels: 0.44 us -> 1.16 us  [merge(): pl.pallas_call(merge_kernel, in_specs=[vmem], out_specs=vmem, out_shape=j...]
  transfers between devices with their start and end apart: 10 -> 10, of which waited for: 4 -> 5; matrix products, arithmetic and copies ran while one was open for 0% -> 0% of each run, Pallas kernels for 17% -> 18%
where the time goes in v12:
time: 65.9 us; the launch traced here: 65.5 us
  starting transfers between devices  34.6 us (53%)
  Pallas kernels  20.5 us (31%)
  waiting for transfers between devices  8.61 us (13%)
  local copies, waits for them, and re-layouts  0.98 us (1%)
  between operations  0.81 us (1%)
    all_to_all x1, starting transfers between devices, per_device(): arrived = exchanged(packed, axis_index_groups=everyone)  9.08 us
    ppermute x5, starting transfers between devices, exchange(): return lax.ppermute(piece, 'pre', [(i, i ^ turn) for i in range(groups)])  8.61 us
    all_to_all x1, starting transfers between devices, per_device(): exchanged(result, axis_index_groups=everyone)  7.99 us
    all_to_all x1, starting transfers between devices, per_device(): result = merge(exchanged(parts, axis_index_groups=plane))  7.6 us
    pallas_call x1, Pallas kernels, produce(): pl.pallas_call(functools.partial(produce_kernel, groups, owners), in_spec...  6.79 us
    pallas_call x1, Pallas kernels, attend(): pl.pallas_call(far_kernel, in_specs=[vmem] * 8, out_specs=[vmem] * 2, out...  4.56 us
    pallas_call x1, Pallas kernels, attend(): pl.pallas_call(near_kernel, in_specs=[vmem] * 6 + [pl.BlockSpec(memory_sp...  3.48 us
    all_to_all x1, waiting for transfers between devices, per_device(): exchanged(result, axis_index_groups=everyone)  2.76 us
  transfers between devices with their start and end apart: 10, of which 5 were waited for; matrix products, arithmetic and copies ran while one was open for 0% of the time, Pallas kernels for 18%

profile of v12, /device:TPU:1, one launch (start us, length us, event | category | flops | bytes accessed | tf_op | source)
XLA Modules:
  0.0 65.5 jit_solution(18131585212026095208)
XLA Ops:
  0.7 6.8 %produce.1 = (bf16[576,256]{1,0:T(8,128)(2,1)}, bf16[64,8,640]{2,1,0:T(8,128)(2,1)}) custom-call(s32[4]{0:T(128)} %lengths_ref, s32[4096]{0:T(1024)} %dest_hbm.1, bf16[256,7168]{1,0:T(8,128)(2,1)} %hidden_hbm.1, bf16[576,7168]{1,0:T(8,128)(2,1)} %bitcast.10, f32[1,512]{1,0:T(1,128)} %bitcast.11, f32[32,128]{1,0:T(8,128)} %constant.20.clone.freq_hbm), custom_call_target="tpu_custom_call" | custom-call | tf_op jit(solution)/shard_map/produce/pallas_call | solution.py:159
  7.5 4.7 %collective-permute-start = (bf16[576,256]{1,0:T(8,128)(2,1)}, bf16[576,256]{1,0:T(8,128)(2,1)S(1)}, u32[]{:S(2)}, u32[]{:S(2)}) collective-permute-start(bf16[576,256]{1,0:T(8,128)(2,1)} %get-tuple-element.16.own_hbm), channel_id=1, source_target_pairs={{0,96},{32,64},{64,32},{96,0},{1,97},{33,65},{65,33},{97,1},{2,98}... | collective-permute-start | bytes 884744 | tf_op jit(solution)/shard_map/ppermute | solution.py:581
  12.2 9.1 %all-to-all-start.2 = ((bf16[64,8,640]{2,1,0:T(8,128)(2,1)}), bf16[64,8,640]{2,1,0:T(8,128)(2,1)S(1)}, u32[]{:S(2)}, u32[]{:S(2)}) async-start(bf16[64,8,640]{2,1,0:T(8,128)(2,1)} %get-tuple-element.27), calls=%async_computation.2 | async-start | bytes 1310720 | tf_op jit(solution)/shard_map/all_to_all | solution.py:639
  21.2 0.0 collective-permute-done.k1
  21.3 0.0 collective-permute-done.1.k2
  21.3 0.3 collective-permute-start.2
  21.6 1.0 %copy-done.2 = bf16[576,256]{1,0:T(8,128)(2,1)S(1)} copy-done((bf16[576,256]{1,0:T(8,128)(2,1)S(1)}, bf16[576,256]{1,0:T(8,128)(2,1)}, u32[]{:S(2)}) %copy-start.2) | copy-done | bytes 294936
  22.6 1.0 %prepare.1 = (f32[256,768]{1,0:T(8,128)S(1)}, f32[256,256]{1,0:T(8,128)S(1)}, s32[256,128]{1,0:T(8,128)S(1)}, bf16[576,256]{1,0:T(8,128)(2,1)S(1)}) custom-call(s32[4]{0:T(128)S(1)} %copy-done.4, s32[8]{0:T(128)S(1)} %copy-done.5, s32[4,8]{1,0:T(4,128)S(1)} %copy-done.3, bf16[576,256]{1,0:T(8,128)(2,1)S(1)} %copy-done.2), custom_call_target="tpu_custom_call" | custom-call | tf_op jit(solution)/shard_map/prepare/pallas_call | solution.py:270
  23.7 3.5 %attend_near.1 = (f32[4,256,512]{2,1,0:T(8,128)S(1)}, f32[4,256,128]{2,1,0:T(8,128)S(1)}, bf16[32,512,128]{2,1,0:T(8,128)(2,1)S(1)}) custom-call(f32[256,768]{1,0:T(8,128)S(1)} %get-tuple-element.20.bias_ref, bf16[32,4,8,512]{3,2,1,0:T(8,128)(2,1)S(1)} %bitcast.6, bf16[32,4,8,64]{3,2,1,0:T(8,128)(2,1)S(1)} %bitcast.8, ...), custom_call_target="tpu_custom_call" | custom-call | tf_op jit(solution)/shard_map/attend_near/pallas_call | solution.py:423
  27.1 1.3 %collective-permute-done.2.k3 = bf16[576,256]{1,0:T(8,128)(2,1)S(1)} collective-permute-done((bf16[576,256]{1,0:T(8,128)(2,1)S(1)}, bf16[576,256]{1,0:T(8,128)(2,1)S(1)}, u32[]{:S(2)}, u32[]{:S(2)}) %collective-permute-start.2) | collective-permute-done | bytes 294944 | tf_op jit(solution)/shard_map/ppermute | solution.py:594
  28.5 4.6 %attend_far.1 = (f32[16,40,128]{2,1,0:T(8,128)S(1)}, f32[16,40,128]{2,1,0:T(8,128)S(1)}) custom-call(f32[256,256]{1,0:T(8,128)S(1)} %get-tuple-element.18.bias_ref, s32[256,128]{1,0:T(8,128)S(1)} %get-tuple-element.19.valid_ref, bf16[32,4,8,512]{3,2,1,0:T(8,128)(2,1)S(1)} %bitcast.7, bf16[32,4,8,64]{3,2,1,0:T(8,128)(2,1)S(1)} %bitcast.9, ...), custom_call_target="tpu_custom_call" | custom-call | tf_op jit(solution)/shard_map/attend_far/pallas_call | solution.py:437
  33.0 1.0 %collective-permute-start.3 = (f32[16,40,128]{2,1,0:T(8,128)S(1)}, f32[16,40,128]{2,1,0:T(8,128)S(1)}, u32[]{:S(2)}, u32[]{:S(2)}) collective-permute-start(f32[16,40,128]{2,1,0:T(8,128)S(1)} %get-tuple-element.26), channel_id=1, source_target_pairs={{0,1},{1,0},{2,3},{3,2},{4,5},{5,4},{6,7},{7,6},{8,9},{9,8},{10,11... | collective-permute-start | bytes 983048 | tf_op jit(solution)/shard_map/ppermute | solution.py:643
  34.0 1.3 %collective-permute-done.3.other_ref = f32[16,40,128]{2,1,0:T(8,128)S(1)} collective-permute-done((f32[16,40,128]{2,1,0:T(8,128)S(1)}, f32[16,40,128]{2,1,0:T(8,128)S(1)}, u32[]{:S(2)}, u32[]{:S(2)}) %collective-permute-start.3) | collective-permute-done | bytes 327712 | tf_op jit(solution)/shard_map/ppermute | solution.py:643
  35.3 1.2 %merge_pair.1 = f32[16,40,128]{2,1,0:T(8,128)} custom-call(f32[16,40,128]{2,1,0:T(8,128)S(1)} %get-tuple-element.25.mine_ref, f32[16,40,128]{2,1,0:T(8,128)S(1)} %collective-permute-done.3.other_ref), custom_call_target="tpu_custom_call" | custom-call | tf_op jit(solution)/shard_map/merge_pair/pallas_call | solution.py:485
  36.5 7.6 %all-to-all-start = ((f32[16,40,128]{2,1,0:T(8,128)}), f32[16,40,128]{2,1,0:T(8,128)S(1)}, u32[]{:S(2)}, u32[]{:S(2)}) async-start(f32[16,40,128]{2,1,0:T(8,128)} %merge_pair.1), calls=%async_computation | async-start | bytes 655360 | tf_op jit(solution)/shard_map/all_to_all | solution.py:644
  44.1 0.5 place.1.p0
  44.7 1.3 %collective-permute-start.4 = (bf16[576,256]{1,0:T(8,128)(2,1)S(1)}, bf16[576,256]{1,0:T(8,128)(2,1)S(1)}, u32[]{:S(2)}, u32[]{:S(2)}) collective-permute-start(bf16[576,256]{1,0:T(8,128)(2,1)S(1)} %place.1.p0), channel_id=1, source_target_pairs={{0,96},{32,64},{64,32},{96,0},{1,97},{33,65},{65,33},{97,1},{2,98}... | collective-permute-start | bytes 884744 | tf_op jit(solution)/shard_map/ppermute | solution.py:581
  46.0 2.7 %collective-permute-start.6 = (bf16[576,256]{1,0:T(8,128)(2,1)S(1)}, bf16[576,256]{1,0:T(8,128)(2,1)S(1)}, u32[]{:S(2)}, u32[]{:S(2)}) collective-permute-start(bf16[576,256]{1,0:T(8,128)(2,1)S(1)} %place.1.p0), channel_id=1, source_target_pairs={{0,64},{32,96},{64,0},{96,32},{1,65},{33,97},{65,1},{97,33},{2,66}... | collective-permute-start | bytes 884744 | tf_op jit(solution)/shard_map/ppermute | solution.py:581
  48.6 0.7 %all-to-all-done.parts_ref = f32[16,40,128]{2,1,0:T(8,128)S(1)} async-done(((f32[16,40,128]{2,1,0:T(8,128)}), f32[16,40,128]{2,1,0:T(8,128)S(1)}, u32[]{:S(2)}, u32[]{:S(2)}) %all-to-all-start) | async-done | bytes 327712 | tf_op jit(solution)/shard_map/all_to_all | solution.py:644
  49.3 1.2 %merge.1 = bf16[32,32,128]{2,1,0:T(8,128)(2,1)} custom-call(f32[16,40,128]{2,1,0:T(8,128)S(1)} %all-to-all-done.parts_ref), custom_call_target="tpu_custom_call" | custom-call | tf_op jit(solution)/shard_map/merge/pallas_call | solution.py:515
  50.5 8.0 %all-to-all-start.1 = ((bf16[32,32,128]{2,1,0:T(8,128)(2,1)}), bf16[32,32,128]{2,1,0:T(8,128)(2,1)S(1)}, u32[]{:S(2)}, u32[]{:S(2)}) async-start(bf16[32,32,128]{2,1,0:T(8,128)(2,1)} %merge.1), calls=%async_computation.1 | async-start | bytes 524288 | tf_op jit(solution)/shard_map/all_to_all | solution.py:645
  58.5 2.5 %collective-permute-done.6.p3 = bf16[576,256]{1,0:T(8,128)(2,1)S(1)} collective-permute-done((bf16[576,256]{1,0:T(8,128)(2,1)S(1)}, bf16[576,256]{1,0:T(8,128)(2,1)S(1)}, u32[]{:S(2)}, u32[]{:S(2)}) %collective-permute-start.6) | collective-permute-done | bytes 294944 | tf_op jit(solution)/shard_map/ppermute | solution.py:581
  61.0 2.8 %all-to-all-done.1.result_ref = bf16[32,32,128]{2,1,0:T(8,128)(2,1)S(1)} async-done(((bf16[32,32,128]{2,1,0:T(8,128)(2,1)}), bf16[32,32,128]{2,1,0:T(8,128)(2,1)S(1)}, u32[]{:S(2)}, u32[]{:S(2)}) %all-to-all-start.1) | async-done | bytes 262176 | tf_op jit(solution)/shard_map/all_to_all | solution.py:645
  63.8 1.7 %finish.1 = (bf16[32,4096]{1,0:T(8,128)(2,1)}, bf16[576,1024]{1,0:T(8,128)(2,1)}) custom-call(bf16[32,32,128]{2,1,0:T(8,128)(2,1)S(1)} %all-to-all-done.1.result_ref, bf16[576,256]{1,0:T(8,128)(2,1)S(1)} %place.1.p0, bf16[576,256]{1,0:T(8,128)(2,1)S(1)} %collective-permute-done.4.p1, bf16[576,256]{1,0:T(8,128)(2,1)S(1)} %collective-permute-done.5.p2, ...), custom_call_target="tpu_custom_call" | custom-call | tf_op jit(solution)/shard_map/finish/pallas_call | solution.py:563
  (17 shorter events, 0.1 us)
Async XLA Ops:
  0.6 21.0 %copy-start.3 = (s32[4,8]{1,0:T(4,128)S(1)}, s32[4,8]{1,0:T(4,128)}, u32[]{:S(2)}) copy-start(s32[4,8]{1,0:T(4,128)} %position_ref.1) | copy-start | bytes 388
  0.6 21.0 %copy-start.4 = (s32[4]{0:T(128)S(1)}, s32[4]{0:T(128)}, u32[]{:S(2)}) copy-start(s32[4]{0:T(128)} %lengths_ref) | copy-start | bytes 52
  0.7 21.0 %copy-start.5 = (s32[8]{0:T(128)S(1)}, s32[8]{0:T(128)}, u32[]{:S(2)}) copy-start(s32[8]{0:T(128)} %request_ref.1) | copy-start | bytes 100
  0.7 23.0 %copy-start = (bf16[4,8,32,512]{3,2,1,0:T(8,128)(2,1)S(1)}, bf16[4,8,32,512]{3,2,1,0:T(8,128)(2,1)}, u32[]{:S(2)}) copy-start(bf16[4,8,32,512]{3,2,1,0:T(8,128)(2,1)} %param.14) | copy-start | bytes 3145732
  0.7 23.0 %copy-start.1 = (bf16[4,8,32,64]{3,2,1,0:T(8,128)(2,1)S(1)}, bf16[4,8,32,64]{3,2,1,0:T(8,128)(2,1)}, u32[]{:S(2)}) copy-start(bf16[4,8,32,64]{3,2,1,0:T(8,128)(2,1)} %param.15) | copy-start | bytes 393220
  7.5 13.8 %collective-permute-start = (bf16[576,256]{1,0:T(8,128)(2,1)}, bf16[576,256]{1,0:T(8,128)(2,1)S(1)}, u32[]{:S(2)}, u32[]{:S(2)}) collective-permute-start(bf16[576,256]{1,0:T(8,128)(2,1)} %get-tuple-element.16.own_hbm), channel_id=1, source_target_pairs={{0,96},{32,64},{64,32},{96,0},{1,97},{33,65},{65,33},{97,1},{2,98}... | collective-permute-start | bytes 884744 | tf_op jit(solution)/shard_map/ppermute | solution.py:581
  12.1 9.1 %collective-permute-start.1 = (bf16[576,256]{1,0:T(8,128)(2,1)}, bf16[576,256]{1,0:T(8,128)(2,1)S(1)}, u32[]{:S(2)}, u32[]{:S(2)}) collective-permute-start(bf16[576,256]{1,0:T(8,128)(2,1)} %get-tuple-element.16.own_hbm), channel_id=1, source_target_pairs={{0,32},{32,0},{64,96},{96,64},{1,33},{33,1},{65,97},{97,65},{2,34}... | collective-permute-start | bytes 884744 | tf_op jit(solution)/shard_map/ppermute | solution.py:581
  12.2 24.4 %all-to-all-start.2 = ((bf16[64,8,640]{2,1,0:T(8,128)(2,1)}), bf16[64,8,640]{2,1,0:T(8,128)(2,1)S(1)}, u32[]{:S(2)}, u32[]{:S(2)}) async-start(bf16[64,8,640]{2,1,0:T(8,128)(2,1)} %get-tuple-element.27), calls=%async_computation.2 | async-start | bytes 1310720 | tf_op jit(solution)/shard_map/all_to_all | solution.py:639
  21.3 7.2 %collective-permute-start.2 = (bf16[576,256]{1,0:T(8,128)(2,1)S(1)}, bf16[576,256]{1,0:T(8,128)(2,1)S(1)}, u32[]{:S(2)}, u32[]{:S(2)}) collective-permute-start(bf16[576,256]{1,0:T(8,128)(2,1)S(1)} %broadcast_select_fusion), channel_id=1, source_target_pairs={{0,32},{1,97},{2,34},{3,99},{4,36},{5,101},{6,38},{7,103},{8,40},{... | collective-permute-start | bytes 884744 | tf_op jit(solution)/shard_map/ppermute | solution.py:594
  21.6 1.0 %copy-start.2 = (bf16[576,256]{1,0:T(8,128)(2,1)S(1)}, bf16[576,256]{1,0:T(8,128)(2,1)}, u32[]{:S(2)}) copy-start(bf16[576,256]{1,0:T(8,128)(2,1)} %get-tuple-element.16.own_hbm) | copy-start | bytes 884740
  33.0 2.2 %collective-permute-start.3 = (f32[16,40,128]{2,1,0:T(8,128)S(1)}, f32[16,40,128]{2,1,0:T(8,128)S(1)}, u32[]{:S(2)}, u32[]{:S(2)}) collective-permute-start(f32[16,40,128]{2,1,0:T(8,128)S(1)} %get-tuple-element.26), channel_id=1, source_target_pairs={{0,1},{1,0},{2,3},{3,2},{4,5},{5,4},{6,7},{7,6},{8,9},{9,8},{10,11... | collective-permute-start | bytes 983048 | tf_op jit(solution)/shard_map/ppermute | solution.py:643
  36.5 12.8 %all-to-all-start = ((f32[16,40,128]{2,1,0:T(8,128)}), f32[16,40,128]{2,1,0:T(8,128)S(1)}, u32[]{:S(2)}, u32[]{:S(2)}) async-start(f32[16,40,128]{2,1,0:T(8,128)} %merge_pair.1), calls=%async_computation | async-start | bytes 655360 | tf_op jit(solution)/shard_map/all_to_all | solution.py:644
  44.7 13.8 %collective-permute-start.4 = (bf16[576,256]{1,0:T(8,128)(2,1)S(1)}, bf16[576,256]{1,0:T(8,128)(2,1)S(1)}, u32[]{:S(2)}, u32[]{:S(2)}) collective-permute-start(bf16[576,256]{1,0:T(8,128)(2,1)S(1)} %place.1.p0), channel_id=1, source_target_pairs={{0,96},{32,64},{64,32},{96,0},{1,97},{33,65},{65,33},{97,1},{2,98}... | collective-permute-start | bytes 884744 | tf_op jit(solution)/shard_map/ppermute | solution.py:581
  45.9 12.6 %collective-permute-start.5 = (bf16[576,256]{1,0:T(8,128)(2,1)S(1)}, bf16[576,256]{1,0:T(8,128)(2,1)S(1)}, u32[]{:S(2)}, u32[]{:S(2)}) collective-permute-start(bf16[576,256]{1,0:T(8,128)(2,1)S(1)} %place.1.p0), channel_id=1, source_target_pairs={{0,32},{32,0},{64,96},{96,64},{1,33},{33,1},{65,97},{97,65},{2,34}... | collective-permute-start | bytes 884744 | tf_op jit(solution)/shard_map/ppermute | solution.py:581
  46.0 15.1 %collective-permute-start.6 = (bf16[576,256]{1,0:T(8,128)(2,1)S(1)}, bf16[576,256]{1,0:T(8,128)(2,1)S(1)}, u32[]{:S(2)}, u32[]{:S(2)}) collective-permute-start(bf16[576,256]{1,0:T(8,128)(2,1)S(1)} %place.1.p0), channel_id=1, source_target_pairs={{0,64},{32,96},{64,0},{96,32},{1,65},{33,97},{65,1},{97,33},{2,66}... | collective-permute-start | bytes 884744 | tf_op jit(solution)/shard_map/ppermute | solution.py:581
  50.5 13.3 %all-to-all-start.1 = ((bf16[32,32,128]{2,1,0:T(8,128)(2,1)}), bf16[32,32,128]{2,1,0:T(8,128)(2,1)S(1)}, u32[]{:S(2)}, u32[]{:S(2)}) async-start(bf16[32,32,128]{2,1,0:T(8,128)(2,1)} %merge.1), calls=%async_computation.1 | async-start | bytes 524288 | tf_op jit(solution)/shard_map/all_to_all | solution.py:645

commit v13 on v12

--- a/solution.py
+++ b/solution.py
@@ -523,7 +523,7 @@
     )(parts)
 
 
-def finish_kernel(result_ref, p0, p1, p2, p3, out_ref, cache_hbm, wide_ref, sems):
+def assemble_kernel(p0, p1, p2, p3, cache_hbm, sems):
     group = lax.axis_index("pre")
     copies = []
     for k, (turn, piece) in enumerate(zip(TURNS, (p0, p1, p2, p3))):
@@ -534,6 +534,24 @@
         )
     for copy in copies:
         copy.start()
+    for copy in copies:
+        copy.wait()
+
+
+def assemble(pieces):
+    width, rows = pieces[0].shape
+    return pl.pallas_call(
+        assemble_kernel,
+        in_specs=[pl.BlockSpec(memory_space=pltpu.VMEM)] * 4,
+        out_specs=pl.BlockSpec(memory_space=pl.ANY),
+        out_shape=jax.ShapeDtypeStruct((width, rows * len(pieces)), pieces[0].dtype),
+        scratch_shapes=[pltpu.SemaphoreType.DMA((len(pieces),))],
+        compiler_params=params(4),
+        name="assemble",
+    )(*pieces)
+
+
+def spread_kernel(result_ref, out_ref, wide_ref):
     items, heads, lanes = result_ref.shape
 
     def widen(k, carry):
@@ -552,29 +570,20 @@
         return carry
 
     lax.fori_loop(0, heads, body, 0, unroll=4)
-    for copy in copies:
-        copy.wait()
-
-
-def finish(result, pieces):
+
+
+def spread(result):
     items, heads, lanes = result.shape
-    width, rows = pieces[0].shape
     vmem = pl.BlockSpec(memory_space=pltpu.VMEM)
     return pl.pallas_call(
-        finish_kernel,
-        in_specs=[vmem] * 5,
-        out_specs=[vmem, pl.BlockSpec(memory_space=pl.ANY)],
-        out_shape=[
-            jax.ShapeDtypeStruct((items, heads * lanes), result.dtype),
-            jax.ShapeDtypeStruct((width, rows * len(pieces)), pieces[0].dtype),
-        ],
-        scratch_shapes=[
-            pltpu.VMEM((items * heads, lanes), jnp.float32),
-            pltpu.SemaphoreType.DMA((len(pieces),)),
-        ],
-        compiler_params=params(6),
-        name="finish",
-    )(result, *pieces)
+        spread_kernel,
+        in_specs=[vmem],
+        out_specs=vmem,
+        out_shape=jax.ShapeDtypeStruct((items, heads * lanes), result.dtype),
+        scratch_shapes=[pltpu.VMEM((items * heads, lanes), jnp.float32)],
+        compiler_params=params(4),
+        name="spread",
+    )(result)
 
 
 def exchange(piece, groups, turn):
@@ -642,7 +651,8 @@
 
     parts = merge_pair(keep, lax.ppermute(send, "dec", sibling))
     result = merge(exchanged(parts, axis_index_groups=plane))
-    result, kv_cache = finish(exchanged(result, axis_index_groups=everyone), pieces)
+    kv_cache = assemble(pieces)
+    result = spread(exchanged(result, axis_index_groups=everyone))
     attention_out = result.reshape(steps, batch, -1)
     kv_cache = kv_cache.T
     return (attention_out, kv_cache)

time: 65.9 us -> 65.4 us (level)
  waiting for transfers between devices: 8.61 us -> 7.57 us
    all_to_all x1, waiting for transfers between devices: 2.76 us -> 1.71 us  [per_device(): result = spread(exchanged(result, axis_index_groups=everyone))]
    pallas_call x1 -> x2, Pallas kernels: 1.74 us -> 2.19 us  [the longest x1 1.15 us: spread(): pl.pallas_call(spread_kernel, in_specs=[vmem], out_specs=vmem, out_shape=...]
  transfers between devices with their start and end apart: 10 -> 10, of which waited for: 5 -> 5; matrix products, arithmetic and copies ran while one was open for 0% -> 0% of each run, Pallas kernels for 18% -> 20%
where the time goes in v13:
time: 65.4 us; the launch traced here: 65 us
  starting transfers between devices  34.6 us (53%)
  Pallas kernels  21 us (32%)
  waiting for transfers between devices  7.57 us (12%)
  local copies, waits for them, and re-layouts  0.98 us (1%)
  between operations  0.81 us (1%)
    all_to_all x1, starting transfers between devices, per_device(): arrived = exchanged(packed, axis_index_groups=everyone)  9.08 us
    ppermute x5, starting transfers between devices, exchange(): return lax.ppermute(piece, 'pre', [(i, i ^ turn) for i in range(groups)])  8.61 us
    all_to_all x1, starting transfers between devices, per_device(): result = spread(exchanged(result, axis_index_groups=everyone))  7.99 us
    all_to_all x1, starting transfers between devices, per_device(): result = merge(exchanged(parts, axis_index_groups=plane))  7.6 us
    pallas_call x1, Pallas kernels, produce(): pl.pallas_call(functools.partial(produce_kernel, groups, owners), in_spec...  6.79 us
    pallas_call x1, Pallas kernels, attend(): pl.pallas_call(far_kernel, in_specs=[vmem] * 8, out_specs=[vmem] * 2, out...  4.56 us
    pallas_call x1, Pallas kernels, attend(): pl.pallas_call(near_kernel, in_specs=[vmem] * 6 + [pl.BlockSpec(memory_sp...  3.48 us
    ppermute x5, waiting for transfers between devices, exchange(): return lax.ppermute(piece, 'pre', [(i, i ^ turn) for i in range(groups)])  2.54 us
  transfers between devices with their start and end apart: 10, of which 5 were waited for; matrix products, arithmetic and copies ran while one was open for 0% of the time, Pallas kernels for 20%

profile of v13, /device:TPU:1, one launch (start us, length us, event | category | flops | bytes accessed | tf_op | source)
XLA Modules:
  0.0 65.0 jit_solution(5453970032663104039)
XLA Ops:
  0.7 6.8 %produce.1 = (bf16[576,256]{1,0:T(8,128)(2,1)}, bf16[64,8,640]{2,1,0:T(8,128)(2,1)}) custom-call(s32[4]{0:T(128)} %lengths_ref, s32[4096]{0:T(1024)} %dest_hbm.1, bf16[256,7168]{1,0:T(8,128)(2,1)} %hidden_hbm.1, bf16[576,7168]{1,0:T(8,128)(2,1)} %bitcast.10, f32[1,512]{1,0:T(1,128)} %bitcast.13, f32[32,128]{1,0:T(8,128)} %constant.20.clone.freq_hbm), custom_call_target="tpu_custom_call" | custom-call | tf_op jit(solution)/shard_map/produce/pallas_call | solution.py:159
  7.5 4.7 %collective-permute-start = (bf16[576,256]{1,0:T(8,128)(2,1)}, bf16[576,256]{1,0:T(8,128)(2,1)S(1)}, u32[]{:S(2)}, u32[]{:S(2)}) collective-permute-start(bf16[576,256]{1,0:T(8,128)(2,1)} %get-tuple-element.14.own_hbm), channel_id=1, source_target_pairs={{0,96},{32,64},{64,32},{96,0},{1,97},{33,65},{65,33},{97,1},{2,98}... | collective-permute-start | bytes 884744 | tf_op jit(solution)/shard_map/ppermute | solution.py:590
  12.1 0.0 collective-permute-start.1
  12.2 9.1 %all-to-all-start.2 = ((bf16[64,8,640]{2,1,0:T(8,128)(2,1)}), bf16[64,8,640]{2,1,0:T(8,128)(2,1)S(1)}, u32[]{:S(2)}, u32[]{:S(2)}) async-start(bf16[64,8,640]{2,1,0:T(8,128)(2,1)} %get-tuple-element.25), calls=%async_computation.2 | async-start | bytes 1310720 | tf_op jit(solution)/shard_map/all_to_all | solution.py:648
  21.3 0.3 collective-permute-start.2
  21.6 1.0 %copy-done.2 = bf16[576,256]{1,0:T(8,128)(2,1)S(1)} copy-done((bf16[576,256]{1,0:T(8,128)(2,1)S(1)}, bf16[576,256]{1,0:T(8,128)(2,1)}, u32[]{:S(2)}) %copy-start.2) | copy-done | bytes 294936
  22.6 1.0 %prepare.1 = (f32[256,768]{1,0:T(8,128)S(1)}, f32[256,256]{1,0:T(8,128)S(1)}, s32[256,128]{1,0:T(8,128)S(1)}, bf16[576,256]{1,0:T(8,128)(2,1)S(1)}) custom-call(s32[4]{0:T(128)S(1)} %copy-done.4, s32[8]{0:T(128)S(1)} %copy-done.5, s32[4,8]{1,0:T(4,128)S(1)} %copy-done.3, bf16[576,256]{1,0:T(8,128)(2,1)S(1)} %copy-done.2), custom_call_target="tpu_custom_call" | custom-call | tf_op jit(solution)/shard_map/prepare/pallas_call | solution.py:270
  23.7 3.5 %attend_near.1 = (f32[4,256,512]{2,1,0:T(8,128)S(1)}, f32[4,256,128]{2,1,0:T(8,128)S(1)}, bf16[32,512,128]{2,1,0:T(8,128)(2,1)S(1)}) custom-call(f32[256,768]{1,0:T(8,128)S(1)} %get-tuple-element.18.bias_ref, bf16[32,4,8,512]{3,2,1,0:T(8,128)(2,1)S(1)} %bitcast.6, bf16[32,4,8,64]{3,2,1,0:T(8,128)(2,1)S(1)} %bitcast.8, ...), custom_call_target="tpu_custom_call" | custom-call | tf_op jit(solution)/shard_map/attend_near/pallas_call | solution.py:423
  27.1 1.3 %collective-permute-done.2.k3 = bf16[576,256]{1,0:T(8,128)(2,1)S(1)} collective-permute-done((bf16[576,256]{1,0:T(8,128)(2,1)S(1)}, bf16[576,256]{1,0:T(8,128)(2,1)S(1)}, u32[]{:S(2)}, u32[]{:S(2)}) %collective-permute-start.2) | collective-permute-done | bytes 294944 | tf_op jit(solution)/shard_map/ppermute | solution.py:603
  28.5 4.6 %attend_far.1 = (f32[16,40,128]{2,1,0:T(8,128)S(1)}, f32[16,40,128]{2,1,0:T(8,128)S(1)}) custom-call(f32[256,256]{1,0:T(8,128)S(1)} %get-tuple-element.16.bias_ref, s32[256,128]{1,0:T(8,128)S(1)} %get-tuple-element.17.valid_ref, bf16[32,4,8,512]{3,2,1,0:T(8,128)(2,1)S(1)} %bitcast.7, bf16[32,4,8,64]{3,2,1,0:T(8,128)(2,1)S(1)} %bitcast.9, ...), custom_call_target="tpu_custom_call" | custom-call | tf_op jit(solution)/shard_map/attend_far/pallas_call | solution.py:437
  33.0 1.0 %collective-permute-start.3 = (f32[16,40,128]{2,1,0:T(8,128)S(1)}, f32[16,40,128]{2,1,0:T(8,128)S(1)}, u32[]{:S(2)}, u32[]{:S(2)}) collective-permute-start(f32[16,40,128]{2,1,0:T(8,128)S(1)} %get-tuple-element.24), channel_id=1, source_target_pairs={{0,1},{1,0},{2,3},{3,2},{4,5},{5,4},{6,7},{7,6},{8,9},{9,8},{10,11... | collective-permute-start | bytes 983048 | tf_op jit(solution)/shard_map/ppermute | solution.py:652
  34.0 1.3 %collective-permute-done.3.other_ref = f32[16,40,128]{2,1,0:T(8,128)S(1)} collective-permute-done((f32[16,40,128]{2,1,0:T(8,128)S(1)}, f32[16,40,128]{2,1,0:T(8,128)S(1)}, u32[]{:S(2)}, u32[]{:S(2)}) %collective-permute-start.3) | collective-permute-done | bytes 327712 | tf_op jit(solution)/shard_map/ppermute | solution.py:652
  35.3 1.2 %merge_pair.1 = f32[16,40,128]{2,1,0:T(8,128)} custom-call(f32[16,40,128]{2,1,0:T(8,128)S(1)} %get-tuple-element.23.mine_ref, f32[16,40,128]{2,1,0:T(8,128)S(1)} %collective-permute-done.3.other_ref), custom_call_target="tpu_custom_call" | custom-call | tf_op jit(solution)/shard_map/merge_pair/pallas_call | solution.py:485
  36.5 7.6 %all-to-all-start = ((f32[16,40,128]{2,1,0:T(8,128)}), f32[16,40,128]{2,1,0:T(8,128)S(1)}, u32[]{:S(2)}, u32[]{:S(2)}) async-start(f32[16,40,128]{2,1,0:T(8,128)} %merge_pair.1), calls=%async_computation | async-start | bytes 655360 | tf_op jit(solution)/shard_map/all_to_all | solution.py:653
  44.1 0.5 place.1.p0
  44.7 1.3 %collective-permute-start.4 = (bf16[576,256]{1,0:T(8,128)(2,1)S(1)}, bf16[576,256]{1,0:T(8,128)(2,1)S(1)}, u32[]{:S(2)}, u32[]{:S(2)}) collective-permute-start(bf16[576,256]{1,0:T(8,128)(2,1)S(1)} %place.1.p0), channel_id=1, source_target_pairs={{0,96},{32,64},{64,32},{96,0},{1,97},{33,65},{65,33},{97,1},{2,98}... | collective-permute-start | bytes 884744 | tf_op jit(solution)/shard_map/ppermute | solution.py:590
  46.0 2.7 %collective-permute-start.6 = (bf16[576,256]{1,0:T(8,128)(2,1)S(1)}, bf16[576,256]{1,0:T(8,128)(2,1)S(1)}, u32[]{:S(2)}, u32[]{:S(2)}) collective-permute-start(bf16[576,256]{1,0:T(8,128)(2,1)S(1)} %place.1.p0), channel_id=1, source_target_pairs={{0,64},{32,96},{64,0},{96,32},{1,65},{33,97},{65,1},{97,33},{2,66}... | collective-permute-start | bytes 884744 | tf_op jit(solution)/shard_map/ppermute | solution.py:590
  48.6 0.7 %all-to-all-done.parts_ref = f32[16,40,128]{2,1,0:T(8,128)S(1)} async-done(((f32[16,40,128]{2,1,0:T(8,128)}), f32[16,40,128]{2,1,0:T(8,128)S(1)}, u32[]{:S(2)}, u32[]{:S(2)}) %all-to-all-start) | async-done | bytes 327712 | tf_op jit(solution)/shard_map/all_to_all | solution.py:653
  49.4 1.2 %merge.1 = bf16[32,32,128]{2,1,0:T(8,128)(2,1)} custom-call(f32[16,40,128]{2,1,0:T(8,128)S(1)} %all-to-all-done.parts_ref), custom_call_target="tpu_custom_call" | custom-call | tf_op jit(solution)/shard_map/merge/pallas_call | solution.py:515
  50.5 8.0 %all-to-all-start.1 = ((bf16[32,32,128]{2,1,0:T(8,128)(2,1)}), bf16[32,32,128]{2,1,0:T(8,128)(2,1)S(1)}, u32[]{:S(2)}, u32[]{:S(2)}) async-start(bf16[32,32,128]{2,1,0:T(8,128)(2,1)} %merge.1), calls=%async_computation.1 | async-start | bytes 524288 | tf_op jit(solution)/shard_map/all_to_all | solution.py:655
  58.5 2.5 %collective-permute-done.6.p3 = bf16[576,256]{1,0:T(8,128)(2,1)S(1)} collective-permute-done((bf16[576,256]{1,0:T(8,128)(2,1)S(1)}, bf16[576,256]{1,0:T(8,128)(2,1)S(1)}, u32[]{:S(2)}, u32[]{:S(2)}) %collective-permute-start.6) | collective-permute-done | bytes 294944 | tf_op jit(solution)/shard_map/ppermute | solution.py:590
  61.0 1.0 %assemble.1 = bf16[576,1024]{1,0:T(8,128)(2,1)} custom-call(bf16[576,256]{1,0:T(8,128)(2,1)S(1)} %place.1.p0, bf16[576,256]{1,0:T(8,128)(2,1)S(1)} %collective-permute-done.4.p1, bf16[576,256]{1,0:T(8,128)(2,1)S(1)} %collective-permute-done.5.p2, bf16[576,256]{1,0:T(8,128)(2,1)S(1)} %collective-permute-done.6.p3), custom_call_target="tpu_custom_call" | custom-call | tf_op jit(solution)/shard_map/assemble/pallas_call | solution.py:543
  62.1 1.7 %all-to-all-done.1.result_ref = bf16[32,32,128]{2,1,0:T(8,128)(2,1)S(1)} async-done(((bf16[32,32,128]{2,1,0:T(8,128)(2,1)}), bf16[32,32,128]{2,1,0:T(8,128)(2,1)S(1)}, u32[]{:S(2)}, u32[]{:S(2)}) %all-to-all-start.1) | async-done | bytes 262176 | tf_op jit(solution)/shard_map/all_to_all | solution.py:655
  63.8 1.2 %spread.1 = bf16[32,4096]{1,0:T(8,128)(2,1)} custom-call(bf16[32,32,128]{2,1,0:T(8,128)(2,1)S(1)} %all-to-all-done.1.result_ref), custom_call_target="tpu_custom_call" | custom-call | tf_op jit(solution)/shard_map/spread/pallas_call | solution.py:578
  (18 shorter events, 0.1 us)
Async XLA Ops:
  0.6 21.0 %copy-start.3 = (s32[4,8]{1,0:T(4,128)S(1)}, s32[4,8]{1,0:T(4,128)}, u32[]{:S(2)}) copy-start(s32[4,8]{1,0:T(4,128)} %position_ref.1) | copy-start | bytes 388
  0.6 21.0 %copy-start.4 = (s32[4]{0:T(128)S(1)}, s32[4]{0:T(128)}, u32[]{:S(2)}) copy-start(s32[4]{0:T(128)} %lengths_ref) | copy-start | bytes 52
  0.7 21.0 %copy-start.5 = (s32[8]{0:T(128)S(1)}, s32[8]{0:T(128)}, u32[]{:S(2)}) copy-start(s32[8]{0:T(128)} %request_ref.1) | copy-start | bytes 100
  0.7 23.0 %copy-start = (bf16[4,8,32,512]{3,2,1,0:T(8,128)(2,1)S(1)}, bf16[4,8,32,512]{3,2,1,0:T(8,128)(2,1)}, u32[]{:S(2)}) copy-start(bf16[4,8,32,512]{3,2,1,0:T(8,128)(2,1)} %param.14) | copy-start | bytes 3145732
  0.7 23.0 %copy-start.1 = (bf16[4,8,32,64]{3,2,1,0:T(8,128)(2,1)S(1)}, bf16[4,8,32,64]{3,2,1,0:T(8,128)(2,1)}, u32[]{:S(2)}) copy-start(bf16[4,8,32,64]{3,2,1,0:T(8,128)(2,1)} %param.15) | copy-start | bytes 393220
  7.5 13.8 %collective-permute-start = (bf16[576,256]{1,0:T(8,128)(2,1)}, bf16[576,256]{1,0:T(8,128)(2,1)S(1)}, u32[]{:S(2)}, u32[]{:S(2)}) collective-permute-start(bf16[576,256]{1,0:T(8,128)(2,1)} %get-tuple-element.14.own_hbm), channel_id=1, source_target_pairs={{0,96},{32,64},{64,32},{96,0},{1,97},{33,65},{65,33},{97,1},{2,98}... | collective-permute-start | bytes 884744 | tf_op jit(solution)/shard_map/ppermute | solution.py:590
  12.1 9.1 %collective-permute-start.1 = (bf16[576,256]{1,0:T(8,128)(2,1)}, bf16[576,256]{1,0:T(8,128)(2,1)S(1)}, u32[]{:S(2)}, u32[]{:S(2)}) collective-permute-start(bf16[576,256]{1,0:T(8,128)(2,1)} %get-tuple-element.14.own_hbm), channel_id=1, source_target_pairs={{0,32},{32,0},{64,96},{96,64},{1,33},{33,1},{65,97},{97,65},{2,34}... | collective-permute-start | bytes 884744 | tf_op jit(solution)/shard_map/ppermute | solution.py:590
  12.2 24.4 %all-to-all-start.2 = ((bf16[64,8,640]{2,1,0:T(8,128)(2,1)}), bf16[64,8,640]{2,1,0:T(8,128)(2,1)S(1)}, u32[]{:S(2)}, u32[]{:S(2)}) async-start(bf16[64,8,640]{2,1,0:T(8,128)(2,1)} %get-tuple-element.25), calls=%async_computation.2 | async-start | bytes 1310720 | tf_op jit(solution)/shard_map/all_to_all | solution.py:648
  21.3 7.2 %collective-permute-start.2 = (bf16[576,256]{1,0:T(8,128)(2,1)S(1)}, bf16[576,256]{1,0:T(8,128)(2,1)S(1)}, u32[]{:S(2)}, u32[]{:S(2)}) collective-permute-start(bf16[576,256]{1,0:T(8,128)(2,1)S(1)} %broadcast_select_fusion), channel_id=1, source_target_pairs={{0,32},{1,97},{2,34},{3,99},{4,36},{5,101},{6,38},{7,103},{8,40},{... | collective-permute-start | bytes 884744 | tf_op jit(solution)/shard_map/ppermute | solution.py:603
  21.6 1.0 %copy-start.2 = (bf16[576,256]{1,0:T(8,128)(2,1)S(1)}, bf16[576,256]{1,0:T(8,128)(2,1)}, u32[]{:S(2)}) copy-start(bf16[576,256]{1,0:T(8,128)(2,1)} %get-tuple-element.14.own_hbm) | copy-start | bytes 884740
  33.0 2.2 %collective-permute-start.3 = (f32[16,40,128]{2,1,0:T(8,128)S(1)}, f32[16,40,128]{2,1,0:T(8,128)S(1)}, u32[]{:S(2)}, u32[]{:S(2)}) collective-permute-start(f32[16,40,128]{2,1,0:T(8,128)S(1)} %get-tuple-element.24), channel_id=1, source_target_pairs={{0,1},{1,0},{2,3},{3,2},{4,5},{5,4},{6,7},{7,6},{8,9},{9,8},{10,11... | collective-permute-start | bytes 983048 | tf_op jit(solution)/shard_map/ppermute | solution.py:652
  36.5 12.8 %all-to-all-start = ((f32[16,40,128]{2,1,0:T(8,128)}), f32[16,40,128]{2,1,0:T(8,128)S(1)}, u32[]{:S(2)}, u32[]{:S(2)}) async-start(f32[16,40,128]{2,1,0:T(8,128)} %merge_pair.1), calls=%async_computation | async-start | bytes 655360 | tf_op jit(solution)/shard_map/all_to_all | solution.py:653
  44.7 13.8 %collective-permute-start.4 = (bf16[576,256]{1,0:T(8,128)(2,1)S(1)}, bf16[576,256]{1,0:T(8,128)(2,1)S(1)}, u32[]{:S(2)}, u32[]{:S(2)}) collective-permute-start(bf16[576,256]{1,0:T(8,128)(2,1)S(1)} %place.1.p0), channel_id=1, source_target_pairs={{0,96},{32,64},{64,32},{96,0},{1,97},{33,65},{65,33},{97,1},{2,98}... | collective-permute-start | bytes 884744 | tf_op jit(solution)/shard_map/ppermute | solution.py:590
  46.0 12.6 %collective-permute-start.5 = (bf16[576,256]{1,0:T(8,128)(2,1)S(1)}, bf16[576,256]{1,0:T(8,128)(2,1)S(1)}, u32[]{:S(2)}, u32[]{:S(2)}) collective-permute-start(bf16[576,256]{1,0:T(8,128)(2,1)S(1)} %place.1.p0), channel_id=1, source_target_pairs={{0,32},{32,0},{64,96},{96,64},{1,33},{33,1},{65,97},{97,65},{2,34}... | collective-permute-start | bytes 884744 | tf_op jit(solution)/shard_map/ppermute | solution.py:590
  46.0 15.1 %collective-permute-start.6 = (bf16[576,256]{1,0:T(8,128)(2,1)S(1)}, bf16[576,256]{1,0:T(8,128)(2,1)S(1)}, u32[]{:S(2)}, u32[]{:S(2)}) collective-permute-start(bf16[576,256]{1,0:T(8,128)(2,1)S(1)} %place.1.p0), channel_id=1, source_target_pairs={{0,64},{32,96},{64,0},{96,32},{1,65},{33,97},{65,1},{97,33},{2,66}... | collective-permute-start | bytes 884744 | tf_op jit(solution)/shard_map/ppermute | solution.py:590
  50.5 13.3 %all-to-all-start.1 = ((bf16[32,32,128]{2,1,0:T(8,128)(2,1)}), bf16[32,32,128]{2,1,0:T(8,128)(2,1)S(1)}, u32[]{:S(2)}, u32[]{:S(2)}) async-start(bf16[32,32,128]{2,1,0:T(8,128)(2,1)} %merge.1), calls=%async_computation.1 | async-start | bytes 524288 | tf_op jit(solution)/shard_map/all_to_all | solution.py:655
